TPU v7x, 32 devices: a whole 2x2x4 slice. The times are simulated.
32 devices in a mesh: section: 2 (over core), batch: 4 (over z), tensor: 4 (over y, x).
Axes of the slice: x: 2, y: 2, z: 4, core: 2. Of those that a mesh axis runs over, the one named last changes fastest.
Arguments:
- token_ids: int32 [8, 1024], P('batch'), may hold values from 0 to 32767
- seq_lengths: int32 [8], P('batch'), may hold values from 64 to 1024, as said below
- embed_table: float32 [32768, 768], P(('section', 'tensor'), 'batch'), may hold values from -0.21875 to 0.21875
- norm_gains: float32 [2, 2, 768], P(None, None, ('section', 'batch', 'tensor')), may hold values from 0.5 to 1.5
- final_gain: float32 [768], P(('section', 'batch', 'tensor')), may hold values from 0.5 to 1.5
- qkv_weight: float32 [2, 768, 3, 768], P('section', 'batch', None, 'tensor'), may hold values from -0.21875 to 0.21875
- qkv_conv: float32 [2, 3, 3, 12, 64], P('section', None, None, 'tensor', 'batch'), may hold values from -3 to 3
- out_weight: float32 [2, 768, 768], P('section', 'tensor', 'batch'), may hold values from -2.5 to 2.5
- up_weight: float32 [2, 768, 3072], P('section', 'batch', 'tensor'), may hold values from -0.21875 to 0.21875
- down_weight: float32 [2, 3072, 768], P('section', 'tensor', 'batch'), may hold values from -0.109375 to 0.109375
- logit_grad: bfloat16 [8, 1024, 32768], P('batch', None, ('section', 'tensor')), may hold values from -6 to 6
Outputs:
- logits: bfloat16 [8, 1024, 32768], P('batch', None, ('section', 'tensor'))
- table_grad: float32 [32768, 768], P(('section', 'tensor'), 'batch')
- gains_grad: float32 [2, 2, 768], P(None, None, ('section', 'batch', 'tensor'))
- final_gain_grad: float32 [768], P(('section', 'batch', 'tensor'))
- qkv_grad: float32 [2, 768, 3, 768], P('section', 'batch', None, 'tensor')
- conv_grad: float32 [2, 3, 3, 12, 64], P('section', None, None, 'tensor', 'batch')
- out_grad: float32 [2, 768, 768], P('section', 'tensor', 'batch')
- up_grad: float32 [2, 768, 3072], P('section', 'batch', 'tensor')
- down_grad: float32 [2, 3072, 768], P('section', 'tensor', 'batch')
Inputs may be any that keep to these rules, and one draw needn't show every extreme that they name: `seq_lengths`: among the 2 sequences of each index of batch (aligned blocks of 2) at least one has length 1024.
All inputs are finite; a program needn't handle non-finite values.
Results may differ from a plain program's by a relative error of at most 0.025.
Values may be sent and summed in bfloat16 or wider, within the bound.
A program may use at most 192 MiB of HBM per device.

v0:
```python
import math

import jax
import jax.numpy as jnp
from jax import lax
from jax.sharding import PartitionSpec as P

D = 768
HEAD = 64


norm_eps = 1e-06
masked_score = -1e30


def swapped(block, axis, bit):
    count = lax.axis_size(axis)
    route = []
    for low in range(count):
        high = low | 1 << bit
        if high != low and high < count:
            route += [(low, high), (high, low)]
    return lax.ppermute(block, axis, route)


def rms_norm(values, gain):
    factor = lax.rsqrt(jnp.mean(values * values, axis=-1, keepdims=True) + norm_eps)
    return values * factor * gain


def contract_rows(left, right):
    return lax.dot_general(
        left, right, (((0,), (0,)), ((), ())), preferred_element_type=jnp.float32
    )


def contract_columns(left, right):
    return lax.dot_general(
        left, right, (((1,), (1,)), ((), ())), preferred_element_type=jnp.float32
    )


def gather_rows(rows):
    return lax.all_gather(rows, "tensor", axis=0, tiled=True)


def summed_rows(left, right, flipped):

    def term():
        if flipped:
            return contract_columns(left, right)
        return jnp.dot(left, right, preferred_element_type=jnp.float32)

    return lax.psum_scatter(
        term().astype(jnp.bfloat16), "tensor", scatter_dimension=0, tiled=True
    ).astype(jnp.float32)


def causal_mix(projected, taps):
    once = jnp.pad(projected, ((1, 0), (0, 0)))[:-1]
    twice = jnp.pad(projected, ((2, 0), (0, 0)))[:-2]
    return taps[0] * projected + taps[1] * once + taps[2] * twice


def causal_mix_back(grad, projected, taps):
    ahead_one = jnp.pad(grad, ((0, 1), (0, 0)))[1:]
    ahead_two = jnp.pad(grad, ((0, 2), (0, 0)))[2:]
    grad_in = taps[0] * grad + taps[1] * ahead_one + taps[2] * ahead_two
    once = jnp.pad(projected, ((1, 0), (0, 0)))[:-1]
    twice = jnp.pad(projected, ((2, 0), (0, 0)))[:-2]
    grad_taps = jnp.stack(
        [jnp.sum(grad * projected, 0), jnp.sum(grad * once, 0), jnp.sum(grad * twice, 0)]
    )
    return (grad_in, grad_taps)


def allowed_keys(lead, reach, length):
    query_at = jnp.arange(lead, reach)[:, None]
    key_at = jnp.arange(reach)[None, :]
    return (key_at <= query_at) & (key_at < length)


def attend(queries, keys_all, values_all, length):
    total = queries.shape[0]
    block = min(512, total)
    factor = queries.shape[-1] ** (-0.5)
    outputs = []
    totals = []
    for index in range(total // block):
        lead = index * block
        reach = lead + block
        scores = (
            jnp.einsum(
                "qhd,khd->hqk",
                queries[lead:reach],
                keys_all[:reach],
                preferred_element_type=jnp.float32,
            )
            * factor
        )
        scores = jnp.where(allowed_keys(lead, reach, length)[None], scores, masked_score)
        peak = jnp.max(scores, axis=-1, keepdims=True)
        raised = jnp.exp(scores - peak)
        weight_sum = jnp.sum(raised, axis=-1, keepdims=True)
        probs = (raised / weight_sum).astype(jnp.bfloat16)
        result = jnp.einsum(
            "hqk,khd->qhd", probs, values_all[:reach], preferred_element_type=jnp.float32
        )
        outputs.append(result.astype(jnp.bfloat16))
        totals.append((peak + jnp.log(weight_sum))[..., 0])
    return (jnp.concatenate(outputs, 0), jnp.concatenate(totals, 1))


def attend_back(grad_out, queries, keys_all, values_all, length, totals):
    total = queries.shape[0]
    block = min(512, total)
    factor = queries.shape[-1] ** (-0.5)
    grad_queries = []
    grad_keys = jnp.zeros(keys_all.shape, jnp.float32)
    grad_values = jnp.zeros(values_all.shape, jnp.float32)
    for index in range(total // block):
        lead = index * block
        reach = lead + block
        scores = (
            jnp.einsum(
                "qhd,khd->hqk",
                queries[lead:reach],
                keys_all[:reach],
                preferred_element_type=jnp.float32,
            )
            * factor
        )
        allowed = allowed_keys(lead, reach, length)[None]
        probs = jnp.where(allowed, jnp.exp(scores - totals[:, lead:reach, None]), 0.0)
        grad_block = grad_out[lead:reach]
        grad_probs = jnp.einsum(
            "qhd,khd->hqk", grad_block, values_all[:reach], preferred_element_type=jnp.float32
        )
        inner = jnp.sum(probs * grad_probs, axis=-1, keepdims=True)
        grad_scores = (probs * (grad_probs - inner)).astype(jnp.bfloat16)
        grad_queries.append(
            jnp.einsum(
                "hqk,khd->qhd", grad_scores, keys_all[:reach], preferred_element_type=jnp.float32
            )
            * factor
        )
        grad_keys = grad_keys.at[:reach].add(
            jnp.einsum(
                "hqk,qhd->khd", grad_scores, queries[lead:reach], preferred_element_type=jnp.float32
            )
            * factor
        )
        grad_values = grad_values.at[:reach].add(
            jnp.einsum(
                "hqk,qhd->khd",
                probs.astype(jnp.bfloat16),
                grad_block,
                preferred_element_type=jnp.float32,
            )
        )
    return (jnp.concatenate(grad_queries, 0), grad_keys, grad_values)


def layer_forward(resid, length, weights):
    gain_attn, gain_ffn, qkv_mat, taps, out_mat, up_mat, down_mat = weights
    local_width = out_mat.shape[0]
    heads_here = local_width // HEAD
    normed = rms_norm(resid, gain_attn).astype(jnp.bfloat16)
    gathered = gather_rows(normed)
    projected = jnp.dot(gathered, qkv_mat, preferred_element_type=jnp.float32)
    mixed = causal_mix(projected, taps).astype(jnp.bfloat16)
    triple = mixed.reshape(-1, 3, heads_here, HEAD)
    context, totals = attend(triple[:, 0], triple[:, 1], triple[:, 2], length)
    context = context.reshape(-1, local_width)
    middle = resid + summed_rows(context, out_mat, False)
    normed_ffn = rms_norm(middle, gain_ffn).astype(jnp.bfloat16)
    gathered_ffn = gather_rows(normed_ffn)
    hidden = jnp.dot(gathered_ffn, up_mat, preferred_element_type=jnp.float32)
    active = jnp.square(jnp.maximum(hidden, 0.0)).astype(jnp.bfloat16)
    output = middle + summed_rows(active, down_mat, False)
    kept = (resid, gathered, projected, mixed, context, totals, middle, gathered_ffn, hidden)
    return (output, kept)


def layer_backward(grad_out, length, weights, kept):
    gain_attn, gain_ffn, qkv_mat, taps, out_mat, up_mat, down_mat = weights
    resid, gathered, projected, mixed, context, totals, middle, gathered_ffn, hidden = kept
    local_width = out_mat.shape[0]
    heads_here = local_width // HEAD
    grad_rows = gather_rows(grad_out.astype(jnp.bfloat16))
    active = jnp.square(jnp.maximum(hidden, 0.0)).astype(jnp.bfloat16)
    grad_down = contract_rows(active, grad_rows)
    grad_active = contract_columns(grad_rows, down_mat)
    grad_hidden = (grad_active * 2.0 * jnp.maximum(hidden, 0.0)).astype(jnp.bfloat16)
    grad_up = contract_rows(gathered_ffn, grad_hidden)
    grad_normed_ffn = summed_rows(grad_hidden, up_mat, True)
    ffn_pull = jax.vjp(rms_norm, middle, gain_ffn)[1]
    grad_middle_norm, grad_gain_ffn = ffn_pull(grad_normed_ffn)
    grad_middle = grad_out + grad_middle_norm
    grad_rows_attn = gather_rows(grad_middle.astype(jnp.bfloat16))
    grad_outmat = contract_rows(context, grad_rows_attn)
    grad_context = (
        contract_columns(grad_rows_attn, out_mat).astype(jnp.bfloat16).reshape(-1, heads_here, HEAD)
    )
    triple = mixed.reshape(-1, 3, heads_here, HEAD)
    grad_queries, grad_keys, grad_values = attend_back(
        grad_context, triple[:, 0], triple[:, 1], triple[:, 2], length, totals
    )
    grad_mixed = jnp.stack([grad_queries, grad_keys, grad_values], 1).reshape(-1, 3 * local_width)
    grad_projected, grad_taps = causal_mix_back(grad_mixed, projected, taps)
    grad_projected = grad_projected.astype(jnp.bfloat16)
    grad_qkv = contract_rows(gathered, grad_projected)
    grad_normed = summed_rows(grad_projected, qkv_mat, True)
    attn_pull = jax.vjp(rms_norm, resid, gain_attn)[1]
    grad_resid_norm, grad_gain_attn = attn_pull(grad_normed)
    grad_in = grad_middle + grad_resid_norm
    return (
        grad_in,
        (grad_gain_attn, grad_gain_ffn, grad_qkv, grad_taps, grad_outmat, grad_up, grad_down),
    )


def head_pass(rows, final_scale, table_slice, grad_logits, length):
    normed = rms_norm(rows, final_scale).astype(jnp.bfloat16)
    gathered = gather_rows(normed)
    logits = contract_columns(gathered, table_slice)
    positions = jnp.arange(gathered.shape[0])
    grad_masked = jnp.where((positions < length)[:, None], grad_logits, jnp.zeros((), jnp.bfloat16))
    grad_normed = summed_rows(grad_masked, table_slice, False)
    grad_table = contract_rows(grad_masked, gathered)
    norm_pull = jax.vjp(rms_norm, rows, final_scale)[1]
    grad_rows, grad_gain = norm_pull(grad_normed)
    return (logits.astype(jnp.bfloat16), grad_rows, grad_table, grad_gain)


def pick_section(first, early_item, late_item):
    return jax.tree.map(lambda left, right: jnp.where(first, left, right), early_item, late_item)


def send_back(message):
    return swapped(message.astype(jnp.bfloat16), "section", 0).astype(message.dtype)


def on_device(
    token_ids,
    seq_lengths,
    embed_table,
    norm_gains,
    final_gain,
    qkv_weight,
    qkv_conv,
    out_weight,
    up_weight,
    down_weight,
    logit_grad,
):
    section = lax.axis_index("section")
    first = section == 0
    tensor_at = lax.axis_index("tensor")
    tensor_count = lax.axis_size("tensor")
    section_count = lax.axis_size("section")
    micro_count = token_ids.shape[0]
    slot_length = token_ids.shape[1]
    half_count = micro_count // 2
    shard_rows = slot_length // tensor_count
    root_scale = math.sqrt(D)
    qkv_gathered, conv_gathered, out_gathered, up_gathered, down_gathered, table_slice = (
        lax.all_gather(qkv_weight.astype(jnp.bfloat16), "batch", axis=1, tiled=True),
        lax.all_gather(qkv_conv.astype(jnp.bfloat16), "batch", axis=4, tiled=True),
        lax.all_gather(out_weight.astype(jnp.bfloat16), "batch", axis=2, tiled=True),
        lax.all_gather(up_weight.astype(jnp.bfloat16), "batch", axis=1, tiled=True),
        lax.all_gather(down_weight.astype(jnp.bfloat16), "batch", axis=2, tiled=True),
        lax.all_gather(embed_table.astype(jnp.bfloat16), "batch", axis=1, tiled=True),
    )
    gains_all, final_all = (
        lax.all_gather(
            norm_gains.astype(jnp.bfloat16), ("section", "batch", "tensor"), axis=2, tiled=True
        ),
        lax.all_gather(
            final_gain.astype(jnp.bfloat16), ("section", "batch", "tensor"), axis=0, tiled=True
        ),
    )
    local_width = qkv_gathered.shape[3]
    heads_here = conv_gathered.shape[3]
    layer_gains = lax.dynamic_index_in_dim(gains_all, section, 0, keepdims=False).astype(
        jnp.float32
    )
    final_scale = final_all.astype(jnp.float32)
    taps = (
        conv_gathered[0]
        .astype(jnp.float32)
        .reshape(3, 3, local_width)
        .transpose(1, 0, 2)
        .reshape(3, 3 * local_width)
    )
    weights = (
        layer_gains[0],
        layer_gains[1],
        qkv_gathered[0].reshape(D, 3 * local_width),
        taps,
        out_gathered[0],
        up_gathered[0],
        down_gathered[0],
    )
    vocab_rows = table_slice.shape[0]
    ordered = (
        token_ids.reshape(section_count, half_count, tensor_count, shard_rows)
        .transpose(0, 2, 1, 3)
        .reshape(-1)
    )
    owner_start = (section * tensor_count + tensor_at) * vocab_rows
    local_ids = ordered - owner_start
    inside = (local_ids >= 0) & (local_ids < vocab_rows)
    safe_ids = jnp.clip(local_ids, 0, vocab_rows - 1)
    picked = jnp.where(inside[:, None], table_slice[safe_ids], jnp.zeros((), jnp.bfloat16)).astype(
        jnp.float32
    )
    embedded = (
        lax.psum_scatter(
            picked.astype(jnp.bfloat16), ("section", "tensor"), scatter_dimension=0, tiled=True
        )
        .astype(jnp.float32)
        .reshape(half_count, shard_rows, D)
    )
    zero_rows = jnp.zeros((shard_rows, D), jnp.bfloat16)
    received = (zero_rows, zero_rows)
    kept_list = []
    final_rows = []
    for tick in range(micro_count + 1):
        if tick < half_count:
            from_embed = embedded[tick]
        else:
            from_embed = received[0].astype(jnp.float32)
        section_input = jnp.where(first, from_embed * root_scale, received[0].astype(jnp.float32))
        length = jnp.where(
            first, seq_lengths[min(tick, micro_count - 1)], seq_lengths[max(tick - 1, 0)]
        )
        output, kept = layer_forward(section_input, length, weights)
        kept_list.append(kept)
        sent = output.astype(jnp.bfloat16)
        upcoming = tick + 1 - half_count
        if 0 <= upcoming < half_count:
            from_second = embedded[upcoming].astype(jnp.bfloat16)
        else:
            from_second = zero_rows
        received = swapped((jnp.where(first, sent, from_second), sent), "section", 0)
        if tick >= 1:
            final_rows.append(jnp.where(first, received[1], sent).astype(jnp.float32))
    logits_parts = []
    own_head = []
    head_table = jnp.zeros((vocab_rows, D), jnp.float32)
    final_gain_sum = jnp.zeros((D,), jnp.float32)
    for index in range(micro_count):
        logits_part, grad_rows, grad_table, grad_gain = head_pass(
            final_rows[index], final_scale, table_slice, logit_grad[index], seq_lengths[index]
        )
        logits_parts.append(logits_part)
        own_head.append(grad_rows)
        head_table = head_table + grad_table
        final_gain_sum = final_gain_sum + grad_gain
    zero_grads = jnp.zeros((shard_rows, D), jnp.float32)
    received_back = send_back(jnp.where(first, jnp.stack([own_head[0], zero_grads]), 0.0))
    grad_totals = None
    first_pieces = [None] * half_count
    second_pieces = [None] * half_count
    for tick in range(micro_count + 1):
        to_first = received_back[0] if tick >= 1 else zero_grads
        to_second = own_head[tick] + received_back[0] if tick < micro_count else zero_grads
        grad_out = jnp.where(first, to_first, to_second)
        chosen = pick_section(
            first, kept_list[max(tick - 1, 0)], kept_list[min(tick + 1, micro_count)]
        )
        length = jnp.where(
            first, seq_lengths[max(tick - 1, 0)], seq_lengths[min(tick, micro_count - 1)]
        )
        grad_in, grads = layer_backward(grad_out, length, weights, chosen)
        if grad_totals is None:
            grad_totals = grads
        else:
            grad_totals = jax.tree.map(lambda left, right: left + right, grad_totals, grads)
        embed_grad = (grad_in * root_scale).astype(jnp.bfloat16)
        if 1 <= tick <= half_count:
            first_pieces[tick - 1] = embed_grad
        ahead = own_head[tick + 1] if tick + 1 < micro_count else zero_grads
        behind = embed_grad.astype(jnp.float32) if tick - 1 >= half_count else zero_grads
        front = jnp.where(first, ahead, grad_in.astype(jnp.bfloat16).astype(jnp.float32))
        rear = jnp.where(first, behind, zero_grads)
        received_back = send_back(jnp.stack([front, rear]))
        if tick - 1 >= half_count:
            second_pieces[tick - 1 - half_count] = received_back[1].astype(jnp.bfloat16)
    pieces = jnp.concatenate(
        [
            jnp.where(first, early_piece, late_piece)
            for early_piece, late_piece in zip(first_pieces, second_pieces)
        ],
        0,
    )
    all_grads = lax.all_gather(pieces, ("section", "tensor"), axis=0, tiled=True)
    grad_gain_attn, grad_gain_ffn, grad_qkv, grad_taps, grad_outmat, grad_up, grad_down = (
        grad_totals
    )
    qkv_part = grad_qkv.reshape(1, D, 3, local_width)
    conv_part = grad_taps.reshape(3, 3, heads_here, HEAD).transpose(1, 0, 2, 3)[None]
    out_part = grad_outmat[None]
    up_part = grad_up[None]
    down_part = grad_down[None]
    layer_gain = jnp.stack([grad_gain_attn, grad_gain_ffn])
    placed = jnp.where((jnp.arange(section_count) == section)[:, None, None], layer_gain[None], 0.0)
    gains_done, final_done = (
        lax.psum_scatter(placed, ("section", "batch", "tensor"), scatter_dimension=2, tiled=True),
        lax.psum_scatter(
            final_gain_sum, ("section", "batch", "tensor"), scatter_dimension=0, tiled=True
        ),
    )
    embed_part = (
        jnp.zeros((vocab_rows, D), jnp.float32)
        .at[safe_ids]
        .add(jnp.where(inside[:, None], all_grads.astype(jnp.float32), 0.0))
    )
    qkv_done, conv_done, out_done, up_done, down_done, table_done = (
        lax.psum_scatter(
            qkv_part.astype(jnp.bfloat16), "batch", scatter_dimension=1, tiled=True
        ).astype(jnp.float32),
        lax.psum_scatter(
            conv_part.astype(jnp.bfloat16), "batch", scatter_dimension=4, tiled=True
        ).astype(jnp.float32),
        lax.psum_scatter(
            out_part.astype(jnp.bfloat16), "batch", scatter_dimension=2, tiled=True
        ).astype(jnp.float32),
        lax.psum_scatter(
            up_part.astype(jnp.bfloat16), "batch", scatter_dimension=1, tiled=True
        ).astype(jnp.float32),
        lax.psum_scatter(
            down_part.astype(jnp.bfloat16), "batch", scatter_dimension=2, tiled=True
        ).astype(jnp.float32),
        lax.psum_scatter(
            (head_table + embed_part).astype(jnp.bfloat16), "batch", scatter_dimension=1, tiled=True
        ).astype(jnp.float32),
    )
    return (
        jnp.stack(logits_parts),
        table_done,
        gains_done,
        final_done,
        qkv_done,
        conv_done,
        out_done,
        up_done,
        down_done,
    )


def solution(mesh):
    in_specs = (
        P("batch", None),
        P("batch"),
        P(("section", "tensor"), "batch"),
        P(None, None, ("section", "batch", "tensor")),
        P(("section", "batch", "tensor")),
        P("section", "batch", None, "tensor"),
        P("section", None, None, "tensor", "batch"),
        P("section", "tensor", "batch"),
        P("section", "batch", "tensor"),
        P("section", "tensor", "batch"),
        P("batch", None, ("section", "tensor")),
    )
    out_specs = (
        P("batch", None, ("section", "tensor")),
        P(("section", "tensor"), "batch"),
        P(None, None, ("section", "batch", "tensor")),
        P(("section", "batch", "tensor")),
        P("section", "batch", None, "tensor"),
        P("section", None, None, "tensor", "batch"),
        P("section", "tensor", "batch"),
        P("section", "batch", "tensor"),
        P("section", "tensor", "batch"),
    )
    return jax.shard_map(
        on_device, mesh=mesh, in_specs=in_specs, out_specs=out_specs, check_vma=False
    )
```

profile of v0, /device:TPU:0, one launch (start us, length us, event | category | flops | bytes accessed | tf_op | source)
XLA Modules:
  0.0 1709.0 jit_solution(2363739791018547496)
XLA Ops:
  10.7 118.0 %all-gather.19.cloned.1.call-done = bf16[4096,768]{0,1:T(8,128)(2,1)} async-done(((bf16[4096,192]{0,1:T(8,128)(2,1)}), bf16[4096,768]{0,1:T(8,128)(2,1)}) %all-gather.19.cloned.1.call-update) | async-done | bytes 6291472 | tf_op jit(solution)/shard_map/all_gather | solution.py:273
  128.7 8.6 copy.100
  137.3 12.1 gather_fusion
  152.1 67.9 %all_gather.71 = bf16[2,2,768]{1,0,2:T(2,128)(2,1)S(1)} all-gather(bf16[2,2,24]{1,0,2:T(2,128)(2,1)S(1)} %copy.104), channel_id=1, replica_groups=mesh['section'=2,'batch'=4,'tensor'=4] {'section','batch','tensor'}, dimensions={2}, use_global_device_ids=true | all-gather | bytes 6336 | tf_op jit(solution)/shard_map/all_gather | solution.py:276
  231.5 14.0 all_gather.70
  246.6 16.3 all_gather.74
  264.6 26.3 %all_gather.73 = bf16[1,768,3,192]{3,2,0,1:T(4,128)(2,1)S(1)} all-gather(bf16[1,192,3,192]{3,2,0,1:T(4,128)(2,1)S(1)} %copy.105), channel_id=1, replica_groups=mesh['section'=2,'batch'=4,'tensor'=4] {'batch'}, dimensions={1}, use_global_device_ids=true | all-gather | bytes 1105920 | tf_op jit(solution)/shard_map/all_gather | solution.py:268
  312.7 28.2 %reduce-scatter.33.cloned.1.call-done = bf16[256,768]{1,0:T(8,128)(2,1)} async-done(((bf16[1024,768]{1,0:T(8,128)(2,1)}), bf16[256,768]{1,0:T(8,128)(2,1)}) %reduce-scatter.33.cloned.1.call-update) | async-done | bytes 393232 | tf_op jit(solution)/shard_map/reduce_scatter | solution.py:54
  345.0 28.4 %all-gather.25.cloned.1.call-done = bf16[1,768,768]{2,1,0:T(8,128)(2,1)} async-done(((bf16[1,192,768]{2,1,0:T(8,128)(2,1)}), bf16[1,768,768]{2,1,0:T(8,128)(2,1)}) %all-gather.25.cloned.1.call-update) | async-done | bytes 1179664 | tf_op jit(solution)/shard_map/all_gather | solution.py:271
  373.4 32.5 %all-gather.23.cloned.1.call-done = bf16[1024,768]{1,0:T(8,128)(2,1)} async-done(((bf16[256,768]{1,0:T(8,128)(2,1)}), bf16[1024,768]{1,0:T(8,128)(2,1)}) %all-gather.23.cloned.1.call-update) | async-done | bytes 1572880 | tf_op jit(solution)/shard_map/all_gather | solution.py:44
  409.0 29.0 %all-gather.27.cloned.1.call-done = bf16[1,768,768]{1,2,0:T(8,128)(2,1)} async-done(((bf16[1,768,192]{1,2,0:T(8,128)(2,1)}), bf16[1,768,768]{1,2,0:T(8,128)(2,1)}) %all-gather.27.cloned.1.call-update) | async-done | bytes 1179664 | tf_op jit(solution)/shard_map/all_gather | solution.py:272
  441.9 30.2 %reduce-scatter.35.cloned.1.call-done = bf16[256,768]{1,0:T(8,128)(2,1)} async-done(((bf16[1024,768]{1,0:T(8,128)(2,1)}), bf16[256,768]{1,0:T(8,128)(2,1)}) %reduce-scatter.35.cloned.1.call-update) | async-done | bytes 393232 | tf_op jit(solution)/shard_map/reduce_scatter | solution.py:54
  477.8 30.2 %all-gather.29.cloned.1.call-done = bf16[1024,768]{1,0:T(8,128)(2,1)} async-done(((bf16[256,768]{1,0:T(8,128)(2,1)}), bf16[1024,768]{1,0:T(8,128)(2,1)}) %all-gather.29.cloned.1.call-update) | async-done | bytes 1572880 | tf_op jit(solution)/shard_map/all_gather | solution.py:44
  525.3 31.0 %reduce-scatter.37.cloned.1.call-done = bf16[256,768]{1,0:T(8,128)(2,1)} async-done(((bf16[1024,768]{1,0:T(8,128)(2,1)}), bf16[256,768]{1,0:T(8,128)(2,1)}) %reduce-scatter.37.cloned.1.call-update) | async-done | bytes 393232 | tf_op jit(solution)/shard_map/reduce_scatter | solution.py:54
  561.1 30.7 %all-gather.31.cloned.1.call-done = bf16[1024,768]{1,0:T(8,128)(2,1)} async-done(((bf16[256,768]{1,0:T(8,128)(2,1)}), bf16[1024,768]{1,0:T(8,128)(2,1)}) %all-gather.31.cloned.1.call-update) | async-done | bytes 1572880 | tf_op jit(solution)/shard_map/all_gather | solution.py:44
  599.3 12.1 fusion.82
  611.5 18.8 %reduce-scatter.39.cloned.1.call-done = bf16[256,768]{1,0:T(8,128)(2,1)} async-done(((bf16[1024,768]{1,0:T(8,128)(2,1)}), bf16[256,768]{1,0:T(8,128)(2,1)}) %reduce-scatter.39.cloned.1.call-update) | async-done | bytes 393232 | tf_op jit(solution)/shard_map/reduce_scatter | solution.py:54
  634.0 39.6 %all-reduce.27 = bf16[768]{0:T(1024)(128)(2,1)} all-reduce(bf16[768]{0:T(1024)(128)(2,1)S(1)} %dynamic-update-slice.30), channel_id=1, replica_groups=mesh['section'=2,'batch'=4,'tensor'=4] {'section','batch','tensor'}, use_global_device_ids=true, to_apply=%add.27 | all-reduce | flops 768 | bytes 3072
  702.0 16.6 all-gather.41.cloned.1.call-done
  727.2 24.9 %all-gather.35.cloned.1.call-done = bf16[1024,768]{1,0:T(8,128)(2,1)} async-done(((bf16[256,768]{1,0:T(8,128)(2,1)}), bf16[1024,768]{1,0:T(8,128)(2,1)}) %all-gather.35.cloned.1.call-update) | async-done | bytes 1572880 | tf_op jit(solution)/shard_map/all_gather | solution.py:44
  770.0 16.1 reduce-scatter.49.cloned.1.call-done
  804.4 18.8 %all-gather.43.cloned.1.call-done = bf16[1024,768]{1,0:T(8,128)(2,1)} async-done(((bf16[256,768]{1,0:T(8,128)(2,1)}), bf16[1024,768]{1,0:T(8,128)(2,1)}) %all-gather.43.cloned.1.call-update) | async-done | bytes 1572880 | tf_op jit(solution)/shard_map/all_gather | solution.py:44
  857.8 34.8 %reduce-scatter.51.cloned.1.call-done = bf16[256,768]{1,0:T(8,128)(2,1)} async-done(((bf16[1024,768]{1,0:T(8,128)(2,1)}), bf16[256,768]{1,0:T(8,128)(2,1)}) %reduce-scatter.51.cloned.1.call-update) | async-done | bytes 393232 | tf_op jit(solution)/shard_map/reduce_scatter | solution.py:54
  898.0 31.1 %all-gather.37.cloned.1.call-done = bf16[1024,768]{1,0:T(8,128)(2,1)} async-done(((bf16[256,768]{1,0:T(8,128)(2,1)}), bf16[1024,768]{1,0:T(8,128)(2,1)}) %all-gather.37.cloned.1.call-update) | async-done | bytes 1572880 | tf_op jit(solution)/shard_map/all_gather | solution.py:44
  936.8 12.1 fusion.81
  948.9 18.9 %reduce-scatter.43.cloned.1.call-done = bf16[256,768]{1,0:T(8,128)(2,1)} async-done(((bf16[1024,768]{1,0:T(8,128)(2,1)}), bf16[256,768]{1,0:T(8,128)(2,1)}) %reduce-scatter.43.cloned.1.call-update) | async-done | bytes 393232 | tf_op jit(solution)/shard_map/reduce_scatter | solution.py:54
  973.0 29.5 %reduce-scatter.45.cloned.1.call-done = bf16[256,768]{1,0:T(8,128)(2,1)} async-done(((bf16[1024,768]{1,0:T(8,128)(2,1)}), bf16[256,768]{1,0:T(8,128)(2,1)}) %reduce-scatter.45.cloned.1.call-update) | async-done | bytes 393232 | tf_op jit(solution)/shard_map/reduce_scatter | solution.py:54
  1012.1 31.1 %all-gather.45.cloned.1.call-done = bf16[1024,768]{1,0:T(8,128)(2,1)} async-done(((bf16[256,768]{1,0:T(8,128)(2,1)}), bf16[1024,768]{1,0:T(8,128)(2,1)}) %all-gather.45.cloned.1.call-update) | async-done | bytes 1572880 | tf_op jit(solution)/shard_map/all_gather | solution.py:44
  1051.6 30.2 %reduce-scatter.53.cloned.1.call-done = bf16[256,768]{1,0:T(8,128)(2,1)} async-done(((bf16[1024,768]{1,0:T(8,128)(2,1)}), bf16[256,768]{1,0:T(8,128)(2,1)}) %reduce-scatter.53.cloned.1.call-update) | async-done | bytes 393232 | tf_op jit(solution)/shard_map/reduce_scatter | solution.py:54
  1100.4 18.7 %all-gather.47.cloned.1.call-done = bf16[1024,768]{1,0:T(8,128)(2,1)} async-done(((bf16[256,768]{1,0:T(8,128)(2,1)}), bf16[1024,768]{1,0:T(8,128)(2,1)}) %all-gather.47.cloned.1.call-update) | async-done | bytes 1572880 | tf_op jit(solution)/shard_map/all_gather | solution.py:44
  1145.7 29.8 %reduce-scatter.55.cloned.1.call-done = bf16[256,768]{1,0:T(8,128)(2,1)} async-done(((bf16[1024,768]{1,0:T(8,128)(2,1)}), bf16[256,768]{1,0:T(8,128)(2,1)}) %reduce-scatter.55.cloned.1.call-update) | async-done | bytes 393232 | tf_op jit(solution)/shard_map/reduce_scatter | solution.py:54
  1185.5 31.1 %all-gather.49.cloned.1.call-done = bf16[1024,768]{1,0:T(8,128)(2,1)} async-done(((bf16[256,768]{1,0:T(8,128)(2,1)}), bf16[1024,768]{1,0:T(8,128)(2,1)}) %all-gather.49.cloned.1.call-update) | async-done | bytes 1572880 | tf_op jit(solution)/shard_map/all_gather | solution.py:44
  1224.8 31.0 %reduce-scatter.57.cloned.1.call-done = bf16[256,768]{1,0:T(8,128)(2,1)} async-done(((bf16[1024,768]{1,0:T(8,128)(2,1)}), bf16[256,768]{1,0:T(8,128)(2,1)}) %reduce-scatter.57.cloned.1.call-update) | async-done | bytes 393232 | tf_op jit(solution)/shard_map/reduce_scatter | solution.py:54
  1265.6 25.8 %all-gather.51.cloned.1.call-done = bf16[1024,768]{1,0:T(8,128)(2,1)} async-done(((bf16[256,768]{1,0:T(8,128)(2,1)}), bf16[1024,768]{1,0:T(8,128)(2,1)}) %all-gather.51.cloned.1.call-update) | async-done | bytes 1572880 | tf_op jit(solution)/shard_map/all_gather | solution.py:44
  1318.7 29.0 %reduce-scatter.59.cloned.1.call-done = bf16[256,768]{1,0:T(8,128)(2,1)} async-done(((bf16[1024,768]{1,0:T(8,128)(2,1)}), bf16[256,768]{1,0:T(8,128)(2,1)}) %reduce-scatter.59.cloned.1.call-update) | async-done | bytes 393232 | tf_op jit(solution)/shard_map/reduce_scatter | solution.py:54
  1380.7 12.7 fusion.30
  1413.7 14.6 convolution_add_fusion
  1428.3 20.3 %all-gather.53.cloned.1.call-done = bf16[2048,768]{1,0:T(8,128)(2,1)} async-done(((bf16[256,768]{1,0:T(8,128)(2,1)}), bf16[2048,768]{1,0:T(8,128)(2,1)}) %all-gather.53.cloned.1.call-update) | async-done | bytes 3145744 | tf_op jit(solution)/shard_map/all_gather | solution.py:398
  1448.6 25.1 %scatter_custom_fusion = f32[4096,768]{1,0:T(8,128)} fusion(f32[4096,768]{1,0:T(8,128)} %convolution_add_fusion, s32[2048]{0:T(1024)} %bitcast.561, bf16[2048,768]{1,0:T(8,128)(2,1)} %all-gather.53.cloned.1.call-done, f32[]{:T(128)} %constant.381.clone.1, pred[2048]{0:T(1024)(128)(4,1)S(1)} %copy-done.115), kind=kCustom, calls=%fused_computation.8 | custom fusion | flops 4718592 | bytes 15731200 | tf_op jit(solution)/shard_map/scatter-add | solution.py:418
  1473.6 7.8 convert_element_type.591
  1481.5 8.5 copy.137
  1491.4 10.0 convert_bitcast_fusion.1
  1501.5 9.9 convert_bitcast_fusion
  1522.9 8.0 reduce-scatter.67.cloned.1.call-done
  1532.5 19.9 %reduce-scatter.69.cloned.1.call-done = bf16[192,192]{1,0:T(8,128)(2,1)} async-done(((bf16[768,192]{1,0:T(8,128)(2,1)}), bf16[192,192]{1,0:T(8,128)(2,1)}) %reduce-scatter.69.cloned.1.call-update) | async-done | bytes 73744
  1554.2 28.7 %reduce-scatter.61.cloned.1.call-done = bf16[1,192,3,192]{3,1,2,0:T(8,128)(2,1)} async-done(((bf16[1,768,3,192]{3,1,2,0:T(8,128)(2,1)}), bf16[1,192,3,192]{3,1,2,0:T(8,128)(2,1)}) %reduce-scatter.61.cloned.1.call-update) | async-done | bytes 221200 | tf_op jit(solution)/shard_map/reduce_scatter | solution.py:421
  1584.9 42.7 %all-reduce.30 = (f32[2,2,768]{2,1,0:T(2,128)S(1)}, f32[768]{0:T(1024)S(1)}) all-reduce(f32[2,2,768]{2,1,0:T(2,128)S(1)} %broadcast_select_fusion.11, f32[768]{0:T(1024)S(1)} %add.626), channel_id=18, replica_groups=mesh['section'=2,'batch'=4,'tensor'=4] {'section','batch','tensor'}, use_global_device_ids=true, to_apply=%region_63.64.clone | all-reduce | flops 3840 | bytes 30720
  1628.8 66.9 %reduce-scatter.65.cloned.1.call-done = bf16[192,4096]{1,0:T(8,128)(2,1)} async-done(((bf16[768,4096]{1,0:T(8,128)(2,1)}), bf16[192,4096]{1,0:T(8,128)(2,1)}) %reduce-scatter.65.cloned.1.call-update) | async-done | bytes 1572880
  (703 shorter events, 410.8 us)
Async XLA Ops:
  7.2 121.5 %all-gather.19.cloned.1.call-start = ((), (), s32[]{:S(2)}) async-start(), calls=%async_computation.21 | async-start | bytes 7864320 | tf_op jit(solution)/shard_map/all_gather | solution.py:273
  10.5 214.4 %reduce-scatter.31.cloned.1.call-start = ((), (), s32[]{:S(2)}) async-start(), calls=%async_computation.22 | async-start | bytes 3538944 | tf_op jit(solution)/shard_map/reduce_scatter | solution.py:319
  151.3 145.9 %all-gather.21.cloned.1.call-start = ((), (), s32[]{:S(2)}) async-start(), calls=%async_computation.23 | async-start | bytes 1966080 | tf_op jit(solution)/shard_map/all_gather | solution.py:44
  228.1 112.8 %reduce-scatter.33.cloned.1.call-start = ((), (), s32[]{:S(2)}) async-start(), calls=%async_computation.24 | async-start | bytes 1966080 | tf_op jit(solution)/shard_map/reduce_scatter | solution.py:54
  246.0 264.9 %copy-start.80 = (f32[576]{0:T(1024)}, f32[576]{0:T(1024)S(1)}, u32[]{:S(2)}) copy-start(f32[576]{0:T(1024)S(1)} %mul.839) | copy-start | bytes 6916
  311.6 61.7 %all-gather.25.cloned.1.call-start = ((), (), s32[]{:S(2)}) async-start(), calls=%async_computation.26 | async-start | bytes 1474560 | tf_op jit(solution)/shard_map/all_gather | solution.py:271
  312.5 93.5 %all-gather.23.cloned.1.call-start = ((), (), s32[]{:S(2)}) async-start(), calls=%async_computation.25 | async-start | bytes 1966080 | tf_op jit(solution)/shard_map/all_gather | solution.py:44
  344.1 93.9 %all-gather.27.cloned.1.call-start = ((), (), s32[]{:S(2)}) async-start(), calls=%async_computation.27 | async-start | bytes 1474560 | tf_op jit(solution)/shard_map/all_gather | solution.py:272
  344.9 127.2 %reduce-scatter.35.cloned.1.call-start = ((), (), s32[]{:S(2)}) async-start(), calls=%async_computation.28 | async-start | bytes 1966080 | tf_op jit(solution)/shard_map/reduce_scatter | solution.py:54
  441.9 66.1 %all-gather.29.cloned.1.call-start = ((), (), s32[]{:S(2)}) async-start(), calls=%async_computation.29 | async-start | bytes 1966080 | tf_op jit(solution)/shard_map/all_gather | solution.py:44
  473.4 1.8 collective-permute-start
  476.9 79.5 %reduce-scatter.37.cloned.1.call-start = ((), (), s32[]{:S(2)}) async-start(), calls=%async_computation.30 | async-start | bytes 1966080 | tf_op jit(solution)/shard_map/reduce_scatter | solution.py:54
  525.3 66.5 %all-gather.31.cloned.1.call-start = ((), (), s32[]{:S(2)}) async-start(), calls=%async_computation.31 | async-start | bytes 1966080 | tf_op jit(solution)/shard_map/all_gather | solution.py:44
  560.6 69.7 %reduce-scatter.39.cloned.1.call-start = ((), (), s32[]{:S(2)}) async-start(), calls=%async_computation.32 | async-start | bytes 1966080 | tf_op jit(solution)/shard_map/reduce_scatter | solution.py:54
  599.2 78.1 %reduce-scatter.47.cloned.1.call-start = ((), (), s32[]{:S(2)}) async-start(), calls=%async_computation.40 | async-start | bytes 1966080 | tf_op jit(solution)/shard_map/reduce_scatter | solution.py:54
  611.4 107.2 %all-gather.41.cloned.1.call-start = ((), (), s32[]{:S(2)}) async-start(), calls=%async_computation.41 | async-start | bytes 1966080 | tf_op jit(solution)/shard_map/all_gather | solution.py:44
  632.6 41.7 %collective-permute-start.1 = (bf16[256,768]{1,0:T(8,128)(2,1)}, bf16[256,768]{1,0:T(8,128)(2,1)}, u32[]{:S(2)}, u32[]{:S(2)}) collective-permute-start(bf16[256,768]{1,0:T(8,128)(2,1)} %get-tuple-element.298), channel_id=1, source_target_pairs={{0,16},{16,0},{1,17},{17,1},{2,18},{18,2},{3,19},{19,3},{4,20},{20... | collective-permute-start | bytes 1179656 | tf_op jit(solution)/shard_map/ppermute | solution.py:23
  682.3 2.4 collective-permute-start.4
  686.7 65.4 %all-gather.35.cloned.1.call-start = ((), (), s32[]{:S(2)}) async-start(), calls=%async_computation.34 | async-start | bytes 1966080 | tf_op jit(solution)/shard_map/all_gather | solution.py:44
  686.7 2.0 collective-permute-start.2
  690.4 95.7 %reduce-scatter.49.cloned.1.call-start = ((), (), s32[]{:S(2)}) async-start(), calls=%async_computation.42 | async-start | bytes 1966080 | tf_op jit(solution)/shard_map/reduce_scatter | solution.py:54
  725.7 97.4 %all-gather.43.cloned.1.call-start = ((), (), s32[]{:S(2)}) async-start(), calls=%async_computation.43 | async-start | bytes 1966080 | tf_op jit(solution)/shard_map/all_gather | solution.py:44
  792.0 65.8 %reduce-scatter.41.cloned.1.call-start = ((), (), s32[]{:S(2)}) async-start(), calls=%async_computation.35 | async-start | bytes 1966080 | tf_op jit(solution)/shard_map/reduce_scatter | solution.py:54
  804.4 88.2 %reduce-scatter.51.cloned.1.call-start = ((), (), s32[]{:S(2)}) async-start(), calls=%async_computation.44 | async-start | bytes 1966080 | tf_op jit(solution)/shard_map/reduce_scatter | solution.py:54
  850.3 78.9 %all-gather.37.cloned.1.call-start = ((), (), s32[]{:S(2)}) async-start(), calls=%async_computation.36 | async-start | bytes 1966080 | tf_op jit(solution)/shard_map/all_gather | solution.py:44
  898.0 69.8 %reduce-scatter.43.cloned.1.call-start = ((), (), s32[]{:S(2)}) async-start(), calls=%async_computation.37 | async-start | bytes 1966080 | tf_op jit(solution)/shard_map/reduce_scatter | solution.py:54
  936.7 65.9 %reduce-scatter.45.cloned.1.call-start = ((), (), s32[]{:S(2)}) async-start(), calls=%async_computation.39 | async-start | bytes 1966080 | tf_op jit(solution)/shard_map/reduce_scatter | solution.py:54
  948.9 94.3 %all-gather.45.cloned.1.call-start = ((), (), s32[]{:S(2)}) async-start(), calls=%async_computation.45 | async-start | bytes 1966080 | tf_op jit(solution)/shard_map/all_gather | solution.py:44
  969.2 1.8 collective-permute-start.3
  1007.7 2.4 collective-permute-start.5
  1012.1 69.8 %reduce-scatter.53.cloned.1.call-start = ((), (), s32[]{:S(2)}) async-start(), calls=%async_computation.46 | async-start | bytes 1966080 | tf_op jit(solution)/shard_map/reduce_scatter | solution.py:54
  1050.3 68.8 %all-gather.47.cloned.1.call-start = ((), (), s32[]{:S(2)}) async-start(), calls=%async_computation.47 | async-start | bytes 1966080 | tf_op jit(solution)/shard_map/all_gather | solution.py:44
  1088.0 87.6 %reduce-scatter.55.cloned.1.call-start = ((), (), s32[]{:S(2)}) async-start(), calls=%async_computation.48 | async-start | bytes 1966080 | tf_op jit(solution)/shard_map/reduce_scatter | solution.py:54
  1144.5 72.1 %all-gather.49.cloned.1.call-start = ((), (), s32[]{:S(2)}) async-start(), calls=%async_computation.49 | async-start | bytes 1966080 | tf_op jit(solution)/shard_map/all_gather | solution.py:44
  1181.4 2.4 collective-permute-start.6
  1185.5 70.3 %reduce-scatter.57.cloned.1.call-start = ((), (), s32[]{:S(2)}) async-start(), calls=%async_computation.50 | async-start | bytes 1966080 | tf_op jit(solution)/shard_map/reduce_scatter | solution.py:54
  1224.7 66.7 %all-gather.51.cloned.1.call-start = ((), (), s32[]{:S(2)}) async-start(), calls=%async_computation.51 | async-start | bytes 1966080 | tf_op jit(solution)/shard_map/all_gather | solution.py:44
  1260.3 87.5 %reduce-scatter.59.cloned.1.call-start = ((), (), s32[]{:S(2)}) async-start(), calls=%async_computation.52 | async-start | bytes 1966080 | tf_op jit(solution)/shard_map/reduce_scatter | solution.py:54
  1316.6 64.1 %all-gather.33.cloned.1.call-start = ((), (), s32[]{:S(2)}) async-start(), calls=%async_computation.33 | async-start | bytes 1966080 | tf_op jit(solution)/shard_map/all_gather | solution.py:44
  1317.4 96.4 %all-gather.39.cloned.1.call-start = ((), (), s32[]{:S(2)}) async-start(), calls=%async_computation.38 | async-start | bytes 1966080 | tf_op jit(solution)/shard_map/all_gather | solution.py:44
  1318.1 130.5 %all-gather.53.cloned.1.call-start = ((), (), s32[]{:S(2)}) async-start(), calls=%async_computation.53 | async-start | bytes 3538944 | tf_op jit(solution)/shard_map/all_gather | solution.py:398
  1352.4 2.4 collective-permute-start.7
  1355.6 162.7 %reduce-scatter.71.cloned.1.call-start = ((), (), s32[]{:S(2)}) async-start(), calls=%async_computation.59 | async-start | bytes 1474560
  1370.9 150.2 %reduce-scatter.63.cloned.1.call-start = ((), (), s32[]{:S(2)}) async-start(), calls=%async_computation.55 | async-start | bytes 1474560 | tf_op jit(solution)/shard_map/reduce_scatter | solution.py:430
  1379.3 151.6 %reduce-scatter.67.cloned.1.call-start = ((), (), s32[]{:S(2)}) async-start(), calls=%async_computation.57 | async-start | bytes 20480
  1403.1 149.3 %reduce-scatter.69.cloned.1.call-start = ((), (), s32[]{:S(2)}) async-start(), calls=%async_computation.58 | async-start | bytes 491520
  1406.6 176.3 %reduce-scatter.61.cloned.1.call-start = ((), (), s32[]{:S(2)}) async-start(), calls=%async_computation.54 | async-start | bytes 1474560 | tf_op jit(solution)/shard_map/reduce_scatter | solution.py:421
  1412.5 283.2 %reduce-scatter.65.cloned.1.call-start = ((), (), s32[]{:S(2)}) async-start(), calls=%async_computation.56 | async-start | bytes 7864320
  (164 other events, 1587.3 us)
Sparse Core Ops, SparseCore 0:
  10.6 118.0 all-gather.18
  151.4 46.0 reduce-scatter.30
  228.2 27.1 all-gather.20
  311.8 29.0 reduce-scatter.32
  342.9 30.4 all-gather.24
  375.8 30.0 all-gather.22
  407.6 30.4 all-gather.26
  442.0 30.0 reduce-scatter.34
  477.0 30.9 all-gather.28
  525.4 30.9 reduce-scatter.36
  560.7 30.9 all-gather.30
  599.3 30.9 reduce-scatter.38
  633.5 31.2 reduce-scatter.46
  686.8 31.7 all-gather.40
  721.1 30.9 all-gather.34
  755.2 30.9 reduce-scatter.48
  792.2 30.9 all-gather.42
  826.9 30.9 reduce-scatter.40
  861.6 30.9 reduce-scatter.50
  898.1 30.9 all-gather.36
  936.8 30.9 reduce-scatter.42
  971.6 30.9 reduce-scatter.44
  1012.2 30.9 all-gather.44
  1050.5 31.3 reduce-scatter.52
  1088.1 30.9 all-gather.46
  1144.6 30.9 reduce-scatter.54
  1185.6 30.9 all-gather.48
  1224.8 30.9 reduce-scatter.56
  1260.4 30.9 all-gather.50
  1316.8 30.9 reduce-scatter.58
  1349.7 30.9 all-gather.32
  1382.7 30.9 all-gather.38
  1416.2 32.3 all-gather.52
  1451.0 29.1 reduce-scatter.70
  1482.6 27.8 reduce-scatter.62
  1513.3 17.5 reduce-scatter.66
  1533.6 18.7 reduce-scatter.68
  1555.4 27.4 reduce-scatter.60
  1585.2 110.5 reduce-scatter.64
where the time goes:
time: 1720 us; the launch traced here: 1710 us
  waiting for transfers between devices  960 us (56%)
  matrix products  235 us (14%)
  blocking collectives  207 us (12%)
  other arithmetic  188 us (11%)
  local copies, waits for them, and re-layouts  95.3 us (6%)
  between operations  19.6 us (1%)
    reduce_scatter x14, waiting for transfers between devices, summed_rows(): lax.psum_scatter(term().astype(jnp.bfloat16), 'tensor', scatter_dimension...  333 us
    all_gather x14, waiting for transfers between devices, gather_rows(): return lax.all_gather(rows, 'tensor', axis=0, tiled=True)  293 us
    all_gather x1, waiting for transfers between devices, on_device(): lax.all_gather(embed_table.astype(jnp.bfloat16), 'batch', axis=1, tiled=T...  118 us
    unnamed x43, waiting for transfers between devices  96.8 us
    unnamed x2, blocking collectives  82.4 us
    all_gather x1, blocking collectives, on_device(): lax.all_gather(norm_gains.astype(jnp.bfloat16), ('section', 'batch', 'ten...  67.9 us
    unnamed x354, local copies, waits for them, and re-layouts  60.4 us
    dot_general x14, matrix products, contract_rows(): lax.dot_general(left, right, (((0,), (0,)), ((), ())), preferred_element_...  56 us
  transfers between devices with their start and end apart: 47, of which 41 were waited for; matrix products, arithmetic and copies ran while one was open for 18% of the time, Pallas kernels for 0%

commit v1 on v0

v1 whole, which is shorter than its diff:
```python
import math

import jax
import jax.numpy as jnp
from jax import lax
from jax.sharding import PartitionSpec as P

D = 768
HEAD = 64

norm_eps = 1e-06
masked_score = -1e30
bf16 = jnp.bfloat16
f32 = jnp.float32


def mm(left, right, left_dim, right_dim):
    return lax.dot_general(
        left, right, (((left_dim,), (right_dim,)), ((), ())), preferred_element_type=f32
    )


def norm_factor(rows):
    return lax.rsqrt(jnp.mean(rows * rows, axis=-1, keepdims=True) + norm_eps)


def norm_back(grad, rows, gain):
    factor = norm_factor(rows)
    scaled = grad * gain
    inner = jnp.mean(scaled * rows, axis=-1, keepdims=True)
    grad_rows = factor * scaled - rows * (factor * factor * factor * inner)
    return grad_rows, jnp.sum(grad * rows * factor, axis=0)


def swap_core(block):
    return lax.ppermute(block, "section", [(0, 1), (1, 0)])


def from_peer(block, mask):
    count = lax.axis_size("tensor")
    return lax.ppermute(block, "tensor", [(at, at ^ mask) for at in range(count)])


def gather_rows(rows):
    count = lax.axis_size("tensor")
    return jnp.stack([rows] + [from_peer(rows, mask) for mask in range(1, count)])


def scatter_rows(parts):
    count = lax.axis_size("tensor")
    total = parts[0].astype(f32)
    for mask in range(1, count):
        total = total + from_peer(parts[mask], mask).astype(f32)
    return total


def in_order(parts, me):
    return jnp.concatenate([parts[me ^ at] for at in range(parts.shape[0])], 0)


def out_of_order(rows, me, count):
    split = rows.reshape(count, -1, rows.shape[-1])
    return jnp.stack([split[me ^ at] for at in range(count)])


def causal_mix(projected, taps):
    once = jnp.pad(projected, ((1, 0), (0, 0)))[:-1]
    twice = jnp.pad(projected, ((2, 0), (0, 0)))[:-2]
    return taps[0] * projected + taps[1] * once + taps[2] * twice


def causal_mix_back(grad, projected, taps):
    ahead_one = jnp.pad(grad, ((0, 1), (0, 0)))[1:]
    ahead_two = jnp.pad(grad, ((0, 2), (0, 0)))[2:]
    grad_in = taps[0] * grad + taps[1] * ahead_one + taps[2] * ahead_two
    once = jnp.pad(projected, ((1, 0), (0, 0)))[:-1]
    twice = jnp.pad(projected, ((2, 0), (0, 0)))[:-2]
    grad_taps = jnp.stack(
        [jnp.sum(grad * projected, 0), jnp.sum(grad * once, 0), jnp.sum(grad * twice, 0)]
    )
    return (grad_in, grad_taps)


def allowed_keys(lead, reach, length):
    query_at = jnp.arange(lead, reach)[:, None]
    key_at = jnp.arange(reach)[None, :]
    return (key_at <= query_at) & (key_at < length)


def attend(queries, keys_all, values_all, length):
    total = queries.shape[0]
    block = min(512, total)
    factor = queries.shape[-1] ** (-0.5)
    outputs = []
    totals = []
    for index in range(total // block):
        lead = index * block
        reach = lead + block
        scores = (
            jnp.einsum("qhd,khd->hqk", queries[lead:reach], keys_all[:reach], preferred_element_type=f32)
            * factor
        )
        scores = jnp.where(allowed_keys(lead, reach, length)[None], scores, masked_score)
        peak = jnp.max(scores, axis=-1, keepdims=True)
        raised = jnp.exp(scores - peak)
        weight_sum = jnp.sum(raised, axis=-1, keepdims=True)
        probs = (raised / weight_sum).astype(bf16)
        result = jnp.einsum("hqk,khd->qhd", probs, values_all[:reach], preferred_element_type=f32)
        outputs.append(result.astype(bf16))
        totals.append((peak + jnp.log(weight_sum))[..., 0])
    return (jnp.concatenate(outputs, 0), jnp.concatenate(totals, 1))


def attend_back(grad_out, queries, keys_all, values_all, length, totals):
    total = queries.shape[0]
    block = min(512, total)
    factor = queries.shape[-1] ** (-0.5)
    grad_queries = []
    grad_keys = jnp.zeros(keys_all.shape, f32)
    grad_values = jnp.zeros(values_all.shape, f32)
    for index in range(total // block):
        lead = index * block
        reach = lead + block
        scores = (
            jnp.einsum("qhd,khd->hqk", queries[lead:reach], keys_all[:reach], preferred_element_type=f32)
            * factor
        )
        allowed = allowed_keys(lead, reach, length)[None]
        probs = jnp.where(allowed, jnp.exp(scores - totals[:, lead:reach, None]), 0.0)
        grad_block = grad_out[lead:reach]
        grad_probs = jnp.einsum(
            "qhd,khd->hqk", grad_block, values_all[:reach], preferred_element_type=f32
        )
        inner = jnp.sum(probs * grad_probs, axis=-1, keepdims=True)
        grad_scores = (probs * (grad_probs - inner)).astype(bf16)
        grad_queries.append(
            jnp.einsum("hqk,khd->qhd", grad_scores, keys_all[:reach], preferred_element_type=f32)
            * factor
        )
        grad_keys = grad_keys.at[:reach].add(
            jnp.einsum("hqk,qhd->khd", grad_scores, queries[lead:reach], preferred_element_type=f32)
            * factor
        )
        grad_values = grad_values.at[:reach].add(
            jnp.einsum("hqk,qhd->khd", probs.astype(bf16), grad_block, preferred_element_type=f32)
        )
    return (jnp.concatenate(grad_queries, 0), grad_keys, grad_values)


def layer_forward(resid, length, weights, me):
    gain_attn, gain_ffn, qkv_mat, taps, out_turned, up_mat, down_turned = weights
    count = lax.axis_size("tensor")
    local_width = out_turned.shape[1]
    heads_here = local_width // HEAD
    normed = (resid * norm_factor(resid) * gain_attn).astype(bf16)
    gathered = in_order(gather_rows(normed), me)
    projected = mm(gathered, qkv_mat, 1, 0)
    mixed = causal_mix(projected, taps).astype(bf16)
    triple = mixed.reshape(-1, 3, heads_here, HEAD)
    context, totals = attend(triple[:, 0], triple[:, 1], triple[:, 2], length)
    context = context.reshape(-1, local_width)
    partial = out_of_order(mm(context, out_turned, 1, 1).astype(bf16), me, count)
    middle = resid + scatter_rows(partial)
    normed_ffn = (middle * norm_factor(middle) * gain_ffn).astype(bf16)
    gathered_ffn = gather_rows(normed_ffn).reshape(-1, D)
    hidden = mm(gathered_ffn, up_mat, 1, 0)
    active = jnp.square(jnp.maximum(hidden, 0.0)).astype(bf16)
    lowered = mm(active, down_turned, 1, 1).astype(bf16).reshape(count, -1, D)
    output = middle + scatter_rows(lowered)
    kept = (resid, gathered, projected, mixed, context, totals, middle, gathered_ffn, hidden, active)
    return (output, kept)


def layer_backward(grad_out, length, weights, kept, me):
    gain_attn, gain_ffn, qkv_mat, taps, out_turned, up_mat, down_turned = weights
    resid, gathered, projected, mixed, context, totals, middle, gathered_ffn, hidden, active = kept
    count = lax.axis_size("tensor")
    local_width = out_turned.shape[1]
    heads_here = local_width // HEAD
    grad_rows = gather_rows(grad_out.astype(bf16)).reshape(-1, D)
    grad_active = mm(grad_rows, down_turned, 1, 0)
    grad_hidden = (grad_active * 2.0 * jnp.maximum(hidden, 0.0)).astype(bf16)
    grad_normed_ffn = scatter_rows(mm(grad_hidden, up_mat, 1, 1).astype(bf16).reshape(count, -1, D))
    grad_down = mm(grad_rows, active, 0, 0)
    grad_up = mm(gathered_ffn, grad_hidden, 0, 0)
    grad_middle_norm, grad_gain_ffn = norm_back(grad_normed_ffn, middle, gain_ffn)
    grad_middle = grad_out + grad_middle_norm
    grad_rows_attn = in_order(gather_rows(grad_middle.astype(bf16)), me)
    grad_outmat = mm(grad_rows_attn, context, 0, 0)
    grad_context = mm(grad_rows_attn, out_turned, 1, 0).astype(bf16).reshape(-1, heads_here, HEAD)
    triple = mixed.reshape(-1, 3, heads_here, HEAD)
    grad_queries, grad_keys, grad_values = attend_back(
        grad_context, triple[:, 0], triple[:, 1], triple[:, 2], length, totals
    )
    grad_mixed = jnp.stack([grad_queries, grad_keys, grad_values], 1).reshape(-1, 3 * local_width)
    grad_projected, grad_taps = causal_mix_back(grad_mixed, projected, taps)
    grad_projected = grad_projected.astype(bf16)
    partial = mm(grad_projected, qkv_mat, 1, 1).astype(bf16)
    grad_normed = scatter_rows(out_of_order(partial, me, count))
    grad_qkv = mm(gathered, grad_projected, 0, 0)
    grad_resid_norm, grad_gain_attn = norm_back(grad_normed, resid, gain_attn)
    grad_in = grad_middle + grad_resid_norm
    attn_blob = jnp.concatenate([grad_qkv.astype(bf16), grad_outmat.astype(bf16)], 1)
    ffn_blob = jnp.concatenate([grad_up.astype(bf16), grad_down.astype(bf16)], 1)
    return (grad_in, attn_blob, ffn_blob, grad_gain_attn, grad_gain_ffn, grad_taps)


def both_layers(block):
    gathered = lax.all_gather(block, "batch", axis=0, tiled=True)
    return gathered, swap_core(gathered)


def on_device(
    token_ids,
    seq_lengths,
    embed_table,
    norm_gains,
    final_gain,
    qkv_weight,
    qkv_conv,
    out_weight,
    up_weight,
    down_weight,
    logit_grad,
):
    section = lax.axis_index("section")
    first = section == 0
    me = lax.axis_index("tensor")
    at_batch = lax.axis_index("batch")
    tensor_count = lax.axis_size("tensor")
    batch_count = lax.axis_size("batch")
    section_count = lax.axis_size("section")
    slot_length = token_ids.shape[1]
    shard_rows = slot_length // tensor_count
    local_width = out_weight.shape[1]
    heads_here = local_width // HEAD
    hidden_width = up_weight.shape[2]
    root_scale = math.sqrt(D)
    depth = D // batch_count
    length = seq_lengths[section]

    table_own = embed_table.astype(bf16).T
    attn_own = jnp.concatenate(
        [
            qkv_weight[0].reshape(depth, 3 * local_width).astype(bf16),
            out_weight[0].astype(bf16).T,
        ],
        1,
    )
    ffn_own = jnp.concatenate([up_weight[0].astype(bf16), down_weight[0].astype(bf16).T], 1)
    small = jnp.concatenate(
        [
            norm_gains.astype(bf16).reshape(-1),
            final_gain.astype(bf16),
            qkv_conv.astype(bf16).reshape(-1),
        ]
    )
    gain_width = final_gain.shape[0]
    small_all = lax.all_gather(small, ("section", "batch", "tensor"), axis=0, tiled=False)
    gains_all = small_all[:, : 5 * gain_width].astype(f32).reshape(-1, 5, gain_width)
    gains_all = gains_all.transpose(1, 0, 2).reshape(5, D)
    taps_all = small_all[:, 5 * gain_width :].reshape(
        section_count, batch_count, tensor_count, 3, 3, heads_here, -1
    )
    taps_here = lax.dynamic_index_in_dim(taps_all, me, 2, keepdims=False).astype(f32)
    taps_here = taps_here.transpose(0, 3, 2, 4, 1, 5).reshape(section_count, 3, 3 * local_width)
    final_scale = gains_all[4]

    attn_mine, attn_other = both_layers(attn_own)
    ffn_mine, ffn_other = both_layers(ffn_own)
    table_turned = lax.all_gather(table_own, "batch", axis=0, tiled=True)

    weights = []
    for layer in range(section_count):
        attn_layer = jnp.where(section == layer, attn_mine, attn_other)
        ffn_layer = jnp.where(section == layer, ffn_mine, ffn_other)
        weights.append(
            (
                gains_all[2 * layer],
                gains_all[2 * layer + 1],
                attn_layer[:, : 3 * local_width],
                taps_here[layer],
                attn_layer[:, 3 * local_width :],
                ffn_layer[:, :hidden_width],
                ffn_layer[:, hidden_width:],
            )
        )

    vocab_rows = embed_table.shape[0]
    all_ids = lax.all_gather(token_ids, "batch", axis=0, tiled=False)
    owner_start = (section * tensor_count + me) * vocab_rows
    local_ids = all_ids - owner_start
    inside = (local_ids >= 0) & (local_ids < vocab_rows)
    safe_ids = jnp.clip(local_ids, 0, vocab_rows - 1)
    picked = jnp.where(inside[..., None], embed_table.astype(bf16)[safe_ids], jnp.zeros((), bf16))
    picked = picked.reshape(batch_count, section_count, tensor_count, shard_rows, depth)
    mine = lax.dynamic_index_in_dim(picked, section, 1, keepdims=False)
    theirs = lax.dynamic_index_in_dim(picked, 1 - section, 1, keepdims=False)
    joined = mine + swap_core(theirs)
    total = lax.dynamic_index_in_dim(joined, me, 1, keepdims=False)
    for mask in range(1, tensor_count):
        total = total + from_peer(
            lax.dynamic_index_in_dim(joined, me ^ mask, 1, keepdims=False), mask
        )
    embedded = lax.all_to_all(total, "batch", 0, 0, tiled=False)
    embedded = embedded.transpose(1, 0, 2).reshape(shard_rows, D)

    resid = embedded.astype(f32) * root_scale
    output, kept_first = layer_forward(resid, length, weights[0], me)
    output, kept_second = layer_forward(output.astype(bf16).astype(f32), length, weights[1], me)
    final_rows = output.astype(bf16).astype(f32)

    valid = jnp.arange(slot_length)[None, :] < seq_lengths[:, None]
    grad_both = mm(logit_grad.reshape(-1, vocab_rows), table_turned, 1, 1).astype(bf16)
    grad_both = grad_both.reshape(section_count, slot_length, D)
    grad_both = jnp.where(valid[..., None], grad_both, jnp.zeros((), bf16))
    grad_mine = lax.dynamic_index_in_dim(grad_both, section, 0, keepdims=False)
    grad_theirs = lax.dynamic_index_in_dim(grad_both, 1 - section, 0, keepdims=False)
    grad_joined = (grad_mine.astype(f32) + swap_core(grad_theirs).astype(f32)).astype(bf16)
    grad_final = scatter_rows(out_of_order(grad_joined, me, tensor_count))

    normed_final = (final_rows * norm_factor(final_rows) * final_scale).astype(bf16)
    final_all = in_order(gather_rows(normed_final), me)
    final_other = swap_core(final_all)
    final_both = jnp.stack(
        [jnp.where(first, final_all, final_other), jnp.where(first, final_other, final_all)]
    )
    logits = jnp.einsum(
        "srd,dv->srv", final_both, table_turned, preferred_element_type=f32
    ).astype(bf16)
    masked_final = jnp.where(valid[..., None], final_both, jnp.zeros((), bf16))
    head_table = mm(masked_final.reshape(-1, D), logit_grad.reshape(-1, vocab_rows), 0, 0)
    head_done = lax.psum_scatter(head_table.astype(bf16), "batch", scatter_dimension=0, tiled=True)

    grad_rows, grad_final_gain = norm_back(grad_final, final_rows, final_scale)
    grad_rows, attn_second, ffn_second, gain_2a, gain_2f, taps_second = layer_backward(
        grad_rows, length, weights[1], kept_second, me
    )
    grad_rows = grad_rows.astype(bf16).astype(f32)
    grad_rows, attn_first, ffn_first, gain_1a, gain_1f, taps_first = layer_backward(
        grad_rows, length, weights[0], kept_first, me
    )
    embed_grad = (grad_rows * root_scale).astype(bf16)

    def reduced(blob):
        halves = blob.reshape(batch_count, section_count, depth // section_count, -1)
        keep = lax.dynamic_index_in_dim(halves, section, 1, keepdims=False)
        send = lax.dynamic_index_in_dim(halves, 1 - section, 1, keepdims=False)
        part = (keep.astype(f32) + swap_core(send).astype(f32)).astype(bf16)
        return lax.psum_scatter(part, "batch", scatter_dimension=0, tiled=False)

    def placed(first_part, second_part):
        keep = jnp.where(first, first_part, second_part)
        got = swap_core(jnp.where(first, second_part, first_part))
        return jnp.where(
            first, jnp.concatenate([keep, got], 0), jnp.concatenate([got, keep], 0)
        ).astype(f32)

    attn_done = placed(reduced(attn_first), reduced(attn_second))
    ffn_done = placed(reduced(ffn_first), reduced(ffn_second))
    qkv_done = attn_done[:, : 3 * local_width].reshape(1, depth, 3, local_width)
    out_done = attn_done[:, 3 * local_width :].T[None]
    up_done = ffn_done[:, :hidden_width][None]
    down_done = ffn_done[:, hidden_width:].T[None]

    gain_sums = lax.psum(
        jnp.stack([gain_1a, gain_1f, gain_2a, gain_2f, grad_final_gain]),
        ("section", "batch", "tensor"),
    )
    taps_sums = lax.psum(jnp.stack([taps_first, taps_second]), ("section", "batch"))
    whole_at = (section * batch_count + at_batch) * tensor_count + me
    gain_part = lax.dynamic_slice_in_dim(gain_sums, whole_at * gain_width, gain_width, 1)
    gains_done = gain_part[:4].reshape(2, 2, gain_width)
    final_done = gain_part[4]
    conv_part = lax.dynamic_index_in_dim(taps_sums, section, 0, keepdims=False)
    conv_part = conv_part.reshape(3, 3, heads_here, HEAD).transpose(1, 0, 2, 3)
    conv_done = lax.dynamic_slice_in_dim(
        conv_part, at_batch * qkv_conv.shape[4], qkv_conv.shape[4], 3
    )[None]

    spread = embed_grad.reshape(shard_rows, batch_count, depth).transpose(1, 0, 2)
    spread = lax.all_to_all(spread, "batch", 0, 0, tiled=False)
    around = gather_rows(spread)
    around = jnp.stack([around[me ^ at] for at in range(tensor_count)])
    other = swap_core(around)
    every = jnp.stack([jnp.where(first, around, other), jnp.where(first, other, around)])
    every = every.transpose(2, 0, 1, 3, 4).reshape(-1, depth)
    flat_ids = safe_ids.reshape(-1)
    embed_part = (
        jnp.zeros((vocab_rows, depth), f32)
        .at[flat_ids]
        .add(jnp.where(inside.reshape(-1)[:, None], every.astype(f32), 0.0))
    )
    table_done = head_done.astype(f32).T + embed_part
    return (
        logits,
        table_done,
        gains_done,
        final_done,
        qkv_done,
        conv_done,
        out_done,
        up_done,
        down_done,
    )


def solution(mesh):
    in_specs = (
        P("batch", None),
        P("batch"),
        P(("section", "tensor"), "batch"),
        P(None, None, ("section", "batch", "tensor")),
        P(("section", "batch", "tensor")),
        P("section", "batch", None, "tensor"),
        P("section", None, None, "tensor", "batch"),
        P("section", "tensor", "batch"),
        P("section", "batch", "tensor"),
        P("section", "tensor", "batch"),
        P("batch", None, ("section", "tensor")),
    )
    out_specs = (
        P("batch", None, ("section", "tensor")),
        P(("section", "tensor"), "batch"),
        P(None, None, ("section", "batch", "tensor")),
        P(("section", "batch", "tensor")),
        P("section", "batch", None, "tensor"),
        P("section", None, None, "tensor", "batch"),
        P("section", "tensor", "batch"),
        P("section", "batch", "tensor"),
        P("section", "tensor", "batch"),
    )
    return jax.shard_map(
        on_device, mesh=mesh, in_specs=in_specs, out_specs=out_specs, check_vma=False
    )
```

time: 1720 us -> 984 us (0.57)
  waiting for transfers between devices: 960 us -> 275 us
  matrix products: 235 us -> 121 us
  starting transfers between devices: 4.91 us -> 81.7 us
  local copies, waits for them, and re-layouts: 95.3 us -> 151 us
  blocking collectives: 207 us -> 164 us
  other arithmetic: 188 us -> 163 us
    all_gather x18 -> x3, waiting for transfers between devices: 489 us -> 19.9 us  [the longest x1 19.9 us: on_device(): table_turned = lax.all_gather(table_own, 'batch', axis=0, tiled=True)]
    reduce_scatter x17 -> x5, waiting for transfers between devices: 362 us -> 0.01 us  [the longest x4 0.01 us: reduced(): return lax.psum_scatter(part, 'batch', scatter_dimension=0, tiled=False)]
    ppermute x8 -> x72, waiting for transfers between devices: 11.8 us -> 252 us  [the longest x60 251 us: from_peer(): lax.ppermute(block, 'tensor', [(at, at ^ mask) for at in range(count)])]
    all_gather x4 -> x1, blocking collectives: 124 us -> 14.9 us  [on_device(): all_ids = lax.all_gather(token_ids, 'batch', axis=0, tiled=False)]
    psum x0 -> x2, blocking collectives: none -> 106 us  [the longest x1 55 us: on_device(): lax.psum(jnp.stack([gain_1a, gain_1f, gain_2a, gain_2f, grad_final_gain])...]
    unnamed x43 -> x8, waiting for transfers between devices: 96.8 us -> 0.13 us
    dot_general x54 -> x31, matrix products: 194 us -> 97.2 us  [the longest x26 72.4 us: mm(): lax.dot_general(left, right, (((left_dim,), (right_dim,)), ((), ())), pre...]
    ppermute x8 -> x72, starting transfers between devices: 0.63 us -> 73.5 us  [the longest x60 71.8 us: from_peer(): lax.ppermute(block, 'tensor', [(at, at ^ mask) for at in range(count)])]
  transfers between devices with their start and end apart: 47 -> 82, of which waited for: 41 -> 52; matrix products, arithmetic and copies ran while one was open for 18% -> 32% of each run, Pallas kernels for 0% -> 0%
where the time goes in v1:
time: 984 us; the launch traced here: 974 us
  waiting for transfers between devices  275 us (28%)
  blocking collectives  164 us (17%)
  other arithmetic  163 us (17%)
  local copies, waits for them, and re-layouts  151 us (15%)
  matrix products  121 us (12%)
  starting transfers between devices  81.7 us (8%)
  between operations  17.2 us (2%)
    ppermute x60, waiting for transfers between devices, from_peer(): lax.ppermute(block, 'tensor', [(at, at ^ mask) for at in range(count)])  251 us
    dot_general x26, matrix products, mm(): lax.dot_general(left, right, (((left_dim,), (right_dim,)), ((), ())), pre...  72.4 us
    ppermute x60, starting transfers between devices, from_peer(): lax.ppermute(block, 'tensor', [(at, at ^ mask) for at in range(count)])  71.8 us
    psum x1, blocking collectives, on_device(): lax.psum(jnp.stack([gain_1a, gain_1f, gain_2a, gain_2f, grad_final_gain])...  55 us
    scatter-add x1, other arithmetic, on_device(): embed_part = jnp.zeros((vocab_rows, depth), f32).at[flat_ids].add(jnp.whe...  52.7 us
    psum x1, blocking collectives, on_device(): lax.psum(jnp.stack([taps_first, taps_second]), ('section', 'batch'))  51.4 us
    unnamed x1, blocking collectives  43.1 us
    gather x2, local copies, waits for them, and re-layouts, on_device(): embed_table.astype(bf16)[safe_ids]  40.2 us
  transfers between devices with their start and end apart: 82, of which 52 were waited for; matrix products, arithmetic and copies ran while one was open for 32% of the time, Pallas kernels for 0%

profile of v1, /device:TPU:0, one launch (start us, length us, event | category | flops | bytes accessed | tf_op | source)
XLA Modules:
  0.0 973.5 jit_solution(5725273682936571705)
XLA Ops:
  10.5 14.9 %all-gather.2 = s32[4,2,1024]{2,1,0:T(2,128)S(1)} all-gather(s32[1,2,1024]{2,1,0:T(2,128)S(1)} %bitcast.561), channel_id=2, replica_groups=mesh['section'=2,'batch'=4,'tensor'=4] {'batch'}, dimensions={0}, use_global_device_ids=true | all-gather | bytes 40960 | tf_op jit(solution)/shard_map/all_gather | solution.py:290
  32.5 33.2 %gather_fusion = bf16[8192,192]{1,0:T(8,128)(2,1)} fusion(bf16[4096,192]{1,0:T(8,128)(2,1)S(1)} %copy.135, s32[8192]{0:T(1024)S(1)} %broadcast_clamp_fusion), kind=kCustom, calls=%fused_computation | custom fusion | bytes 6324224 | tf_op jit(solution)/shard_map/gather | solution.py:295
  65.7 7.0 copy.136
  78.5 43.1 %all-reduce.12 = bf16[17664]{0:T(1024)(128)(2,1)S(1)} all-reduce(bf16[17664]{0:T(1024)(128)(2,1)S(1)} %dynamic-update-slice.20), channel_id=3, replica_groups=mesh['section'=2,'batch'=4,'tensor'=4] {'section','batch','tensor'}, use_global_device_ids=true, to_apply=%add.12 | all-reduce | flops 17664 | bytes 70656
  128.8 7.5 collective-permute-done.1
  136.3 7.4 collective-permute-done.3
  166.3 8.5 collective-permute-done.6
  174.9 4.6 collective-permute-done.5
  205.2 6.5 collective-permute-done.8
  211.8 8.3 collective-permute-done.10
  228.1 5.9 collective-permute-done.12
  235.3 6.0 collective-permute-done.13
  255.6 7.3 collective-permute-done.15
  262.9 4.6 collective-permute-done.17
  323.9 19.9 %all-gather.11.cloned.1.call-done = bf16[768,4096]{1,0:T(8,128)(2,1)} async-done(((bf16[192,4096]{1,0:T(8,128)(2,1)}), bf16[768,4096]{1,0:T(8,128)(2,1)}) %all-gather.11.cloned.1.call-update) | async-done | bytes 6291472 | tf_op jit(solution)/shard_map/all_gather | solution.py:271
  343.8 18.2 %convolution_convert_fusion.1 = bf16[2048,768]{1,0:T(8,128)(2,1)S(1)} fusion(bf16[2048,4096]{1,0:T(8,128)(2,1)} %bitcast.563, bf16[768,4096]{1,0:T(8,128)(2,1)} %all-gather.11.cloned.1.call-done), kind=kOutput, calls=%fused_computation.20 | convolution fusion | flops 12886474752 | bytes 26214400 | tf_op jit(solution)/shard_map/dot_general | solution.py:18
  388.0 7.9 collective-permute-done.29
  398.4 5.1 collective-permute-done.35
  403.4 9.0 collective-permute-done.37
  418.6 9.5 collective-permute-done.40
  428.1 6.4 collective-permute-done.39
  441.3 8.5 collective-permute-done.41
  449.8 7.6 collective-permute-done.43
  464.6 9.4 collective-permute-done.46
  474.0 5.1 collective-permute-done.45
  496.4 4.5 multiply_reduce_fusion.6
  506.8 7.9 collective-permute-done.47
  514.6 8.4 collective-permute-done.49
  533.1 5.8 collective-permute-done.52
  538.9 5.2 collective-permute-done.51
  559.8 7.2 collective-permute-done.55
  578.4 5.8 collective-permute-done.58
  584.3 4.6 collective-permute-done.57
  632.6 9.4 collective-permute-done.32
  642.0 7.5 collective-permute-done.31
  679.9 19.2 %bitcast_convert_fusion = bf16[768,4096]{1,0:T(8,128)(2,1)} fusion(bf16[2,1024,4096]{2,1,0:T(8,128)(2,1)} %param.45, pred[2,1024]{1,0:T(4,128)(4,1)S(1)} %copy-done.118, bf16[1,1024,768]{2,1,0:T(8,128)(2,1)S(1)} %get-tuple-element.210, bf16[1,1024,768]{2,1,0:T(8,128)(2,1)S(1)} %get-tuple-element.209), kind=kOutput, calls=%fused_computation.2 | convolution fusion | flops 12891193344 | bytes 26216448 | tf_op jit(solution)/shard_map/dot_general | solution.py:18
  702.8 8.7 collective-permute-done.59
  711.5 8.5 collective-permute-done.61
  728.3 51.4 %psum.15 = f32[2,3,576]{2,1,0:T(4,128)S(1)} all-reduce(f32[2,3,576]{2,1,0:T(4,128)S(1)} %pad_maximum_fusion.37), channel_id=1, replica_groups=mesh['section'=2,'batch'=4,'tensor'=4] {'section','batch'}, use_global_device_ids=true, to_apply=%region_38.39 | all-reduce | flops 3456 | bytes 27648 | tf_op jit(solution)/shard_map/psum | solution.py:370
  784.1 55.0 %psum.14 = f32[5,768]{1,0:T(8,128)S(1)} all-reduce(f32[5,768]{1,0:T(8,128)S(1)} %stack.313), channel_id=1, replica_groups=mesh['section'=2,'batch'=4,'tensor'=4] {'section','batch','tensor'}, use_global_device_ids=true, to_apply=%region_29.30 | all-reduce | flops 3840 | bytes 30720 | tf_op jit(solution)/shard_map/psum | solution.py:366
  843.6 19.9 %convolution_convert_fusion = bf16[2,1024,4096]{2,1,0:T(8,128)(2,1)} fusion(bf16[768,4096]{1,0:T(8,128)(2,1)} %all-gather.11.cloned.1.call-done, bf16[1,1024,768]{2,1,0:T(8,128)(2,1)} %copy-done.48, bf16[1,1024,768]{2,1,0:T(8,128)(2,1)S(1)} %copy-done.47), kind=kOutput, calls=%fused_computation.3 | convolution fusion | flops 12894863360 | bytes 26214400 | tf_op jit(solution)/shard_map/srd,dv->srv/dot_general | solution.py:328
  869.2 6.7 copy.166
  875.9 8.2 reshape.849
  884.1 6.1 broadcast_select_fusion
  890.3 8.4 copy.168
  903.4 5.1 copy.167
  908.5 52.7 %scatter_fusion = f32[4096,192]{1,0:T(8,128)} fusion(f32[4096,192]{1,0:T(8,128)} %copy.167, s32[8192]{0:T(1024)S(1)} %bitcast.559, f32[8192,192]{1,0:T(8,128)} %copy.168), kind=kCustom, calls=%fused_computation.1 | custom fusion | flops 1572864 | bytes 18907136 | tf_op jit(solution)/shard_map/scatter-add | solution.py:392
  961.3 5.3 copy.176
  (704 shorter events, 363.1 us)
Async XLA Ops:
  7.2 149.0 %all-gather.7.cloned.1.call-start = ((), (), s32[]{:S(2)}) async-start(), calls=%async_computation.7 | async-start | bytes 1474560 | tf_op jit(solution)/shard_map/all_gather | solution.py:209
  10.4 192.6 %all-gather.9.cloned.1.call-start = ((), (), s32[]{:S(2)}) async-start(), calls=%async_computation.8 | async-start | bytes 2949120 | tf_op jit(solution)/shard_map/all_gather | solution.py:209
  75.1 46.7 %collective-permute-start = (bf16[4,4,256,192]{2,3,1,0:T(8,128)(2,1)S(1)}, bf16[4,4,256,192]{2,3,1,0:T(8,128)(2,1)}, u32[]{:S(2)}, u32[]{:S(2)}) collective-permute-start(bf16[4,4,256,192]{2,3,1,0:T(8,128)(2,1)S(1)} %dynamic-slice_bitcast_fusion.1), channel_id=1, source_target_pairs={{0,16},{16,0},{1,17},{17,1},{2,18},{18,2},{3,19},{19,3},{4,20},{20... | collective-permute-start | bytes 4718600 | tf_op jit(solution)/shard_map/ppermute | solution.py:36
  126.2 17.6 %collective-permute-start.3 = (bf16[4,256,192]{1,2,0:T(8,128)(2,1)S(1)}, bf16[4,256,192]{1,2,0:T(8,128)(2,1)}, u32[]{:S(2)}, u32[]{:S(2)}) collective-permute-start(bf16[4,256,192]{1,2,0:T(8,128)(2,1)S(1)} %get-tuple-element.267), channel_id=1, source_target_pairs={{0,3},{1,2},{2,1},{3,0},{4,7},{5,6},{6,5},{7,4},{8,11},{9,10},{10,... | collective-permute-start | bytes 1179656 | tf_op jit(solution)/shard_map/ppermute | solution.py:41
  127.7 17.4 %collective-permute-start.2 = (bf16[4,256,192]{1,2,0:T(8,128)(2,1)S(1)}, bf16[4,256,192]{1,2,0:T(8,128)(2,1)}, u32[]{:S(2)}, u32[]{:S(2)}) collective-permute-start(bf16[4,256,192]{1,2,0:T(8,128)(2,1)S(1)} %get-tuple-element.268), channel_id=1, source_target_pairs={{0,2},{1,3},{2,0},{3,1},{4,6},{5,7},{6,4},{7,5},{8,10},{9,11},{10,... | collective-permute-start | bytes 1179656 | tf_op jit(solution)/shard_map/ppermute | solution.py:41
  150.7 193.1 %all-gather.11.cloned.1.call-start = ((), (), s32[]{:S(2)}) async-start(), calls=%async_computation.9 | async-start | bytes 7864320 | tf_op jit(solution)/shard_map/all_gather | solution.py:271
  156.2 25.1 %collective-permute-start.7 = (bf16[768,768]{1,0:T(8,128)(2,1)}, bf16[768,768]{1,0:T(8,128)(2,1)}, u32[]{:S(2)}, u32[]{:S(2)}) collective-permute-start(bf16[768,768]{1,0:T(8,128)(2,1)} %all-gather.7.cloned.1.call-done), channel_id=1, source_target_pairs={{0,16},{16,0},{1,17},{17,1},{2,18},{18,2},{3,19},{19,3},{4,20},{20... | collective-permute-start | bytes 3538952 | tf_op jit(solution)/shard_map/ppermute | solution.py:36
  201.0 19.1 %collective-permute-start.10 = (bf16[256,768]{1,0:T(8,128)(2,1)S(1)}, bf16[256,768]{1,0:T(8,128)(2,1)S(1)}, u32[]{:S(2)}, u32[]{:S(2)}) collective-permute-start(bf16[256,768]{1,0:T(8,128)(2,1)S(1)} %get-tuple-element.260), channel_id=1, source_target_pairs={{0,3},{1,2},{2,1},{3,0},{4,7},{5,6},{6,5},{7,4},{8,11},{9,10},{10,... | collective-permute-start | bytes 1179656 | tf_op jit(solution)/shard_map/ppermute | solution.py:41
  202.4 18.8 %collective-permute-start.9 = (bf16[256,768]{1,0:T(8,128)(2,1)S(1)}, bf16[256,768]{1,0:T(8,128)(2,1)S(1)}, u32[]{:S(2)}, u32[]{:S(2)}) collective-permute-start(bf16[256,768]{1,0:T(8,128)(2,1)S(1)} %get-tuple-element.261), channel_id=1, source_target_pairs={{0,2},{1,3},{2,0},{3,1},{4,6},{5,7},{6,4},{7,5},{8,10},{9,11},{10,... | collective-permute-start | bytes 1179656 | tf_op jit(solution)/shard_map/ppermute | solution.py:41
  203.0 38.5 %collective-permute-start.14 = (bf16[768,1536]{1,0:T(8,128)(2,1)}, bf16[768,1536]{1,0:T(8,128)(2,1)}, u32[]{:S(2)}, u32[]{:S(2)}) collective-permute-start(bf16[768,1536]{1,0:T(8,128)(2,1)} %all-gather.9.cloned.1.call-done), channel_id=1, source_target_pairs={{0,16},{16,0},{1,17},{17,1},{2,18},{18,2},{3,19},{19,3},{4,20},{20... | collective-permute-start | bytes 7077896 | tf_op jit(solution)/shard_map/ppermute | solution.py:36
  224.9 16.5 %collective-permute-start.13 = (bf16[256,768]{1,0:T(8,128)(2,1)S(1)}, bf16[256,768]{1,0:T(8,128)(2,1)S(1)}, u32[]{:S(2)}, u32[]{:S(2)}) collective-permute-start(bf16[256,768]{1,0:T(8,128)(2,1)S(1)} %multiply_convert_fusion.10), channel_id=1, source_target_pairs={{0,3},{1,2},{2,1},{3,0},{4,7},{5,6},{6,5},{7,4},{8,11},{9,10},{10,... | collective-permute-start | bytes 1179656 | tf_op jit(solution)/shard_map/ppermute | solution.py:41
  227.7 614.3 %reduce-scatter.10.cloned.1.call-start = ((), (), s32[]{:S(2)}) async-start(), calls=%async_computation.12 | async-start | bytes 737280 | tf_op jit(solution)/shard_map/reduce_scatter | solution.py:350
  252.7 16.7 %collective-permute-start.16 = (bf16[256,768]{1,0:T(8,128)(2,1)S(1)}, bf16[256,768]{1,0:T(8,128)(2,1)S(1)}, u32[]{:S(2)}, u32[]{:S(2)}) collective-permute-start(bf16[256,768]{1,0:T(8,128)(2,1)S(1)} %get-tuple-element.258), channel_id=1, source_target_pairs={{0,2},{1,3},{2,0},{3,1},{4,6},{5,7},{6,4},{7,5},{8,10},{9,11},{10,... | collective-permute-start | bytes 1179656 | tf_op jit(solution)/shard_map/ppermute | solution.py:41
  320.4 48.6 %collective-permute-start.25 = (bf16[256,768]{1,0:T(8,128)(2,1)}, bf16[256,768]{1,0:T(8,128)(2,1)S(1)}, u32[]{:S(2)}, u32[]{:S(2)}) collective-permute-start(bf16[256,768]{1,0:T(8,128)(2,1)} %multiply_convert_fusion.9), channel_id=1, source_target_pairs={{0,2},{1,3},{2,0},{3,1},{4,6},{5,7},{6,4},{7,5},{8,10},{9,11},{10,... | collective-permute-start | bytes 1179656 | tf_op jit(solution)/shard_map/ppermute | solution.py:41
  321.1 48.0 %collective-permute-start.24 = (bf16[256,768]{1,0:T(8,128)(2,1)}, bf16[256,768]{1,0:T(8,128)(2,1)}, u32[]{:S(2)}, u32[]{:S(2)}) collective-permute-start(bf16[256,768]{1,0:T(8,128)(2,1)} %multiply_convert_fusion.9), channel_id=1, source_target_pairs={{0,1},{1,0},{2,3},{3,2},{4,5},{5,4},{6,7},{7,6},{8,9},{9,8},{10,11... | collective-permute-start | bytes 1179656 | tf_op jit(solution)/shard_map/ppermute | solution.py:41
  322.5 46.6 %collective-permute-start.26 = (bf16[256,768]{1,0:T(8,128)(2,1)}, bf16[256,768]{1,0:T(8,128)(2,1)}, u32[]{:S(2)}, u32[]{:S(2)}) collective-permute-start(bf16[256,768]{1,0:T(8,128)(2,1)} %multiply_convert_fusion.9), channel_id=1, source_target_pairs={{0,3},{1,2},{2,1},{3,0},{4,7},{5,6},{6,5},{7,4},{8,11},{9,10},{10,... | collective-permute-start | bytes 1179656 | tf_op jit(solution)/shard_map/ppermute | solution.py:41
  376.1 19.8 %collective-permute-start.29 = (bf16[256,768]{1,0:T(8,128)(2,1)S(1)}, bf16[256,768]{1,0:T(8,128)(2,1)S(1)}, u32[]{:S(2)}, u32[]{:S(2)}) collective-permute-start(bf16[256,768]{1,0:T(8,128)(2,1)S(1)} %get-tuple-element.247), channel_id=1, source_target_pairs={{0,3},{1,2},{2,1},{3,0},{4,7},{5,6},{6,5},{7,4},{8,11},{9,10},{10,... | collective-permute-start | bytes 1179656 | tf_op jit(solution)/shard_map/ppermute | solution.py:41
  377.5 20.4 %collective-permute-start.28 = (bf16[256,768]{1,0:T(8,128)(2,1)S(1)}, bf16[256,768]{1,0:T(8,128)(2,1)S(1)}, u32[]{:S(2)}, u32[]{:S(2)}) collective-permute-start(bf16[256,768]{1,0:T(8,128)(2,1)S(1)} %get-tuple-element.248), channel_id=1, source_target_pairs={{0,2},{1,3},{2,0},{3,1},{4,6},{5,7},{6,4},{7,5},{8,10},{9,11},{10,... | collective-permute-start | bytes 1179656 | tf_op jit(solution)/shard_map/ppermute | solution.py:41
  380.1 23.3 %collective-permute-start.35 = (bf16[256,768]{1,0:T(8,128)(2,1)S(1)}, bf16[256,768]{1,0:T(8,128)(2,1)S(1)}, u32[]{:S(2)}, u32[]{:S(2)}) collective-permute-start(bf16[256,768]{1,0:T(8,128)(2,1)S(1)} %get-tuple-element.239), channel_id=1, source_target_pairs={{0,1},{1,0},{2,3},{3,2},{4,5},{5,4},{6,7},{7,6},{8,9},{9,8},{10,11... | collective-permute-start | bytes 1179656 | tf_op jit(solution)/shard_map/ppermute | solution.py:41
  381.6 30.8 %collective-permute-start.37 = (bf16[256,768]{1,0:T(8,128)(2,1)S(1)}, bf16[256,768]{1,0:T(8,128)(2,1)S(1)}, u32[]{:S(2)}, u32[]{:S(2)}) collective-permute-start(bf16[256,768]{1,0:T(8,128)(2,1)S(1)} %get-tuple-element.240), channel_id=1, source_target_pairs={{0,3},{1,2},{2,1},{3,0},{4,7},{5,6},{6,5},{7,4},{8,11},{9,10},{10,... | collective-permute-start | bytes 1179656 | tf_op jit(solution)/shard_map/ppermute | solution.py:41
  386.5 27.2 %collective-permute-start.36 = (bf16[256,768]{1,0:T(8,128)(2,1)S(1)}, bf16[256,768]{1,0:T(8,128)(2,1)S(1)}, u32[]{:S(2)}, u32[]{:S(2)}) collective-permute-start(bf16[256,768]{1,0:T(8,128)(2,1)S(1)} %get-tuple-element.241), channel_id=1, source_target_pairs={{0,2},{1,3},{2,0},{3,1},{4,6},{5,7},{6,4},{7,5},{8,10},{9,11},{10,... | collective-permute-start | bytes 1179656 | tf_op jit(solution)/shard_map/ppermute | solution.py:41
  416.6 17.9 %collective-permute-start.39 = (bf16[256,768]{1,0:T(8,128)(2,1)S(1)}, bf16[256,768]{1,0:T(8,128)(2,1)S(1)}, u32[]{:S(2)}, u32[]{:S(2)}) collective-permute-start(bf16[256,768]{1,0:T(8,128)(2,1)S(1)} %fusion.133), channel_id=1, source_target_pairs={{0,2},{1,3},{2,0},{3,1},{4,6},{5,7},{6,4},{7,5},{8,10},{9,11},{10,... | collective-permute-start | bytes 1179656 | tf_op jit(solution)/shard_map/ppermute | solution.py:41
  418.1 16.5 %collective-permute-start.38 = (bf16[256,768]{1,0:T(8,128)(2,1)S(1)}, bf16[256,768]{1,0:T(8,128)(2,1)S(1)}, u32[]{:S(2)}, u32[]{:S(2)}) collective-permute-start(bf16[256,768]{1,0:T(8,128)(2,1)S(1)} %fusion.133), channel_id=1, source_target_pairs={{0,1},{1,0},{2,3},{3,2},{4,5},{5,4},{6,7},{7,6},{8,9},{9,8},{10,11... | collective-permute-start | bytes 1179656 | tf_op jit(solution)/shard_map/ppermute | solution.py:41
  438.6 18.7 %collective-permute-start.43 = (bf16[256,768]{1,0:T(8,128)(2,1)S(1)}, bf16[256,768]{1,0:T(8,128)(2,1)S(1)}, u32[]{:S(2)}, u32[]{:S(2)}) collective-permute-start(bf16[256,768]{1,0:T(8,128)(2,1)S(1)} %get-tuple-element.237), channel_id=1, source_target_pairs={{0,3},{1,2},{2,1},{3,0},{4,7},{5,6},{6,5},{7,4},{8,11},{9,10},{10,... | collective-permute-start | bytes 1179656 | tf_op jit(solution)/shard_map/ppermute | solution.py:41
  439.8 18.8 %collective-permute-start.42 = (bf16[256,768]{1,0:T(8,128)(2,1)S(1)}, bf16[256,768]{1,0:T(8,128)(2,1)S(1)}, u32[]{:S(2)}, u32[]{:S(2)}) collective-permute-start(bf16[256,768]{1,0:T(8,128)(2,1)S(1)} %get-tuple-element.238), channel_id=1, source_target_pairs={{0,2},{1,3},{2,0},{3,1},{4,6},{5,7},{6,4},{7,5},{8,10},{9,11},{10,... | collective-permute-start | bytes 1179656 | tf_op jit(solution)/shard_map/ppermute | solution.py:41
  462.4 16.7 %collective-permute-start.45 = (bf16[256,768]{1,0:T(8,128)(2,1)S(1)}, bf16[256,768]{1,0:T(8,128)(2,1)S(1)}, u32[]{:S(2)}, u32[]{:S(2)}) collective-permute-start(bf16[256,768]{1,0:T(8,128)(2,1)S(1)} %get-tuple-element.192), channel_id=1, source_target_pairs={{0,2},{1,3},{2,0},{3,1},{4,6},{5,7},{6,4},{7,5},{8,10},{9,11},{10,... | collective-permute-start | bytes 1179656 | tf_op jit(solution)/shard_map/ppermute | solution.py:41
  503.9 19.1 %collective-permute-start.49 = (bf16[256,768]{1,0:T(8,128)(2,1)S(1)}, bf16[256,768]{1,0:T(8,128)(2,1)S(1)}, u32[]{:S(2)}, u32[]{:S(2)}) collective-permute-start(bf16[256,768]{1,0:T(8,128)(2,1)S(1)} %get-tuple-element.230), channel_id=1, source_target_pairs={{0,3},{1,2},{2,1},{3,0},{4,7},{5,6},{6,5},{7,4},{8,11},{9,10},{10,... | collective-permute-start | bytes 1179656 | tf_op jit(solution)/shard_map/ppermute | solution.py:41
  505.5 18.9 %collective-permute-start.48 = (bf16[256,768]{1,0:T(8,128)(2,1)S(1)}, bf16[256,768]{1,0:T(8,128)(2,1)S(1)}, u32[]{:S(2)}, u32[]{:S(2)}) collective-permute-start(bf16[256,768]{1,0:T(8,128)(2,1)S(1)} %get-tuple-element.231), channel_id=1, source_target_pairs={{0,2},{1,3},{2,0},{3,1},{4,6},{5,7},{6,4},{7,5},{8,10},{9,11},{10,... | collective-permute-start | bytes 1179656 | tf_op jit(solution)/shard_map/ppermute | solution.py:41
  527.2 16.8 %collective-permute-start.51 = (bf16[256,768]{1,0:T(8,128)(2,1)S(1)}, bf16[256,768]{1,0:T(8,128)(2,1)S(1)}, u32[]{:S(2)}, u32[]{:S(2)}) collective-permute-start(bf16[256,768]{1,0:T(8,128)(2,1)S(1)} %fusion.118), channel_id=1, source_target_pairs={{0,2},{1,3},{2,0},{3,1},{4,6},{5,7},{6,4},{7,5},{8,10},{9,11},{10,... | collective-permute-start | bytes 1179656 | tf_op jit(solution)/shard_map/ppermute | solution.py:41
  548.2 18.8 %collective-permute-start.55 = (bf16[256,768]{1,0:T(8,128)(2,1)S(1)}, bf16[256,768]{1,0:T(8,128)(2,1)}, u32[]{:S(2)}, u32[]{:S(2)}) collective-permute-start(bf16[256,768]{1,0:T(8,128)(2,1)S(1)} %get-tuple-element.227), channel_id=1, source_target_pairs={{0,3},{1,2},{2,1},{3,0},{4,7},{5,6},{6,5},{7,4},{8,11},{9,10},{10,... | collective-permute-start | bytes 1179656 | tf_op jit(solution)/shard_map/ppermute | solution.py:41
  549.8 18.7 %collective-permute-start.54 = (bf16[256,768]{1,0:T(8,128)(2,1)S(1)}, bf16[256,768]{1,0:T(8,128)(2,1)}, u32[]{:S(2)}, u32[]{:S(2)}) collective-permute-start(bf16[256,768]{1,0:T(8,128)(2,1)S(1)} %get-tuple-element.228), channel_id=1, source_target_pairs={{0,2},{1,3},{2,0},{3,1},{4,6},{5,7},{6,4},{7,5},{8,10},{9,11},{10,... | collective-permute-start | bytes 1179656 | tf_op jit(solution)/shard_map/ppermute | solution.py:41
  556.3 21.1 %collective-permute-start.67 = (bf16[4,96,768]{2,1,0:T(8,128)(2,1)S(1)}, bf16[4,96,768]{2,1,0:T(8,128)(2,1)S(1)}, u32[]{:S(2)}, u32[]{:S(2)}) collective-permute-start(bf16[4,96,768]{2,1,0:T(8,128)(2,1)S(1)} %dynamic-slice_bitcast_fusion.4), channel_id=1, source_target_pairs={{0,16},{16,0},{1,17},{17,1},{2,18},{18,2},{3,19},{19,3},{4,20},{20... | collective-permute-start | bytes 1769480 | tf_op jit(solution)/shard_map/ppermute | solution.py:36
  578.4 263.6 %reduce-scatter.8.cloned.1.call-start = ((), (), s32[]{:S(2)}) async-start(), calls=%async_computation.11 | async-start | bytes 737280 | tf_op jit(solution)/shard_map/reduce_scatter | solution.py:350
  626.3 24.6 %collective-permute-start.70 = (bf16[4,96,1536]{2,1,0:T(8,128)(2,1)S(1)}, bf16[4,96,1536]{2,1,0:T(8,128)(2,1)}, u32[]{:S(2)}, u32[]{:S(2)}) collective-permute-start(bf16[4,96,1536]{2,1,0:T(8,128)(2,1)S(1)} %dynamic-slice_bitcast_fusion.2), channel_id=1, source_target_pairs={{0,16},{16,0},{1,17},{17,1},{2,18},{18,2},{3,19},{19,3},{4,20},{20... | collective-permute-start | bytes 3538952 | tf_op jit(solution)/shard_map/ppermute | solution.py:36
  629.0 236.9 %reduce-scatter.14.cloned.1.call-start = ((), (), s32[]{:S(2)}) async-start(), calls=%async_computation.14 | async-start | bytes 1474560 | tf_op jit(solution)/shard_map/reduce_scatter | solution.py:350
  630.4 19.1 %collective-permute-start.31 = (bf16[256,768]{1,0:T(8,128)(2,1)S(1)}, bf16[256,768]{1,0:T(8,128)(2,1)S(1)}, u32[]{:S(2)}, u32[]{:S(2)}) collective-permute-start(bf16[256,768]{1,0:T(8,128)(2,1)S(1)} %copy-done.37), channel_id=1, source_target_pairs={{0,2},{1,3},{2,0},{3,1},{4,6},{5,7},{6,4},{7,5},{8,10},{9,11},{10,... | collective-permute-start | bytes 1179656 | tf_op jit(solution)/shard_map/ppermute | solution.py:41
  631.7 17.8 %collective-permute-start.30 = (bf16[256,768]{1,0:T(8,128)(2,1)S(1)}, bf16[256,768]{1,0:T(8,128)(2,1)S(1)}, u32[]{:S(2)}, u32[]{:S(2)}) collective-permute-start(bf16[256,768]{1,0:T(8,128)(2,1)S(1)} %copy-done.37), channel_id=1, source_target_pairs={{0,1},{1,0},{2,3},{3,2},{4,5},{5,4},{6,7},{7,6},{8,9},{9,8},{10,11... | collective-permute-start | bytes 1179656 | tf_op jit(solution)/shard_map/ppermute | solution.py:41
  653.9 212.0 %reduce-scatter.12.cloned.1.call-start = ((), (), s32[]{:S(2)}) async-start(), calls=%async_computation.13 | async-start | bytes 1474560 | tf_op jit(solution)/shard_map/reduce_scatter | solution.py:350
  674.8 225.2 %reduce-scatter.6.cloned.1.call-start = ((), (), s32[]{:S(2)}) async-start(), calls=%async_computation.10 | async-start | bytes 7864320 | tf_op jit(solution)/shard_map/reduce_scatter | solution.py:333
  700.5 19.6 %collective-permute-start.61 = (bf16[256,768]{1,0:T(8,128)(2,1)}, bf16[256,768]{1,0:T(8,128)(2,1)}, u32[]{:S(2)}, u32[]{:S(2)}) collective-permute-start(bf16[256,768]{1,0:T(8,128)(2,1)} %get-tuple-element.220), channel_id=1, source_target_pairs={{0,3},{1,2},{2,1},{3,0},{4,7},{5,6},{6,5},{7,4},{8,11},{9,10},{10,... | collective-permute-start | bytes 1179656 | tf_op jit(solution)/shard_map/ppermute | solution.py:41
  702.1 19.1 %collective-permute-start.60 = (bf16[256,768]{1,0:T(8,128)(2,1)S(1)}, bf16[256,768]{1,0:T(8,128)(2,1)}, u32[]{:S(2)}, u32[]{:S(2)}) collective-permute-start(bf16[256,768]{1,0:T(8,128)(2,1)S(1)} %copy-done.55), channel_id=1, source_target_pairs={{0,2},{1,3},{2,0},{3,1},{4,6},{5,7},{6,4},{7,5},{8,10},{9,11},{10,... | collective-permute-start | bytes 1179656 | tf_op jit(solution)/shard_map/ppermute | solution.py:41
  724.5 55.3 %all-to-all-start.1 = ((bf16[4,256,192]{1,2,0:T(8,128)(2,1)}), bf16[4,256,192]{1,2,0:T(8,128)(2,1)S(1)}, u32[]{:S(2)}, u32[]{:S(2)}) async-start(bf16[4,256,192]{1,2,0:T(8,128)(2,1)} %bitcast.165), calls=%async_computation.2 | async-start | bytes 786432 | tf_op jit(solution)/shard_map/all_to_all | solution.py:382
  779.8 60.5 %collective-permute-start.64 = (bf16[4,256,192]{1,2,0:T(8,128)(2,1)S(1)}, bf16[4,256,192]{1,2,0:T(8,128)(2,1)S(1)}, u32[]{:S(2)}, u32[]{:S(2)}) collective-permute-start(bf16[4,256,192]{1,2,0:T(8,128)(2,1)S(1)} %all-to-all-done.1), channel_id=1, source_target_pairs={{0,3},{1,2},{2,1},{3,0},{4,7},{5,6},{6,5},{7,4},{8,11},{9,10},{10,... | collective-permute-start | bytes 1179656 | tf_op jit(solution)/shard_map/ppermute | solution.py:41
  779.9 60.4 %collective-permute-start.63 = (bf16[4,256,192]{1,2,0:T(8,128)(2,1)S(1)}, bf16[4,256,192]{1,2,0:T(8,128)(2,1)S(1)}, u32[]{:S(2)}, u32[]{:S(2)}) collective-permute-start(bf16[4,256,192]{1,2,0:T(8,128)(2,1)S(1)} %all-to-all-done.1), channel_id=1, source_target_pairs={{0,2},{1,3},{2,0},{3,1},{4,6},{5,7},{6,4},{7,5},{8,10},{9,11},{10,... | collective-permute-start | bytes 1179656 | tf_op jit(solution)/shard_map/ppermute | solution.py:41
  780.4 59.9 %collective-permute-start.62 = (bf16[4,256,192]{1,2,0:T(8,128)(2,1)S(1)}, bf16[4,256,192]{1,2,0:T(8,128)(2,1)S(1)}, u32[]{:S(2)}, u32[]{:S(2)}) collective-permute-start(bf16[4,256,192]{1,2,0:T(8,128)(2,1)S(1)} %all-to-all-done.1), channel_id=1, source_target_pairs={{0,1},{1,0},{2,3},{3,2},{4,5},{5,4},{6,7},{7,6},{8,9},{9,8},{10,11... | collective-permute-start | bytes 1179656 | tf_op jit(solution)/shard_map/ppermute | solution.py:41
  842.0 25.1 %collective-permute-start.65 = (bf16[4,4,256,192]{2,3,1,0:T(8,128)(2,1)}, bf16[4,4,256,192]{2,3,1,0:T(8,128)(2,1)}, u32[]{:S(2)}, u32[]{:S(2)}) collective-permute-start(bf16[4,4,256,192]{2,3,1,0:T(8,128)(2,1)} %pad_maximum_fusion.22), channel_id=1, source_target_pairs={{0,16},{16,0},{1,17},{17,1},{2,18},{18,2},{3,19},{19,3},{4,20},{20... | collective-permute-start | bytes 4718600 | tf_op jit(solution)/shard_map/ppermute | solution.py:36
  843.0 20.5 %collective-permute-start.68 = (bf16[96,768]{1,0:T(8,128)(2,1)S(1)}, bf16[96,768]{1,0:T(8,128)(2,1)S(1)}, u32[]{:S(2)}, u32[]{:S(2)}) collective-permute-start(bf16[96,768]{1,0:T(8,128)(2,1)S(1)} %get-tuple-element.279), channel_id=1, source_target_pairs={{0,16},{16,0},{1,17},{17,1},{2,18},{18,2},{3,19},{19,3},{4,20},{20... | collective-permute-start | bytes 442376 | tf_op jit(solution)/shard_map/ppermute | solution.py:36
  867.0 31.8 %collective-permute-start.71 = (bf16[96,1536]{1,0:T(8,128)(2,1)S(1)}, bf16[96,1536]{1,0:T(8,128)(2,1)S(1)}, u32[]{:S(2)}, u32[]{:S(2)}) collective-permute-start(bf16[96,1536]{1,0:T(8,128)(2,1)S(1)} %get-tuple-element.272), channel_id=1, source_target_pairs={{0,16},{16,0},{1,17},{17,1},{2,18},{18,2},{3,19},{19,3},{4,20},{20... | collective-permute-start | bytes 884744 | tf_op jit(solution)/shard_map/ppermute | solution.py:36
  (185 other events, 1475.5 us)
Sparse Core Ops, SparseCore 0:
  10.5 33.3 all-gather.6
  78.0 52.3 all-gather.8
  227.8 115.9 all-gather.10
  578.5 19.5 reduce-scatter.9
  629.1 19.1 reduce-scatter.7
  654.0 26.4 reduce-scatter.13
  682.8 27.8 reduce-scatter.11
  713.0 118.0 reduce-scatter.5

commit v2 on v1

v2 whole, which is shorter than its diff:
```python
import functools
import math

import jax
import jax.numpy as jnp
from jax import lax
from jax.experimental import pallas as pl
from jax.experimental.pallas import tpu as pltpu
from jax.sharding import PartitionSpec as P

D = 768
HEAD = 64

norm_eps = 1e-06
masked_score = -1e30
bf16 = jnp.bfloat16
f32 = jnp.float32


def mm(left, right, left_dim, right_dim):
    return lax.dot_general(
        left, right, (((left_dim,), (right_dim,)), ((), ())), preferred_element_type=f32
    )


def norm_factor(rows):
    return lax.rsqrt(jnp.mean(rows * rows, axis=-1, keepdims=True) + norm_eps)


def norm_back(grad, rows, gain):
    factor = norm_factor(rows)
    scaled = grad * gain
    inner = jnp.mean(scaled * rows, axis=-1, keepdims=True)
    grad_rows = factor * scaled - rows * (factor * factor * factor * inner)
    return grad_rows, jnp.sum(grad * rows * factor, axis=0)


MESH = pl.DeviceIdType.MESH


def place():
    core = lax.axis_index("section")
    tensor = lax.axis_index("tensor")
    return core, tensor // 2, tensor % 2, tensor


def remote(src, dst, send, recv, device):
    return pltpu.make_async_remote_copy(
        src_ref=src,
        dst_ref=dst,
        send_sem=send,
        recv_sem=recv,
        device_id=device,
        device_id_type=MESH,
    )


def greet(devices):
    barrier = pltpu.get_barrier_semaphore()
    for device in devices:
        pl.semaphore_signal(barrier, inc=1, device_id=device, device_id_type=MESH)
    pl.semaphore_wait(barrier, len(devices))


def comm_call(body, out_shape, scratch, collective_id, *operands, cargo=None):
    shapes = list(out_shape) if isinstance(out_shape, (list, tuple)) else [out_shape]
    in_specs = [pl.BlockSpec(memory_space=pltpu.VMEM)] * len(operands)
    out_specs = [pl.BlockSpec(memory_space=pltpu.VMEM)] * len(shapes)
    scratch = list(scratch)
    count_in, count_out = len(operands), len(shapes)
    if cargo is not None:
        kind, layer, array = cargo
        operands = operands + (array,)
        in_specs.append(pl.BlockSpec(memory_space=pl.ANY))
        if kind == "out":
            landing = [jax.ShapeDtypeStruct(array.shape, array.dtype)]
        else:
            batches, _, rows, width = array.shape
            landing = [jax.ShapeDtypeStruct((batches, rows, width), array.dtype)] * 2
        shapes += landing
        out_specs += [pl.BlockSpec(memory_space=pl.ANY)] * len(landing)
        scratch += [pltpu.SemaphoreType.DMA((3,))] * 2

    def kernel(*refs):
        ins, rest = refs[: len(operands)], refs[len(operands) :]
        outs, rest = rest[: len(shapes)], rest[len(shapes) :]
        if cargo is None:
            body(*ins, *outs, *rest)
            return
        send, recv = rest[-2:]
        load = functools.partial(
            Outward if kind == "out" else Inward, layer, ins[-1], outs[count_out:], send, recv
        )
        body(*ins[:-1], *outs[:count_out], *rest[:-2], load=load)

    results = pl.pallas_call(
        kernel,
        out_shape=shapes,
        in_specs=in_specs,
        out_specs=out_specs,
        scratch_shapes=scratch,
        compiler_params=pltpu.CompilerParams(
            collective_id=collective_id, has_side_effects=True, vmem_limit_bytes=40 << 20
        ),
    )(*operands)
    return results if len(shapes) > 1 else results[0]


class Outward:
    def __init__(self, layer, source, landing, send, recv):
        core, y, _, tensor = place()
        target = landing[0]
        self.layer, self.core, self.y = layer, core, y
        self.near = remote(source, target, send.at[0], recv.at[0], {"section": 1 - core})
        self.far = remote(
            source, target, send.at[1], recv.at[0], {"section": y, "tensor": tensor + 2 - 4 * y}
        )
        self.local = pltpu.make_async_copy(source, target, recv.at[1])

    def start(self):
        @pl.when(self.core == self.layer)
        def _():
            self.far.start()

            @pl.when(self.y == self.layer)
            def _():
                self.local.start()

            @pl.when(self.y != self.layer)
            def _():
                self.near.start()

    def wait(self):
        stays = (self.core == self.layer) & (self.y == self.layer)

        @pl.when(stays)
        def _():
            self.local.wait()

        @pl.when(jnp.logical_not(stays))
        def _():
            self.far.wait_recv()

        @pl.when(self.core == self.layer)
        def _():
            self.far.wait_send()

            @pl.when(self.y != self.layer)
            def _():
                self.near.wait_send()


class Inward:
    def __init__(self, layer, source, landing, send, recv):
        core, y, _, tensor = place()
        above = tensor + 2 - 4 * y
        self.near = core == y
        self.to_core = remote(
            source.at[:, 1 - y], landing[0], send.at[0], recv.at[0], {"section": 1 - core}
        )
        self.to_same = remote(
            source.at[:, 1 - y], landing[0], send.at[0], recv.at[0], {"tensor": above}
        )
        self.to_both = remote(
            source.at[:, y],
            landing[1],
            send.at[1],
            recv.at[1],
            {"section": 1 - core, "tensor": above},
        )
        self.fill = pltpu.make_async_copy(source.at[:, y], landing[1], recv.at[2])

    def start(self):
        @pl.when(self.near)
        def _():
            self.to_core.start()
            self.fill.start()

        @pl.when(jnp.logical_not(self.near))
        def _():
            self.to_same.start()
            self.to_both.start()

    def wait(self):
        @pl.when(self.near)
        def _():
            self.to_same.wait_recv()
            self.fill.wait()
            self.to_core.wait_send()

        @pl.when(jnp.logical_not(self.near))
        def _():
            self.to_core.wait_recv()
            self.to_both.wait_recv()
            self.to_same.wait_send()
            self.to_both.wait_send()


def greet_group(other, beside, load):
    if load is None:
        greet([other, beside])
        return None
    _, y, _, tensor = place()
    above = tensor + 2 - 4 * y
    greet([other, beside, {"section": 0, "tensor": above}, {"section": 1, "tensor": above}])
    made = load()
    made.start()
    return made


PIECES = 4


def group_gather_kernel(own, out, send, recv, load=None):
    core, _, x, tensor = place()
    other = {"section": 1 - core}
    beside = {"tensor": tensor + 1 - 2 * x}
    here = 2 * core + x
    there = 2 * core + 1 - x
    cargo = greet_group(other, beside, load)
    piece = own.shape[0] // PIECES
    cuts = [pl.ds(at * piece, piece) for at in range(PIECES)]
    across = []
    for at, cut in enumerate(cuts):
        copy = remote(own.at[cut], out.at[here, cut], send.at[at], recv.at[at], beside)
        copy.start()
        across.append(copy)
    last = 2 * PIECES
    direct = remote(own, out.at[here], send.at[last], recv.at[last], other)
    direct.start()
    out[here] = own[...]
    passed = []
    for at, cut in enumerate(cuts):
        across[at].wait_recv()
        copy = remote(
            out.at[there, cut],
            out.at[there, cut],
            send.at[PIECES + at],
            recv.at[PIECES + at],
            other,
        )
        copy.start()
        passed.append(copy)
    for copy in across:
        copy.wait_send()
    direct.wait()
    for copy in passed:
        copy.wait()
    if cargo is not None:
        cargo.wait()


def group_gather(rows, collective_id, cargo=None):
    count, width = rows.shape
    return comm_call(
        group_gather_kernel,
        jax.ShapeDtypeStruct((4, count, width), rows.dtype),
        [pltpu.SemaphoreType.DMA((2 * PIECES + 1,))] * 2,
        collective_id,
        rows,
        cargo=cargo,
    )


def group_reduce_kernel(parts, out, near, far, mixed, send, recv, load=None):
    core, _, x, tensor = place()
    other = {"section": 1 - core}
    beside = {"tensor": tensor + 1 - 2 * x}
    here = 2 * core + x
    there = 2 * core + 1 - x
    over_here = 2 * (1 - core) + x
    over_there = 2 * (1 - core) + 1 - x
    cargo = greet_group(other, beside, load)
    piece = out.shape[0] // PIECES
    cuts = [pl.ds(at * piece, piece) for at in range(PIECES)]
    first = []
    for at, cut in enumerate(cuts):
        copy = remote(
            parts.at[over_there, cut], near.at[1, cut], send.at[at], recv.at[at], other
        )
        copy.start()
        first.append(copy)
    last = 2 * PIECES
    direct = remote(parts.at[over_here], near.at[0], send.at[last], recv.at[last], other)
    direct.start()
    across = []
    for at, cut in enumerate(cuts):
        first[at].wait_recv()
        mixed[cut] = (parts[there, cut].astype(f32) + near[1, cut].astype(f32)).astype(bf16)
        copy = remote(
            mixed.at[cut], far.at[cut], send.at[PIECES + at], recv.at[PIECES + at], beside
        )
        copy.start()
        across.append(copy)
    direct.wait()
    for at, cut in enumerate(cuts):
        across[at].wait_recv()
        out[cut] = (
            parts[here, cut].astype(f32) + near[0, cut].astype(f32) + far[cut].astype(f32)
        )
    for copy in first + across:
        copy.wait_send()
    if cargo is not None:
        cargo.wait()


def group_reduce(parts, collective_id, cargo=None):
    _, count, width = parts.shape
    return comm_call(
        group_reduce_kernel,
        jax.ShapeDtypeStruct((count, width), f32),
        [
            pltpu.VMEM((2, count, width), bf16),
            pltpu.VMEM((count, width), bf16),
            pltpu.VMEM((count, width), bf16),
        ]
        + [pltpu.SemaphoreType.DMA((2 * PIECES + 1,))] * 2,
        collective_id,
        parts,
        cargo=cargo,
    )


def turn_kernel(backward, rounded, *refs, load=None):
    if backward:
        parts, rows, gain, passed, gathered, fresh, gain_grad, near, far, mixed, send, recv = refs
    else:
        parts, rows, gain, gathered, fresh, near, far, mixed, send, recv = refs
    core, _, x, tensor = place()
    other = {"section": 1 - core}
    beside = {"tensor": tensor + 1 - 2 * x}
    here = 2 * core + x
    there = 2 * core + 1 - x
    over_here = 2 * (1 - core) + x
    over_there = 2 * (1 - core) + 1 - x
    cargo = greet_group(other, beside, load)
    piece = fresh.shape[0] // PIECES
    cuts = [pl.ds(at * piece, piece) for at in range(PIECES)]

    def start(src, dst, kind, at, device):
        index = kind * PIECES + at
        made = remote(src, dst, send.at[index], recv.at[index], device)
        made.start()
        return made

    handed, direct = [], []
    for at, cut in enumerate(cuts):
        handed.append(start(parts.at[over_there, cut], near.at[1, cut], 0, at, other))
        direct.append(start(parts.at[over_here, cut], near.at[0, cut], 1, at, other))
    across = []
    for at, cut in enumerate(cuts):
        handed[at].wait_recv()
        mixed[cut] = (parts[there, cut].astype(f32) + near[1, cut].astype(f32)).astype(bf16)
        across.append(start(mixed.at[cut], far.at[cut], 2, at, beside))
    out_across, out_direct, onward = [], [], []
    gains = gain[...]
    for at in range(PIECES + 1):
        if at < PIECES:
            cut = cuts[at]
            direct[at].wait_recv()
            across[at].wait_recv()
            total = (
                parts[here, cut].astype(f32) + near[0, cut].astype(f32) + far[cut].astype(f32)
            )
            held = rows[cut]
            if backward:
                factor = norm_factor(held)
                scaled = total * gains
                inner = jnp.mean(scaled * held, axis=-1, keepdims=True)
                new = passed[cut] + factor * scaled - held * (factor * factor * factor * inner)
                gain_part = jnp.sum(total * held * factor, axis=0, keepdims=True)
                gain_grad[...] = gain_part if at == 0 else gain_grad[...] + gain_part
                if rounded:
                    new = new.astype(bf16).astype(f32)
                shown = new.astype(bf16)
            else:
                new = held + total
                if rounded:
                    new = new.astype(bf16).astype(f32)
                shown = (new * norm_factor(new) * gains).astype(bf16)
            fresh[cut] = new
            gathered[here, cut] = shown
            out_across.append(start(gathered.at[here, cut], gathered.at[here, cut], 3, at, beside))
            out_direct.append(start(gathered.at[here, cut], gathered.at[here, cut], 4, at, other))
        if at >= 1:
            cut = cuts[at - 1]
            out_across[at - 1].wait_recv()
            onward.append(start(gathered.at[there, cut], gathered.at[there, cut], 5, at - 1, other))
    for made in handed + direct + across + out_across:
        made.wait_send()
    for made in out_direct + onward:
        made.wait()
    if cargo is not None:
        cargo.wait()


def turn(parts, rows, gain, collective_id, rounded, passed=None, cargo=None):
    _, count, width = parts.shape
    backward = passed is not None
    shapes = [
        jax.ShapeDtypeStruct((4, count, width), bf16),
        jax.ShapeDtypeStruct((count, width), f32),
    ]
    operands = [parts, rows, gain.reshape(1, width)]
    if backward:
        shapes.append(jax.ShapeDtypeStruct((1, width), f32))
        operands.append(passed)
    return comm_call(
        functools.partial(turn_kernel, backward, rounded),
        shapes,
        [
            pltpu.VMEM((2, count, width), bf16),
            pltpu.VMEM((count, width), bf16),
            pltpu.VMEM((count, width), bf16),
        ]
        + [pltpu.SemaphoreType.DMA((6 * PIECES,))] * 2,
        collective_id,
        *operands,
        cargo=cargo,
    )


def plane_gather_kernel(own, out, send, recv):
    core, y, x, tensor = place()
    other = {"section": 1 - core}
    beside = {"tensor": tensor + 1 - 2 * x}
    above = {"tensor": tensor + 2 - 4 * y}
    greet([other, beside, above])
    half = own.shape[0] // 2
    cut = [pl.ds(0, half), pl.ds(half, half)]

    def slot(along_y, along_x):
        return 4 * along_y + 2 * core + along_x

    me = slot(y, x)
    at_x, at_y, at_both = slot(y, 1 - x), slot(1 - y, x), slot(1 - y, 1 - x)

    def copy(src, where, index, device):
        made = remote(src, out.at[where], send.at[index], recv.at[index], device)
        made.start()
        return made

    to_x = [remote(own.at[cut[h]], out.at[me, cut[h]], send.at[h], recv.at[h], beside) for h in (0, 1)]
    to_y = [remote(own.at[cut[h]], out.at[me, cut[h]], send.at[2 + h], recv.at[2 + h], above) for h in (0, 1)]
    to_x[0].start()
    to_y[1].start()
    to_x[1].start()
    to_y[0].start()
    pending = [copy(own, me, 4, other)]
    out[me] = own[...]

    def onward(where, h, index, device):
        made = remote(
            out.at[where, cut[h]], out.at[where, cut[h]], send.at[index], recv.at[index], device
        )
        made.start()
        return made

    to_x[0].wait_recv()
    diag_y = onward(at_x, 0, 5, above)
    pending.append(onward(at_x, 0, 6, other))
    to_y[1].wait_recv()
    diag_x = onward(at_y, 1, 7, beside)
    pending.append(onward(at_y, 1, 8, other))
    to_x[1].wait_recv()
    pending.append(onward(at_x, 1, 9, other))
    to_y[0].wait_recv()
    pending.append(onward(at_y, 0, 10, other))
    diag_y.wait_recv()
    pending.append(onward(at_both, 0, 11, other))
    diag_x.wait_recv()
    pending.append(onward(at_both, 1, 12, other))
    for made in to_x + to_y + [diag_x, diag_y]:
        made.wait_send()
    for made in pending:
        made.wait()


def plane_gather(block, collective_id):
    count, width = block.shape
    return comm_call(
        plane_gather_kernel,
        jax.ShapeDtypeStruct((8, count, width), block.dtype),
        [pltpu.SemaphoreType.DMA((13,))] * 2,
        collective_id,
        block,
    )


def plane_reduce_kernel(parts, out, near, mixed, via_x, via_y, from_x, from_y, hop_x, hop_y, send, recv):
    core, y, x, tensor = place()
    other = {"section": 1 - core}
    beside = {"tensor": tensor + 1 - 2 * x}
    above = {"tensor": tensor + 2 - 4 * y}
    greet([other, beside, above])
    half = out.shape[0] // 2
    cut = [pl.ds(0, half), pl.ds(half, half)]

    def slot(at_core, along_y, along_x):
        return 4 * along_y + 2 * at_core + along_x

    targets = [(1 - y, 1 - x), (y, 1 - x), (1 - y, x), (y, x)]
    handed = []
    for index, (along_y, along_x) in enumerate(targets):
        made = remote(
            parts.at[slot(1 - core, along_y, along_x)],
            near.at[index],
            send.at[index],
            recv.at[index],
            other,
        )
        made.start()
        handed.append(made)

    def joined(index, where=slice(None)):
        along_y, along_x = targets[index]
        mine = parts[slot(core, along_y, along_x), where]
        return mine.astype(f32) + near[index, where].astype(f32)

    def start(src, dst, index, device):
        made = remote(src, dst, send.at[index], recv.at[index], device)
        made.start()
        return made

    handed[0].wait_recv()
    mixed[0] = joined(0).astype(bf16)
    diag_x = start(mixed.at[0, cut[0]], via_x, 4, beside)
    diag_y = start(mixed.at[0, cut[1]], via_y, 5, above)
    handed[1].wait_recv()
    mixed[1] = joined(1).astype(bf16)
    straight_x = start(mixed.at[1, cut[0]], from_x.at[cut[0]], 6, beside)
    handed[2].wait_recv()
    mixed[2] = joined(2).astype(bf16)
    straight_y = start(mixed.at[2, cut[1]], from_y.at[cut[1]], 7, above)
    diag_x.wait_recv()
    hop_y[...] = (mixed[2, cut[0]].astype(f32) + via_x[...].astype(f32)).astype(bf16)
    turned_y = start(hop_y, from_y.at[cut[0]], 8, above)
    diag_y.wait_recv()
    hop_x[...] = (mixed[1, cut[1]].astype(f32) + via_y[...].astype(f32)).astype(bf16)
    turned_x = start(hop_x, from_x.at[cut[1]], 9, beside)
    handed[3].wait_recv()
    straight_x.wait_recv()
    turned_y.wait_recv()
    out[cut[0]] = joined(3, cut[0]) + from_x[cut[0]].astype(f32) + from_y[cut[0]].astype(f32)
    straight_y.wait_recv()
    turned_x.wait_recv()
    out[cut[1]] = joined(3, cut[1]) + from_x[cut[1]].astype(f32) + from_y[cut[1]].astype(f32)
    for made in handed + [diag_x, diag_y, straight_x, straight_y, turned_x, turned_y]:
        made.wait_send()


def plane_reduce(parts, collective_id):
    _, count, width = parts.shape
    half = count // 2
    return comm_call(
        plane_reduce_kernel,
        jax.ShapeDtypeStruct((count, width), f32),
        [
            pltpu.VMEM((4, count, width), bf16),
            pltpu.VMEM((3, count, width), bf16),
            pltpu.VMEM((half, width), bf16),
            pltpu.VMEM((half, width), bf16),
            pltpu.VMEM((count, width), bf16),
            pltpu.VMEM((count, width), bf16),
            pltpu.VMEM((half, width), bf16),
            pltpu.VMEM((half, width), bf16),
        ]
        + [pltpu.SemaphoreType.DMA((10,))] * 2,
        collective_id,
        parts,
    )


def batch_gather_kernel(count, *refs):
    kinds = (len(refs) - 2) // 2
    ins, outs, (send, recv) = refs[:kinds], refs[kinds : 2 * kinds], refs[2 * kinds :]
    me = lax.axis_index("batch")
    peers = [{"batch": lax.rem(me + step, count)} for step in range(1, count)]
    greet(peers)
    copies = []
    for index, peer in enumerate(peers):
        for kind in range(kinds):
            at = index * kinds + kind
            copies.append(remote(ins[kind], outs[kind].at[me], send.at[at], recv.at[at], peer))
            copies[-1].start()
    for kind in range(kinds):
        outs[kind][me] = ins[kind][...]
    for copy in copies:
        copy.wait()


def batch_gather(blocks, collective_id):
    count = lax.axis_size("batch")
    return comm_call(
        functools.partial(batch_gather_kernel, count),
        [jax.ShapeDtypeStruct((count,) + block.shape, block.dtype) for block in blocks],
        [pltpu.SemaphoreType.DMA(((count - 1) * len(blocks),))] * 2,
        collective_id,
        *blocks,
    )


def batch_trade_kernel(count, parts, out, send, recv):
    me = lax.axis_index("batch")
    peers = [lax.rem(me + step, count) for step in range(1, count)]
    greet([{"batch": peer} for peer in peers])
    copies = []
    for index, peer in enumerate(peers):
        copies.append(
            remote(parts.at[peer], out.at[me], send.at[index], recv.at[index], {"batch": peer})
        )
        copies[-1].start()
    out[me] = parts[me]
    for copy in copies:
        copy.wait()


def batch_trade(parts):
    count = parts.shape[0]
    return comm_call(
        functools.partial(batch_trade_kernel, count),
        jax.ShapeDtypeStruct(parts.shape, parts.dtype),
        [pltpu.SemaphoreType.DMA((count - 1,))] * 2,
        8,
        parts,
    )


def causal_mix(projected, taps):
    once = jnp.pad(projected, ((1, 0), (0, 0)))[:-1]
    twice = jnp.pad(projected, ((2, 0), (0, 0)))[:-2]
    return taps[0] * projected + taps[1] * once + taps[2] * twice


def causal_mix_back(grad, projected, taps):
    ahead_one = jnp.pad(grad, ((0, 1), (0, 0)))[1:]
    ahead_two = jnp.pad(grad, ((0, 2), (0, 0)))[2:]
    grad_in = taps[0] * grad + taps[1] * ahead_one + taps[2] * ahead_two
    once = jnp.pad(projected, ((1, 0), (0, 0)))[:-1]
    twice = jnp.pad(projected, ((2, 0), (0, 0)))[:-2]
    grad_taps = [
        jnp.sum(grad * projected, 0),
        jnp.sum(grad * once, 0),
        jnp.sum(grad * twice, 0),
    ]
    return (grad_in, grad_taps)


def allowed_keys(lead, reach, length):
    query_at = jnp.arange(lead, reach)[:, None]
    key_at = jnp.arange(reach)[None, :]
    return (key_at <= query_at) & (key_at < length)


def attend(queries, keys_all, values_all, length):
    total = queries.shape[0]
    block = min(512, total)
    factor = queries.shape[-1] ** (-0.5)
    outputs = []
    totals = []
    for index in range(total // block):
        lead = index * block
        reach = lead + block
        scores = (
            jnp.einsum("qhd,khd->hqk", queries[lead:reach], keys_all[:reach], preferred_element_type=f32)
            * factor
        )
        scores = jnp.where(allowed_keys(lead, reach, length)[None], scores, masked_score)
        peak = jnp.max(scores, axis=-1, keepdims=True)
        raised = jnp.exp(scores - peak)
        weight_sum = jnp.sum(raised, axis=-1, keepdims=True)
        probs = (raised / weight_sum).astype(bf16)
        result = jnp.einsum("hqk,khd->qhd", probs, values_all[:reach], preferred_element_type=f32)
        outputs.append(result.astype(bf16))
        totals.append((peak + jnp.log(weight_sum))[..., 0])
    return (jnp.concatenate(outputs, 0), jnp.concatenate(totals, 1))


def attend_back(grad_out, queries, keys_all, values_all, length, totals):
    total = queries.shape[0]
    block = min(512, total)
    factor = queries.shape[-1] ** (-0.5)
    grad_queries = []
    grad_keys = jnp.zeros(keys_all.shape, f32)
    grad_values = jnp.zeros(values_all.shape, f32)
    for index in range(total // block):
        lead = index * block
        reach = lead + block
        scores = (
            jnp.einsum("qhd,khd->hqk", queries[lead:reach], keys_all[:reach], preferred_element_type=f32)
            * factor
        )
        allowed = allowed_keys(lead, reach, length)[None]
        probs = jnp.where(allowed, jnp.exp(scores - totals[:, lead:reach, None]), 0.0)
        grad_block = grad_out[lead:reach]
        grad_probs = jnp.einsum(
            "qhd,khd->hqk", grad_block, values_all[:reach], preferred_element_type=f32
        )
        inner = jnp.sum(probs * grad_probs, axis=-1, keepdims=True)
        grad_scores = (probs * (grad_probs - inner)).astype(bf16)
        grad_queries.append(
            jnp.einsum("hqk,khd->qhd", grad_scores, keys_all[:reach], preferred_element_type=f32)
            * factor
        )
        grad_keys = grad_keys.at[:reach].add(
            jnp.einsum("hqk,qhd->khd", grad_scores, queries[lead:reach], preferred_element_type=f32)
            * factor
        )
        grad_values = grad_values.at[:reach].add(
            jnp.einsum("hqk,qhd->khd", probs.astype(bf16), grad_block, preferred_element_type=f32)
        )
    return (jnp.concatenate(grad_queries, 0), grad_keys, grad_values)


def attention_forward(gathered, length, weights):
    qkv_mat, taps, out_turned = weights
    local_width = out_turned.shape[1]
    heads_here = local_width // HEAD
    projected = mm(gathered, qkv_mat, 1, 0)
    mixed = causal_mix(projected, taps).astype(bf16)
    triple = mixed.reshape(-1, 3, heads_here, HEAD)
    context, totals = attend(triple[:, 0], triple[:, 1], triple[:, 2], length)
    context = context.reshape(-1, local_width)
    partial = mm(context, out_turned, 1, 1).astype(bf16).reshape(4, -1, D)
    return partial, (gathered, projected, mixed, context, totals)


def attention_backward(grad_rows, length, weights, kept):
    qkv_mat, taps, out_turned = weights
    gathered, projected, mixed, context, totals = kept
    local_width = out_turned.shape[1]
    heads_here = local_width // HEAD
    grad_context = mm(grad_rows, out_turned, 1, 0).astype(bf16).reshape(-1, heads_here, HEAD)
    triple = mixed.reshape(-1, 3, heads_here, HEAD)
    grad_queries, grad_keys, grad_values = attend_back(
        grad_context, triple[:, 0], triple[:, 1], triple[:, 2], length, totals
    )
    grad_mixed = jnp.stack([grad_queries, grad_keys, grad_values], 1).reshape(-1, 3 * local_width)
    grad_projected, grad_taps = causal_mix_back(grad_mixed, projected, taps)
    grad_projected = grad_projected.astype(bf16)
    partial = mm(grad_projected, qkv_mat, 1, 1).astype(bf16).reshape(4, -1, D)
    grad_qkv = mm(gathered, grad_projected, 0, 0)
    grad_outmat = mm(grad_rows, context, 0, 0)
    blob = jnp.concatenate([grad_qkv.astype(bf16), grad_outmat.astype(bf16)], 1)
    return partial, blob, grad_taps


def ffn_forward(gathered, weights):
    up_mat, down_turned = weights
    hidden = mm(gathered, up_mat, 1, 0)
    active = jnp.square(jnp.maximum(hidden, 0.0)).astype(bf16)
    partial = mm(active, down_turned, 1, 1).astype(bf16).reshape(4, -1, D)
    return partial, (gathered, hidden, active)


def ffn_backward(grad_rows, weights, kept):
    up_mat, down_turned = weights
    gathered, hidden, active = kept
    grad_active = mm(grad_rows, down_turned, 1, 0)
    grad_hidden = (grad_active * 2.0 * jnp.maximum(hidden, 0.0)).astype(bf16)
    partial = mm(grad_hidden, up_mat, 1, 1).astype(bf16).reshape(4, -1, D)
    grad_down = mm(grad_rows, active, 0, 0)
    grad_up = mm(gathered, grad_hidden, 0, 0)
    blob = jnp.concatenate([grad_up.astype(bf16), grad_down.astype(bf16)], 1)
    return partial, blob


LOOK = 512


def lookup_kernel(ids, table, out):
    total = jnp.zeros((table.shape[0], ids.shape[2]), f32)
    wanted = ids[0]
    row = lax.broadcasted_iota(jnp.int32, (LOOK, ids.shape[2]), 0)
    for lead in range(0, table.shape[1], LOOK):
        hit = jnp.where(row == wanted - lead, 1.0, 0.0).astype(bf16)
        total += jnp.dot(table[:, lead : lead + LOOK], hit, preferred_element_type=f32)
    out[0, 0] = total.astype(bf16)


def lookup(table, ids):
    batches, parts, _, slots = ids.shape
    depth, vocab_rows = table.shape
    return pl.pallas_call(
        lookup_kernel,
        grid=(batches * parts,),
        out_shape=jax.ShapeDtypeStruct((parts, batches, depth, slots), bf16),
        in_specs=[
            pl.BlockSpec((1, 1, slots), lambda at: (at, 0, 0)),
            pl.BlockSpec((depth, vocab_rows), lambda at: (0, 0)),
        ],
        out_specs=pl.BlockSpec((1, 1, depth, slots), lambda at: (at % parts, at // parts, 0, 0)),
        compiler_params=pltpu.CompilerParams(vmem_limit_bytes=40 << 20),
    )(ids.reshape(batches * parts, 1, slots), table)


def spread_kernel(batches, ids, grads, base, out):
    at = pl.program_id(0)
    columns = out.shape[1]
    slots = ids.shape[2]
    row = lax.broadcasted_iota(jnp.int32, (columns, slots), 0) + at * columns

    def step(index, total):
        for part in range(8):
            hit = jnp.where(row == ids[index * 8 + part], 1.0, 0.0).astype(bf16)
            total += mm(grads[part, index], hit, 1, 1)
        return total

    out[...] = lax.fori_loop(0, batches, step, base[...].astype(f32))


def spread(grads, ids, base):
    parts, batches, depth, slots = grads.shape
    vocab_rows = base.shape[1]
    columns = 512
    return pl.pallas_call(
        functools.partial(spread_kernel, batches),
        grid=(vocab_rows // columns,),
        out_shape=jax.ShapeDtypeStruct((depth, vocab_rows), f32),
        in_specs=[
            pl.BlockSpec((batches * parts, 1, slots), lambda at: (0, 0, 0)),
            pl.BlockSpec((parts, batches, depth, slots), lambda at: (0, 0, 0, 0)),
            pl.BlockSpec((depth, columns), lambda at: (0, at)),
        ],
        out_specs=pl.BlockSpec((depth, columns), lambda at: (0, at)),
        compiler_params=pltpu.CompilerParams(vmem_limit_bytes=40 << 20),
    )(ids.reshape(batches * parts, 1, slots), grads, base)


def summed(landed):
    one, two = landed
    return (one.astype(f32) + two.astype(f32)).astype(bf16)


def over_batch(block):
    return lax.psum_scatter(block, "batch", scatter_dimension=0, tiled=False)


def tie(*values):
    return lax.optimization_barrier(values)


def on_device(
    token_ids,
    seq_lengths,
    embed_table,
    norm_gains,
    final_gain,
    qkv_weight,
    qkv_conv,
    out_weight,
    up_weight,
    down_weight,
    logit_grad,
):
    section = lax.axis_index("section")
    first = section == 0
    core, seq_at, x_at, _ = place()
    quarter = 2 * core + x_at
    me = lax.axis_index("tensor")
    at_batch = lax.axis_index("batch")
    tensor_count = lax.axis_size("tensor")
    batch_count = lax.axis_size("batch")
    section_count = lax.axis_size("section")
    slot_length = token_ids.shape[1]
    shard_rows = slot_length // tensor_count
    local_width = out_weight.shape[1]
    heads_here = local_width // HEAD
    hidden_width = up_weight.shape[2]
    root_scale = math.sqrt(D)
    depth = D // batch_count
    length = seq_lengths[seq_at]
    sequences = token_ids.shape[0]

    table_own = embed_table.astype(bf16).T
    attn_own = jnp.concatenate(
        [
            qkv_weight[0].reshape(depth, 3 * local_width).astype(bf16),
            out_weight[0].astype(bf16).T,
        ],
        1,
    )
    ffn_own = jnp.concatenate([up_weight[0].astype(bf16), down_weight[0].astype(bf16).T], 1)
    attn_all = lax.all_gather(attn_own, "batch", axis=0, tiled=True)
    ffn_all = lax.all_gather(ffn_own, "batch", axis=0, tiled=True)
    table_turned = lax.all_gather(table_own, "batch", axis=0, tiled=True)

    gain_width = final_gain.shape[0]
    small = jnp.concatenate(
        [norm_gains.astype(f32).reshape(-1), final_gain.astype(f32), qkv_conv.astype(f32).reshape(-1)]
    )
    small_rows = -(-small.shape[0] // 1024) * 8
    small = jnp.pad(small, (0, small_rows * 128 - small.shape[0])).reshape(small_rows, 128)
    all_ids, small = batch_gather([token_ids.reshape(-1, 128), small], 5)
    small = plane_gather(small.reshape(batch_count * small_rows, 128), 6)
    small = small.reshape(2, 2, 2, batch_count, -1).transpose(1, 3, 0, 2, 4)
    small = small.reshape(section_count, batch_count, tensor_count, -1).astype(bf16).astype(f32)
    gains_all = small[..., : 5 * gain_width].reshape(-1, 5, gain_width)
    gains_all = gains_all.transpose(1, 0, 2).reshape(5, D)
    taps_size = qkv_conv.size
    taps_all = small[..., 5 * gain_width : 5 * gain_width + taps_size].reshape(
        section_count, batch_count, tensor_count, 3, 3, heads_here, -1
    )
    taps_here = lax.dynamic_index_in_dim(taps_all, quarter, 2, keepdims=False)
    taps_here = taps_here.transpose(0, 3, 2, 4, 1, 5).reshape(section_count, 3, 3 * local_width)
    final_scale = gains_all[4]

    vocab_rows = embed_table.shape[0]
    owner_start = (section * tensor_count + me) * vocab_rows
    local_ids = all_ids.reshape(batch_count, sequences * 4, 1, shard_rows) - owner_start
    picked = lookup(table_own, local_ids)
    total = plane_reduce(picked.reshape(8, D, shard_rows), 3).astype(bf16)
    embedded = batch_trade(total.reshape(batch_count, depth, shard_rows))
    embedded = embedded.reshape(D, shard_rows).T

    def attn_weights(block, layer):
        return block[:, : 3 * local_width], taps_here[layer], block[:, 3 * local_width :]

    def ffn_weights(block):
        return block[:, :hidden_width], block[:, hidden_width:]

    first_rows = embedded.astype(f32) * root_scale
    normed = (first_rows * norm_factor(first_rows) * gains_all[0]).astype(bf16)
    gathered, block = group_gather(normed, 1, cargo=("out", 0, attn_all))
    attn_first = attn_weights(block, 0)
    partial, attn_kept_first = attention_forward(gathered.reshape(-1, D), length, attn_first)
    gathered, first_middle, block = turn(
        partial, first_rows, gains_all[1], 20, False, cargo=("out", 0, ffn_all)
    )
    ffn_first = ffn_weights(block)
    partial, ffn_kept_first = ffn_forward(gathered.reshape(-1, D), ffn_first)
    gathered, second_rows, block = turn(
        partial, first_middle, gains_all[2], 21, True, cargo=("out", 1, attn_all)
    )
    attn_second = attn_weights(block, 1)
    partial, attn_kept_second = attention_forward(gathered.reshape(-1, D), length, attn_second)
    gathered, second_middle, block = turn(
        partial, second_rows, gains_all[3], 24, False, cargo=("out", 1, ffn_all)
    )
    ffn_second = ffn_weights(block)
    partial, ffn_kept_second = ffn_forward(gathered.reshape(-1, D), ffn_second)

    def halves(blob):
        return blob.reshape(batch_count, 2, depth // 2, blob.shape[1])

    grad_both = mm(logit_grad.reshape(-1, vocab_rows), table_turned, 1, 1).astype(bf16)
    grad_final = plane_reduce(grad_both.reshape(8, shard_rows, D), 4)
    own_at = quarter * shard_rows + jnp.arange(shard_rows)
    grad_final = jnp.where((own_at < length)[:, None], grad_final, 0.0)

    partial, grad_final = tie(partial, grad_final)
    final_rows = (second_middle + group_reduce(partial, 2)).astype(bf16).astype(f32)
    normed_final = (final_rows * norm_factor(final_rows) * final_scale).astype(bf16)
    final_both = plane_gather(normed_final, 7).reshape(-1, D)
    logits = mm(final_both, table_turned, 1, 0).astype(bf16).reshape(sequences, slot_length, -1)
    valid = (jnp.arange(slot_length)[None, :] < seq_lengths[:, None]).reshape(-1, 1)
    masked_final = jnp.where(valid, final_both, jnp.zeros((), bf16))
    head_table = mm(masked_final, logit_grad.reshape(-1, vocab_rows), 0, 0).astype(bf16)
    grad_final, head_table = tie(grad_final, head_table)
    head_done = lax.psum_scatter(head_table, "batch", scatter_dimension=0, tiled=True)

    grad_rows, grad_final_gain = norm_back(grad_final, final_rows, final_scale)
    gathered = group_gather(grad_rows.astype(bf16), 13).reshape(-1, D)
    partial, blob = ffn_backward(gathered, ffn_second, ffn_kept_second)
    gathered, grad_rows, gain_2f, *landed = turn(
        partial, second_middle, gains_all[3], 22, False, passed=grad_rows,
        cargo=("in", 1, halves(blob)),
    )
    ffn_second_sum = summed(landed)
    partial, blob, taps_second = attention_backward(
        gathered.reshape(-1, D), length, attn_second, attn_kept_second
    )
    gathered, grad_rows, gain_2a, *landed = turn(
        partial, second_rows, gains_all[2], 23, True, passed=grad_rows,
        cargo=("in", 1, halves(blob)),
    )
    attn_second_sum = summed(landed)
    partial, blob = ffn_backward(gathered.reshape(-1, D), ffn_first, ffn_kept_first)
    gathered, grad_rows, gain_1f, *landed = turn(
        partial, first_middle, gains_all[1], 25, False, passed=grad_rows,
        cargo=("in", 0, halves(blob)),
    )
    ffn_first_sum = summed(landed)
    partial, blob, taps_first = attention_backward(
        gathered.reshape(-1, D), length, attn_first, attn_kept_first
    )
    partial, head_done = tie(partial, head_done)
    ffn_second_done, attn_second_done = over_batch(ffn_second_sum), over_batch(attn_second_sum)
    grad_norm, *landed = group_reduce(partial, 14, cargo=("in", 0, halves(blob)))
    attn_first_sum = summed(landed)
    grad_norm, gain_1a = norm_back(grad_norm, first_rows, gains_all[0])
    grad_rows = grad_rows + grad_norm
    grad_rows, ffn_second_done, attn_second_done = tie(
        grad_rows, ffn_second_done, attn_second_done
    )
    ffn_first_done, attn_first_done = over_batch(ffn_first_sum), over_batch(attn_first_sum)

    def placed(first_part, second_part):
        keep = jnp.where(first, first_part, second_part)
        got = lax.ppermute(jnp.where(first, second_part, first_part), "section", [(0, 1), (1, 0)])
        return jnp.where(
            first, jnp.concatenate([keep, got], 0), jnp.concatenate([got, keep], 0)
        ).astype(f32)

    attn_done = placed(attn_first_done, attn_second_done)
    ffn_done = placed(ffn_first_done, ffn_second_done)
    qkv_done = attn_done[:, : 3 * local_width].reshape(1, depth, 3, local_width)
    out_done = attn_done[:, 3 * local_width :].T[None]
    up_done = ffn_done[:, :hidden_width][None]
    down_done = ffn_done[:, hidden_width:].T[None]

    embed_grad = (grad_rows * root_scale).astype(bf16).T
    traded = batch_trade(embed_grad.reshape(batch_count, depth, shard_rows))
    every = plane_gather(traded.reshape(D, shard_rows), 10)
    every = every.reshape(8, batch_count, depth, shard_rows)
    table_done = spread(every, local_ids, head_done).T

    def row_at(index, vector):
        padded = jnp.pad(vector, (0, D - vector.shape[0]))[None]
        return jnp.where(jnp.arange(16)[:, None] == index, padded, 0.0)

    vectors = [gain_1a, gain_1f[0], gain_2a[0], gain_2f[0], grad_final_gain, *taps_first, *taps_second]
    rows = sum(row_at(index, vector) for index, vector in enumerate(vectors))
    rows = plane_gather(rows, 11)
    gain_sums = jnp.sum(rows[:, :5], 0)
    holders = rows.reshape(2, 4, 16, D)[:, :, 5:11].reshape(2, 4, 2, 3, D)
    taps_sums = jnp.sum(lax.dynamic_index_in_dim(holders, me, 1, keepdims=False), 0)
    taps_sums = lax.dynamic_index_in_dim(taps_sums, section, 0, keepdims=False)
    sums = jnp.pad(jnp.concatenate([gain_sums, taps_sums]), ((0, 0), (0, 0)))
    sums = batch_gather([sums], 12)
    sums = jnp.sum(sums, 0)
    whole_at = (section * batch_count + at_batch) * tensor_count + me
    gain_part = lax.dynamic_slice_in_dim(sums[:5], whole_at * gain_width, gain_width, 1)
    gains_done = gain_part[:4].reshape(2, 2, gain_width)
    final_done = gain_part[4]
    conv_part = sums[5:8, : 3 * local_width].reshape(3, 3, heads_here, HEAD).transpose(1, 0, 2, 3)
    conv_done = lax.dynamic_slice_in_dim(
        conv_part, at_batch * qkv_conv.shape[4], qkv_conv.shape[4], 3
    )[None]
    return (
        logits,
        table_done,
        gains_done,
        final_done,
        qkv_done,
        conv_done,
        out_done,
        up_done,
        down_done,
    )


def solution(mesh):
    in_specs = (
        P("batch", None),
        P("batch"),
        P(("section", "tensor"), "batch"),
        P(None, None, ("section", "batch", "tensor")),
        P(("section", "batch", "tensor")),
        P("section", "batch", None, "tensor"),
        P("section", None, None, "tensor", "batch"),
        P("section", "tensor", "batch"),
        P("section", "batch", "tensor"),
        P("section", "tensor", "batch"),
        P("batch", None, ("section", "tensor")),
    )
    out_specs = (
        P("batch", None, ("section", "tensor")),
        P(("section", "tensor"), "batch"),
        P(None, None, ("section", "batch", "tensor")),
        P(("section", "batch", "tensor")),
        P("section", "batch", None, "tensor"),
        P("section", None, None, "tensor", "batch"),
        P("section", "tensor", "batch"),
        P("section", "batch", "tensor"),
        P("section", "tensor", "batch"),
    )
    return jax.shard_map(
        on_device, mesh=mesh, in_specs=in_specs, out_specs=out_specs, check_vma=False
    )
```

time: 984 us -> 677 us (0.69)
  Pallas kernels: 0 us -> 402 us
  waiting for transfers between devices: 275 us -> 0.3 us
  blocking collectives: 164 us -> 0 us
  local copies, waits for them, and re-layouts: 151 us -> 50.3 us
  other arithmetic: 163 us -> 64.7 us
  starting transfers between devices: 81.7 us -> 3.66 us
  matrix products: 121 us -> 134 us
    pallas_call x0 -> x22, Pallas kernels: none -> 402 us  [the longest x20 353 us: comm_call(): pl.pallas_call(kernel, out_shape=shapes, in_specs=in_specs, out_specs=out...]
    ppermute x72 -> x2, waiting for transfers between devices: 252 us -> 0.01 us  [placed(): lax.ppermute(jnp.where(first, second_part, first_part), 'section', [(0, 1...]
    psum x2 -> x0, blocking collectives: 106 us -> none  [the longest x1 55 us: on_device(): lax.psum(jnp.stack([gain_1a, gain_1f, gain_2a, gain_2f, grad_final_gain])...]
    ppermute x72 -> x2, starting transfers between devices: 73.5 us -> 2.34 us  [placed(): lax.ppermute(jnp.where(first, second_part, first_part), 'section', [(0, 1...]
    scatter-add x1 -> x0, other arithmetic: 52.7 us -> none  [on_device(): embed_part = jnp.zeros((vocab_rows, depth), f32).at[flat_ids].add(jnp.whe...]
    unnamed x1 -> x0, blocking collectives: 43.1 us -> none
    gather x2 -> x0, local copies, waits for them, and re-layouts: 40.2 us -> none  [on_device(): embed_table.astype(bf16)[safe_ids]]
    dot_general x26 -> x27, matrix products: 72.4 us -> 99.6 us  [mm(): lax.dot_general(left, right, (((left_dim,), (right_dim,)), ((), ())), pre...]
  transfers between devices with their start and end apart: 82 -> 10, of which waited for: 52 -> 0; matrix products, arithmetic and copies ran while one was open for 32% -> 27% of each run, Pallas kernels for 0% -> 52%
where the time goes in v2:
time: 677 us; the launch traced here: 672 us
  Pallas kernels  402 us (59%)
  matrix products  134 us (20%)
  other arithmetic  64.7 us (10%)
  local copies, waits for them, and re-layouts  50.3 us (7%)
  between operations  16.9 us (2%)
    pallas_call x20, Pallas kernels, comm_call(): pl.pallas_call(kernel, out_shape=shapes, in_specs=in_specs, out_specs=out...  353 us
    dot_general x27, matrix products, mm(): lax.dot_general(left, right, (((left_dim,), (right_dim,)), ((), ())), pre...  99.6 us
    pallas_call x1, Pallas kernels, spread(): pl.pallas_call(functools.partial(spread_kernel, batches), grid=(vocab_row...  29.4 us
    unnamed x271, local copies, waits for them, and re-layouts  27.1 us
    pallas_call x1, Pallas kernels, lookup(): pl.pallas_call(lookup_kernel, grid=(batches * parts,), out_shape=jax.Shap...  19.4 us
  transfers between devices with their start and end apart: 10, of which 0 were waited for; matrix products, arithmetic and copies ran while one was open for 27% of the time, Pallas kernels for 52%

profile of v2, /device:TPU:0, one launch (start us, length us, event | category | flops | bytes accessed | tf_op | source)
XLA Modules:
  0.0 671.7 jit_solution(1849403329017969375)
XLA Ops:
  18.2 8.5 %shard_map.198 = (s32[4,16,128]{2,1,0:T(8,128)S(1)}, f32[4,8,128]{2,1,0:T(8,128)S(1)}) custom-call(s32[16,128]{1,0:T(8,128)S(1)} %reshape.727.refs_0_, f32[8,128]{1,0:T(8,128)S(1)} %fusion.120.refs_1_), custom_call_target="tpu_custom_call" | custom-call | tf_op jit(solution)/shard_map/pallas_call | solution.py:96
  26.8 7.9 %shard_map.199 = f32[8,32,128]{2,1,0:T(8,128)S(1)} custom-call(f32[32,128]{1,0:T(8,128)S(1)} %bitcast.341), custom_call_target="tpu_custom_call" | custom-call | tf_op jit(solution)/shard_map/pallas_call | solution.py:96
  37.7 19.4 %shard_map.200 = bf16[8,4,192,256]{3,2,1,0:T(8,128)(2,1)S(1)} custom-call(s32[32,1,256]{2,1,0:T(1,128)S(1)} %bitcast.339, bf16[192,4096]{1,0:T(8,128)(2,1)S(1)} %copy-done), custom_call_target="tpu_custom_call" | custom-call | tf_op jit(solution)/shard_map/pallas_call | solution.py:784
  57.1 17.8 %shard_map.201 = f32[768,256]{1,0:T(8,128)S(1)} custom-call(bf16[8,768,256]{2,1,0:T(8,128)(2,1)S(1)} %bitcast.315), custom_call_target="tpu_custom_call" | custom-call | tf_op jit(solution)/shard_map/pallas_call | solution.py:96
  74.9 16.6 %shard_map.202 = bf16[4,192,256]{2,1,0:T(8,128)(2,1)S(1)} custom-call(bf16[4,192,256]{2,1,0:T(8,128)(2,1)S(1)} %bitcast.333), custom_call_target="tpu_custom_call" | custom-call | tf_op jit(solution)/shard_map/pallas_call | solution.py:96
  94.7 15.5 %shard_map.203 = (bf16[4,256,768]{2,1,0:T(8,128)(2,1)S(1)}, bf16[768,768]{1,0:T(8,128)(2,1)S(1)}) custom-call(bf16[256,768]{1,0:T(8,128)(2,1)S(1)} %get-tuple-element.268.refs_0_, bf16[768,768]{1,0:T(8,128)(2,1)S(1)} %copy-done.7), custom_call_target="tpu_custom_call" | custom-call | tf_op jit(solution)/shard_map/pallas_call | solution.py:96
  124.3 29.3 %shard_map.204 = (bf16[4,256,768]{2,1,0:T(8,128)(2,1)S(1)}, f32[256,768]{1,0:T(8,128)S(1)}, bf16[768,1536]{1,0:T(8,128)(2,1)S(1)}) custom-call(bf16[4,256,768]{2,1,0:T(8,128)(2,1)S(1)} %bitcast.322, f32[256,768]{1,0:T(8,128)S(1)} %get-tuple-element.267.refs_1_, f32[1,768]{1,0:T(1,128)S(1)} %slice.454.refs_2_, bf16[768,1536]{1,0:T(8,128)(2,1)S(1)} %copy-done.1), custom_call_target="tpu_custom_call" | custom-call | tf_op jit(solution)/shard_map/pallas_call | solution.py:96
  157.1 25.6 %shard_map.205 = (bf16[4,256,768]{2,1,0:T(8,128)(2,1)S(1)}, f32[256,768]{1,0:T(8,128)S(1)}, bf16[768,768]{1,0:T(8,128)(2,1)S(1)}) custom-call(bf16[4,256,768]{2,1,0:T(8,128)(2,1)S(1)} %bitcast.327, f32[256,768]{1,0:T(8,128)S(1)} %get-tuple-element.183.refs_1_, f32[1,768]{1,0:T(1,128)S(1)} %slice.458.refs_2_, bf16[768,768]{1,0:T(8,128)(2,1)S(1)} %copy-done.8), custom_call_target="tpu_custom_call" | custom-call | tf_op jit(solution)/shard_map/pallas_call | solution.py:96
  191.5 2.2 fusion.76
  195.5 23.6 %shard_map.206 = (bf16[4,256,768]{2,1,0:T(8,128)(2,1)S(1)}, f32[256,768]{1,0:T(8,128)S(1)}, bf16[768,1536]{1,0:T(8,128)(2,1)S(1)}) custom-call(bf16[4,256,768]{2,1,0:T(8,128)(2,1)S(1)} %bitcast.323, f32[256,768]{1,0:T(8,128)S(1)} %get-tuple-element.186.refs_1_, f32[1,768]{1,0:T(1,128)S(1)} %slice.476.refs_2_, bf16[768,1536]{1,0:T(8,128)(2,1)S(1)} %copy-done.2), custom_call_target="tpu_custom_call" | custom-call | tf_op jit(solution)/shard_map/pallas_call | solution.py:96
  224.1 18.2 %convolution_convert_fusion.2 = bf16[2048,768]{1,0:T(8,128)(2,1)S(1)} fusion(bf16[2048,4096]{1,0:T(8,128)(2,1)} %bitcast.404, bf16[768,4096]{1,0:T(8,128)(2,1)} %all-gather.8.cloned.1.call-done), kind=kOutput, calls=%fused_computation.16 | convolution fusion | flops 12886474752 | bytes 26214400 | tf_op jit(solution)/shard_map/dot_general | solution.py:21
  242.3 22.4 %shard_map.207 = f32[256,768]{1,0:T(8,128)S(1)} custom-call(bf16[8,256,768]{2,1,0:T(8,128)(2,1)S(1)} %bitcast.326), custom_call_target="tpu_custom_call" | custom-call | tf_op jit(solution)/shard_map/pallas_call | solution.py:96
  265.8 12.8 %shard_map.208 = f32[256,768]{1,0:T(8,128)S(1)} custom-call(bf16[4,256,768]{2,1,0:T(8,128)(2,1)S(1)} %bitcast.329), custom_call_target="tpu_custom_call" | custom-call | tf_op jit(solution)/shard_map/pallas_call | solution.py:96
  279.0 17.0 %shard_map.209 = bf16[8,256,768]{2,1,0:T(8,128)(2,1)S(1)} custom-call(bf16[256,768]{1,0:T(8,128)(2,1)S(1)} %fusion.98.refs_0_), custom_call_target="tpu_custom_call" | custom-call | tf_op jit(solution)/shard_map/pallas_call | solution.py:96
  296.5 18.9 %convolution_convert_fusion.1 = bf16[768,4096]{1,0:T(8,128)(2,1)} fusion(bf16[2048,768]{1,0:T(8,128)(2,1)S(1)} %bitcast.382, bf16[2048,4096]{1,0:T(8,128)(2,1)} %bitcast.405), kind=kOutput, calls=%fused_computation.1 | convolution fusion | flops 12888047616 | bytes 26214400 | tf_op jit(solution)/shard_map/dot_general | solution.py:21
  318.8 2.2 fusion.102
  321.0 2.5 fusion.144
  323.5 12.5 %shard_map.210 = bf16[4,256,768]{2,1,0:T(8,128)(2,1)S(1)} custom-call(bf16[256,768]{1,0:T(8,128)(2,1)S(1)} %get-tuple-element.259.refs_0_), custom_call_target="tpu_custom_call" | custom-call | tf_op jit(solution)/shard_map/pallas_call | solution.py:96
  341.9 4.3 copy.76
  346.2 3.4 convolution_convert_fusion.6
  349.6 22.9 %shard_map.211 = (bf16[4,256,768]{2,1,0:T(8,128)(2,1)S(1)}, f32[256,768]{1,0:T(8,128)S(1)}, f32[1,768]{1,0:T(1,128)S(1)}, bf16[4,96,1536]{2,1,0:T(8,128)(2,1)S(1)}, bf16[4,96,1536]{2,1,0:T(8,128)(2,1)S(1)}) custom-call(bf16[4,256,768]{2,1,0:T(8,128)(2,1)S(1)} %bitcast.335, f32[256,768]{1,0:T(8,128)S(1)} %copy-done.15, f32[1,768]{1,0:T(1,128)S(1)} %slice.476.refs_2_, ...), custom_call_target="tpu_custom_call" | custom-call | tf_op jit(solution)/shard_map/pallas_call | solution.py:96
  372.6 2.3 convolution_convert_fusion.18
  379.5 2.6 multiply_reduce_fusion.1
  390.9 4.6 multiply_reduce_fusion.6
  397.8 2.4 copy.80
  400.2 3.2 convolution_convert_fusion.4
  403.4 29.3 %shard_map.212 = (bf16[4,256,768]{2,1,0:T(8,128)(2,1)S(1)}, f32[256,768]{1,0:T(8,128)S(1)}, f32[1,768]{1,0:T(1,128)S(1)}, bf16[4,96,768]{2,1,0:T(8,128)(2,1)S(1)}, bf16[4,96,768]{2,1,0:T(8,128)(2,1)S(1)}) custom-call(bf16[4,256,768]{2,1,0:T(8,128)(2,1)S(1)} %bitcast.328, f32[256,768]{1,0:T(8,128)S(1)} %copy-done.13, f32[1,768]{1,0:T(1,128)S(1)} %slice.458.refs_2_, ...), custom_call_target="tpu_custom_call" | custom-call | tf_op jit(solution)/shard_map/pallas_call | solution.py:96
  435.7 4.3 multiply_convert_fusion.3
  440.0 2.6 convolution_convert_fusion.5
  442.5 2.5 convolution_convert_fusion.12
  445.1 2.5 convolution_convert_fusion.11
  447.7 3.2 pad_maximum_fusion.2
  450.8 4.3 copy.81
  460.5 22.9 %shard_map.213 = (bf16[4,256,768]{2,1,0:T(8,128)(2,1)S(1)}, f32[256,768]{1,0:T(8,128)S(1)}, f32[1,768]{1,0:T(1,128)S(1)}, bf16[4,96,1536]{2,1,0:T(8,128)(2,1)S(1)}, bf16[4,96,1536]{2,1,0:T(8,128)(2,1)S(1)}) custom-call(bf16[4,256,768]{2,1,0:T(8,128)(2,1)S(1)} %bitcast.334, f32[256,768]{1,0:T(8,128)S(1)} %copy-done.11, f32[1,768]{1,0:T(1,128)S(1)} %slice.454.refs_2_, ...), custom_call_target="tpu_custom_call" | custom-call | tf_op jit(solution)/shard_map/pallas_call | solution.py:96
  492.0 3.4 multiply_reduce_fusion.2
  495.4 3.0 multiply_convert_fusion.2
  498.5 2.6 multiply_reduce_fusion
  508.9 2.5 fusion.50
  515.7 18.7 %convolution_convert_fusion = bf16[2048,4096]{1,0:T(8,128)(2,1)} fusion(bf16[2048,768]{1,0:T(8,128)(2,1)S(1)} %bitcast.313, bf16[768,4096]{1,0:T(8,128)(2,1)} %all-gather.8.cloned.1.call-done), kind=kOutput, calls=%fused_computation | convolution fusion | flops 12893290496 | bytes 26214400 | tf_op jit(solution)/shard_map/dot_general | solution.py:21
  534.5 5.3 multiply_reduce_fusion.9
  545.9 2.3 convolution_convert_fusion.15
  549.7 3.0 convolution_convert_fusion.3
  552.8 19.0 %shard_map.214 = (f32[256,768]{1,0:T(8,128)S(1)}, bf16[4,96,768]{2,1,0:T(8,128)(2,1)S(1)}, bf16[4,96,768]{2,1,0:T(8,128)(2,1)S(1)}) custom-call(bf16[4,256,768]{2,1,0:T(8,128)(2,1)S(1)} %bitcast.336, bf16[4,2,96,768]{3,2,1,0:T(8,128)(2,1)S(1)} %bitcast.324), custom_call_target="tpu_custom_call" | custom-call | tf_op jit(solution)/shard_map/pallas_call | solution.py:96
  574.2 16.8 %shard_map.215 = bf16[4,192,256]{2,1,0:T(8,128)(2,1)S(1)} custom-call(bf16[4,192,256]{2,1,0:T(8,128)(2,1)S(1)} %bitcast.332), custom_call_target="tpu_custom_call" | custom-call | tf_op jit(solution)/shard_map/pallas_call | solution.py:96
  595.2 8.1 %shard_map.218 = f32[8,16,768]{2,1,0:T(8,128)S(1)} custom-call(f32[16,768]{1,0:T(8,128)S(1)} %select_add_fusion.refs_0_), custom_call_target="tpu_custom_call" | custom-call | tf_op jit(solution)/shard_map/pallas_call | solution.py:96
  603.5 8.1 %shard_map.219 = f32[4,8,768]{2,1,0:T(8,128)S(1)} custom-call(f32[8,768]{1,0:T(8,128)S(1)} %pad_maximum_fusion.10.refs_0_), custom_call_target="tpu_custom_call" | custom-call | tf_op jit(solution)/shard_map/pallas_call | solution.py:96
  613.1 16.7 %shard_map.216 = bf16[8,768,256]{2,1,0:T(8,128)(2,1)S(1)} custom-call(bf16[768,256]{1,0:T(8,128)(2,1)S(1)} %bitcast.330), custom_call_target="tpu_custom_call" | custom-call | tf_op jit(solution)/shard_map/pallas_call | solution.py:96
  629.8 29.4 %shard_map.217 = f32[192,4096]{1,0:T(8,128)} custom-call(s32[32,1,256]{2,1,0:T(1,128)S(1)} %bitcast.340, bf16[8,4,192,256]{3,2,1,0:T(8,128)(2,1)S(1)} %bitcast.314, bf16[192,4096]{1,0:T(8,128)(2,1)S(1)} %copy-done.18), custom_call_target="tpu_custom_call" | custom-call | tf_op jit(solution)/shard_map/pallas_call | solution.py:816
  (467 shorter events, 125.8 us)
Async XLA Ops:
  7.2 86.2 %all-gather.4.cloned.1.call-start = ((), (), s32[]{:S(2)}) async-start(), calls=%async_computation.5 | async-start | bytes 1474560 | tf_op jit(solution)/shard_map/all_gather | solution.py:884
  10.6 112.0 %all-gather.6.cloned.1.call-start = ((), (), s32[]{:S(2)}) async-start(), calls=%async_computation.6 | async-start | bytes 2949120 | tf_op jit(solution)/shard_map/all_gather | solution.py:885
  13.9 210.2 %all-gather.8.cloned.1.call-start = ((), (), s32[]{:S(2)}) async-start(), calls=%async_computation.7 | async-start | bytes 7864320 | tf_op jit(solution)/shard_map/all_gather | solution.py:886
  15.3 22.3 %copy-start = (bf16[192,4096]{1,0:T(8,128)(2,1)S(1)}, bf16[192,4096]{1,0:T(8,128)(2,1)}, u32[]{:S(2)}) copy-start(bf16[192,4096]{1,0:T(8,128)(2,1)} %convert_bitcast_fusion.table) | copy-start | bytes 4718596
  15.3 537.4 %reduce-scatter.6.cloned.1.call-start = ((), (), s32[]{:S(2)}) async-start(), calls=%async_computation.8 | async-start | bytes 7864320 | tf_op jit(solution)/shard_map/reduce_scatter | solution.py:960
  36.6 56.7 %copy-start.86 = (f32[768]{0:T(1024)}, f32[768]{0:T(1024)S(1)}, u32[]{:S(2)}) copy-start(f32[768]{0:T(1024)S(1)} %mul.429) | copy-start | bytes 9220
  37.5 73.9 %copy-start.88 = (f32[576]{0:T(1024)}, f32[576]{0:T(1024)S(1)}, u32[]{:S(2)}) copy-start(f32[576]{0:T(1024)S(1)} %mul.436) | copy-start | bytes 6916
  37.5 73.8 %copy-start.90 = (f32[576]{0:T(1024)}, f32[576]{0:T(1024)S(1)}, u32[]{:S(2)}) copy-start(f32[576]{0:T(1024)S(1)} %mul.433) | copy-start | bytes 6916
  37.6 73.7 %copy-start.92 = (f32[576]{0:T(1024)}, f32[576]{0:T(1024)S(1)}, u32[]{:S(2)}) copy-start(f32[576]{0:T(1024)S(1)} %mul.418) | copy-start | bytes 6916
  37.6 19.5 %copy-start.39 = (s32[4,16,128]{2,1,0:T(8,128)}, s32[4,16,128]{2,1,0:T(8,128)S(1)}, u32[]{:S(2)}) copy-start(s32[4,16,128]{2,1,0:T(8,128)S(1)} %broadcast_subtract_fusion) | copy-start | bytes 98308
  92.1 19.3 %copy-start.107 = (f32[256]{0:T(256)}, f32[256]{0:T(256)S(1)}, u32[]{:S(2)}) copy-start(f32[256]{0:T(256)S(1)} %multiply_reduce_fusion.12) | copy-start | bytes 3076
  93.2 98.3 %copy-start.61 = (pred[512,1024]{1,0:T(8,128)(4,1)}, pred[512,1024]{1,0:T(8,128)(4,1)S(1)}, u32[]{:S(2)}) copy-start(pred[512,1024]{1,0:T(8,128)(4,1)S(1)} %fusion.24) | copy-start | bytes 1572868
  219.2 59.5 %copy-start.14 = (f32[256,768]{1,0:T(8,128)}, f32[256,768]{1,0:T(8,128)S(1)}, u32[]{:S(2)}) copy-start(f32[256,768]{1,0:T(8,128)S(1)} %get-tuple-element.187.refs_1_) | copy-start | bytes 2359300
  315.4 258.3 %reduce-scatter.10.cloned.1.call-start = ((), (), s32[]{:S(2)}) async-start(), calls=%async_computation.10 | async-start | bytes 737280 | tf_op jit(solution)/shard_map/reduce_scatter | solution.py:836
  349.6 25.3 %copy-start.73 = (bf16[1024,576]{0,1:T(8,128)(2,1)S(1)}, bf16[1024,576]{0,1:T(8,128)(2,1)}, u32[]{:S(2)}) copy-start(bf16[1024,576]{0,1:T(8,128)(2,1)} %copy-done.72) | copy-start | bytes 3538948
  447.6 126.1 %reduce-scatter.8.cloned.1.call-start = ((), (), s32[]{:S(2)}) async-start(), calls=%async_computation.9 | async-start | bytes 1474560 | tf_op jit(solution)/shard_map/reduce_scatter | solution.py:836
  491.5 100.5 %reduce-scatter.14.cloned.1.call-start = ((), (), s32[]{:S(2)}) async-start(), calls=%async_computation.12 | async-start | bytes 1474560 | tf_op jit(solution)/shard_map/reduce_scatter | solution.py:836
  512.8 147.1 %reduce-scatter.12.cloned.1.call-start = ((), (), s32[]{:S(2)}) async-start(), calls=%async_computation.11 | async-start | bytes 737280 | tf_op jit(solution)/shard_map/reduce_scatter | solution.py:836
  515.6 18.8 %copy-start.67 = (f32[1024,576]{0,1:T(8,128)S(1)}, f32[1024,576]{0,1:T(8,128)}, u32[]{:S(2)}) copy-start(f32[1024,576]{0,1:T(8,128)} %copy-done.66) | copy-start | bytes 7077892
  552.7 19.9 %copy-start.87 = (f32[768]{0:T(1024)S(1)}, f32[768]{0:T(1024)}, u32[]{:S(2)}) copy-start(f32[768]{0:T(1024)} %copy-done.86) | copy-start | bytes 9220
  552.7 20.7 %copy-start.28 = (f32[256,768]{1,0:T(8,128)S(1)}, f32[256,768]{1,0:T(8,128)}, u32[]{:S(2)}) copy-start(f32[256,768]{1,0:T(8,128)} %copy-done.27) | copy-start | bytes 2359300
  552.8 19.9 %copy-start.65 = (f32[768,256]{0,1:T(8,128)S(1)}, f32[768,256]{0,1:T(8,128)}, u32[]{:S(2)}) copy-start(f32[768,256]{0,1:T(8,128)} %copy-done.64) | copy-start | bytes 2359300
  552.8 19.9 %copy-start.106 = (f32[256]{0:T(256)S(1)}, f32[256]{0:T(256)}, u32[]{:S(2)}) copy-start(f32[256]{0:T(256)} %get-tuple-element.283) | copy-start | bytes 3076
  552.8 20.2 %copy-start.108 = (f32[256]{0:T(256)S(1)}, f32[256]{0:T(256)}, u32[]{:S(2)}) copy-start(f32[256]{0:T(256)} %copy-done.107) | copy-start | bytes 3076
  574.0 20.9 %copy-start.94 = (f32[768]{0:T(1024)S(1)}, f32[768]{0:T(1024)}, u32[]{:S(2)}) copy-start(f32[768]{0:T(1024)} %get-tuple-element.252) | copy-start | bytes 9220
  574.0 20.9 %copy-start.95 = (f32[768]{0:T(1024)S(1)}, f32[768]{0:T(1024)}, u32[]{:S(2)}) copy-start(f32[768]{0:T(1024)} %pad.91) | copy-start | bytes 9220
  574.0 20.9 %copy-start.96 = (f32[768]{0:T(1024)S(1)}, f32[768]{0:T(1024)}, u32[]{:S(2)}) copy-start(f32[768]{0:T(1024)} %pad.93) | copy-start | bytes 9220
  574.0 20.9 %copy-start.97 = (f32[768]{0:T(1024)S(1)}, f32[768]{0:T(1024)}, u32[]{:S(2)}) copy-start(f32[768]{0:T(1024)} %pad.92) | copy-start | bytes 9220
  574.0 20.9 %copy-start.98 = (f32[768]{0:T(1024)S(1)}, f32[768]{0:T(1024)}, u32[]{:S(2)}) copy-start(f32[768]{0:T(1024)} %pad.89) | copy-start | bytes 9220
  574.0 20.9 %copy-start.99 = (f32[768]{0:T(1024)S(1)}, f32[768]{0:T(1024)}, u32[]{:S(2)}) copy-start(f32[768]{0:T(1024)} %reduce.25) | copy-start | bytes 9220
  574.1 20.9 %copy-start.100 = (f32[768]{0:T(1024)S(1)}, f32[768]{0:T(1024)}, u32[]{:S(2)}) copy-start(f32[768]{0:T(1024)} %reduce.24) | copy-start | bytes 9220
  574.1 20.9 %copy-start.101 = (f32[768]{0:T(1024)S(1)}, f32[768]{0:T(1024)}, u32[]{:S(2)}) copy-start(f32[768]{0:T(1024)} %reduce.23) | copy-start | bytes 9220
  574.1 20.9 %copy-start.111 = (pred[16]{0:T(512)(128)(4,1)S(1)}, pred[16]{0:T(512)(128)(4,1)}, u32[]{:S(2)}) copy-start(pred[16]{0:T(512)(128)(4,1)} %get-tuple-element.309) | copy-start | bytes 52
  574.1 20.9 %copy-start.112 = (pred[16]{0:T(512)(128)(4,1)S(1)}, pred[16]{0:T(512)(128)(4,1)}, u32[]{:S(2)}) copy-start(pred[16]{0:T(512)(128)(4,1)} %get-tuple-element.310) | copy-start | bytes 52
  574.1 20.9 %copy-start.113 = (pred[16]{0:T(512)(128)(4,1)S(1)}, pred[16]{0:T(512)(128)(4,1)}, u32[]{:S(2)}) copy-start(pred[16]{0:T(512)(128)(4,1)} %iota_compare_fusion.15) | copy-start | bytes 52
  574.1 20.9 %copy-start.114 = (pred[16]{0:T(512)(128)(4,1)S(1)}, pred[16]{0:T(512)(128)(4,1)}, u32[]{:S(2)}) copy-start(pred[16]{0:T(512)(128)(4,1)} %get-tuple-element.307) | copy-start | bytes 52
  574.1 20.9 %copy-start.115 = (pred[16]{0:T(512)(128)(4,1)S(1)}, pred[16]{0:T(512)(128)(4,1)}, u32[]{:S(2)}) copy-start(pred[16]{0:T(512)(128)(4,1)} %get-tuple-element.308) | copy-start | bytes 52
  574.1 20.9 %copy-start.116 = (pred[16]{0:T(512)(128)(4,1)S(1)}, pred[16]{0:T(512)(128)(4,1)}, u32[]{:S(2)}) copy-start(pred[16]{0:T(512)(128)(4,1)} %get-tuple-element.305) | copy-start | bytes 52
  574.1 20.9 %copy-start.117 = (pred[16]{0:T(512)(128)(4,1)S(1)}, pred[16]{0:T(512)(128)(4,1)}, u32[]{:S(2)}) copy-start(pred[16]{0:T(512)(128)(4,1)} %get-tuple-element.306) | copy-start | bytes 52
  574.1 20.9 %copy-start.118 = (pred[16]{0:T(512)(128)(4,1)S(1)}, pred[16]{0:T(512)(128)(4,1)}, u32[]{:S(2)}) copy-start(pred[16]{0:T(512)(128)(4,1)} %get-tuple-element.303) | copy-start | bytes 52
  574.2 20.9 %copy-start.119 = (pred[16]{0:T(512)(128)(4,1)S(1)}, pred[16]{0:T(512)(128)(4,1)}, u32[]{:S(2)}) copy-start(pred[16]{0:T(512)(128)(4,1)} %get-tuple-element.304) | copy-start | bytes 52
  574.2 20.9 %copy-start.120 = (pred[16]{0:T(512)(128)(4,1)S(1)}, pred[16]{0:T(512)(128)(4,1)}, u32[]{:S(2)}) copy-start(pred[16]{0:T(512)(128)(4,1)} %get-tuple-element.301) | copy-start | bytes 52
  574.2 20.9 %copy-start.121 = (pred[16]{0:T(512)(128)(4,1)S(1)}, pred[16]{0:T(512)(128)(4,1)}, u32[]{:S(2)}) copy-start(pred[16]{0:T(512)(128)(4,1)} %get-tuple-element.302) | copy-start | bytes 52
  593.0 66.8 %collective-permute-start.1 = (bf16[96,1536]{1,0:T(8,128)(2,1)S(1)}, bf16[96,1536]{1,0:T(8,128)(2,1)S(1)}, u32[]{:S(2)}, u32[]{:S(2)}) collective-permute-start(bf16[96,1536]{1,0:T(8,128)(2,1)S(1)} %get-tuple-element.270), channel_id=1, source_target_pairs={{0,16},{16,0},{1,17},{17,1},{2,18},{18,2},{3,19},{19,3},{4,20},{20... | collective-permute-start | bytes 884744 | tf_op jit(solution)/shard_map/ppermute | solution.py:1000
  603.3 26.5 %copy-start.18 = (bf16[192,4096]{1,0:T(8,128)(2,1)S(1)}, bf16[192,4096]{1,0:T(8,128)(2,1)}, u32[]{:S(2)}) copy-start(bf16[192,4096]{1,0:T(8,128)(2,1)} %reduce-scatter.6.cloned.1.call-done.base) | copy-start | bytes 4718596
  603.3 26.5 %copy-start.40 = (s32[4,16,128]{2,1,0:T(8,128)S(1)}, s32[4,16,128]{2,1,0:T(8,128)}, u32[]{:S(2)}) copy-start(s32[4,16,128]{2,1,0:T(8,128)} %copy-done.39) | copy-start | bytes 98308
  629.8 30.1 %copy-start.85 = (bf16[1,96,768]{2,1,0:T(8,128)(2,1)S(1)}, bf16[1,96,768]{2,1,0:T(8,128)(2,1)}, u32[]{:S(2)}) copy-start(bf16[1,96,768]{2,1,0:T(8,128)(2,1)} %reduce-scatter.10.cloned.1.call-done) | copy-start | bytes 442372
  660.9 1.5 collective-permute-start
  (95 other events, 439.4 us)
Sparse Core Ops, SparseCore 0:
  10.7 33.8 all-gather.3
  46.7 58.0 all-gather.5
  106.4 114.0 all-gather.7
  315.5 116.2 reduce-scatter.5
  447.7 27.6 reduce-scatter.9
  491.6 40.7 reduce-scatter.7
  534.8 27.8 reduce-scatter.13
  592.1 24.3 reduce-scatter.11

commit v3 on v2

--- a/solution.py
+++ b/solution.py
@@ -68,18 +68,22 @@
     out_specs = [pl.BlockSpec(memory_space=pltpu.VMEM)] * len(shapes)
     scratch = list(scratch)
     count_in, count_out = len(operands), len(shapes)
+    loads = 0
     if cargo is not None:
-        kind, layer, array = cargo
-        operands = operands + (array,)
-        in_specs.append(pl.BlockSpec(memory_space=pl.ANY))
-        if kind == "out":
-            landing = [jax.ShapeDtypeStruct(array.shape, array.dtype)]
-        else:
-            batches, _, rows, width = array.shape
-            landing = [jax.ShapeDtypeStruct((batches, rows, width), array.dtype)] * 2
+        kind, layer, arrays = cargo
+        loads = len(arrays)
+        operands = operands + tuple(arrays)
+        in_specs += [pl.BlockSpec(memory_space=pl.ANY)] * loads
+        landing = []
+        for array in arrays:
+            if kind == "out":
+                landing.append(jax.ShapeDtypeStruct(array.shape, array.dtype))
+            else:
+                batches, _, rows, width = array.shape
+                landing += [jax.ShapeDtypeStruct((batches, rows, width), array.dtype)] * 2
         shapes += landing
         out_specs += [pl.BlockSpec(memory_space=pl.ANY)] * len(landing)
-        scratch += [pltpu.SemaphoreType.DMA((3,))] * 2
+        scratch += [pltpu.SemaphoreType.DMA((loads, 3))] * 2
 
     def kernel(*refs):
         ins, rest = refs[: len(operands)], refs[len(operands) :]
@@ -88,10 +92,22 @@
             body(*ins, *outs, *rest)
             return
         send, recv = rest[-2:]
-        load = functools.partial(
-            Outward if kind == "out" else Inward, layer, ins[-1], outs[count_out:], send, recv
-        )
-        body(*ins[:-1], *outs[:count_out], *rest[:-2], load=load)
+        made = Outward if kind == "out" else Inward
+        lands = len(landing) // loads
+
+        def load():
+            return [
+                made(
+                    layer,
+                    ins[count_in + at],
+                    outs[count_out + lands * at : count_out + lands * (at + 1)],
+                    send.at[at],
+                    recv.at[at],
+                )
+                for at in range(loads)
+            ]
+
+        body(*ins[:count_in], *outs[:count_out], *rest[:-2], load=load)
 
     results = pl.pallas_call(
         kernel,
@@ -199,12 +215,13 @@
 def greet_group(other, beside, load):
     if load is None:
         greet([other, beside])
-        return None
+        return []
     _, y, _, tensor = place()
     above = tensor + 2 - 4 * y
     greet([other, beside, {"section": 0, "tensor": above}, {"section": 1, "tensor": above}])
     made = load()
-    made.start()
+    for one in made:
+        one.start()
     return made
 
 
@@ -246,8 +263,8 @@
     direct.wait()
     for copy in passed:
         copy.wait()
-    if cargo is not None:
-        cargo.wait()
+    for one in cargo:
+        one.wait()
 
 
 def group_gather(rows, collective_id, cargo=None):
@@ -300,11 +317,12 @@
         )
     for copy in first + across:
         copy.wait_send()
-    if cargo is not None:
-        cargo.wait()
+    for one in cargo:
+        one.wait()
 
 
 def group_reduce(parts, collective_id, cargo=None):
+    parts = parts.reshape(4, -1, D)
     _, count, width = parts.shape
     return comm_call(
         group_reduce_kernel,
@@ -390,11 +408,12 @@
         made.wait_send()
     for made in out_direct + onward:
         made.wait()
-    if cargo is not None:
-        cargo.wait()
+    for one in cargo:
+        one.wait()
 
 
 def turn(parts, rows, gain, collective_id, rounded, passed=None, cargo=None):
+    parts = parts.reshape(4, -1, D)
     _, count, width = parts.shape
     backward = passed is not None
     shapes = [
@@ -420,12 +439,23 @@
     )
 
 
+def plane_peers():
+    core, y, x, tensor = place()
+    return [
+        {"section": 1 - core},
+        {"tensor": tensor + 1 - 2 * x},
+        {"tensor": tensor + 2 - 4 * y},
+    ]
+
+
 def plane_gather_kernel(own, out, send, recv):
-    core, y, x, tensor = place()
-    other = {"section": 1 - core}
-    beside = {"tensor": tensor + 1 - 2 * x}
-    above = {"tensor": tensor + 2 - 4 * y}
-    greet([other, beside, above])
+    greet(plane_peers())
+    plane_exchange(own, out, send, recv)
+
+
+def plane_exchange(own, out, send, recv):
+    core, y, x, _ = place()
+    other, beside, above = plane_peers()
     half = own.shape[0] // 2
     cut = [pl.ds(0, half), pl.ds(half, half)]
 
@@ -571,21 +601,28 @@
     )
 
 
+def batch_peers(count):
+    me = lax.axis_index("batch")
+    return [{"batch": lax.rem(me + step, count)} for step in range(1, count)]
+
+
+def batch_exchange(count, ins, outs, send, recv):
+    me = lax.axis_index("batch")
+    copies = []
+    for index, peer in enumerate(batch_peers(count)):
+        for kind in range(len(ins)):
+            at = index * len(ins) + kind
+            copies.append(remote(ins[kind], outs[kind].at[me], send.at[at], recv.at[at], peer))
+            copies[-1].start()
+    for kind in range(len(ins)):
+        outs[kind][me] = ins[kind][...]
+    return copies
+
+
 def batch_gather_kernel(count, *refs):
     kinds = (len(refs) - 2) // 2
-    ins, outs, (send, recv) = refs[:kinds], refs[kinds : 2 * kinds], refs[2 * kinds :]
-    me = lax.axis_index("batch")
-    peers = [{"batch": lax.rem(me + step, count)} for step in range(1, count)]
-    greet(peers)
-    copies = []
-    for index, peer in enumerate(peers):
-        for kind in range(kinds):
-            at = index * kinds + kind
-            copies.append(remote(ins[kind], outs[kind].at[me], send.at[at], recv.at[at], peer))
-            copies[-1].start()
-    for kind in range(kinds):
-        outs[kind][me] = ins[kind][...]
-    for copy in copies:
+    greet(batch_peers(count))
+    for copy in batch_exchange(count, refs[:kinds], refs[kinds : 2 * kinds], *refs[2 * kinds :]):
         copy.wait()
 
 
@@ -600,149 +637,322 @@
     )
 
 
-def batch_trade_kernel(count, parts, out, send, recv):
+def plane_and_batch_kernel(count, own, few, out, few_out, send, recv, few_send, few_recv):
+    greet(plane_peers() + batch_peers(count))
+    copies = batch_exchange(count, [few], [few_out], few_send, few_recv)
+    plane_exchange(own, out, send, recv)
+    for copy in copies:
+        copy.wait()
+
+
+def plane_and_batch_gather(block, few, collective_id):
+    count = lax.axis_size("batch")
+    return comm_call(
+        functools.partial(plane_and_batch_kernel, count),
+        [
+            jax.ShapeDtypeStruct((8,) + block.shape, block.dtype),
+            jax.ShapeDtypeStruct((count,) + few.shape, few.dtype),
+        ],
+        [pltpu.SemaphoreType.DMA((13,))] * 2 + [pltpu.SemaphoreType.DMA((count - 1,))] * 2,
+        collective_id,
+        block,
+        few,
+    )
+
+
+def batch_trade_kernel(count, parts, few, out, few_out, send, recv, few_send, few_recv):
     me = lax.axis_index("batch")
-    peers = [lax.rem(me + step, count) for step in range(1, count)]
-    greet([{"batch": peer} for peer in peers])
+    greet(plane_peers() + batch_peers(count))
     copies = []
-    for index, peer in enumerate(peers):
+    for index, peer in enumerate(batch_peers(count)):
         copies.append(
-            remote(parts.at[peer], out.at[me], send.at[index], recv.at[index], {"batch": peer})
+            remote(parts.at[peer["batch"]], out.at[me], send.at[index], recv.at[index], peer)
         )
         copies[-1].start()
     out[me] = parts[me]
+    plane_exchange(few, few_out, few_send, few_recv)
     for copy in copies:
         copy.wait()
 
 
-def batch_trade(parts):
+def batch_trade(parts, few, collective_id):
     count = parts.shape[0]
     return comm_call(
         functools.partial(batch_trade_kernel, count),
-        jax.ShapeDtypeStruct(parts.shape, parts.dtype),
-        [pltpu.SemaphoreType.DMA((count - 1,))] * 2,
-        8,
+        [
+            jax.ShapeDtypeStruct(parts.shape, parts.dtype),
+            jax.ShapeDtypeStruct((8,) + few.shape, few.dtype),
+        ],
+        [pltpu.SemaphoreType.DMA((count - 1,))] * 2 + [pltpu.SemaphoreType.DMA((13,))] * 2,
+        collective_id,
         parts,
-    )
-
-
-def causal_mix(projected, taps):
-    once = jnp.pad(projected, ((1, 0), (0, 0)))[:-1]
-    twice = jnp.pad(projected, ((2, 0), (0, 0)))[:-2]
-    return taps[0] * projected + taps[1] * once + taps[2] * twice
-
-
-def causal_mix_back(grad, projected, taps):
-    ahead_one = jnp.pad(grad, ((0, 1), (0, 0)))[1:]
-    ahead_two = jnp.pad(grad, ((0, 2), (0, 0)))[2:]
-    grad_in = taps[0] * grad + taps[1] * ahead_one + taps[2] * ahead_two
-    once = jnp.pad(projected, ((1, 0), (0, 0)))[:-1]
-    twice = jnp.pad(projected, ((2, 0), (0, 0)))[:-2]
-    grad_taps = [
-        jnp.sum(grad * projected, 0),
-        jnp.sum(grad * once, 0),
-        jnp.sum(grad * twice, 0),
-    ]
-    return (grad_in, grad_taps)
-
-
-def allowed_keys(lead, reach, length):
-    query_at = jnp.arange(lead, reach)[:, None]
-    key_at = jnp.arange(reach)[None, :]
-    return (key_at <= query_at) & (key_at < length)
-
-
-def attend(queries, keys_all, values_all, length):
-    total = queries.shape[0]
-    block = min(512, total)
-    factor = queries.shape[-1] ** (-0.5)
-    outputs = []
-    totals = []
-    for index in range(total // block):
-        lead = index * block
-        reach = lead + block
-        scores = (
-            jnp.einsum("qhd,khd->hqk", queries[lead:reach], keys_all[:reach], preferred_element_type=f32)
-            * factor
+        few,
+    )
+
+
+ROWS = 256
+
+
+PACKED = ((0, 0), (0, 1), (1, 0), (1, 1), (2, 0), (2, 1), (0, 2), (1, 2), (2, 2))
+
+
+def packed(blocks, out):
+    cuts = [blocks[:, kind, HEAD * head : HEAD * head + HEAD] for kind, head in PACKED]
+    return jnp.concatenate(cuts + [out[:, 2 * HEAD :], out[:, : 2 * HEAD]], 1)
+
+
+def unpacked(block):
+    place_of = {pair: at * HEAD for at, pair in enumerate(PACKED)}
+    kinds = []
+    for kind in range(3):
+        cuts = [
+            block[:, place_of[kind, head] : place_of[kind, head] + HEAD] for head in range(3)
+        ]
+        kinds.append(jnp.concatenate(cuts, 1))
+    return jnp.stack(kinds, 1)
+
+
+def attention_heads(mixed, queries, keys, values):
+    low = lax.broadcasted_iota(jnp.int32, (mixed.shape[0], 128), 1) < HEAD
+    tile = [mixed[:, 128 * at : 128 * at + 128] for at in range(5)]
+    scaled = tile[0] * (HEAD**-0.5)
+    queries[0] = jnp.where(low, scaled, 0.0).astype(bf16)
+    queries[1] = jnp.where(low, 0.0, scaled).astype(bf16)
+    queries[2] = jnp.where(low, tile[3] * (HEAD**-0.5), 0.0).astype(bf16)
+    keys[0] = tile[1].astype(bf16)
+    keys[1] = pltpu.roll(tile[3], HEAD, 1).astype(bf16)
+    values[0] = tile[2].astype(bf16)
+    values[1] = tile[4].astype(bf16)
+
+
+def key_bias(length, total):
+    at = lax.broadcasted_iota(jnp.int32, (1, total), 1)
+    return jnp.where(at < length, 0.0, masked_score)
+
+
+def masked(scores, bias, lead):
+    scores = scores + bias
+    row = lax.broadcasted_iota(jnp.int32, (ROWS, ROWS), 0)
+    column = lax.broadcasted_iota(jnp.int32, (ROWS, ROWS), 1)
+    last = jnp.where(column <= row, scores[:, lead:], masked_score)
+    return last if lead == 0 else jnp.concatenate([scores[:, :lead], last], 1)
+
+
+def attention_forward_kernel(
+    length, x, weight, taps, partial, mixed_out, projected_out, context, totals, projected, queries, keys, values
+):
+    total = x.shape[0]
+    width = 5 * 128
+    projected[:8] = jnp.zeros((8, width), f32)
+    for lead in range(0, total, ROWS):
+        block = jnp.dot(x[lead : lead + ROWS], weight[:, :width], preferred_element_type=f32)
+        projected[lead + 8 : lead + 8 + ROWS] = block
+        projected_out[lead : lead + ROWS] = block.astype(bf16)
+    for lead in range(0, total, ROWS):
+        mixed = taps[0:1] * projected[lead + 8 : lead + 8 + ROWS]
+        mixed += taps[1:2] * projected[lead + 7 : lead + 7 + ROWS]
+        mixed += taps[2:3] * projected[lead + 6 : lead + 6 + ROWS]
+        mixed = mixed.astype(bf16)
+        mixed_out[lead : lead + ROWS] = mixed
+        rows = pl.ds(lead, ROWS)
+        attention_heads(
+            mixed.astype(f32), queries.at[:, rows], keys.at[:, rows], values.at[:, rows]
         )
-        scores = jnp.where(allowed_keys(lead, reach, length)[None], scores, masked_score)
-        peak = jnp.max(scores, axis=-1, keepdims=True)
-        raised = jnp.exp(scores - peak)
-        weight_sum = jnp.sum(raised, axis=-1, keepdims=True)
-        probs = (raised / weight_sum).astype(bf16)
-        result = jnp.einsum("hqk,khd->qhd", probs, values_all[:reach], preferred_element_type=f32)
-        outputs.append(result.astype(bf16))
-        totals.append((peak + jnp.log(weight_sum))[..., 0])
-    return (jnp.concatenate(outputs, 0), jnp.concatenate(totals, 1))
-
-
-def attend_back(grad_out, queries, keys_all, values_all, length, totals):
-    total = queries.shape[0]
-    block = min(512, total)
-    factor = queries.shape[-1] ** (-0.5)
-    grad_queries = []
-    grad_keys = jnp.zeros(keys_all.shape, f32)
-    grad_values = jnp.zeros(values_all.shape, f32)
-    for index in range(total // block):
-        lead = index * block
-        reach = lead + block
-        scores = (
-            jnp.einsum("qhd,khd->hqk", queries[lead:reach], keys_all[:reach], preferred_element_type=f32)
-            * factor
+    bias = key_bias(length[0], total)
+    lane = lax.broadcasted_iota(jnp.int32, (ROWS, 128), 1)
+    low = lane < HEAD
+    for lead in range(0, total, ROWS):
+        reach = lead + ROWS
+        found = []
+        log_sums = jnp.zeros((ROWS, 128), f32)
+        for head in range(3):
+            scores = mm(queries[head, lead:reach], keys[head // 2, :reach], 1, 1)
+            scores = masked(scores, bias[:, :reach], lead)
+            peak = jnp.max(scores, axis=1, keepdims=True)
+            raised = jnp.exp(scores - peak)
+            weight_sum = jnp.sum(raised, axis=1, keepdims=True)
+            probs = (raised * (1.0 / weight_sum)).astype(bf16)
+            found.append(
+                jnp.dot(probs, values[head // 2, :reach], preferred_element_type=f32)
+            )
+            log_sums = jnp.where(lane == head, peak + jnp.log(weight_sum), log_sums)
+        totals[lead:reach] = log_sums
+        joined = jnp.concatenate(
+            [
+                jnp.where(low, 0.0, pltpu.roll(found[2], HEAD, 1)),
+                jnp.where(low, found[0], found[1]),
+            ],
+            1,
+        ).astype(bf16)
+        context[lead:reach] = joined
+        partial[lead:reach] = mm(joined, weight[:, 512:768], 1, 1).astype(bf16)
+
+
+def attention_call(body, out_shape, scratch, length, *operands):
+    whole = pl.BlockSpec(memory_space=pltpu.VMEM)
+    return pl.pallas_call(
+        body,
+        out_shape=out_shape,
+        in_specs=[pl.BlockSpec(memory_space=pltpu.SMEM)] + [whole] * len(operands),
+        out_specs=[whole] * len(out_shape),
+        scratch_shapes=scratch,
+        compiler_params=pltpu.CompilerParams(vmem_limit_bytes=50 << 20),
+    )(length.reshape(1), *operands)
+
+
+def attention_forward(x, length, weight, taps):
+    total = x.shape[0]
+    partial, *kept = attention_call(
+        attention_forward_kernel,
+        [
+            jax.ShapeDtypeStruct((total, D), bf16),
+            jax.ShapeDtypeStruct((total, 640), bf16),
+            jax.ShapeDtypeStruct((total, 640), bf16),
+            jax.ShapeDtypeStruct((total, 256), bf16),
+            jax.ShapeDtypeStruct((total, 128), f32),
+        ],
+        [
+            pltpu.VMEM((total + 8, 640), f32),
+            pltpu.VMEM((3, total, 128), bf16),
+            pltpu.VMEM((2, total, 128), bf16),
+            pltpu.VMEM((2, total, 128), bf16),
+        ],
+        length,
+        x,
+        weight,
+        taps,
+    )
+    return partial, (x, *kept)
+
+
+def attention_backward_kernel(
+    length,
+    grads,
+    x,
+    weight,
+    taps,
+    mixed,
+    projected,
+    context,
+    totals,
+    partial,
+    weight_grad,
+    taps_grad,
+    queries,
+    keys,
+    values,
+    outer,
+    key_grad,
+    value_grad,
+    mixed_grad,
+    projected_grad,
+    turned,
+):
+    total = x.shape[0]
+    width = 5 * 128
+    low = lax.broadcasted_iota(jnp.int32, (ROWS, 128), 1) < HEAD
+    for lead in range(0, total, ROWS):
+        rows = pl.ds(lead, ROWS)
+        attention_heads(
+            mixed[lead : lead + ROWS].astype(f32),
+            queries.at[:, rows],
+            keys.at[:, rows],
+            values.at[:, rows],
         )
-        allowed = allowed_keys(lead, reach, length)[None]
-        probs = jnp.where(allowed, jnp.exp(scores - totals[:, lead:reach, None]), 0.0)
-        grad_block = grad_out[lead:reach]
-        grad_probs = jnp.einsum(
-            "qhd,khd->hqk", grad_block, values_all[:reach], preferred_element_type=f32
+        block = jnp.dot(grads[lead : lead + ROWS], weight[:, 512:768], preferred_element_type=f32)
+        third, pair = block[:, :128], block[:, 128:]
+        outer[0, lead : lead + ROWS] = jnp.where(low, pair, 0.0).astype(bf16)
+        outer[1, lead : lead + ROWS] = jnp.where(low, 0.0, pair).astype(bf16)
+        outer[2, lead : lead + ROWS] = jnp.where(low, pltpu.roll(third, HEAD, 1), 0.0).astype(bf16)
+    mixed_grad[total:] = jnp.zeros((8, width), f32)
+    bias = key_bias(length[0], total)
+    for lead in reversed(range(0, total, ROWS)):
+        reach = lead + ROWS
+        query_grad = []
+        for head in range(3):
+            its_keys, its_values = keys[head // 2, :reach], values[head // 2, :reach]
+            scores = mm(queries[head, lead:reach], its_keys, 1, 1)
+            scores = masked(scores, bias[:, :reach], lead)
+            probs = jnp.exp(scores - totals[lead:reach, head : head + 1])
+            grad_probs = mm(outer[head, lead:reach], its_values, 1, 1)
+            product = probs * grad_probs
+            inner = jnp.sum(product, axis=1, keepdims=True)
+            grad_scores = (product - probs * inner).astype(bf16)
+            query_grad.append(jnp.dot(grad_scores, its_keys, preferred_element_type=f32))
+            value_part = mm(probs.astype(bf16), outer[head, lead:reach], 0, 0)
+            key_part = mm(grad_scores, queries[head, lead:reach], 0, 0)
+            if lead + ROWS == total and head != 1:
+                value_grad[head // 2] = value_part
+                key_grad[head // 2] = key_part
+            else:
+                value_grad[head // 2, :reach] += value_part
+                key_grad[head // 2, :reach] += key_part
+        scale = HEAD**-0.5
+        mixed_grad[lead:reach, 0:128] = jnp.where(low, query_grad[0], query_grad[1]) * scale
+        mixed_grad[lead:reach, 384:512] = query_grad[2] * scale
+    grown = jnp.zeros((8, width), f32)
+    for lead in reversed(range(0, total, ROWS)):
+        reach = lead + ROWS
+        mixed_grad[lead:reach, 128:256] = key_grad[0, lead:reach]
+        mixed_grad[lead:reach, 256:384] = value_grad[0, lead:reach]
+        mixed_grad[lead:reach, 384:512] = jnp.where(
+            low, mixed_grad[lead:reach, 384:512], pltpu.roll(key_grad[1, lead:reach], HEAD, 1)
         )
-        inner = jnp.sum(probs * grad_probs, axis=-1, keepdims=True)
-        grad_scores = (probs * (grad_probs - inner)).astype(bf16)
-        grad_queries.append(
-            jnp.einsum("hqk,khd->qhd", grad_scores, keys_all[:reach], preferred_element_type=f32)
-            * factor
-        )
-        grad_keys = grad_keys.at[:reach].add(
-            jnp.einsum("hqk,qhd->khd", grad_scores, queries[lead:reach], preferred_element_type=f32)
-            * factor
-        )
-        grad_values = grad_values.at[:reach].add(
-            jnp.einsum("hqk,qhd->khd", probs.astype(bf16), grad_block, preferred_element_type=f32)
-        )
-    return (jnp.concatenate(grad_queries, 0), grad_keys, grad_values)
-
-
-def attention_forward(gathered, length, weights):
-    qkv_mat, taps, out_turned = weights
-    local_width = out_turned.shape[1]
-    heads_here = local_width // HEAD
-    projected = mm(gathered, qkv_mat, 1, 0)
-    mixed = causal_mix(projected, taps).astype(bf16)
-    triple = mixed.reshape(-1, 3, heads_here, HEAD)
-    context, totals = attend(triple[:, 0], triple[:, 1], triple[:, 2], length)
-    context = context.reshape(-1, local_width)
-    partial = mm(context, out_turned, 1, 1).astype(bf16).reshape(4, -1, D)
-    return partial, (gathered, projected, mixed, context, totals)
-
-
-def attention_backward(grad_rows, length, weights, kept):
-    qkv_mat, taps, out_turned = weights
-    gathered, projected, mixed, context, totals = kept
-    local_width = out_turned.shape[1]
-    heads_here = local_width // HEAD
-    grad_context = mm(grad_rows, out_turned, 1, 0).astype(bf16).reshape(-1, heads_here, HEAD)
-    triple = mixed.reshape(-1, 3, heads_here, HEAD)
-    grad_queries, grad_keys, grad_values = attend_back(
-        grad_context, triple[:, 0], triple[:, 1], triple[:, 2], length, totals
-    )
-    grad_mixed = jnp.stack([grad_queries, grad_keys, grad_values], 1).reshape(-1, 3 * local_width)
-    grad_projected, grad_taps = causal_mix_back(grad_mixed, projected, taps)
-    grad_projected = grad_projected.astype(bf16)
-    partial = mm(grad_projected, qkv_mat, 1, 1).astype(bf16).reshape(4, -1, D)
-    grad_qkv = mm(gathered, grad_projected, 0, 0)
-    grad_outmat = mm(grad_rows, context, 0, 0)
-    blob = jnp.concatenate([grad_qkv.astype(bf16), grad_outmat.astype(bf16)], 1)
-    return partial, blob, grad_taps
+        mixed_grad[lead:reach, 512:640] = value_grad[1, lead:reach]
+        here = projected[lead:reach].astype(f32)
+        back = jnp.zeros((ROWS, width), f32)
+        parts = []
+        for tap in range(3):
+            ahead = mixed_grad[lead + tap : reach + tap]
+            back += taps[tap : tap + 1] * ahead
+            parts.append(jnp.sum(ahead * here, axis=0, keepdims=True))
+        grown += jnp.concatenate(parts + [jnp.zeros((5, width), f32)], 0)
+        back = back.astype(bf16)
+        partial[lead:reach] = mm(back, weight[:, :width], 1, 1).astype(bf16)
+        projected_grad[lead:reach] = back
+    taps_grad[...] = grown
+    turned[0] = x[...].T
+    turned[1] = grads[...].T
+    for lead in range(0, D, ROWS):
+        reach = lead + ROWS
+        across = jnp.dot(turned[0, lead:reach], projected_grad[...], preferred_element_type=f32)
+        outward = jnp.dot(turned[1, lead:reach], context[...], preferred_element_type=f32)
+        weight_grad[lead:reach, :512] = across[:, :512].astype(bf16)
+        weight_grad[lead:reach, 512:640] = (across[:, 512:] + outward[:, :128]).astype(bf16)
+        weight_grad[lead:reach, 640:] = outward[:, 128:].astype(bf16)
+
+
+def attention_backward(grads, length, weight, taps, kept):
+    x, mixed, projected, context, totals = kept
+    total = x.shape[0]
+    return attention_call(
+        attention_backward_kernel,
+        [
+            jax.ShapeDtypeStruct((total, D), bf16),
+            jax.ShapeDtypeStruct((D, 768), bf16),
+            jax.ShapeDtypeStruct((8, 640), f32),
+        ],
+        [
+            pltpu.VMEM((3, total, 128), bf16),
+            pltpu.VMEM((2, total, 128), bf16),
+            pltpu.VMEM((2, total, 128), bf16),
+            pltpu.VMEM((3, total, 128), bf16),
+            pltpu.VMEM((2, total, 128), f32),
+            pltpu.VMEM((2, total, 128), f32),
+            pltpu.VMEM((total + 8, 640), f32),
+            pltpu.VMEM((total, 640), bf16),
+            pltpu.VMEM((2, D, total), bf16),
+        ],
+        length,
+        grads,
+        x,
+        weight,
+        taps,
+        mixed,
+        projected,
+        context,
+        totals,
+    )
 
 
 def ffn_forward(gathered, weights):
@@ -761,21 +971,21 @@
     partial = mm(grad_hidden, up_mat, 1, 1).astype(bf16).reshape(4, -1, D)
     grad_down = mm(grad_rows, active, 0, 0)
     grad_up = mm(gathered, grad_hidden, 0, 0)
-    blob = jnp.concatenate([grad_up.astype(bf16), grad_down.astype(bf16)], 1)
-    return partial, blob
+    return partial, [grad_up.astype(bf16), grad_down.astype(bf16)]
 
 
 LOOK = 512
 
 
 def lookup_kernel(ids, table, out):
-    total = jnp.zeros((table.shape[0], ids.shape[2]), f32)
-    wanted = ids[0]
-    row = lax.broadcasted_iota(jnp.int32, (LOOK, ids.shape[2]), 0)
-    for lead in range(0, table.shape[1], LOOK):
-        hit = jnp.where(row == wanted - lead, 1.0, 0.0).astype(bf16)
-        total += jnp.dot(table[:, lead : lead + LOOK], hit, preferred_element_type=f32)
-    out[0, 0] = total.astype(bf16)
+    for part in range(ids.shape[0]):
+        total = jnp.zeros((table.shape[0], ids.shape[2]), f32)
+        wanted = ids[part]
+        row = lax.broadcasted_iota(jnp.int32, (LOOK, ids.shape[2]), 0)
+        for lead in range(0, table.shape[1], LOOK):
+            hit = jnp.where(row == wanted - lead, 1.0, 0.0).astype(bf16)
+            total += jnp.dot(table[:, lead : lead + LOOK], hit, preferred_element_type=f32)
+        out[part, 0] = total.astype(bf16)
 
 
 def lookup(table, ids):
@@ -783,53 +993,80 @@
     depth, vocab_rows = table.shape
     return pl.pallas_call(
         lookup_kernel,
-        grid=(batches * parts,),
+        grid=(batches,),
         out_shape=jax.ShapeDtypeStruct((parts, batches, depth, slots), bf16),
         in_specs=[
-            pl.BlockSpec((1, 1, slots), lambda at: (at, 0, 0)),
+            pl.BlockSpec((parts, 1, slots), lambda at: (at, 0, 0)),
             pl.BlockSpec((depth, vocab_rows), lambda at: (0, 0)),
         ],
-        out_specs=pl.BlockSpec((1, 1, depth, slots), lambda at: (at % parts, at // parts, 0, 0)),
+        out_specs=pl.BlockSpec((parts, 1, depth, slots), lambda at: (0, at, 0, 0)),
         compiler_params=pltpu.CompilerParams(vmem_limit_bytes=40 << 20),
     )(ids.reshape(batches * parts, 1, slots), table)
 
 
-def spread_kernel(batches, ids, grads, base, out):
+def spread_kernel(ids, grads, base, out, wanted):
     at = pl.program_id(0)
     columns = out.shape[1]
-    slots = ids.shape[2]
-    row = lax.broadcasted_iota(jnp.int32, (columns, slots), 0) + at * columns
+    parts, batches, _, slots = grads.shape
+
+    @pl.when(at == 0)
+    def _():
+        def turned(group, carry):
+            across = ids[pl.ds(pl.multiple_of(group * 8, 8), 8)].T
+            for part in range(8):
+                wanted[group * 8 + part] = jnp.broadcast_to(
+                    across[:, part : part + 1], (slots, 128)
+                ).astype(jnp.int16)
+            return carry
+
+        lax.fori_loop(0, batches * parts // 8, turned, 0)
+
+    lane = lax.broadcasted_iota(jnp.int16, (slots, 128), 1) + (at * columns).astype(jnp.int16)
+    together = min(batches, 4)
 
     def step(index, total):
-        for part in range(8):
-            hit = jnp.where(row == ids[index * 8 + part], 1.0, 0.0).astype(bf16)
-            total += mm(grads[part, index], hit, 1, 1)
+        for inner in range(together):
+            batch = index * together + inner
+            for part in range(parts):
+                here = wanted[batch * parts + part]
+                hit = jnp.concatenate(
+                    [
+                        jnp.where(here == lane + jnp.int16(lead), bf16(1), bf16(0))
+                        for lead in range(0, columns, 128)
+                    ],
+                    1,
+                )
+                total += jnp.dot(grads[part, batch], hit, preferred_element_type=f32)
         return total
 
-    out[...] = lax.fori_loop(0, batches, step, base[...].astype(f32))
+    out[...] = lax.fori_loop(0, batches // together, step, base[...].astype(f32))
 
 
 def spread(grads, ids, base):
     parts, batches, depth, slots = grads.shape
     vocab_rows = base.shape[1]
-    columns = 512
+    columns = 256
     return pl.pallas_call(
-        functools.partial(spread_kernel, batches),
+        spread_kernel,
         grid=(vocab_rows // columns,),
         out_shape=jax.ShapeDtypeStruct((depth, vocab_rows), f32),
         in_specs=[
-            pl.BlockSpec((batches * parts, 1, slots), lambda at: (0, 0, 0)),
+            pl.BlockSpec((batches * parts, slots), lambda at: (0, 0)),
             pl.BlockSpec((parts, batches, depth, slots), lambda at: (0, 0, 0, 0)),
             pl.BlockSpec((depth, columns), lambda at: (0, at)),
         ],
         out_specs=pl.BlockSpec((depth, columns), lambda at: (0, at)),
-        compiler_params=pltpu.CompilerParams(vmem_limit_bytes=40 << 20),
-    )(ids.reshape(batches * parts, 1, slots), grads, base)
+        scratch_shapes=[pltpu.VMEM((batches * parts, slots, 128), jnp.int16)],
+        compiler_params=pltpu.CompilerParams(vmem_limit_bytes=56 << 20),
+    )(ids.reshape(batches * parts, slots), grads, base)
 
 
 def summed(landed):
-    one, two = landed
-    return (one.astype(f32) + two.astype(f32)).astype(bf16)
+    sums = [
+        (one.astype(f32) + two.astype(f32)).astype(bf16)
+        for one, two in zip(landed[::2], landed[1::2])
+    ]
+    return jnp.concatenate(sums, -1)
 
 
 def over_batch(block):
@@ -873,75 +1110,71 @@
     sequences = token_ids.shape[0]
 
     table_own = embed_table.astype(bf16).T
-    attn_own = jnp.concatenate(
-        [
-            qkv_weight[0].reshape(depth, 3 * local_width).astype(bf16),
-            out_weight[0].astype(bf16).T,
-        ],
-        1,
-    )
+    attn_own = packed(qkv_weight[0].astype(bf16), out_weight[0].astype(bf16).T)
     ffn_own = jnp.concatenate([up_weight[0].astype(bf16), down_weight[0].astype(bf16).T], 1)
     attn_all = lax.all_gather(attn_own, "batch", axis=0, tiled=True)
     ffn_all = lax.all_gather(ffn_own, "batch", axis=0, tiled=True)
     table_turned = lax.all_gather(table_own, "batch", axis=0, tiled=True)
 
     gain_width = final_gain.shape[0]
-    small = jnp.concatenate(
-        [norm_gains.astype(f32).reshape(-1), final_gain.astype(f32), qkv_conv.astype(f32).reshape(-1)]
-    )
-    small_rows = -(-small.shape[0] // 1024) * 8
-    small = jnp.pad(small, (0, small_rows * 128 - small.shape[0])).reshape(small_rows, 128)
+    whole_at = (section * batch_count + at_batch) * tensor_count + me
+    gains_own = jnp.concatenate([norm_gains.reshape(4, gain_width), final_gain[None]])
+    gains_own = lax.dynamic_update_slice_in_dim(
+        jnp.zeros((5, D), f32), gains_own.astype(bf16).astype(f32), whole_at * gain_width, 1
+    )
+    taps_own = qkv_conv[0].astype(bf16).astype(f32).transpose(1, 0, 2, 3)
+    taps_own = lax.dynamic_update_slice_in_dim(
+        jnp.zeros((3, 3, heads_here, HEAD), f32), taps_own, at_batch * qkv_conv.shape[4], 3
+    ).reshape(3, 3, local_width)
+    small = jnp.concatenate([gains_own, packed(taps_own, jnp.zeros((3, local_width), f32))])
     all_ids, small = batch_gather([token_ids.reshape(-1, 128), small], 5)
-    small = plane_gather(small.reshape(batch_count * small_rows, 128), 6)
-    small = small.reshape(2, 2, 2, batch_count, -1).transpose(1, 3, 0, 2, 4)
-    small = small.reshape(section_count, batch_count, tensor_count, -1).astype(bf16).astype(f32)
-    gains_all = small[..., : 5 * gain_width].reshape(-1, 5, gain_width)
-    gains_all = gains_all.transpose(1, 0, 2).reshape(5, D)
-    taps_size = qkv_conv.size
-    taps_all = small[..., 5 * gain_width : 5 * gain_width + taps_size].reshape(
-        section_count, batch_count, tensor_count, 3, 3, heads_here, -1
-    )
-    taps_here = lax.dynamic_index_in_dim(taps_all, quarter, 2, keepdims=False)
-    taps_here = taps_here.transpose(0, 3, 2, 4, 1, 5).reshape(section_count, 3, 3 * local_width)
-    final_scale = gains_all[4]
+    small = jnp.sum(small, 0)
 
     vocab_rows = embed_table.shape[0]
     owner_start = (section * tensor_count + me) * vocab_rows
     local_ids = all_ids.reshape(batch_count, sequences * 4, 1, shard_rows) - owner_start
     picked = lookup(table_own, local_ids)
     total = plane_reduce(picked.reshape(8, D, shard_rows), 3).astype(bf16)
-    embedded = batch_trade(total.reshape(batch_count, depth, shard_rows))
+    embedded, small = batch_trade(total.reshape(batch_count, depth, shard_rows), small, 8)
+    gains_all = jnp.sum(small[:, :5], 0)
+    final_scale = gains_all[4]
+    taps_here = [
+        lax.dynamic_index_in_dim(
+            small, 4 * (quarter // 2) + 2 * layer + quarter % 2, 0, keepdims=False
+        )[5:, :640]
+        for layer in range(section_count)
+    ]
     embedded = embedded.reshape(D, shard_rows).T
-
-    def attn_weights(block, layer):
-        return block[:, : 3 * local_width], taps_here[layer], block[:, 3 * local_width :]
 
     def ffn_weights(block):
         return block[:, :hidden_width], block[:, hidden_width:]
 
     first_rows = embedded.astype(f32) * root_scale
     normed = (first_rows * norm_factor(first_rows) * gains_all[0]).astype(bf16)
-    gathered, block = group_gather(normed, 1, cargo=("out", 0, attn_all))
-    attn_first = attn_weights(block, 0)
-    partial, attn_kept_first = attention_forward(gathered.reshape(-1, D), length, attn_first)
+    gathered, attn_first = group_gather(normed, 1, cargo=("out", 0, [attn_all]))
+    partial, attn_kept_first = attention_forward(
+        gathered.reshape(-1, D), length, attn_first, taps_here[0]
+    )
     gathered, first_middle, block = turn(
-        partial, first_rows, gains_all[1], 20, False, cargo=("out", 0, ffn_all)
+        partial, first_rows, gains_all[1], 20, False, cargo=("out", 0, [ffn_all])
     )
     ffn_first = ffn_weights(block)
     partial, ffn_kept_first = ffn_forward(gathered.reshape(-1, D), ffn_first)
-    gathered, second_rows, block = turn(
-        partial, first_middle, gains_all[2], 21, True, cargo=("out", 1, attn_all)
-    )
-    attn_second = attn_weights(block, 1)
-    partial, attn_kept_second = attention_forward(gathered.reshape(-1, D), length, attn_second)
+    gathered, second_rows, attn_second = turn(
+        partial, first_middle, gains_all[2], 21, True, cargo=("out", 1, [attn_all])
+    )
+    partial, attn_kept_second = attention_forward(
+        gathered.reshape(-1, D), length, attn_second, taps_here[1]
+    )
     gathered, second_middle, block = turn(
-        partial, second_rows, gains_all[3], 24, False, cargo=("out", 1, ffn_all)
+        partial, second_rows, gains_all[3], 24, False, cargo=("out", 1, [ffn_all])
     )
     ffn_second = ffn_weights(block)
     partial, ffn_kept_second = ffn_forward(gathered.reshape(-1, D), ffn_second)
 
     def halves(blob):
-        return blob.reshape(batch_count, 2, depth // 2, blob.shape[1])
+        blob = blob if isinstance(blob, list) else [blob]
+        return [one.reshape(batch_count, 2, depth // 2, one.shape[1]) for one in blob]
 
     grad_both = mm(logit_grad.reshape(-1, vocab_rows), table_turned, 1, 1).astype(bf16)
     grad_final = plane_reduce(grad_both.reshape(8, shard_rows, D), 4)
@@ -968,7 +1201,7 @@
     )
     ffn_second_sum = summed(landed)
     partial, blob, taps_second = attention_backward(
-        gathered.reshape(-1, D), length, attn_second, attn_kept_second
+        gathered.reshape(-1, D), length, attn_second, taps_here[1], attn_kept_second
     )
     gathered, grad_rows, gain_2a, *landed = turn(
         partial, second_rows, gains_all[2], 23, True, passed=grad_rows,
@@ -976,25 +1209,52 @@
     )
     attn_second_sum = summed(landed)
     partial, blob = ffn_backward(gathered.reshape(-1, D), ffn_first, ffn_kept_first)
+    partial, head_done = tie(partial, head_done)
     gathered, grad_rows, gain_1f, *landed = turn(
         partial, first_middle, gains_all[1], 25, False, passed=grad_rows,
         cargo=("in", 0, halves(blob)),
     )
     ffn_first_sum = summed(landed)
     partial, blob, taps_first = attention_backward(
-        gathered.reshape(-1, D), length, attn_first, attn_kept_first
-    )
-    partial, head_done = tie(partial, head_done)
-    ffn_second_done, attn_second_done = over_batch(ffn_second_sum), over_batch(attn_second_sum)
+        gathered.reshape(-1, D), length, attn_first, taps_here[0], attn_kept_first
+    )
+    ffn_second_done = over_batch(ffn_second_sum)
+    partial, ffn_second_done = tie(partial, ffn_second_done)
+    attn_second_done, ffn_first_done = over_batch(attn_second_sum), over_batch(ffn_first_sum)
     grad_norm, *landed = group_reduce(partial, 14, cargo=("in", 0, halves(blob)))
     attn_first_sum = summed(landed)
     grad_norm, gain_1a = norm_back(grad_norm, first_rows, gains_all[0])
     grad_rows = grad_rows + grad_norm
-    grad_rows, ffn_second_done, attn_second_done = tie(
-        grad_rows, ffn_second_done, attn_second_done
-    )
-    ffn_first_done, attn_first_done = over_batch(ffn_first_sum), over_batch(attn_first_sum)
-
+    grad_rows, attn_second_done, ffn_first_done = tie(
+        grad_rows, attn_second_done, ffn_first_done
+    )
+    attn_first_done = over_batch(attn_first_sum)
+
+    embed_grad = (grad_rows * root_scale).astype(bf16).T
+    def row_at(index, vector):
+        padded = jnp.pad(vector, (0, D - vector.shape[0]))[None]
+        return jnp.where(jnp.arange(16)[:, None] == index, padded, 0.0)
+
+    vectors = [gain_1a, gain_1f[0], gain_2a[0], gain_2f[0], grad_final_gain, *taps_first[:3], *taps_second[:3]]
+    rows = sum(row_at(index, vector) for index, vector in enumerate(vectors))
+    traded, rows = batch_trade(embed_grad.reshape(batch_count, depth, shard_rows), rows, 9)
+    gain_sums = jnp.sum(rows[:, :5], 0)
+    holders = rows.reshape(2, 4, 16, D)[:, :, 5:11].reshape(2, 4, 2, 3, D)
+    taps_sums = jnp.sum(lax.dynamic_index_in_dim(holders, me, 1, keepdims=False), 0)
+    taps_sums = lax.dynamic_index_in_dim(taps_sums, section, 0, keepdims=False)
+    sums = jnp.concatenate([gain_sums, taps_sums])
+    every, sums = plane_and_batch_gather(traded.reshape(D, shard_rows), sums, 10)
+    sums, attn_first_done = tie(sums, attn_first_done)
+    every = every.reshape(8, batch_count, depth, shard_rows)
+    table_done = spread(every, local_ids, head_done).T
+    sums = jnp.sum(sums, 0)
+    gain_part = lax.dynamic_slice_in_dim(sums[:5], whole_at * gain_width, gain_width, 1)
+    gains_done = gain_part[:4].reshape(2, 2, gain_width)
+    final_done = gain_part[4]
+    conv_part = unpacked(sums[5:8]).reshape(3, 3, heads_here, HEAD).transpose(1, 0, 2, 3)
+    conv_done = lax.dynamic_slice_in_dim(
+        conv_part, at_batch * qkv_conv.shape[4], qkv_conv.shape[4], 3
+    )[None]
     def placed(first_part, second_part):
         keep = jnp.where(first, first_part, second_part)
         got = lax.ppermute(jnp.where(first, second_part, first_part), "section", [(0, 1), (1, 0)])
@@ -1004,39 +1264,10 @@
 
     attn_done = placed(attn_first_done, attn_second_done)
     ffn_done = placed(ffn_first_done, ffn_second_done)
-    qkv_done = attn_done[:, : 3 * local_width].reshape(1, depth, 3, local_width)
-    out_done = attn_done[:, 3 * local_width :].T[None]
+    qkv_done = unpacked(attn_done)[None]
+    out_done = jnp.concatenate([attn_done[:, 640:], attn_done[:, 576:640]], 1).T[None]
     up_done = ffn_done[:, :hidden_width][None]
     down_done = ffn_done[:, hidden_width:].T[None]
-
-    embed_grad = (grad_rows * root_scale).astype(bf16).T
-    traded = batch_trade(embed_grad.reshape(batch_count, depth, shard_rows))
-    every = plane_gather(traded.reshape(D, shard_rows), 10)
-    every = every.reshape(8, batch_count, depth, shard_rows)
-    table_done = spread(every, local_ids, head_done).T
-
-    def row_at(index, vector):
-        padded = jnp.pad(vector, (0, D - vector.shape[0]))[None]
-        return jnp.where(jnp.arange(16)[:, None] == index, padded, 0.0)
-
-    vectors = [gain_1a, gain_1f[0], gain_2a[0], gain_2f[0], grad_final_gain, *taps_first, *taps_second]
-    rows = sum(row_at(index, vector) for index, vector in enumerate(vectors))
-    rows = plane_gather(rows, 11)
-    gain_sums = jnp.sum(rows[:, :5], 0)
-    holders = rows.reshape(2, 4, 16, D)[:, :, 5:11].reshape(2, 4, 2, 3, D)
-    taps_sums = jnp.sum(lax.dynamic_index_in_dim(holders, me, 1, keepdims=False), 0)
-    taps_sums = lax.dynamic_index_in_dim(taps_sums, section, 0, keepdims=False)
-    sums = jnp.pad(jnp.concatenate([gain_sums, taps_sums]), ((0, 0), (0, 0)))
-    sums = batch_gather([sums], 12)
-    sums = jnp.sum(sums, 0)
-    whole_at = (section * batch_count + at_batch) * tensor_count + me
-    gain_part = lax.dynamic_slice_in_dim(sums[:5], whole_at * gain_width, gain_width, 1)
-    gains_done = gain_part[:4].reshape(2, 2, gain_width)
-    final_done = gain_part[4]
-    conv_part = sums[5:8, : 3 * local_width].reshape(3, 3, heads_here, HEAD).transpose(1, 0, 2, 3)
-    conv_done = lax.dynamic_slice_in_dim(
-        conv_part, at_batch * qkv_conv.shape[4], qkv_conv.shape[4], 3
-    )[None]
     return (
         logits,
         table_done,

time: 677 us -> 618 us (0.913)
  matrix products: 134 us -> 85.8 us
  other arithmetic: 64.7 us -> 20.2 us
  Pallas kernels: 402 us -> 438 us
    pallas_call x2 -> x6, Pallas kernels: 48.8 us -> 93 us  [the longest x4 57.4 us: attention_call(): pl.pallas_call(body, out_shape=out_shape, in_specs=[pl.BlockSpec(memory_s...]
    dot_general x24 -> x0, matrix products: 34 us -> none  [the longest x4 9.81 us: attend_back(): jnp.einsum('qhd,khd->hqk', grad_block, values_all[:reach], preferred_elem...]
    reduce_sum x6 -> x2, other arithmetic: 14.9 us -> 0.03 us  [the longest x1 0.02 us: on_device(): gains_all = jnp.sum(small[:, :5], 0)]
    unnamed x271 -> x143, local copies, waits for them, and re-layouts: 27.1 us -> 42 us
    dot_general x27 -> x15, matrix products: 99.6 us -> 85.8 us  [mm(): lax.dot_general(left, right, (((left_dim,), (right_dim,)), ((), ())), pre...]
    convert_element_type x12 -> x6, other arithmetic: 17.1 us -> 3.57 us  [the longest x4 2.46 us: summed(): (one.astype(f32) + two.astype(f32)).astype(bf16)]
    concatenate x4 -> x2, local copies, waits for them, and re-layouts: 11.6 us -> 1.01 us  [packed(): return jnp.concatenate(cuts + [out[:, 2 * HEAD:], out[:, :2 * HEAD]], 1)]
    pallas_call x20 -> x17, Pallas kernels: 353 us -> 345 us  [comm_call(): pl.pallas_call(kernel, out_shape=shapes, in_specs=in_specs, out_specs=out...]
  transfers between devices with their start and end apart: 10 -> 10, of which waited for: 0 -> 0; matrix products, arithmetic and copies ran while one was open for 27% -> 11% of each run, Pallas kernels for 52% -> 63%
where the time goes in v3:
time: 618 us; the launch traced here: 610 us
  Pallas kernels  438 us (71%)
  matrix products  85.8 us (14%)
  local copies, waits for them, and re-layouts  48.5 us (8%)
  other arithmetic  20.2 us (3%)
  between operations  15.6 us (3%)
    pallas_call x17, Pallas kernels, comm_call(): pl.pallas_call(kernel, out_shape=shapes, in_specs=in_specs, out_specs=out...  345 us
    dot_general x15, matrix products, mm(): lax.dot_general(left, right, (((left_dim,), (right_dim,)), ((), ())), pre...  85.8 us
    pallas_call x4, Pallas kernels, attention_call(): pl.pallas_call(body, out_shape=out_shape, in_specs=[pl.BlockSpec(memory_s...  57.4 us
    unnamed x143, local copies, waits for them, and re-layouts  42 us
    pallas_call x1, Pallas kernels, spread(): pl.pallas_call(spread_kernel, grid=(vocab_rows // columns,), out_shape=ja...  21.1 us
    pallas_call x1, Pallas kernels, lookup(): pl.pallas_call(lookup_kernel, grid=(batches,), out_shape=jax.ShapeDtypeSt...  14.5 us
  transfers between devices with their start and end apart: 10, of which 0 were waited for; matrix products, arithmetic and copies ran while one was open for 11% of the time, Pallas kernels for 63%

profile of v3, /device:TPU:0, one launch (start us, length us, event | category | flops | bytes accessed | tf_op | source)
XLA Modules:
  0.0 610.0 jit_solution(5410354426559515120)
XLA Ops:
  17.5 11.3 %shard_map.178 = (s32[4,16,128]{2,1,0:T(8,128)S(1)}, f32[4,8,768]{2,1,0:T(8,128)S(1)}) custom-call(s32[16,128]{1,0:T(8,128)S(1)} %reshape.299.refs_0_, f32[8,768]{1,0:T(8,128)S(1)} %pad_maximum_fusion.3.refs_1_), custom_call_target="tpu_custom_call" | custom-call | tf_op jit(solution)/shard_map/pallas_call | solution.py:112
  28.9 14.5 %shard_map.179 = bf16[8,4,192,256]{3,2,1,0:T(8,128)(2,1)S(1)} custom-call(s32[32,1,256]{2,1,0:T(1,128)S(1)} %bitcast.201, bf16[192,4096]{1,0:T(8,128)(2,1)S(1)} %copy-done), custom_call_target="tpu_custom_call" | custom-call | tf_op jit(solution)/shard_map/pallas_call | solution.py:994
  43.4 18.4 %shard_map.180 = f32[768,256]{1,0:T(8,128)S(1)} custom-call(bf16[8,768,256]{2,1,0:T(8,128)(2,1)S(1)} %bitcast.172), custom_call_target="tpu_custom_call" | custom-call | tf_op jit(solution)/shard_map/pallas_call | solution.py:112
  61.8 18.2 %shard_map.181 = (bf16[4,192,256]{2,1,0:T(8,128)(2,1)S(1)}, f32[8,8,768]{2,1,0:T(8,128)S(1)}) custom-call(bf16[4,192,256]{2,1,0:T(8,128)(2,1)S(1)} %bitcast.183, f32[8,768]{1,0:T(8,128)S(1)} %reduce_sum.107.refs_1_), custom_call_target="tpu_custom_call" | custom-call | tf_op jit(solution)/shard_map/pallas_call | solution.py:112
  82.9 15.6 %shard_map.182 = (bf16[4,256,768]{2,1,0:T(8,128)(2,1)S(1)}, bf16[768,768]{1,0:T(8,128)(2,1)S(1)}) custom-call(bf16[256,768]{1,0:T(8,128)(2,1)S(1)} %get-tuple-element.186.refs_0_, bf16[768,768]{1,0:T(8,128)(2,1)S(1)} %copy-done.5), custom_call_target="tpu_custom_call" | custom-call | tf_op jit(solution)/shard_map/pallas_call | solution.py:112
  99.7 11.5 %shard_map.183 = (bf16[1024,768]{1,0:T(8,128)(2,1)}, bf16[1024,640]{1,0:T(8,128)(2,1)S(1)}, bf16[1024,640]{1,0:T(8,128)(2,1)}, bf16[1024,256]{1,0:T(8,128)(2,1)S(1)}, f32[1024,128]{1,0:T(8,128)S(1)}) custom-call(s32[1]{0:T(128)} %dynamic_slice.24.length, bf16[1024,768]{1,0:T(8,128)(2,1)} %bitcast.173, bf16[768,768]{1,0:T(8,128)(2,1)S(1)} %get-tuple-element.84.weight, ...), custom_call_target="tpu_custom_call" | custom-call | tf_op jit(solution)/shard_map/pallas_call | solution.py:793
  114.9 2.0 copy-done.1
  116.9 1.5 copy-done.21
  118.5 29.3 %shard_map.184 = (bf16[4,256,768]{2,1,0:T(8,128)(2,1)S(1)}, f32[256,768]{1,0:T(8,128)S(1)}, bf16[768,1536]{1,0:T(8,128)(2,1)S(1)}) custom-call(bf16[4,256,768]{2,1,0:T(8,128)(2,1)S(1)} %bitcast.187, f32[256,768]{1,0:T(8,128)S(1)} %get-tuple-element.185.refs_1_, f32[1,768]{1,0:T(1,128)S(1)} %get-tuple-element.218.refs_2_, bf16[768,1536]{1,0:T(8,128)(2,1)S(1)} %copy-done.1), custom_call_target="tpu_custom_call" | custom-call | tf_op jit(solution)/shard_map/pallas_call | solution.py:112
  148.9 1.4 fusion.8
  150.3 1.4 convolution_convert_fusion.6
  152.5 25.6 %shard_map.185 = (bf16[4,256,768]{2,1,0:T(8,128)(2,1)S(1)}, f32[256,768]{1,0:T(8,128)S(1)}, bf16[768,768]{1,0:T(8,128)(2,1)S(1)}) custom-call(bf16[4,256,768]{2,1,0:T(8,128)(2,1)S(1)} %bitcast.179, f32[256,768]{1,0:T(8,128)S(1)} %get-tuple-element.88.refs_1_, f32[1,768]{1,0:T(1,128)S(1)} %get-tuple-element.217.refs_2_, bf16[768,768]{1,0:T(8,128)(2,1)S(1)} %copy-done.6), custom_call_target="tpu_custom_call" | custom-call | tf_op jit(solution)/shard_map/pallas_call | solution.py:112
  179.2 12.3 %shard_map.186 = (bf16[1024,768]{1,0:T(8,128)(2,1)}, bf16[1024,640]{1,0:T(8,128)(2,1)S(1)}, bf16[1024,640]{1,0:T(8,128)(2,1)}, bf16[1024,256]{1,0:T(8,128)(2,1)S(1)}, f32[1024,128]{1,0:T(8,128)S(1)}) custom-call(s32[1]{0:T(128)} %dynamic_slice.24.length, bf16[1024,768]{1,0:T(8,128)(2,1)} %bitcast.175, bf16[768,768]{1,0:T(8,128)(2,1)S(1)} %get-tuple-element.90.weight, ...), custom_call_target="tpu_custom_call" | custom-call | tf_op jit(solution)/shard_map/pallas_call | solution.py:793
  193.3 1.6 copy-done.22
  194.9 23.5 %shard_map.187 = (bf16[4,256,768]{2,1,0:T(8,128)(2,1)S(1)}, f32[256,768]{1,0:T(8,128)S(1)}, bf16[768,1536]{1,0:T(8,128)(2,1)S(1)}) custom-call(bf16[4,256,768]{2,1,0:T(8,128)(2,1)S(1)} %bitcast.188, f32[256,768]{1,0:T(8,128)S(1)} %get-tuple-element.92.refs_1_, f32[1,768]{1,0:T(1,128)S(1)} %get-tuple-element.216.refs_2_, bf16[768,1536]{1,0:T(8,128)(2,1)S(1)} %copy-done.2), custom_call_target="tpu_custom_call" | custom-call | tf_op jit(solution)/shard_map/pallas_call | solution.py:112
  218.5 1.4 fusion.3
  220.3 1.7 copy-done.66
  222.0 1.4 convolution_convert_fusion.5
  223.5 18.4 %convolution_convert_fusion.2 = bf16[2048,768]{1,0:T(8,128)(2,1)S(1)} fusion(bf16[2048,4096]{1,0:T(8,128)(2,1)} %bitcast.221, bf16[768,4096]{1,0:T(8,128)(2,1)} %all-gather.8.cloned.1.call-done), kind=kOutput, calls=%fused_computation.2 | convolution fusion | flops 12886474752 | bytes 26214400 | tf_op jit(solution)/shard_map/dot_general | solution.py:21
  241.9 22.6 %shard_map.188 = f32[256,768]{1,0:T(8,128)S(1)} custom-call(bf16[8,256,768]{2,1,0:T(8,128)(2,1)S(1)} %bitcast.178), custom_call_target="tpu_custom_call" | custom-call | tf_op jit(solution)/shard_map/pallas_call | solution.py:112
  265.5 12.8 %shard_map.189 = f32[256,768]{1,0:T(8,128)S(1)} custom-call(bf16[4,256,768]{2,1,0:T(8,128)(2,1)S(1)} %bitcast.181), custom_call_target="tpu_custom_call" | custom-call | tf_op jit(solution)/shard_map/pallas_call | solution.py:112
  280.4 17.0 %shard_map.190 = bf16[8,256,768]{2,1,0:T(8,128)(2,1)S(1)} custom-call(bf16[256,768]{1,0:T(8,128)(2,1)S(1)} %fusion.12.refs_0_), custom_call_target="tpu_custom_call" | custom-call | tf_op jit(solution)/shard_map/pallas_call | solution.py:112
  297.8 18.9 %convolution_convert_fusion.1 = bf16[768,4096]{1,0:T(8,128)(2,1)} fusion(bf16[2048,768]{1,0:T(8,128)(2,1)S(1)} %bitcast.208, bf16[2048,4096]{1,0:T(8,128)(2,1)} %bitcast.222), kind=kOutput, calls=%fused_computation.1 | convolution fusion | flops 12888047616 | bytes 26214400 | tf_op jit(solution)/shard_map/dot_general | solution.py:21
  317.2 1.6 fusion.16
  320.1 12.6 %shard_map.191 = bf16[4,256,768]{2,1,0:T(8,128)(2,1)S(1)} custom-call(bf16[256,768]{1,0:T(8,128)(2,1)S(1)} %get-tuple-element.179.refs_0_), custom_call_target="tpu_custom_call" | custom-call | tf_op jit(solution)/shard_map/pallas_call | solution.py:112
  332.7 3.3 multiply_convert_fusion.1
  336.0 1.4 convolution_convert_fusion.4
  337.4 1.4 convolution_convert_fusion.10
  339.3 1.4 convolution_convert_fusion.9
  340.8 23.1 %shard_map.192 = (bf16[4,256,768]{2,1,0:T(8,128)(2,1)S(1)}, f32[256,768]{1,0:T(8,128)S(1)}, f32[1,768]{1,0:T(1,128)S(1)}, bf16[4,96,768]{2,1,0:T(8,128)(2,1)S(1)...) custom-call(bf16[4,256,768]{2,1,0:T(8,128)(2,1)S(1)} %bitcast.186, ...), custom_call_target="tpu_custom_call" | custom-call | tf_op jit(solution)/shard_map/pallas_call | solution.py:112
  370.8 16.8 %shard_map.193 = (bf16[1024,768]{1,0:T(8,128)(2,1)}, bf16[768,768]{1,0:T(8,128)(2,1)S(1)}, f32[8,640]{1,0:T(8,128)S(1)}) custom-call(s32[1]{0:T(128)} %dynamic_slice.24.length, bf16[1024,768]{1,0:T(8,128)(2,1)} %bitcast.191, bf16[1024,768]{1,0:T(8,128)(2,1)} %bitcast.176, bf16[768,768]{1,0:T(8,128)(2,1)S(1)} %copy-done.10, f32[3,640]{1,0:T(4,128)S(1)} %slice.278.taps, ...), custom_call_target="tpu_custom_call" | custom-call | tf_op jit(solution)/shard_map/pallas_call | solution.py:793
  387.6 1.5 copy-done.18
  389.1 29.0 %shard_map.194 = (bf16[4,256,768]{2,1,0:T(8,128)(2,1)S(1)}, f32[256,768]{1,0:T(8,128)S(1)}, f32[1,768]{1,0:T(1,128)S(1)}, bf16[4,96,768]{2,1,0:T(8,128)(2,1)S(1)}, bf16[4,96,768]{2,1,0:T(8,128)(2,1)S(1)}) custom-call(bf16[4,256,768]{2,1,0:T(8,128)(2,1)S(1)} %bitcast.180, f32[256,768]{1,0:T(8,128)S(1)} %copy-done.15, ...), custom_call_target="tpu_custom_call" | custom-call | tf_op jit(solution)/shard_map/pallas_call | solution.py:112
  421.1 4.2 multiply_convert_fusion
  426.6 2.6 convolution_convert_fusion.8
  429.2 4.4 convolution_convert_fusion.3
  433.7 4.8 convolution_convert_fusion.7
  439.7 1.4 copy-done.19
  441.1 1.4 copy-done.27
  444.9 23.3 %shard_map.195 = (bf16[4,256,768]{2,1,0:T(8,128)(2,1)S(1)}, f32[256,768]{1,0:T(8,128)S(1)}, f32[1,768]{1,0:T(1,128)S(1)}, bf16[4,96,768]{2,1,0:T(8,128)(2,1)S(1)...) custom-call(bf16[4,256,768]{2,1,0:T(8,128)(2,1)S(1)} %bitcast.184, ...), custom_call_target="tpu_custom_call" | custom-call | tf_op jit(solution)/shard_map/pallas_call | solution.py:112
  470.9 19.3 %convolution_convert_fusion = bf16[2048,4096]{1,0:T(8,128)(2,1)} fusion(bf16[2048,768]{1,0:T(8,128)(2,1)S(1)} %bitcast.171, bf16[768,4096]{1,0:T(8,128)(2,1)} %all-gather.8.cloned.1.call-done), kind=kOutput, calls=%fused_computation | convolution fusion | flops 12893290496 | bytes 26214400 | tf_op jit(solution)/shard_map/dot_general | solution.py:21
  490.3 16.8 %shard_map.196 = (bf16[1024,768]{1,0:T(8,128)(2,1)}, bf16[768,768]{1,0:T(8,128)(2,1)S(1)}, f32[8,640]{1,0:T(8,128)S(1)}) custom-call(s32[1]{0:T(128)} %dynamic_slice.24.length, bf16[1024,768]{1,0:T(8,128)(2,1)} %bitcast.192, bf16[1024,768]{1,0:T(8,128)(2,1)} %bitcast.174, bf16[768,768]{1,0:T(8,128)(2,1)S(1)} %copy-done.8, f32[3,640]{1,0:T(4,128)S(1)} %slice.275.taps, ...), custom_call_target="tpu_custom_call" | custom-call | tf_op jit(solution)/shard_map/pallas_call | solution.py:793
  507.1 1.4 copy-done.20
  508.5 18.5 %shard_map.197 = (f32[256,768]{1,0:T(8,128)S(1)}, bf16[4,96,768]{2,1,0:T(8,128)(2,1)S(1)}, bf16[4,96,768]{2,1,0:T(8,128)(2,1)S(1)}) custom-call(bf16[4,256,768]{2,1,0:T(8,128)(2,1)S(1)} %bitcast.185, bf16[4,2,96,768]{3,2,1,0:T(8,128)(2,1)S(1)} %bitcast.196), custom_call_target="tpu_custom_call" | custom-call | tf_op jit(solution)/shard_map/pallas_call | solution.py:112
  529.5 20.3 %shard_map.198 = (bf16[4,192,256]{2,1,0:T(8,128)(2,1)S(1)}, f32[8,16,768]{2,1,0:T(8,128)S(1)}) custom-call(bf16[4,192,256]{2,1,0:T(8,128)(2,1)S(1)} %bitcast.182, f32[16,768]{1,0:T(8,128)S(1)} %select_add_fusion.refs_1_), custom_call_target="tpu_custom_call" | custom-call | tf_op jit(solution)/shard_map/pallas_call | solution.py:112
  550.1 24.0 %shard_map.199 = (bf16[8,768,256]{2,1,0:T(8,128)(2,1)S(1)}, f32[4,8,768]{2,1,0:T(8,128)S(1)}) custom-call(bf16[768,256]{1,0:T(8,128)(2,1)S(1)} %bitcast.199, f32[8,768]{1,0:T(8,128)S(1)} %pad_maximum_fusion.4.refs_1_), custom_call_target="tpu_custom_call" | custom-call | tf_op jit(solution)/shard_map/pallas_call | solution.py:112
  574.2 1.6 copy-done.11
  578.2 21.1 %shard_map.200 = f32[192,4096]{1,0:T(8,128)} custom-call(s32[32,256]{1,0:T(8,128)} %sub.41.ids, bf16[8,4,192,256]{3,2,1,0:T(8,128)(2,1)} %bitcast.177, bf16[192,4096]{1,0:T(8,128)(2,1)} %reduce-scatter.6.cloned.1.call-done.base), custom_call_target="tpu_custom_call" | custom-call | tf_op jit(solution)/shard_map/pallas_call | solution.py:1049
  (273 shorter events, 54.8 us)
Async XLA Ops:
  7.2 74.4 %all-gather.4.cloned.1.call-start = ((), (), s32[]{:S(2)}) async-start(), calls=%async_computation.5 | async-start | bytes 1474560 | tf_op jit(solution)/shard_map/all_gather | solution.py:1115
  10.4 3.3 copy-start.55
  10.4 104.5 %all-gather.6.cloned.1.call-start = ((), (), s32[]{:S(2)}) async-start(), calls=%async_computation.6 | async-start | bytes 2949120 | tf_op jit(solution)/shard_map/all_gather | solution.py:1116
  13.7 209.8 %all-gather.8.cloned.1.call-start = ((), (), s32[]{:S(2)}) async-start(), calls=%async_computation.7 | async-start | bytes 7864320 | tf_op jit(solution)/shard_map/all_gather | solution.py:1117
  15.1 1.5 copy-start.60
  15.1 1.9 copy-start.64
  15.2 13.7 %copy-start = (bf16[192,4096]{1,0:T(8,128)(2,1)S(1)}, bf16[192,4096]{1,0:T(8,128)(2,1)}, u32[]{:S(2)}) copy-start(bf16[192,4096]{1,0:T(8,128)(2,1)} %convert_bitcast_fusion.table) | copy-start | bytes 4718596
  15.2 423.3 %reduce-scatter.6.cloned.1.call-start = ((), (), s32[]{:S(2)}) async-start(), calls=%async_computation.8 | async-start | bytes 7864320 | tf_op jit(solution)/shard_map/reduce_scatter | solution.py:1193
  80.4 18.1 %copy-start.51 = (f32[768,256]{0,1:T(8,128)}, f32[768,256]{0,1:T(8,128)S(1)}, u32[]{:S(2)}) copy-start(f32[768,256]{0,1:T(8,128)S(1)} %copy.25) | copy-start | bytes 2359300
  114.9 2.0 copy-start.1
  116.9 1.5 copy-start.21
  147.7 2.5 copy-start.43
  147.7 4.2 copy-start.12
  150.3 1.7 copy-start.65
  150.3 2.2 copy-start.6
  179.2 39.2 %copy-start.9 = (bf16[768,768]{1,0:T(8,128)(2,1)}, bf16[768,768]{1,0:T(8,128)(2,1)S(1)}, u32[]{:S(2)}) copy-start(bf16[768,768]{1,0:T(8,128)(2,1)S(1)} %get-tuple-element.90.weight) | copy-start | bytes 3538948
  179.2 39.2 %copy-start.14 = (f32[256,768]{1,0:T(8,128)}, f32[256,768]{1,0:T(8,128)S(1)}, u32[]{:S(2)}) copy-start(f32[256,768]{1,0:T(8,128)S(1)} %get-tuple-element.92.refs_1_) | copy-start | bytes 2359300
  179.2 14.1 %copy-start.2 = (bf16[768,1536]{1,0:T(8,128)(2,1)S(1)}, bf16[768,1536]{1,0:T(8,128)(2,1)}, u32[]{:S(2)}) copy-start(bf16[768,1536]{1,0:T(8,128)(2,1)} %all-gather.6.cloned.1.call-done.refs_3_) | copy-start | bytes 7077892
  193.3 25.1 %copy-start.41 = (f32[1024,128]{1,0:T(8,128)}, f32[1024,128]{1,0:T(8,128)S(1)}, u32[]{:S(2)}) copy-start(f32[1024,128]{1,0:T(8,128)S(1)} %get-tuple-element.103.totals) | copy-start | bytes 1572868
  193.3 1.6 copy-start.22
  218.4 1.9 copy-start.48
  218.5 59.9 %copy-start.16 = (f32[256,768]{1,0:T(8,128)}, f32[256,768]{1,0:T(8,128)S(1)}, u32[]{:S(2)}) copy-start(f32[256,768]{1,0:T(8,128)S(1)} %get-tuple-element.93.refs_1_) | copy-start | bytes 2359300
  220.3 1.7 copy-start.66
  316.7 190.4 %reduce-scatter.8.cloned.1.call-start = ((), (), s32[]{:S(2)}) async-start(), calls=%async_computation.9 | async-start | bytes 1474560 | tf_op jit(solution)/shard_map/reduce_scatter | solution.py:1073
  317.2 1.6 copy-start.54
  318.8 13.9 %copy-start.45 = (bf16[768,1536]{1,0:T(8,128)(2,1)S(1)}, bf16[768,1536]{1,0:T(8,128)(2,1)}, u32[]{:S(2)}) copy-start(bf16[768,1536]{1,0:T(8,128)(2,1)} %copy-done.44) | copy-start | bytes 7077892
  336.0 1.4 copy-start.49
  337.4 1.9 copy-start.67
  339.3 1.4 copy-start.17
  366.5 162.7 %reduce-scatter.10.cloned.1.call-start = ((), (), s32[]{:S(2)}) async-start(), calls=%async_computation.10 | async-start | bytes 737280 | tf_op jit(solution)/shard_map/reduce_scatter | solution.py:1073
  370.8 16.8 %copy-start.15 = (f32[256,768]{1,0:T(8,128)S(1)}, f32[256,768]{1,0:T(8,128)}, u32[]{:S(2)}) copy-start(f32[256,768]{1,0:T(8,128)} %copy-done.14) | copy-start | bytes 2359300
  370.8 16.8 %copy-start.32 = (f32[256,768]{1,0:T(8,128)S(1)}, f32[256,768]{1,0:T(8,128)}, u32[]{:S(2)}) copy-start(f32[256,768]{1,0:T(8,128)} %copy-done.31) | copy-start | bytes 2359300
  387.6 1.5 copy-start.18
  421.1 5.5 copy-start.47
  429.2 100.1 %reduce-scatter.12.cloned.1.call-start = ((), (), s32[]{:S(2)}) async-start(), calls=%async_computation.11 | async-start | bytes 1474560 | tf_op jit(solution)/shard_map/reduce_scatter | solution.py:1073
  470.8 104.9 %reduce-scatter.14.cloned.1.call-start = ((), (), s32[]{:S(2)}) async-start(), calls=%async_computation.12 | async-start | bytes 737280 | tf_op jit(solution)/shard_map/reduce_scatter | solution.py:1073
  470.9 19.4 %copy-start.8 = (bf16[768,768]{1,0:T(8,128)(2,1)S(1)}, bf16[768,768]{1,0:T(8,128)(2,1)}, u32[]{:S(2)}) copy-start(bf16[768,768]{1,0:T(8,128)(2,1)} %copy-done.7) | copy-start | bytes 3538948
  470.9 19.4 %copy-start.36 = (bf16[1024,256]{1,0:T(8,128)(2,1)S(1)}, bf16[1024,256]{1,0:T(8,128)(2,1)}, u32[]{:S(2)}) copy-start(bf16[1024,256]{1,0:T(8,128)(2,1)} %copy-done.35) | copy-start | bytes 1572868
  470.9 19.4 %copy-start.38 = (f32[1024,128]{1,0:T(8,128)S(1)}, f32[1024,128]{1,0:T(8,128)}, u32[]{:S(2)}) copy-start(f32[1024,128]{1,0:T(8,128)} %copy-done.37) | copy-start | bytes 1572868
  490.3 36.8 %copy-start.52 = (f32[768,256]{0,1:T(8,128)S(1)}, f32[768,256]{0,1:T(8,128)}, u32[]{:S(2)}) copy-start(f32[768,256]{0,1:T(8,128)} %copy-done.51) | copy-start | bytes 2359300
  527.4 1.6 copy-start.53
  529.3 46.5 %copy-start.56 = (bf16[1,96,1536]{2,1,0:T(8,128)(2,1)S(1)}, bf16[1,96,1536]{2,1,0:T(8,128)(2,1)}, u32[]{:S(2)}) copy-start(bf16[1,96,1536]{2,1,0:T(8,128)(2,1)} %reduce-scatter.8.cloned.1.call-done) | copy-start | bytes 884740
  529.3 46.5 %copy-start.57 = (bf16[1,96,1536]{2,1,0:T(8,128)(2,1)S(1)}, bf16[1,96,1536]{2,1,0:T(8,128)(2,1)}, u32[]{:S(2)}) copy-start(bf16[1,96,1536]{2,1,0:T(8,128)(2,1)} %reduce-scatter.12.cloned.1.call-done) | copy-start | bytes 884740
  549.9 28.1 %copy-start.58 = (bf16[1,96,768]{2,1,0:T(8,128)(2,1)S(1)}, bf16[1,96,768]{2,1,0:T(8,128)(2,1)}, u32[]{:S(2)}) copy-start(bf16[1,96,768]{2,1,0:T(8,128)(2,1)} %reduce-scatter.10.cloned.1.call-done) | copy-start | bytes 442372
  574.1 1.6 copy-start.11
  575.8 2.2 copy-start.59
  575.9 25.8 %collective-permute-start.1 = (bf16[96,1536]{1,0:T(8,128)(2,1)S(1)}, bf16[96,1536]{1,0:T(8,128)(2,1)S(1)}, u32[]{:S(2)}, u32[]{:S(2)}) collective-permute-start(bf16[96,1536]{1,0:T(8,128)(2,1)S(1)} %get-tuple-element.188), channel_id=1, source_target_pairs={{0,16},{16,0},{1,17},{17,1},{2,18},{18,2},{3,19},{19,3},{4,20},{20... | collective-permute-start | bytes 884744 | tf_op jit(solution)/shard_map/ppermute | solution.py:1260
  578.0 21.8 %collective-permute-start = (bf16[96,768]{1,0:T(8,128)(2,1)S(1)}, bf16[96,768]{1,0:T(8,128)(2,1)S(1)}, u32[]{:S(2)}, u32[]{:S(2)}) collective-permute-start(bf16[96,768]{1,0:T(8,128)(2,1)S(1)} %get-tuple-element.198), channel_id=1, source_target_pairs={{0,16},{16,0},{1,17},{17,1},{2,18},{18,2},{3,19},{19,3},{4,20},{20... | collective-permute-start | bytes 442376 | tf_op jit(solution)/shard_map/ppermute | solution.py:1260
  (31 other events, 35.5 us)
Sparse Core Ops, SparseCore 0:
  10.6 36.1 all-gather.3
  48.9 57.5 all-gather.5
  108.7 114.0 all-gather.7
  316.8 116.4 reduce-scatter.5
  435.5 29.6 reduce-scatter.7
  468.0 20.6 reduce-scatter.9
  491.0 27.5 reduce-scatter.11
  528.5 33.6 reduce-scatter.13

commit v4 on v3

--- a/solution.py
+++ b/solution.py
@@ -62,11 +62,15 @@
     pl.semaphore_wait(barrier, len(devices))
 
 
-def comm_call(body, out_shape, scratch, collective_id, *operands, cargo=None):
+def comm_call(
+    body, out_shape, scratch, collective_id, *operands, cargo=None, streamed=(), room=16
+):
     shapes = list(out_shape) if isinstance(out_shape, (list, tuple)) else [out_shape]
     in_specs = [pl.BlockSpec(memory_space=pltpu.VMEM)] * len(operands)
     out_specs = [pl.BlockSpec(memory_space=pltpu.VMEM)] * len(shapes)
     scratch = list(scratch)
+    operands = operands + tuple(streamed)
+    in_specs += [pl.BlockSpec(memory_space=pl.ANY)] * len(streamed)
     count_in, count_out = len(operands), len(shapes)
     loads = 0
     if cargo is not None:
@@ -116,7 +120,7 @@
         out_specs=out_specs,
         scratch_shapes=scratch,
         compiler_params=pltpu.CompilerParams(
-            collective_id=collective_id, has_side_effects=True, vmem_limit_bytes=40 << 20
+            collective_id=collective_id, has_side_effects=True, vmem_limit_bytes=room << 20
         ),
     )(*operands)
     return results if len(shapes) > 1 else results[0]
@@ -453,7 +457,34 @@
     plane_exchange(own, out, send, recv)
 
 
-def plane_exchange(own, out, send, recv):
+class Chores:
+    def __init__(self, units=()):
+        self.units = list(units)
+
+    def some(self, count):
+        for _ in range(min(count, len(self.units))):
+            self.units.pop(0)()
+
+    def rest(self):
+        self.some(len(self.units))
+
+
+def stream(count, source_at, buffers, sems, work):
+    def fetch(at):
+        return pltpu.make_async_copy(source_at(at), buffers.at[at % 2], sems.at[at % 2])
+
+    def unit(at):
+        fetch(at).wait()
+        work(at, buffers.at[at % 2])
+        if at + 2 < count:
+            fetch(at + 2).start()
+
+    for at in range(min(2, count)):
+        fetch(at).start()
+    return [functools.partial(unit, at) for at in range(count)]
+
+
+def plane_exchange(own, out, send, recv, chores=Chores()):
     core, y, x, _ = place()
     other, beside, above = plane_peers()
     half = own.shape[0] // 2
@@ -486,43 +517,71 @@
         made.start()
         return made
 
+    chores.some(2)
     to_x[0].wait_recv()
     diag_y = onward(at_x, 0, 5, above)
     pending.append(onward(at_x, 0, 6, other))
     to_y[1].wait_recv()
     diag_x = onward(at_y, 1, 7, beside)
     pending.append(onward(at_y, 1, 8, other))
+    chores.some(2)
     to_x[1].wait_recv()
     pending.append(onward(at_x, 1, 9, other))
     to_y[0].wait_recv()
     pending.append(onward(at_y, 0, 10, other))
+    chores.some(2)
     diag_y.wait_recv()
     pending.append(onward(at_both, 0, 11, other))
     diag_x.wait_recv()
     pending.append(onward(at_both, 1, 12, other))
+    chores.rest()
     for made in to_x + to_y + [diag_x, diag_y]:
         made.wait_send()
     for made in pending:
         made.wait()
 
 
-def plane_gather(block, collective_id):
-    count, width = block.shape
+def head_gather_kernel(own, table, grads, out, parts, buffers, sems, send, recv):
+    greet(plane_peers())
+    rows = own.shape[0]
+
+    def work(at, block):
+        parts[at] = mm(block[...], table[...], 1, 1).astype(bf16)
+
+    chores = Chores(
+        stream(8, lambda at: grads.at[pl.ds(rows * at, rows)], buffers, sems, work)
+    )
+    plane_exchange(own, out, send, recv, chores)
+
+
+def head_gather(rows, table, grads):
+    count, width = rows.shape
     return comm_call(
-        plane_gather_kernel,
-        jax.ShapeDtypeStruct((8, count, width), block.dtype),
-        [pltpu.SemaphoreType.DMA((13,))] * 2,
-        collective_id,
-        block,
-    )
-
-
-def plane_reduce_kernel(parts, out, near, mixed, via_x, via_y, from_x, from_y, hop_x, hop_y, send, recv):
-    core, y, x, tensor = place()
-    other = {"section": 1 - core}
-    beside = {"tensor": tensor + 1 - 2 * x}
-    above = {"tensor": tensor + 2 - 4 * y}
-    greet([other, beside, above])
+        head_gather_kernel,
+        [jax.ShapeDtypeStruct((8, count, width), bf16)] * 2,
+        [
+            pltpu.VMEM((2, count, grads.shape[1]), bf16),
+            pltpu.SemaphoreType.DMA((2,)),
+        ]
+        + [pltpu.SemaphoreType.DMA((13,))] * 2,
+        7,
+        rows,
+        table,
+        streamed=[grads],
+        room=28,
+    )
+
+
+def plane_reduce_kernel(parts, out, *scratch):
+    greet(plane_peers())
+    plane_sum(parts, out, *scratch)
+
+
+def plane_sum(
+    parts, out, near, mixed, via_x, via_y, from_x, from_y, hop_x, hop_y, send, recv, chores=Chores()
+):
+    core, y, x, _ = place()
+    other, beside, above = plane_peers()
     half = out.shape[0] // 2
     cut = [pl.ds(0, half), pl.ds(half, half)]
 
@@ -562,12 +621,14 @@
     handed[2].wait_recv()
     mixed[2] = joined(2).astype(bf16)
     straight_y = start(mixed.at[2, cut[1]], from_y.at[cut[1]], 7, above)
+    chores.some(2)
     diag_x.wait_recv()
     hop_y[...] = (mixed[2, cut[0]].astype(f32) + via_x[...].astype(f32)).astype(bf16)
     turned_y = start(hop_y, from_y.at[cut[0]], 8, above)
     diag_y.wait_recv()
     hop_x[...] = (mixed[1, cut[1]].astype(f32) + via_y[...].astype(f32)).astype(bf16)
     turned_x = start(hop_x, from_x.at[cut[1]], 9, beside)
+    chores.rest()
     handed[3].wait_recv()
     straight_x.wait_recv()
     turned_y.wait_recv()
@@ -579,25 +640,68 @@
         made.wait_send()
 
 
+def plane_scratch(count, width):
+    half = count // 2
+    return [
+        pltpu.VMEM((4, count, width), bf16),
+        pltpu.VMEM((3, count, width), bf16),
+        pltpu.VMEM((half, width), bf16),
+        pltpu.VMEM((half, width), bf16),
+        pltpu.VMEM((count, width), bf16),
+        pltpu.VMEM((count, width), bf16),
+        pltpu.VMEM((half, width), bf16),
+        pltpu.VMEM((half, width), bf16),
+    ] + [pltpu.SemaphoreType.DMA((10,))] * 2
+
+
 def plane_reduce(parts, collective_id):
     _, count, width = parts.shape
-    half = count // 2
     return comm_call(
         plane_reduce_kernel,
         jax.ShapeDtypeStruct((count, width), f32),
-        [
-            pltpu.VMEM((4, count, width), bf16),
-            pltpu.VMEM((3, count, width), bf16),
-            pltpu.VMEM((half, width), bf16),
-            pltpu.VMEM((half, width), bf16),
-            pltpu.VMEM((count, width), bf16),
-            pltpu.VMEM((count, width), bf16),
-            pltpu.VMEM((half, width), bf16),
-            pltpu.VMEM((half, width), bf16),
-        ]
-        + [pltpu.SemaphoreType.DMA((10,))] * 2,
+        plane_scratch(count, width),
         collective_id,
         parts,
+    )
+
+
+def head_reduce_kernel(parts, rows, valid, grads, out, table_grad, held, buffers, sems, *scratch):
+    greet(plane_peers())
+    width = buffers.shape[2]
+    for lead in range(0, rows.shape[1], 128):
+        held[:, lead : lead + 128] = rows[:, lead : lead + 128] * valid[...]
+
+    def work(at, block):
+        table_grad[:, width * at : width * at + width] = mm(held[...], block[...], 0, 0).astype(bf16)
+
+    steps = grads.shape[1] // width
+    chores = Chores(
+        stream(steps, lambda at: grads.at[:, pl.ds(width * at, width)], buffers, sems, work)
+    )
+    plane_sum(parts, out, *scratch, chores=chores)
+
+
+def head_reduce(parts, rows, valid, grads):
+    _, count, width = parts.shape
+    step = 512
+    return comm_call(
+        head_reduce_kernel,
+        [
+            jax.ShapeDtypeStruct((count, width), f32),
+            jax.ShapeDtypeStruct((width, grads.shape[1]), bf16),
+        ],
+        [
+            pltpu.VMEM(rows.shape, bf16),
+            pltpu.VMEM((2, rows.shape[0], step), bf16),
+            pltpu.SemaphoreType.DMA((2,)),
+        ]
+        + plane_scratch(count, width),
+        4,
+        parts,
+        rows,
+        valid,
+        streamed=[grads],
+        room=40,
     )
 
 
@@ -796,7 +900,7 @@
         in_specs=[pl.BlockSpec(memory_space=pltpu.SMEM)] + [whole] * len(operands),
         out_specs=[whole] * len(out_shape),
         scratch_shapes=scratch,
-        compiler_params=pltpu.CompilerParams(vmem_limit_bytes=50 << 20),
+        compiler_params=pltpu.CompilerParams(vmem_limit_bytes=32 << 20),
     )(length.reshape(1), *operands)
 
 
@@ -1057,7 +1161,7 @@
         ],
         out_specs=pl.BlockSpec((depth, columns), lambda at: (0, at)),
         scratch_shapes=[pltpu.VMEM((batches * parts, slots, 128), jnp.int16)],
-        compiler_params=pltpu.CompilerParams(vmem_limit_bytes=56 << 20),
+        compiler_params=pltpu.CompilerParams(vmem_limit_bytes=32 << 20),
     )(ids.reshape(batches * parts, slots), grads, base)
 
 
@@ -1176,20 +1280,17 @@
         blob = blob if isinstance(blob, list) else [blob]
         return [one.reshape(batch_count, 2, depth // 2, one.shape[1]) for one in blob]
 
-    grad_both = mm(logit_grad.reshape(-1, vocab_rows), table_turned, 1, 1).astype(bf16)
-    grad_final = plane_reduce(grad_both.reshape(8, shard_rows, D), 4)
+    final_rows = (second_middle + group_reduce(partial, 2)).astype(bf16).astype(f32)
+    normed_final = (final_rows * norm_factor(final_rows) * final_scale).astype(bf16)
+    grads_flat = logit_grad.reshape(-1, vocab_rows)
+    final_both, grad_parts = head_gather(normed_final, table_turned, grads_flat)
+    final_both = final_both.reshape(-1, D)
+    valid = (jnp.arange(slot_length)[None, :] < seq_lengths[:, None]).reshape(-1, 1)
+    valid = jnp.broadcast_to(valid, (valid.shape[0], 128)).astype(bf16)
+    grad_final, head_table = head_reduce(grad_parts, final_both, valid, grads_flat)
     own_at = quarter * shard_rows + jnp.arange(shard_rows)
     grad_final = jnp.where((own_at < length)[:, None], grad_final, 0.0)
-
-    partial, grad_final = tie(partial, grad_final)
-    final_rows = (second_middle + group_reduce(partial, 2)).astype(bf16).astype(f32)
-    normed_final = (final_rows * norm_factor(final_rows) * final_scale).astype(bf16)
-    final_both = plane_gather(normed_final, 7).reshape(-1, D)
     logits = mm(final_both, table_turned, 1, 0).astype(bf16).reshape(sequences, slot_length, -1)
-    valid = (jnp.arange(slot_length)[None, :] < seq_lengths[:, None]).reshape(-1, 1)
-    masked_final = jnp.where(valid, final_both, jnp.zeros((), bf16))
-    head_table = mm(masked_final, logit_grad.reshape(-1, vocab_rows), 0, 0).astype(bf16)
-    grad_final, head_table = tie(grad_final, head_table)
     head_done = lax.psum_scatter(head_table, "batch", scatter_dimension=0, tiled=True)
 
     grad_rows, grad_final_gain = norm_back(grad_final, final_rows, final_scale)
@@ -1228,7 +1329,6 @@
     grad_rows, attn_second_done, ffn_first_done = tie(
         grad_rows, attn_second_done, ffn_first_done
     )
-    attn_first_done = over_batch(attn_first_sum)
 
     embed_grad = (grad_rows * root_scale).astype(bf16).T
     def row_at(index, vector):
@@ -1238,6 +1338,8 @@
     vectors = [gain_1a, gain_1f[0], gain_2a[0], gain_2f[0], grad_final_gain, *taps_first[:3], *taps_second[:3]]
     rows = sum(row_at(index, vector) for index, vector in enumerate(vectors))
     traded, rows = batch_trade(embed_grad.reshape(batch_count, depth, shard_rows), rows, 9)
+    traded, attn_first_sum = tie(traded, attn_first_sum)
+    attn_first_done = over_batch(attn_first_sum)
     gain_sums = jnp.sum(rows[:, :5], 0)
     holders = rows.reshape(2, 4, 16, D)[:, :, 5:11].reshape(2, 4, 2, 3, D)
     taps_sums = jnp.sum(lax.dynamic_index_in_dim(holders, me, 1, keepdims=False), 0)

time: 618 us -> 584 us (0.945)
  matrix products: 85.8 us -> 45.6 us
  local copies, waits for them, and re-layouts: 48.5 us -> 62.1 us
  Pallas kernels: 438 us -> 427 us
    dot_general x15 -> x13, matrix products: 85.8 us -> 45.6 us  [mm(): lax.dot_general(left, right, (((left_dim,), (right_dim,)), ((), ())), pre...]
    pallas_call x4, Pallas kernels: 57.4 us -> 43.5 us  [attention_call(): pl.pallas_call(body, out_shape=out_shape, in_specs=[pl.BlockSpec(memory_s...]
    unnamed x143 -> x244, local copies, waits for them, and re-layouts: 42 us -> 54 us
  transfers between devices with their start and end apart: 10 -> 10, of which waited for: 0 -> 1; matrix products, arithmetic and copies ran while one was open for 11% -> 13% of each run, Pallas kernels for 63% -> 63%
where the time goes in v4:
time: 584 us; the launch traced here: 578 us
  Pallas kernels  427 us (73%)
  local copies, waits for them, and re-layouts  62.1 us (11%)
  matrix products  45.6 us (8%)
  other arithmetic  24.3 us (4%)
  between operations  16.4 us (3%)
    pallas_call x17, Pallas kernels, comm_call(): pl.pallas_call(kernel, out_shape=shapes, in_specs=in_specs, out_specs=out...  350 us
    unnamed x244, local copies, waits for them, and re-layouts  54 us
    dot_general x13, matrix products, mm(): lax.dot_general(left, right, (((left_dim,), (right_dim,)), ((), ())), pre...  45.6 us
    pallas_call x4, Pallas kernels, attention_call(): pl.pallas_call(body, out_shape=out_shape, in_specs=[pl.BlockSpec(memory_s...  43.5 us
    pallas_call x1, Pallas kernels, spread(): pl.pallas_call(spread_kernel, grid=(vocab_rows // columns,), out_shape=ja...  19.3 us
    pallas_call x1, Pallas kernels, lookup(): pl.pallas_call(lookup_kernel, grid=(batches,), out_shape=jax.ShapeDtypeSt...  14.5 us
  transfers between devices with their start and end apart: 10, of which 1 were waited for; matrix products, arithmetic and copies ran while one was open for 13% of the time, Pallas kernels for 63%

profile of v4, /device:TPU:0, one launch (start us, length us, event | category | flops | bytes accessed | tf_op | source)
XLA Modules:
  0.0 577.7 jit_solution(15631726498552364989)
XLA Ops:
  13.8 1.3 convert_bitcast_fusion.table
  18.0 11.3 %shard_map.178 = (s32[4,16,128]{2,1,0:T(8,128)S(1)}, f32[4,8,768]{2,1,0:T(8,128)S(1)}) custom-call(s32[16,128]{1,0:T(8,128)S(1)} %reshape.291.refs_0_, f32[8,768]{1,0:T(8,128)S(1)} %pad_maximum_fusion.3.refs_1_), custom_call_target="tpu_custom_call" | custom-call | tf_op jit(solution)/shard_map/pallas_call | solution.py:116
  29.4 14.5 %shard_map.179 = bf16[8,4,192,256]{3,2,1,0:T(8,128)(2,1)S(1)} custom-call(s32[32,1,256]{2,1,0:T(1,128)S(1)} %bitcast.200, bf16[192,4096]{1,0:T(8,128)(2,1)S(1)} %copy-done), custom_call_target="tpu_custom_call" | custom-call | tf_op jit(solution)/shard_map/pallas_call | solution.py:1098
  43.9 17.5 %shard_map.180 = f32[768,256]{1,0:T(8,128)S(1)} custom-call(bf16[8,768,256]{2,1,0:T(8,128)(2,1)S(1)} %bitcast.170), custom_call_target="tpu_custom_call" | custom-call | tf_op jit(solution)/shard_map/pallas_call | solution.py:116
  61.5 19.5 %shard_map.181 = (bf16[4,192,256]{2,1,0:T(8,128)(2,1)S(1)}, f32[8,8,768]{2,1,0:T(8,128)S(1)}) custom-call(bf16[4,192,256]{2,1,0:T(8,128)(2,1)S(1)} %bitcast.182, f32[8,768]{1,0:T(8,128)S(1)} %reduce_sum.107.refs_1_), custom_call_target="tpu_custom_call" | custom-call | tf_op jit(solution)/shard_map/pallas_call | solution.py:116
  85.2 15.7 %shard_map.182 = (bf16[4,256,768]{2,1,0:T(8,128)(2,1)S(1)}, bf16[768,768]{1,0:T(8,128)(2,1)S(1)}) custom-call(bf16[256,768]{1,0:T(8,128)(2,1)S(1)} %get-tuple-element.190.refs_0_, bf16[768,768]{1,0:T(8,128)(2,1)S(1)} %copy-done.5), custom_call_target="tpu_custom_call" | custom-call | tf_op jit(solution)/shard_map/pallas_call | solution.py:116
  100.9 8.6 %shard_map.183 = (bf16[1024,768]{1,0:T(8,128)(2,1)S(1)}, bf16[1024,640]{1,0:T(8,128)(2,1)S(1)}, bf16[1024,640]{1,0:T(8,128)(2,1)S(1)}, bf16[1024,256]{1,0:T(8,128)(2,1)S(1)}, f32[1024,128]{1,0:T(8,128)S(1)}) custom-call(s32[1]{0:T(128)} %dynamic_slice.24.length, bf16[1024,768]{1,0:T(8,128)(2,1)S(1)} %bitcast.171, ...), custom_call_target="tpu_custom_call" | custom-call | tf_op jit(solution)/shard_map/pallas_call | solution.py:897
  115.6 1.9 copy-done.1
  117.5 1.6 copy-done.24
  119.0 29.2 %shard_map.184 = (bf16[4,256,768]{2,1,0:T(8,128)(2,1)S(1)}, f32[256,768]{1,0:T(8,128)S(1)}, bf16[768,1536]{1,0:T(8,128)(2,1)S(1)}) custom-call(bf16[4,256,768]{2,1,0:T(8,128)(2,1)S(1)} %bitcast.186, f32[256,768]{1,0:T(8,128)S(1)} %get-tuple-element.189.refs_1_, f32[1,768]{1,0:T(1,128)S(1)} %get-tuple-element.222.refs_2_, bf16[768,1536]{1,0:T(8,128)(2,1)S(1)} %copy-done.1), custom_call_target="tpu_custom_call" | custom-call | tf_op jit(solution)/shard_map/pallas_call | solution.py:116
  149.4 1.4 fusion.8
  150.8 1.4 convolution_convert_fusion.4
  153.0 25.6 %shard_map.185 = (bf16[4,256,768]{2,1,0:T(8,128)(2,1)S(1)}, f32[256,768]{1,0:T(8,128)S(1)}, bf16[768,768]{1,0:T(8,128)(2,1)S(1)}) custom-call(bf16[4,256,768]{2,1,0:T(8,128)(2,1)S(1)} %bitcast.178, f32[256,768]{1,0:T(8,128)S(1)} %get-tuple-element.90.refs_1_, f32[1,768]{1,0:T(1,128)S(1)} %get-tuple-element.221.refs_2_, bf16[768,768]{1,0:T(8,128)(2,1)S(1)} %copy-done.6), custom_call_target="tpu_custom_call" | custom-call | tf_op jit(solution)/shard_map/pallas_call | solution.py:116
  178.6 8.8 %shard_map.186 = (bf16[1024,768]{1,0:T(8,128)(2,1)S(1)}, bf16[1024,640]{1,0:T(8,128)(2,1)S(1)}, bf16[1024,640]{1,0:T(8,128)(2,1)S(1)}, bf16[1024,256]{1,0:T(8,128)(2,1)S(1)}, f32[1024,128]{1,0:T(8,128)S(1)}) custom-call(s32[1]{0:T(128)} %dynamic_slice.24.length, bf16[1024,768]{1,0:T(8,128)(2,1)S(1)} %bitcast.173, ...), custom_call_target="tpu_custom_call" | custom-call | tf_op jit(solution)/shard_map/pallas_call | solution.py:897
  187.5 23.7 %shard_map.187 = (bf16[4,256,768]{2,1,0:T(8,128)(2,1)S(1)}, f32[256,768]{1,0:T(8,128)S(1)}, bf16[768,1536]{1,0:T(8,128)(2,1)S(1)}) custom-call(bf16[4,256,768]{2,1,0:T(8,128)(2,1)S(1)} %bitcast.187, f32[256,768]{1,0:T(8,128)S(1)} %get-tuple-element.94.refs_1_, f32[1,768]{1,0:T(1,128)S(1)} %get-tuple-element.220.refs_2_, bf16[768,1536]{1,0:T(8,128)(2,1)S(1)} %copy-done.2), custom_call_target="tpu_custom_call" | custom-call | tf_op jit(solution)/shard_map/pallas_call | solution.py:116
  212.4 1.4 fusion.3
  213.8 1.4 convolution_convert_fusion.3
  215.6 16.7 %shard_map.188 = f32[256,768]{1,0:T(8,128)S(1)} custom-call(bf16[4,256,768]{2,1,0:T(8,128)(2,1)S(1)} %bitcast.180), custom_call_target="tpu_custom_call" | custom-call | tf_op jit(solution)/shard_map/pallas_call | solution.py:116
  233.4 2.8 copy-done.4
  236.2 22.7 %shard_map.189 = (bf16[8,256,768]{2,1,0:T(8,128)(2,1)S(1)}, bf16[8,256,768]{2,1,0:T(8,128)(2,1)S(1)}) custom-call(bf16[256,768]{1,0:T(8,128)(2,1)S(1)} %fusion.12.refs_0_, bf16[768,4096]{1,0:T(8,128)(2,1)S(1)} %copy-done.4, bf16[2048,4096]{1,0:T(8,128)(2,1)} %bitcast.207), custom_call_target="tpu_custom_call" | custom-call | tf_op jit(solution)/shard_map/pallas_call | solution.py:116
  259.3 21.7 %shard_map.190 = (f32[256,768]{1,0:T(8,128)S(1)}, bf16[768,4096]{1,0:T(8,128)(2,1)S(1)}) custom-call(bf16[8,256,768]{2,1,0:T(8,128)(2,1)S(1)} %get-tuple-element.99.refs_0_, bf16[2048,768]{1,0:T(8,128)(2,1)S(1)} %bitcast.176, bf16[2048,128]{1,0:T(8,128)(2,1)S(1)} %broadcast_in_dim.213.refs_2_, bf16[2048,4096]{1,0:T(8,128)(2,1)} %bitcast.208), custom_call_target="tpu_custom_call" | custom-call | tf_op jit(solution)/shard_map/pallas_call | solution.py:116
  281.0 2.7 copy-done.3
  285.6 2.2 fusion.16
  289.6 12.1 %shard_map.191 = bf16[4,256,768]{2,1,0:T(8,128)(2,1)S(1)} custom-call(bf16[256,768]{1,0:T(8,128)(2,1)S(1)} %get-tuple-element.183.refs_0_), custom_call_target="tpu_custom_call" | custom-call | tf_op jit(solution)/shard_map/pallas_call | solution.py:116
  301.6 3.3 multiply_convert_fusion.1
  305.0 1.4 convolution_convert_fusion.2
  306.4 1.5 convolution_convert_fusion.8
  308.3 1.5 convolution_convert_fusion.7
  309.8 23.3 %shard_map.192 = (bf16[4,256,768]{2,1,0:T(8,128)(2,1)S(1)}, f32[256,768]{1,0:T(8,128)S(1)}, f32[1,768]{1,0:T(1,128)S(1)}, bf16[4,96,768]{2,1,0:T(8,128)(2,1)S(1)...) custom-call(bf16[4,256,768]{2,1,0:T(8,128)(2,1)S(1)} %bitcast.185, ...), custom_call_target="tpu_custom_call" | custom-call | tf_op jit(solution)/shard_map/pallas_call | solution.py:116
  341.9 1.4 copy-done.27
  348.0 13.1 %shard_map.193 = (bf16[1024,768]{1,0:T(8,128)(2,1)S(1)}, bf16[768,768]{1,0:T(8,128)(2,1)S(1)}, f32[8,640]{1,0:T(8,128)S(1)}) custom-call(s32[1]{0:T(128)} %dynamic_slice.24.length, bf16[1024,768]{1,0:T(8,128)(2,1)S(1)} %bitcast.190, bf16[1024,768]{1,0:T(8,128)(2,1)S(1)} %bitcast.174, bf16[768,768]{1,0:T(8,128)(2,1)S(1)} %copy-done.10, ...), custom_call_target="tpu_custom_call" | custom-call | tf_op jit(solution)/shard_map/pallas_call | solution.py:897
  361.2 29.7 %shard_map.194 = (bf16[4,256,768]{2,1,0:T(8,128)(2,1)S(1)}, f32[256,768]{1,0:T(8,128)S(1)}, f32[1,768]{1,0:T(1,128)S(1)}, bf16[4,96,768]{2,1,0:T(8,128)(2,1)S(1)}, bf16[4,96,768]{2,1,0:T(8,128)(2,1)S(1)}) custom-call(bf16[4,256,768]{2,1,0:T(8,128)(2,1)S(1)} %bitcast.179, f32[256,768]{1,0:T(8,128)S(1)} %copy-done.14, f32[1,768]{1,0:T(1,128)S(1)} %copy-done.61, ...), custom_call_target="tpu_custom_call" | custom-call | tf_op jit(solution)/shard_map/pallas_call | solution.py:116
  393.7 3.8 multiply_convert_fusion
  398.7 1.5 convolution_convert_fusion.6
  400.3 4.6 convolution_convert_fusion.1
  404.9 2.5 convolution_convert_fusion.5
  407.4 1.4 copy-done.22
  411.2 23.1 %shard_map.195 = (bf16[4,256,768]{2,1,0:T(8,128)(2,1)S(1)}, f32[256,768]{1,0:T(8,128)S(1)}, f32[1,768]{1,0:T(1,128)S(1)}, bf16[4,96,768]{2,1,0:T(8,128)(2,1)S(1)...) custom-call(bf16[4,256,768]{2,1,0:T(8,128)(2,1)S(1)} %bitcast.184, ...), custom_call_target="tpu_custom_call" | custom-call | tf_op jit(solution)/shard_map/pallas_call | solution.py:116
  437.7 19.9 %convolution_convert_fusion = bf16[2048,4096]{1,0:T(8,128)(2,1)} fusion(bf16[2048,768]{1,0:T(8,128)(2,1)} %bitcast.177, bf16[768,4096]{1,0:T(8,128)(2,1)} %all-gather.8.cloned.1.call-done.refs_1_), kind=kOutput, calls=%fused_computation | convolution fusion | flops 12893290496 | bytes 26214400 | tf_op jit(solution)/shard_map/dot_general | solution.py:21
  458.6 1.4 copy-done.29
  460.0 1.3 copy-done.31
  461.3 1.3 copy-done.33
  463.7 13.0 %shard_map.196 = (bf16[1024,768]{1,0:T(8,128)(2,1)S(1)}, bf16[768,768]{1,0:T(8,128)(2,1)S(1)}, f32[8,640]{1,0:T(8,128)S(1)}) custom-call(s32[1]{0:T(128)} %dynamic_slice.24.length, bf16[1024,768]{1,0:T(8,128)(2,1)S(1)} %bitcast.191, bf16[1024,768]{1,0:T(8,128)(2,1)S(1)} %bitcast.172, bf16[768,768]{1,0:T(8,128)(2,1)S(1)} %copy-done.8, ...), custom_call_target="tpu_custom_call" | custom-call | tf_op jit(solution)/shard_map/pallas_call | solution.py:897
  481.8 18.7 %shard_map.197 = (f32[256,768]{1,0:T(8,128)S(1)}, bf16[4,96,768]{2,1,0:T(8,128)(2,1)S(1)}, bf16[4,96,768]{2,1,0:T(8,128)(2,1)S(1)}) custom-call(bf16[4,256,768]{2,1,0:T(8,128)(2,1)S(1)} %bitcast.183, bf16[4,2,96,768]{3,2,1,0:T(8,128)(2,1)S(1)} %bitcast.192), custom_call_target="tpu_custom_call" | custom-call | tf_op jit(solution)/shard_map/pallas_call | solution.py:116
  500.5 1.5 multiply_reduce_fusion
  503.8 20.1 %shard_map.198 = (bf16[4,192,256]{2,1,0:T(8,128)(2,1)S(1)}, f32[8,16,768]{2,1,0:T(8,128)S(1)}) custom-call(bf16[4,192,256]{2,1,0:T(8,128)(2,1)S(1)} %bitcast.181, f32[16,768]{1,0:T(8,128)S(1)} %select_add_fusion.refs_1_), custom_call_target="tpu_custom_call" | custom-call | tf_op jit(solution)/shard_map/pallas_call | solution.py:116
  524.7 19.3 %shard_map.199 = (bf16[8,768,256]{2,1,0:T(8,128)(2,1)S(1)}, f32[4,8,768]{2,1,0:T(8,128)S(1)}) custom-call(bf16[768,256]{1,0:T(8,128)(2,1)S(1)} %bitcast.198, f32[8,768]{1,0:T(8,128)S(1)} %pad_maximum_fusion.4.refs_1_), custom_call_target="tpu_custom_call" | custom-call | tf_op jit(solution)/shard_map/pallas_call | solution.py:116
  544.0 19.3 %shard_map.200 = f32[192,4096]{1,0:T(8,128)} custom-call(s32[32,256]{1,0:T(8,128)S(1)} %copy-done.57, bf16[8,4,192,256]{3,2,1,0:T(8,128)(2,1)S(1)} %bitcast.175, bf16[192,4096]{1,0:T(8,128)(2,1)S(1)} %copy-done.25), custom_call_target="tpu_custom_call" | custom-call | tf_op jit(solution)/shard_map/pallas_call | solution.py:1153
  (367 shorter events, 67.7 us)
Async XLA Ops:
  7.2 76.3 %all-gather.4.cloned.1.call-start = ((), (), s32[]{:S(2)}) async-start(), calls=%async_computation.5 | async-start | bytes 1474560 | tf_op jit(solution)/shard_map/all_gather | solution.py:1219
  10.4 105.1 %all-gather.6.cloned.1.call-start = ((), (), s32[]{:S(2)}) async-start(), calls=%async_computation.6 | async-start | bytes 2949120 | tf_op jit(solution)/shard_map/all_gather | solution.py:1220
  13.7 219.7 %all-gather.8.cloned.1.call-start = ((), (), s32[]{:S(2)}) async-start(), calls=%async_computation.7 | async-start | bytes 7864320 | tf_op jit(solution)/shard_map/all_gather | solution.py:1221
  15.2 392.2 %reduce-scatter.6.cloned.1.call-start = ((), (), s32[]{:S(2)}) async-start(), calls=%async_computation.8 | async-start | bytes 7864320 | tf_op jit(solution)/shard_map/reduce_scatter | solution.py:1294
  29.3 14.5 %copy-start.55 = (s32[4,16,128]{2,1,0:T(8,128)}, s32[4,16,128]{2,1,0:T(8,128)S(1)}, u32[]{:S(2)}) copy-start(s32[4,16,128]{2,1,0:T(8,128)S(1)} %broadcast_subtract_fusion) | copy-start | bytes 98308
  81.0 97.6 %copy-start.58 = (f32[3,640]{1,0:T(4,128)}, f32[3,640]{1,0:T(4,128)S(1)}, u32[]{:S(2)}) copy-start(f32[3,640]{1,0:T(4,128)S(1)} %slice.278.taps) | copy-start | bytes 23044
  83.4 69.2 %copy-start.60 = (f32[1,768]{1,0:T(1,128)}, f32[1,768]{1,0:T(1,128)S(1)}, u32[]{:S(2)}) copy-start(f32[1,768]{1,0:T(1,128)S(1)} %get-tuple-element.221.refs_2_) | copy-start | bytes 9220
  83.4 104.1 %copy-start.62 = (f32[1,768]{1,0:T(1,128)}, f32[1,768]{1,0:T(1,128)S(1)}, u32[]{:S(2)}) copy-start(f32[1,768]{1,0:T(1,128)S(1)} %get-tuple-element.220.refs_2_) | copy-start | bytes 9220
  178.6 32.6 %copy-start.9 = (bf16[768,768]{1,0:T(8,128)(2,1)}, bf16[768,768]{1,0:T(8,128)(2,1)S(1)}, u32[]{:S(2)}) copy-start(bf16[768,768]{1,0:T(8,128)(2,1)S(1)} %get-tuple-element.92.weight) | copy-start | bytes 3538948
  178.6 32.6 %copy-start.13 = (f32[256,768]{1,0:T(8,128)}, f32[256,768]{1,0:T(8,128)S(1)}, u32[]{:S(2)}) copy-start(f32[256,768]{1,0:T(8,128)S(1)} %get-tuple-element.94.refs_1_) | copy-start | bytes 2359300
  187.4 23.8 %copy-start.34 = (bf16[1024,640]{1,0:T(8,128)(2,1)}, bf16[1024,640]{1,0:T(8,128)(2,1)S(1)}, u32[]{:S(2)}) copy-start(bf16[1024,640]{1,0:T(8,128)(2,1)S(1)} %get-tuple-element.102.mixed) | copy-start | bytes 3932164
  187.4 23.8 %copy-start.36 = (bf16[1024,640]{1,0:T(8,128)(2,1)}, bf16[1024,640]{1,0:T(8,128)(2,1)S(1)}, u32[]{:S(2)}) copy-start(bf16[1024,640]{1,0:T(8,128)(2,1)S(1)} %get-tuple-element.103.projected) | copy-start | bytes 3932164
  187.4 23.8 %copy-start.51 = (bf16[1024,256]{1,0:T(8,128)(2,1)}, bf16[1024,256]{1,0:T(8,128)(2,1)S(1)}, u32[]{:S(2)}) copy-start(bf16[1024,256]{1,0:T(8,128)(2,1)S(1)} %get-tuple-element.104.context) | copy-start | bytes 1572868
  187.5 23.8 %copy-start.53 = (f32[1024,128]{1,0:T(8,128)}, f32[1024,128]{1,0:T(8,128)S(1)}, u32[]{:S(2)}) copy-start(f32[1024,128]{1,0:T(8,128)S(1)} %get-tuple-element.105.totals) | copy-start | bytes 1572868
  211.2 21.0 %copy-start.15 = (f32[256,768]{1,0:T(8,128)}, f32[256,768]{1,0:T(8,128)S(1)}, u32[]{:S(2)}) copy-start(f32[256,768]{1,0:T(8,128)S(1)} %get-tuple-element.95.refs_1_) | copy-start | bytes 2359300
  236.2 22.7 %copy-start.92 = (bf16[1,8,2,128]{3,1,2,0:T(8,128)(2,1)S(1)}, bf16[1,8,2,128]{3,1,2,0:T(8,128)(2,1)}, u32[]{:S(2)}) copy-start(bf16[1,8,2,128]{3,1,2,0:T(8,128)(2,1)} %copy.38) | copy-start | bytes 12292
  258.9 22.1 %copy-start.19 = (bf16[8,256,768]{2,1,0:T(8,128)(2,1)}, bf16[8,256,768]{2,1,0:T(8,128)(2,1)S(1)}, u32[]{:S(2)}) copy-start(bf16[8,256,768]{2,1,0:T(8,128)(2,1)S(1)} %get-tuple-element.98) | copy-start | bytes 9437188
  284.6 194.3 %reduce-scatter.8.cloned.1.call-start = ((), (), s32[]{:S(2)}) async-start(), calls=%async_computation.9 | async-start | bytes 1474560 | tf_op jit(solution)/shard_map/reduce_scatter | solution.py:1177
  336.4 167.1 %reduce-scatter.10.cloned.1.call-start = ((), (), s32[]{:S(2)}) async-start(), calls=%async_computation.10 | async-start | bytes 737280 | tf_op jit(solution)/shard_map/reduce_scatter | solution.py:1177
  361.1 29.8 %copy-start.70 = (f32[8,640]{1,0:T(8,128)}, f32[8,640]{1,0:T(8,128)S(1)}, u32[]{:S(2)}) copy-start(f32[8,640]{1,0:T(8,128)S(1)} %get-tuple-element.138) | copy-start | bytes 61444
  400.2 103.3 %reduce-scatter.12.cloned.1.call-start = ((), (), s32[]{:S(2)}) async-start(), calls=%async_computation.11 | async-start | bytes 1474560 | tf_op jit(solution)/shard_map/reduce_scatter | solution.py:1177
  437.6 20.0 %copy-start.67 = (f32[1,768]{1,0:T(1,128)S(1)}, f32[1,768]{1,0:T(1,128)}, u32[]{:S(2)}) copy-start(f32[1,768]{1,0:T(1,128)} %copy-done.66) | copy-start | bytes 9220
  437.6 20.1 %copy-start.65 = (f32[1,768]{1,0:T(1,128)S(1)}, f32[1,768]{1,0:T(1,128)}, u32[]{:S(2)}) copy-start(f32[1,768]{1,0:T(1,128)} %copy-done.64) | copy-start | bytes 9220
  437.6 21.0 %copy-start.69 = (f32[1,768]{1,0:T(1,128)S(1)}, f32[1,768]{1,0:T(1,128)}, u32[]{:S(2)}) copy-start(f32[1,768]{1,0:T(1,128)} %copy-done.68) | copy-start | bytes 9220
  437.6 21.0 %copy-start.8 = (bf16[768,768]{1,0:T(8,128)(2,1)S(1)}, bf16[768,768]{1,0:T(8,128)(2,1)}, u32[]{:S(2)}) copy-start(bf16[768,768]{1,0:T(8,128)(2,1)} %copy-done.7) | copy-start | bytes 3538948
  437.6 21.0 %copy-start.48 = (bf16[1024,256]{1,0:T(8,128)(2,1)S(1)}, bf16[1024,256]{1,0:T(8,128)(2,1)}, u32[]{:S(2)}) copy-start(bf16[1024,256]{1,0:T(8,128)(2,1)} %copy-done.47) | copy-start | bytes 1572868
  437.6 127.0 %reduce-scatter.14.cloned.1.call-start = ((), (), s32[]{:S(2)}) async-start(), calls=%async_computation.12 | async-start | bytes 737280 | tf_op jit(solution)/shard_map/reduce_scatter | solution.py:1177
  478.9 21.6 %copy-start.89 = (f32[768]{0:T(1024)S(1)}, f32[768]{0:T(1024)}, u32[]{:S(2)}) copy-start(f32[768]{0:T(1024)} %copy-done.88) | copy-start | bytes 9220
  478.9 21.6 %copy-start.96 = (f32[256]{0:T(256)S(1)}, f32[256]{0:T(256)}, u32[]{:S(2)}) copy-start(f32[256]{0:T(256)} %get-tuple-element.234) | copy-start | bytes 3076
  481.7 20.4 %copy-start.98 = (f32[256]{0:T(256)S(1)}, f32[256]{0:T(256)}, u32[]{:S(2)}) copy-start(f32[256]{0:T(256)} %copy-done.97) | copy-start | bytes 3076
  481.7 20.4 %copy-start.91 = (f32[768]{0:T(1024)S(1)}, f32[768]{0:T(1024)}, u32[]{:S(2)}) copy-start(f32[768]{0:T(1024)} %get-tuple-element.173) | copy-start | bytes 9220
  481.7 20.4 %copy-start.101 = (pred[16]{0:T(512)(128)(4,1)S(1)}, pred[16]{0:T(512)(128)(4,1)}, u32[]{:S(2)}) copy-start(pred[16]{0:T(512)(128)(4,1)} %iota_compare_fusion.10) | copy-start | bytes 52
  481.7 20.4 %copy-start.102 = (pred[16]{0:T(512)(128)(4,1)S(1)}, pred[16]{0:T(512)(128)(4,1)}, u32[]{:S(2)}) copy-start(pred[16]{0:T(512)(128)(4,1)} %get-tuple-element.248) | copy-start | bytes 52
  481.7 20.4 %copy-start.103 = (pred[16]{0:T(512)(128)(4,1)S(1)}, pred[16]{0:T(512)(128)(4,1)}, u32[]{:S(2)}) copy-start(pred[16]{0:T(512)(128)(4,1)} %get-tuple-element.249) | copy-start | bytes 52
  481.7 20.4 %copy-start.104 = (pred[16]{0:T(512)(128)(4,1)S(1)}, pred[16]{0:T(512)(128)(4,1)}, u32[]{:S(2)}) copy-start(pred[16]{0:T(512)(128)(4,1)} %get-tuple-element.246) | copy-start | bytes 52
  481.7 20.4 %copy-start.105 = (pred[16]{0:T(512)(128)(4,1)S(1)}, pred[16]{0:T(512)(128)(4,1)}, u32[]{:S(2)}) copy-start(pred[16]{0:T(512)(128)(4,1)} %get-tuple-element.247) | copy-start | bytes 52
  481.7 20.4 %copy-start.106 = (pred[16]{0:T(512)(128)(4,1)S(1)}, pred[16]{0:T(512)(128)(4,1)}, u32[]{:S(2)}) copy-start(pred[16]{0:T(512)(128)(4,1)} %get-tuple-element.244) | copy-start | bytes 52
  481.7 20.4 %copy-start.107 = (pred[16]{0:T(512)(128)(4,1)S(1)}, pred[16]{0:T(512)(128)(4,1)}, u32[]{:S(2)}) copy-start(pred[16]{0:T(512)(128)(4,1)} %get-tuple-element.245) | copy-start | bytes 52
  481.7 20.4 %copy-start.108 = (pred[16]{0:T(512)(128)(4,1)S(1)}, pred[16]{0:T(512)(128)(4,1)}, u32[]{:S(2)}) copy-start(pred[16]{0:T(512)(128)(4,1)} %get-tuple-element.242) | copy-start | bytes 52
  481.7 20.4 %copy-start.109 = (pred[16]{0:T(512)(128)(4,1)S(1)}, pred[16]{0:T(512)(128)(4,1)}, u32[]{:S(2)}) copy-start(pred[16]{0:T(512)(128)(4,1)} %get-tuple-element.243) | copy-start | bytes 52
  481.7 20.4 %copy-start.110 = (pred[16]{0:T(512)(128)(4,1)S(1)}, pred[16]{0:T(512)(128)(4,1)}, u32[]{:S(2)}) copy-start(pred[16]{0:T(512)(128)(4,1)} %get-tuple-element.240) | copy-start | bytes 52
  481.8 20.4 %copy-start.111 = (pred[16]{0:T(512)(128)(4,1)S(1)}, pred[16]{0:T(512)(128)(4,1)}, u32[]{:S(2)}) copy-start(pred[16]{0:T(512)(128)(4,1)} %get-tuple-element.241) | copy-start | bytes 52
  503.5 20.5 %copy-start.85 = (bf16[1,96,1536]{2,1,0:T(8,128)(2,1)S(1)}, bf16[1,96,1536]{2,1,0:T(8,128)(2,1)}, u32[]{:S(2)}) copy-start(bf16[1,96,1536]{2,1,0:T(8,128)(2,1)} %reduce-scatter.8.cloned.1.call-done) | copy-start | bytes 884740
  503.6 20.4 %copy-start.86 = (bf16[1,96,1536]{2,1,0:T(8,128)(2,1)S(1)}, bf16[1,96,1536]{2,1,0:T(8,128)(2,1)}, u32[]{:S(2)}) copy-start(bf16[1,96,1536]{2,1,0:T(8,128)(2,1)} %reduce-scatter.12.cloned.1.call-done) | copy-start | bytes 884740
  523.9 20.1 %copy-start.25 = (bf16[192,4096]{1,0:T(8,128)(2,1)S(1)}, bf16[192,4096]{1,0:T(8,128)(2,1)}, u32[]{:S(2)}) copy-start(bf16[192,4096]{1,0:T(8,128)(2,1)} %reduce-scatter.6.cloned.1.call-done.base) | copy-start | bytes 4718596
  523.9 20.1 %copy-start.57 = (s32[32,256]{1,0:T(8,128)S(1)}, s32[32,256]{1,0:T(8,128)}, u32[]{:S(2)}) copy-start(s32[32,256]{1,0:T(8,128)} %sub.41.ids) | copy-start | bytes 98308
  524.0 39.3 %collective-permute-start.1 = (bf16[96,1536]{1,0:T(8,128)(2,1)S(1)}, bf16[96,1536]{1,0:T(8,128)(2,1)S(1)}, u32[]{:S(2)}, u32[]{:S(2)}) collective-permute-start(bf16[96,1536]{1,0:T(8,128)(2,1)S(1)} %get-tuple-element.192), channel_id=1, source_target_pairs={{0,16},{16,0},{1,17},{17,1},{2,18},{18,2},{3,19},{19,3},{4,20},{20... | collective-permute-start | bytes 884744 | tf_op jit(solution)/shard_map/ppermute | solution.py:1362
  567.2 1.4 collective-permute-start
  (81 other events, 201.7 us)
Sparse Core Ops, SparseCore 0:
  10.6 36.1 all-gather.3
  48.9 57.5 all-gather.5
  108.6 114.1 all-gather.7
  284.8 117.0 reduce-scatter.5
  404.0 29.6 reduce-scatter.7
  436.4 20.7 reduce-scatter.9
  459.5 27.4 reduce-scatter.11
  524.1 21.8 reduce-scatter.13

commit v5 on v4

--- a/solution.py
+++ b/solution.py
@@ -32,7 +32,7 @@
     scaled = grad * gain
     inner = jnp.mean(scaled * rows, axis=-1, keepdims=True)
     grad_rows = factor * scaled - rows * (factor * factor * factor * inner)
-    return grad_rows, jnp.sum(grad * rows * factor, axis=0)
+    return grad_rows, jnp.sum(grad * rows * factor, axis=0, keepdims=True)
 
 
 MESH = pl.DeviceIdType.MESH
@@ -63,7 +63,7 @@
 
 
 def comm_call(
-    body, out_shape, scratch, collective_id, *operands, cargo=None, streamed=(), room=16
+    body, out_shape, scratch, collective_id, *operands, cargo=None, streamed=(), room=6
 ):
     shapes = list(out_shape) if isinstance(out_shape, (list, tuple)) else [out_shape]
     in_specs = [pl.BlockSpec(memory_space=pltpu.VMEM)] * len(operands)
@@ -74,17 +74,20 @@
     count_in, count_out = len(operands), len(shapes)
     loads = 0
     if cargo is not None:
-        kind, layer, arrays = cargo
-        loads = len(arrays)
+        kind, items = cargo
+        loads = len(items)
+        arrays = []
+        landing = []
+        for layer, array, lead, width in items:
+            if not any(array is one for one in arrays):
+                arrays.append(array)
+            if kind == "out":
+                landing.append(jax.ShapeDtypeStruct((array.shape[0], width), array.dtype))
+            else:
+                batches, _, rows, _ = array.shape
+                landing += [jax.ShapeDtypeStruct((batches, rows, width), array.dtype)] * 2
         operands = operands + tuple(arrays)
-        in_specs += [pl.BlockSpec(memory_space=pl.ANY)] * loads
-        landing = []
-        for array in arrays:
-            if kind == "out":
-                landing.append(jax.ShapeDtypeStruct(array.shape, array.dtype))
-            else:
-                batches, _, rows, width = array.shape
-                landing += [jax.ShapeDtypeStruct((batches, rows, width), array.dtype)] * 2
+        in_specs += [pl.BlockSpec(memory_space=pl.ANY)] * len(arrays)
         shapes += landing
         out_specs += [pl.BlockSpec(memory_space=pl.ANY)] * len(landing)
         scratch += [pltpu.SemaphoreType.DMA((loads, 3))] * 2
@@ -97,19 +100,18 @@
             return
         send, recv = rest[-2:]
         made = Outward if kind == "out" else Inward
-        lands = len(landing) // loads
+        lands_each = len(landing) // loads
 
         def load():
-            return [
-                made(
-                    layer,
-                    ins[count_in + at],
-                    outs[count_out + lands * at : count_out + lands * (at + 1)],
-                    send.at[at],
-                    recv.at[at],
-                )
-                for at in range(loads)
-            ]
+            loaded = []
+            for at, (layer, array, lead, width) in enumerate(items):
+                source = ins[count_in + [array is one for one in arrays].index(True)]
+                if width < array.shape[-1]:
+                    cut = (slice(None),) * (len(array.shape) - 1) + (pl.ds(lead, width),)
+                    source = source.at[cut]
+                lands = outs[count_out + lands_each * at : count_out + lands_each * (at + 1)]
+                loaded.append(made(layer, source, lands, send.at[at], recv.at[at]))
+            return loaded
 
         body(*ins[:count_in], *outs[:count_out], *rest[:-2], load=load)
 
@@ -568,7 +570,7 @@
         rows,
         table,
         streamed=[grads],
-        room=28,
+        room=40,
     )
 
 
@@ -701,7 +703,7 @@
         rows,
         valid,
         streamed=[grads],
-        room=40,
+        room=42,
     )
 
 
@@ -764,9 +766,21 @@
     )
 
 
-def batch_trade_kernel(count, parts, few, out, few_out, send, recv, few_send, few_recv):
+def batch_trade_kernel(count, leads, parts, *refs, load=None):
+    pieces, refs = refs[: len(leads)], refs[len(leads) :]
+    out, few_out, few, send, recv, few_send, few_recv = refs
+    few[...] = jnp.zeros(few.shape, few.dtype)
+    for lead, piece in zip(leads, pieces):
+        few[lead : lead + piece.shape[0], : piece.shape[1]] = piece[...]
     me = lax.axis_index("batch")
-    greet(plane_peers() + batch_peers(count))
+    core, y, _, tensor = place()
+    peers = plane_peers() + batch_peers(count)
+    if load is not None:
+        peers.append({"section": 1 - core, "tensor": tensor + 2 - 4 * y})
+    greet(peers)
+    cargo = load() if load is not None else []
+    for one in cargo:
+        one.start()
     copies = []
     for index, peer in enumerate(batch_peers(count)):
         copies.append(
@@ -777,25 +791,29 @@
     plane_exchange(few, few_out, few_send, few_recv)
     for copy in copies:
         copy.wait()
-
-
-def batch_trade(parts, few, collective_id):
+    for one in cargo:
+        one.wait()
+
+
+def batch_trade(parts, pieces, rows, collective_id, cargo=None):
     count = parts.shape[0]
     return comm_call(
-        functools.partial(batch_trade_kernel, count),
+        functools.partial(batch_trade_kernel, count, [lead for lead, _ in pieces]),
         [
             jax.ShapeDtypeStruct(parts.shape, parts.dtype),
-            jax.ShapeDtypeStruct((8,) + few.shape, few.dtype),
+            jax.ShapeDtypeStruct((8, rows, D), f32),
         ],
-        [pltpu.SemaphoreType.DMA((count - 1,))] * 2 + [pltpu.SemaphoreType.DMA((13,))] * 2,
+        [pltpu.VMEM((rows, D), f32)]
+        + [pltpu.SemaphoreType.DMA((count - 1,))] * 2
+        + [pltpu.SemaphoreType.DMA((13,))] * 2,
         collective_id,
         parts,
-        few,
+        *[piece for _, piece in pieces],
+        cargo=cargo,
     )
 
 
 ROWS = 256
-
 
 PACKED = ((0, 0), (0, 1), (1, 0), (1, 1), (2, 0), (2, 1), (0, 2), (1, 2), (2, 2))
 
@@ -892,7 +910,7 @@
         partial[lead:reach] = mm(joined, weight[:, 512:768], 1, 1).astype(bf16)
 
 
-def attention_call(body, out_shape, scratch, length, *operands):
+def attention_call(body, out_shape, scratch, room, length, *operands):
     whole = pl.BlockSpec(memory_space=pltpu.VMEM)
     return pl.pallas_call(
         body,
@@ -900,7 +918,7 @@
         in_specs=[pl.BlockSpec(memory_space=pltpu.SMEM)] + [whole] * len(operands),
         out_specs=[whole] * len(out_shape),
         scratch_shapes=scratch,
-        compiler_params=pltpu.CompilerParams(vmem_limit_bytes=32 << 20),
+        compiler_params=pltpu.CompilerParams(vmem_limit_bytes=room << 20),
     )(length.reshape(1), *operands)
 
 
@@ -921,6 +939,7 @@
             pltpu.VMEM((2, total, 128), bf16),
             pltpu.VMEM((2, total, 128), bf16),
         ],
+        14,
         length,
         x,
         weight,
@@ -1047,6 +1066,7 @@
             pltpu.VMEM((total, 640), bf16),
             pltpu.VMEM((2, D, total), bf16),
         ],
+        20,
         length,
         grads,
         x,
@@ -1059,23 +1079,83 @@
     )
 
 
-def ffn_forward(gathered, weights):
-    up_mat, down_turned = weights
-    hidden = mm(gathered, up_mat, 1, 0)
-    active = jnp.square(jnp.maximum(hidden, 0.0)).astype(bf16)
-    partial = mm(active, down_turned, 1, 1).astype(bf16).reshape(4, -1, D)
-    return partial, (gathered, hidden, active)
-
-
-def ffn_backward(grad_rows, weights, kept):
-    up_mat, down_turned = weights
-    gathered, hidden, active = kept
-    grad_active = mm(grad_rows, down_turned, 1, 0)
-    grad_hidden = (grad_active * 2.0 * jnp.maximum(hidden, 0.0)).astype(bf16)
-    partial = mm(grad_hidden, up_mat, 1, 1).astype(bf16).reshape(4, -1, D)
-    grad_down = mm(grad_rows, active, 0, 0)
-    grad_up = mm(gathered, grad_hidden, 0, 0)
-    return partial, [grad_up.astype(bf16), grad_down.astype(bf16)]
+def ffn_forward_kernel(x, up, *refs):
+    downs, partial = refs[:-1], refs[-1]
+    for lead in range(0, x.shape[0], ROWS):
+        hidden = jnp.dot(x[lead : lead + ROWS], up[...], preferred_element_type=f32)
+        active = jnp.square(jnp.maximum(hidden, 0.0)).astype(bf16)
+        total, first = 0.0, 0
+        for down in downs:
+            width = down.shape[1]
+            total += mm(active[:, first : first + width], down[...], 1, 1)
+            first += width
+        partial[lead : lead + ROWS] = total.astype(bf16)
+
+
+def ffn_backward_kernel(grads, x, up, *refs):
+    downs = refs[:-6]
+    partial, up_grad, down_grad, hidden_grad, active, turned = refs[-6:]
+    for lead in range(0, x.shape[0], ROWS):
+        rows = pl.ds(lead, ROWS)
+        hidden = jnp.dot(x[rows], up[...], preferred_element_type=f32)
+        positive = jnp.maximum(hidden, 0.0)
+        active[rows] = jnp.square(positive).astype(bf16)
+        back = [jnp.dot(grads[rows], down[...], preferred_element_type=f32) for down in downs]
+        back = back[0] if len(back) == 1 else jnp.concatenate(back, 1)
+        back = (back * 2.0 * positive).astype(bf16)
+        hidden_grad[rows] = back
+        partial[rows] = mm(back, up[...], 1, 1).astype(bf16)
+    turned[0] = x[...].T
+    turned[1] = grads[...].T
+    for lead in range(0, D, ROWS):
+        rows = pl.ds(lead, ROWS)
+        up_grad[rows] = jnp.dot(
+            turned[0, rows], hidden_grad[...], preferred_element_type=f32
+        ).astype(bf16)
+        down_grad[rows] = jnp.dot(
+            turned[1, rows], active[...], preferred_element_type=f32
+        ).astype(bf16)
+
+
+def local_call(body, out_shape, scratch, *operands):
+    whole = pl.BlockSpec(memory_space=pltpu.VMEM)
+    return pl.pallas_call(
+        body,
+        out_shape=out_shape,
+        in_specs=[whole] * len(operands),
+        out_specs=[whole] * len(out_shape),
+        scratch_shapes=scratch,
+        compiler_params=pltpu.CompilerParams(vmem_limit_bytes=14 << 20),
+    )(*operands)
+
+
+def ffn_forward(x, weights):
+    up, downs = weights
+    (partial,) = local_call(
+        ffn_forward_kernel, [jax.ShapeDtypeStruct(x.shape, bf16)], [], x, up, *downs
+    )
+    return partial
+
+
+def ffn_backward(grads, weights, x):
+    up, downs = weights
+    return local_call(
+        ffn_backward_kernel,
+        [
+            jax.ShapeDtypeStruct(x.shape, bf16),
+            jax.ShapeDtypeStruct(up.shape, bf16),
+            jax.ShapeDtypeStruct(up.shape, bf16),
+        ],
+        [
+            pltpu.VMEM((x.shape[0], up.shape[1]), bf16),
+            pltpu.VMEM((x.shape[0], up.shape[1]), bf16),
+            pltpu.VMEM((2, D, x.shape[0]), bf16),
+        ],
+        grads,
+        x,
+        up,
+        *downs,
+    )
 
 
 LOOK = 512
@@ -1239,46 +1319,60 @@
     local_ids = all_ids.reshape(batch_count, sequences * 4, 1, shard_rows) - owner_start
     picked = lookup(table_own, local_ids)
     total = plane_reduce(picked.reshape(8, D, shard_rows), 3).astype(bf16)
-    embedded, small = batch_trade(total.reshape(batch_count, depth, shard_rows), small, 8)
+    embedded, small = batch_trade(
+        total.reshape(batch_count, depth, shard_rows), [(0, small)], 16, 8
+    )
     gains_all = jnp.sum(small[:, :5], 0)
     final_scale = gains_all[4]
     taps_here = [
         lax.dynamic_index_in_dim(
             small, 4 * (quarter // 2) + 2 * layer + quarter % 2, 0, keepdims=False
-        )[5:, :640]
+        )[5:8, :640]
         for layer in range(section_count)
     ]
     embedded = embedded.reshape(D, shard_rows).T
 
-    def ffn_weights(block):
-        return block[:, :hidden_width], block[:, hidden_width:]
-
+    part = hidden_width // 2
     first_rows = embedded.astype(f32) * root_scale
     normed = (first_rows * norm_factor(first_rows) * gains_all[0]).astype(bf16)
-    gathered, attn_first = group_gather(normed, 1, cargo=("out", 0, [attn_all]))
-    partial, attn_kept_first = attention_forward(
-        gathered.reshape(-1, D), length, attn_first, taps_here[0]
-    )
-    gathered, first_middle, block = turn(
-        partial, first_rows, gains_all[1], 20, False, cargo=("out", 0, [ffn_all])
-    )
-    ffn_first = ffn_weights(block)
-    partial, ffn_kept_first = ffn_forward(gathered.reshape(-1, D), ffn_first)
-    gathered, second_rows, attn_second = turn(
-        partial, first_middle, gains_all[2], 21, True, cargo=("out", 1, [attn_all])
+    gathered, attn_first = group_gather(normed, 1, cargo=("out", [(0, attn_all, 0, D)]))
+    partial, attn_kept_first = attention_forward(gathered.reshape(-1, D), length, attn_first, taps_here[0])
+    gathered, first_middle, up, down = turn(
+        partial,
+        first_rows,
+        gains_all[1],
+        20,
+        False,
+        cargo=("out", [(0, ffn_all, 0, hidden_width), (0, ffn_all, hidden_width, hidden_width)]),
+    )
+    ffn_first = (up, [down])
+    ffn_kept_first = gathered.reshape(-1, D)
+    partial = ffn_forward(ffn_kept_first, ffn_first)
+    gathered, second_rows, attn_second, down_one = turn(
+        partial,
+        first_middle,
+        gains_all[2],
+        21,
+        True,
+        cargo=("out", [(1, attn_all, 0, D), (1, ffn_all, hidden_width, part)]),
     )
     partial, attn_kept_second = attention_forward(
         gathered.reshape(-1, D), length, attn_second, taps_here[1]
     )
-    gathered, second_middle, block = turn(
-        partial, second_rows, gains_all[3], 24, False, cargo=("out", 1, [ffn_all])
-    )
-    ffn_second = ffn_weights(block)
-    partial, ffn_kept_second = ffn_forward(gathered.reshape(-1, D), ffn_second)
+    gathered, second_middle, up, down_two = turn(
+        partial,
+        second_rows,
+        gains_all[3],
+        24,
+        False,
+        cargo=("out", [(1, ffn_all, 0, hidden_width), (1, ffn_all, hidden_width + part, part)]),
+    )
+    ffn_second = (up, [down_one, down_two])
+    ffn_kept_second = gathered.reshape(-1, D)
+    partial = ffn_forward(ffn_kept_second, ffn_second)
 
     def halves(blob):
-        blob = blob if isinstance(blob, list) else [blob]
-        return [one.reshape(batch_count, 2, depth // 2, one.shape[1]) for one in blob]
+        return blob.reshape(batch_count, 2, depth // 2, blob.shape[1])
 
     final_rows = (second_middle + group_reduce(partial, 2)).astype(bf16).astype(f32)
     normed_final = (final_rows * norm_factor(final_rows) * final_scale).astype(bf16)
@@ -1295,58 +1389,72 @@
 
     grad_rows, grad_final_gain = norm_back(grad_final, final_rows, final_scale)
     gathered = group_gather(grad_rows.astype(bf16), 13).reshape(-1, D)
-    partial, blob = ffn_backward(gathered, ffn_second, ffn_kept_second)
-    gathered, grad_rows, gain_2f, *landed = turn(
-        partial, second_middle, gains_all[3], 22, False, passed=grad_rows,
-        cargo=("in", 1, halves(blob)),
-    )
-    ffn_second_sum = summed(landed)
+    partial, up, down = ffn_backward(gathered, ffn_second, ffn_kept_second)
+    up, down = halves(up), halves(down)
+    gathered, grad_rows, gain_2f, *landed_second = turn(
+        partial,
+        second_middle,
+        gains_all[3],
+        22,
+        False,
+        passed=grad_rows,
+        cargo=("in", [(1, up, 0, hidden_width), (1, down, 0, part)]),
+    )
     partial, blob, taps_second = attention_backward(
         gathered.reshape(-1, D), length, attn_second, taps_here[1], attn_kept_second
     )
     gathered, grad_rows, gain_2a, *landed = turn(
-        partial, second_rows, gains_all[2], 23, True, passed=grad_rows,
-        cargo=("in", 1, halves(blob)),
-    )
-    attn_second_sum = summed(landed)
-    partial, blob = ffn_backward(gathered.reshape(-1, D), ffn_first, ffn_kept_first)
-    partial, head_done = tie(partial, head_done)
-    gathered, grad_rows, gain_1f, *landed = turn(
-        partial, first_middle, gains_all[1], 25, False, passed=grad_rows,
-        cargo=("in", 0, halves(blob)),
-    )
-    ffn_first_sum = summed(landed)
+        partial,
+        second_rows,
+        gains_all[2],
+        23,
+        True,
+        passed=grad_rows,
+        cargo=("in", [(1, down, part, part), (1, halves(blob), 0, D)]),
+    )
+    second_sum = summed(landed_second + landed)
+    partial, up, down = ffn_backward(gathered.reshape(-1, D), ffn_first, ffn_kept_first)
+    up, down = halves(up), halves(down)
+    gathered, grad_rows, gain_1f, *landed_first = turn(
+        partial,
+        first_middle,
+        gains_all[1],
+        25,
+        False,
+        passed=grad_rows,
+        cargo=("in", [(0, up, 0, hidden_width), (0, down, 0, part)]),
+    )
+    taps_again, second_sum, head_done, gain_1f = tie(
+        taps_here[0], second_sum, head_done, gain_1f
+    )
     partial, blob, taps_first = attention_backward(
-        gathered.reshape(-1, D), length, attn_first, taps_here[0], attn_kept_first
-    )
-    ffn_second_done = over_batch(ffn_second_sum)
-    partial, ffn_second_done = tie(partial, ffn_second_done)
-    attn_second_done, ffn_first_done = over_batch(attn_second_sum), over_batch(ffn_first_sum)
-    grad_norm, *landed = group_reduce(partial, 14, cargo=("in", 0, halves(blob)))
-    attn_first_sum = summed(landed)
+        gathered.reshape(-1, D), length, attn_first, taps_again, attn_kept_first
+    )
+    second_done = over_batch(second_sum)
+    grad_norm, *landed = group_reduce(
+        partial, 14, cargo=("in", [(0, down, part, part), (0, halves(blob), 0, D)])
+    )
+    first_sum = summed(landed_first + landed)
     grad_norm, gain_1a = norm_back(grad_norm, first_rows, gains_all[0])
     grad_rows = grad_rows + grad_norm
-    grad_rows, attn_second_done, ffn_first_done = tie(
-        grad_rows, attn_second_done, ffn_first_done
-    )
 
     embed_grad = (grad_rows * root_scale).astype(bf16).T
-    def row_at(index, vector):
-        padded = jnp.pad(vector, (0, D - vector.shape[0]))[None]
-        return jnp.where(jnp.arange(16)[:, None] == index, padded, 0.0)
-
-    vectors = [gain_1a, gain_1f[0], gain_2a[0], gain_2f[0], grad_final_gain, *taps_first[:3], *taps_second[:3]]
-    rows = sum(row_at(index, vector) for index, vector in enumerate(vectors))
-    traded, rows = batch_trade(embed_grad.reshape(batch_count, depth, shard_rows), rows, 9)
-    traded, attn_first_sum = tie(traded, attn_first_sum)
-    attn_first_done = over_batch(attn_first_sum)
+    pieces = [(0, gain_1a), (1, gain_1f), (2, gain_2a), (3, gain_2f), (4, grad_final_gain)]
+    traded, rows = batch_trade(
+        embed_grad.reshape(batch_count, depth, shard_rows),
+        pieces + [(8, taps_first), (16, taps_second)],
+        32,
+        9,
+    )
+    rows, first_sum, second_done = tie(rows, first_sum, second_done)
+    first_done = over_batch(first_sum)
     gain_sums = jnp.sum(rows[:, :5], 0)
-    holders = rows.reshape(2, 4, 16, D)[:, :, 5:11].reshape(2, 4, 2, 3, D)
+    holders = rows.reshape(2, 4, 32, D)[:, :, 8:24].reshape(2, 4, 2, 8, D)
     taps_sums = jnp.sum(lax.dynamic_index_in_dim(holders, me, 1, keepdims=False), 0)
-    taps_sums = lax.dynamic_index_in_dim(taps_sums, section, 0, keepdims=False)
+    taps_sums = lax.dynamic_index_in_dim(taps_sums, section, 0, keepdims=False)[:3]
     sums = jnp.concatenate([gain_sums, taps_sums])
     every, sums = plane_and_batch_gather(traded.reshape(D, shard_rows), sums, 10)
-    sums, attn_first_done = tie(sums, attn_first_done)
+    sums, first_done = tie(sums, first_done)
     every = every.reshape(8, batch_count, depth, shard_rows)
     table_done = spread(every, local_ids, head_done).T
     sums = jnp.sum(sums, 0)
@@ -1364,12 +1472,12 @@
             first, jnp.concatenate([keep, got], 0), jnp.concatenate([got, keep], 0)
         ).astype(f32)
 
-    attn_done = placed(attn_first_done, attn_second_done)
-    ffn_done = placed(ffn_first_done, ffn_second_done)
+    done = placed(first_done, second_done)
+    up_done = done[:, :hidden_width][None]
+    down_done = done[:, hidden_width : 2 * hidden_width].T[None]
+    attn_done = done[:, 2 * hidden_width :]
     qkv_done = unpacked(attn_done)[None]
     out_done = jnp.concatenate([attn_done[:, 640:], attn_done[:, 576:640]], 1).T[None]
-    up_done = ffn_done[:, :hidden_width][None]
-    down_done = ffn_done[:, hidden_width:].T[None]
     return (
         logits,
         table_done,

time: 584 us -> 549 us (0.940)
  matrix products: 45.6 us -> 18.6 us
  local copies, waits for them, and re-layouts: 62.1 us -> 43.2 us
  Pallas kernels: 427 us -> 441 us
    dot_general x13 -> x1, matrix products: 45.6 us -> 18.6 us  [mm(): lax.dot_general(left, right, (((left_dim,), (right_dim,)), ((), ())), pre...]
    unnamed x244 -> x209, local copies, waits for them, and re-layouts: 54 us -> 33.2 us
    pallas_call x0 -> x4, Pallas kernels: none -> 19.7 us  [local_call(): pl.pallas_call(body, out_shape=out_shape, in_specs=[whole] * len(operands...]
    pallas_call x17, Pallas kernels: 350 us -> 343 us  [comm_call(): pl.pallas_call(kernel, out_shape=shapes, in_specs=in_specs, out_specs=out...]
  transfers between devices with their start and end apart: 10 -> 7, of which waited for: 1 -> 1; matrix products, arithmetic and copies ran while one was open for 13% -> 9% of each run, Pallas kernels for 63% -> 72%
where the time goes in v5:
time: 549 us; the launch traced here: 543 us
  Pallas kernels  441 us (80%)
  local copies, waits for them, and re-layouts  43.2 us (8%)
  other arithmetic  23.2 us (4%)
  matrix products  18.6 us (3%)
  between operations  16.1 us (3%)
    pallas_call x17, Pallas kernels, comm_call(): pl.pallas_call(kernel, out_shape=shapes, in_specs=in_specs, out_specs=out...  343 us
    pallas_call x4, Pallas kernels, attention_call(): pl.pallas_call(body, out_shape=out_shape, in_specs=[pl.BlockSpec(memory_s...  44.1 us
    unnamed x209, local copies, waits for them, and re-layouts  33.2 us
    pallas_call x4, Pallas kernels, local_call(): pl.pallas_call(body, out_shape=out_shape, in_specs=[whole] * len(operands...  19.7 us
    pallas_call x1, Pallas kernels, spread(): pl.pallas_call(spread_kernel, grid=(vocab_rows // columns,), out_shape=ja...  19.2 us
    dot_general x1, matrix products, mm(): lax.dot_general(left, right, (((left_dim,), (right_dim,)), ((), ())), pre...  18.6 us
    pallas_call x1, Pallas kernels, lookup(): pl.pallas_call(lookup_kernel, grid=(batches,), out_shape=jax.ShapeDtypeSt...  14.5 us
  transfers between devices with their start and end apart: 7, of which 1 were waited for; matrix products, arithmetic and copies ran while one was open for 9% of the time, Pallas kernels for 72%

profile of v5, /device:TPU:0, one launch (start us, length us, event | category | flops | bytes accessed | tf_op | source)
XLA Modules:
  0.0 542.8 jit_solution(5461680456917413288)
XLA Ops:
  10.5 1.2 convert_bitcast_fusion.2
  13.8 1.3 convert_bitcast_fusion.table
  17.5 11.3 %shard_map.178 = (s32[4,16,128]{2,1,0:T(8,128)S(1)}, f32[4,8,768]{2,1,0:T(8,128)S(1)}) custom-call(s32[16,128]{1,0:T(8,128)S(1)} %reshape.229.refs_0_, f32[8,768]{1,0:T(8,128)S(1)} %pad_maximum_fusion.3.refs_1_), custom_call_target="tpu_custom_call" | custom-call | tf_op jit(solution)/shard_map/pallas_call | solution.py:118
  28.9 14.5 %shard_map.179 = bf16[8,4,192,256]{3,2,1,0:T(8,128)(2,1)S(1)} custom-call(s32[32,1,256]{2,1,0:T(1,128)S(1)} %bitcast.199, bf16[192,4096]{1,0:T(8,128)(2,1)S(1)} %copy-done.2), custom_call_target="tpu_custom_call" | custom-call | tf_op jit(solution)/shard_map/pallas_call | solution.py:1178
  43.4 18.3 %shard_map.180 = f32[768,256]{1,0:T(8,128)S(1)} custom-call(bf16[8,768,256]{2,1,0:T(8,128)(2,1)S(1)} %bitcast.163), custom_call_target="tpu_custom_call" | custom-call | tf_op jit(solution)/shard_map/pallas_call | solution.py:118
  61.7 18.3 %shard_map.181 = (bf16[4,192,256]{2,1,0:T(8,128)(2,1)S(1)}, f32[8,16,768]{2,1,0:T(8,128)S(1)}) custom-call(bf16[4,192,256]{2,1,0:T(8,128)(2,1)S(1)} %bitcast.183, f32[8,768]{1,0:T(8,128)S(1)} %reduce_sum.107.refs_1_), custom_call_target="tpu_custom_call" | custom-call | tf_op jit(solution)/shard_map/pallas_call | solution.py:118
  82.1 1.3 copy-done.8
  83.4 15.6 %shard_map.182 = (bf16[4,256,768]{2,1,0:T(8,128)(2,1)S(1)}, bf16[768,768]{1,0:T(8,128)(2,1)S(1)}) custom-call(bf16[256,768]{1,0:T(8,128)(2,1)S(1)} %get-tuple-element.216.refs_0_, bf16[768,768]{1,0:T(8,128)(2,1)S(1)} %copy-done.8), custom_call_target="tpu_custom_call" | custom-call | tf_op jit(solution)/shard_map/pallas_call | solution.py:118
  99.0 8.6 %shard_map.183 = (bf16[1024,768]{1,0:T(8,128)(2,1)S(1)}, bf16[1024,640]{1,0:T(8,128)(2,1)S(1)}, bf16[1024,640]{1,0:T(8,128)(2,1)S(1)}, bf16[1024,256]{1,0:T(8,128)(2,1)S(1)}, f32[1024,128]{1,0:T(8,128)S(1)}) custom-call(s32[1]{0:T(128)} %dynamic_slice.24.length, bf16[1024,768]{1,0:T(8,128)(2,1)S(1)} %bitcast.171, ...), custom_call_target="tpu_custom_call" | custom-call | tf_op jit(solution)/shard_map/pallas_call | solution.py:915
  107.7 1.2 copy-done.4
  109.9 1.1 copy-done.35
  114.8 2.0 copy-done
  116.8 1.5 copy-done.36
  118.3 29.4 %shard_map.184 = (bf16[4,256,768]{2,1,0:T(8,128)(2,1)S(1)}, f32[256,768]{1,0:T(8,128)S(1)}, bf16[768,768]{1,0:T(8,128)(2,1)S(1)}, bf16[768,768]{1,0:T(8,128)(2,1)S(1)}) custom-call(bf16[4,256,768]{2,1,0:T(8,128)(2,1)S(1)} %bitcast.189, f32[256,768]{1,0:T(8,128)S(1)} %get-tuple-element.215.refs_1_, f32[1,768]{1,0:T(1,128)S(1)} %get-tuple-element.236.refs_2_, ...), custom_call_target="tpu_custom_call" | custom-call | tf_op jit(solution)/shard_map/pallas_call | solution.py:118
  147.7 2.8 shard_map.185
  150.8 26.2 %shard_map.186 = (bf16[4,256,768]{2,1,0:T(8,128)(2,1)S(1)}, f32[256,768]{1,0:T(8,128)S(1)}, bf16[768,768]{1,0:T(8,128)(2,1)S(1)}, bf16[768,384]{1,0:T(8,128)(2,1)S(1)}) custom-call(bf16[4,256,768]{2,1,0:T(8,128)(2,1)S(1)} %bitcast.170, f32[256,768]{1,0:T(8,128)S(1)} %get-tuple-element.102.refs_1_, f32[1,768]{1,0:T(1,128)S(1)} %get-tuple-element.235.refs_2_, ...), custom_call_target="tpu_custom_call" | custom-call | tf_op jit(solution)/shard_map/pallas_call | solution.py:118
  177.1 8.7 %shard_map.187 = (bf16[1024,768]{1,0:T(8,128)(2,1)S(1)}, bf16[1024,640]{1,0:T(8,128)(2,1)S(1)}, bf16[1024,640]{1,0:T(8,128)(2,1)S(1)}, bf16[1024,256]{1,0:T(8,128)(2,1)S(1)}, f32[1024,128]{1,0:T(8,128)S(1)}) custom-call(s32[1]{0:T(128)} %dynamic_slice.24.length, bf16[1024,768]{1,0:T(8,128)(2,1)S(1)} %bitcast.173, ...), custom_call_target="tpu_custom_call" | custom-call | tf_op jit(solution)/shard_map/pallas_call | solution.py:915
  189.5 23.4 %shard_map.188 = (bf16[4,256,768]{2,1,0:T(8,128)(2,1)S(1)}, f32[256,768]{1,0:T(8,128)S(1)}, bf16[768,768]{1,0:T(8,128)(2,1)S(1)}, bf16[768,384]{1,0:T(8,128)(2,1)S(1)}) custom-call(bf16[4,256,768]{2,1,0:T(8,128)(2,1)S(1)} %bitcast.190, f32[256,768]{1,0:T(8,128)S(1)} %get-tuple-element.106.refs_1_, f32[1,768]{1,0:T(1,128)S(1)} %get-tuple-element.234.refs_2_, ...), custom_call_target="tpu_custom_call" | custom-call | tf_op jit(solution)/shard_map/pallas_call | solution.py:118
  213.0 3.6 shard_map.189
  216.6 13.1 %shard_map.190 = f32[256,768]{1,0:T(8,128)S(1)} custom-call(bf16[4,256,768]{2,1,0:T(8,128)(2,1)S(1)} %bitcast.164), custom_call_target="tpu_custom_call" | custom-call | tf_op jit(solution)/shard_map/pallas_call | solution.py:118
  231.0 2.8 copy-done.3
  233.7 22.9 %shard_map.191 = (bf16[8,256,768]{2,1,0:T(8,128)(2,1)S(1)}, bf16[8,256,768]{2,1,0:T(8,128)(2,1)S(1)}) custom-call(bf16[256,768]{1,0:T(8,128)(2,1)S(1)} %fusion.3.refs_0_, bf16[768,4096]{1,0:T(8,128)(2,1)S(1)} %copy-done.3, bf16[2048,4096]{1,0:T(8,128)(2,1)} %bitcast.200), custom_call_target="tpu_custom_call" | custom-call | tf_op jit(solution)/shard_map/pallas_call | solution.py:118
  257.0 24.1 %shard_map.192 = (f32[256,768]{1,0:T(8,128)S(1)}, bf16[768,4096]{1,0:T(8,128)(2,1)}) custom-call(bf16[8,256,768]{2,1,0:T(8,128)(2,1)S(1)} %get-tuple-element.113.refs_0_, bf16[2048,768]{1,0:T(8,128)(2,1)S(1)} %bitcast.180, bf16[2048,128]{1,0:T(8,128)(2,1)S(1)} %broadcast_in_dim.61.refs_2_, bf16[2048,4096]{1,0:T(8,128)(2,1)} %bitcast.201), custom_call_target="tpu_custom_call" | custom-call | tf_op jit(solution)/shard_map/pallas_call | solution.py:118
  283.0 2.2 fusion.7
  285.8 1.5 fusion.18
  287.4 12.1 %shard_map.193 = bf16[4,256,768]{2,1,0:T(8,128)(2,1)S(1)} custom-call(bf16[256,768]{1,0:T(8,128)(2,1)S(1)} %get-tuple-element.199.refs_0_), custom_call_target="tpu_custom_call" | custom-call | tf_op jit(solution)/shard_map/pallas_call | solution.py:118
  299.6 6.8 %shard_map.194 = (bf16[1024,768]{1,0:T(8,128)(2,1)S(1)}, bf16[768,768]{1,0:T(8,128)(2,1)S(1)}, bf16[768,768]{1,0:T(8,128)(2,1)S(1)}) custom-call(bf16[1024,768]{1,0:T(8,128)(2,1)S(1)} %bitcast.169, bf16[1024,768]{1,0:T(8,128)(2,1)S(1)} %bitcast.168, bf16[768,768]{1,0:T(8,128)(2,1)S(1)} %copy-done.21, bf16[768,384]{1,0:T(8,128)(2,1)S(1)} %copy-done.32, ...), custom_call_target="tpu_custom_call" | custom-call | tf_op jit(solution)/shard_map/pallas_call | solution.py:1122
  306.5 23.3 %shard_map.195 = (bf16[4,256,768]{2,1,0:T(8,128)(2,1)S(1)}, f32[256,768]{1,0:T(8,128)S(1)}, f32[1,768]{1,0:T(1,128)S(1)}, bf16[4,96,768]{2,1,0:T(8,128)(2,1)S(1)...) custom-call(bf16[4,256,768]{2,1,0:T(8,128)(2,1)S(1)} %bitcast.185, ...), custom_call_target="tpu_custom_call" | custom-call | tf_op jit(solution)/shard_map/pallas_call | solution.py:118
  330.4 13.5 %shard_map.196 = (bf16[1024,768]{1,0:T(8,128)(2,1)S(1)}, bf16[768,768]{1,0:T(8,128)(2,1)S(1)}, f32[8,640]{1,0:T(8,128)S(1)}) custom-call(s32[1]{0:T(128)} %dynamic_slice.24.length, bf16[1024,768]{1,0:T(8,128)(2,1)S(1)} %bitcast.192, bf16[1024,768]{1,0:T(8,128)(2,1)S(1)} %bitcast.174, bf16[768,768]{1,0:T(8,128)(2,1)S(1)} %copy-done.17, ...), custom_call_target="tpu_custom_call" | custom-call | tf_op jit(solution)/shard_map/pallas_call | solution.py:915
  344.0 23.5 %shard_map.197 = (bf16[4,256,768]{2,1,0:T(8,128)(2,1)S(1)}, f32[256,768]{1,0:T(8,128)S(1)}, f32[1,768]{1,0:T(1,128)S(1)}, bf16[4,96,384]{2,1,0:T(8,128)(2,1)S(1)...) custom-call(bf16[4,256,768]{2,1,0:T(8,128)(2,1)S(1)} %bitcast.184, ...), custom_call_target="tpu_custom_call" | custom-call | tf_op jit(solution)/shard_map/pallas_call | solution.py:118
  367.6 6.5 %shard_map.198 = (bf16[1024,768]{1,0:T(8,128)(2,1)S(1)}, bf16[768,768]{1,0:T(8,128)(2,1)S(1)}, bf16[768,768]{1,0:T(8,128)(2,1)S(1)}) custom-call(bf16[1024,768]{1,0:T(8,128)(2,1)S(1)} %bitcast.186, bf16[1024,768]{1,0:T(8,128)(2,1)S(1)} %bitcast.166, bf16[768,768]{1,0:T(8,128)(2,1)S(1)} %copy-done.13, bf16[768,768]{1,0:T(8,128)(2,1)S(1)} %copy-done.15), custom_call_target="tpu_custom_call" | custom-call | tf_op jit(solution)/shard_map/pallas_call | solution.py:1122
  374.1 23.7 %shard_map.199 = (bf16[4,256,768]{2,1,0:T(8,128)(2,1)S(1)}, f32[256,768]{1,0:T(8,128)S(1)}, f32[1,768]{1,0:T(1,128)S(1)}, bf16[4,96,768]{2,1,0:T(8,128)(2,1)S(1)...) custom-call(bf16[4,256,768]{2,1,0:T(8,128)(2,1)S(1)} %bitcast.188, ...), custom_call_target="tpu_custom_call" | custom-call | tf_op jit(solution)/shard_map/pallas_call | solution.py:118
  397.9 1.2 copy-done.38
  402.1 1.3 pad_maximum_fusion
  404.6 1.9 add_convert_fusion.6
  406.4 2.2 add_convert_fusion.1
  408.7 1.4 copy-done.39
  410.1 1.3 copy-done.41
  411.4 1.3 copy-done.43
  412.7 13.3 %shard_map.200 = (bf16[1024,768]{1,0:T(8,128)(2,1)S(1)}, bf16[768,768]{1,0:T(8,128)(2,1)S(1)}, f32[8,640]{1,0:T(8,128)S(1)}) custom-call(s32[1]{0:T(128)} %dynamic_slice.24.length, bf16[1024,768]{1,0:T(8,128)(2,1)S(1)} %bitcast.191, bf16[1024,768]{1,0:T(8,128)(2,1)S(1)} %bitcast.172, bf16[768,768]{1,0:T(8,128)(2,1)S(1)} %copy-done.11, ...), custom_call_target="tpu_custom_call" | custom-call | tf_op jit(solution)/shard_map/pallas_call | solution.py:915
  426.0 17.3 %shard_map.201 = (f32[256,768]{1,0:T(8,128)S(1)}, bf16[4,96,384]{2,1,0:T(8,128)(2,1)S(1)}, bf16[4,96,384]{2,1,0:T(8,128)(2,1)S(1)}, bf16[4,96,768]{2,1,0:T(8,128)(2,1)S(1)}, bf16[4,96,768]{2,1,0:T(8,128)(2,1)S(1)}) custom-call(bf16[4,256,768]{2,1,0:T(8,128)(2,1)S(1)} %bitcast.187, bf16[4,2,96,768]{3,2,1,0:T(8,128)(2,1)S(1)} %bitcast.176, ...), custom_call_target="tpu_custom_call" | custom-call | tf_op jit(solution)/shard_map/pallas_call | solution.py:118
  444.8 1.2 copy.28
  446.0 22.4 %shard_map.202 = (bf16[4,192,256]{2,1,0:T(8,128)(2,1)S(1)}, f32[8,32,768]{2,1,0:T(8,128)S(1)}) custom-call(bf16[4,192,256]{2,1,0:T(8,128)(2,1)S(1)} %bitcast.182, f32[1,768]{1,0:T(1,128)S(1)} %broadcast_in_dim.63.refs_1_, f32[1,768]{1,0:T(1,128)S(1)} %copy-done.79, f32[1,768]{1,0:T(1,128)S(1)} %copy-done.77, f32[1,768]{1,0:T(1,128)S(1)} %copy-done.75, ...), custom_call_target="tpu_custom_call" | custom-call | tf_op jit(solution)/shard_map/pallas_call | solution.py:118
  469.6 1.4 pad_maximum_fusion.1
  471.0 1.5 sub.41.ids
  472.6 18.6 %convolution_convert_fusion = bf16[2048,4096]{1,0:T(8,128)(2,1)} fusion(bf16[2048,768]{1,0:T(8,128)(2,1)S(1)} %bitcast.181, bf16[768,4096]{1,0:T(8,128)(2,1)} %all-gather.8.cloned.1.call-done.refs_1_), kind=kOutput, calls=%fused_computation | convolution fusion | flops 12893290496 | bytes 26214400 | tf_op jit(solution)/shard_map/dot_general | solution.py:21
  491.3 18.1 %shard_map.203 = (bf16[8,768,256]{2,1,0:T(8,128)(2,1)S(1)}, f32[4,8,768]{2,1,0:T(8,128)S(1)}) custom-call(bf16[768,256]{1,0:T(8,128)(2,1)S(1)} %bitcast.198, f32[8,768]{1,0:T(8,128)S(1)} %pad_maximum_fusion.4.refs_1_), custom_call_target="tpu_custom_call" | custom-call | tf_op jit(solution)/shard_map/pallas_call | solution.py:118
  509.5 19.2 %shard_map.204 = f32[192,4096]{1,0:T(8,128)} custom-call(s32[32,256]{1,0:T(8,128)S(1)} %copy-done.63, bf16[8,4,192,256]{3,2,1,0:T(8,128)(2,1)S(1)} %bitcast.179, bf16[192,4096]{1,0:T(8,128)(2,1)S(1)} %copy-done.37), custom_call_target="tpu_custom_call" | custom-call | tf_op jit(solution)/shard_map/pallas_call | solution.py:1233
  (299 shorter events, 36.8 us)
Async XLA Ops:
  7.2 74.9 %all-gather.4.cloned.1.call-start = ((), (), s32[]{:S(2)}) async-start(), calls=%async_computation.3 | async-start | bytes 1474560 | tf_op jit(solution)/shard_map/all_gather | solution.py:1299
  10.4 104.3 %all-gather.6.cloned.1.call-start = ((), (), s32[]{:S(2)}) async-start(), calls=%async_computation.4 | async-start | bytes 2949120 | tf_op jit(solution)/shard_map/all_gather | solution.py:1300
  13.8 217.2 %all-gather.8.cloned.1.call-start = ((), (), s32[]{:S(2)}) async-start(), calls=%async_computation.5 | async-start | bytes 7864320 | tf_op jit(solution)/shard_map/all_gather | solution.py:1301
  15.2 13.7 %copy-start.2 = (bf16[192,4096]{1,0:T(8,128)(2,1)S(1)}, bf16[192,4096]{1,0:T(8,128)(2,1)}, u32[]{:S(2)}) copy-start(bf16[192,4096]{1,0:T(8,128)(2,1)} %convert_bitcast_fusion.table) | copy-start | bytes 4718596
  15.2 388.2 %reduce-scatter.4.cloned.1.call-start = ((), (), s32[]{:S(2)}) async-start(), calls=%async_computation.6 | async-start | bytes 7864320 | tf_op jit(solution)/shard_map/reduce_scatter | solution.py:1388
  28.9 14.5 %copy-start.60 = (s32[4,16,128]{2,1,0:T(8,128)}, s32[4,16,128]{2,1,0:T(8,128)S(1)}, u32[]{:S(2)}) copy-start(s32[4,16,128]{2,1,0:T(8,128)S(1)} %broadcast_subtract_fusion) | copy-start | bytes 98308
  80.1 96.9 %copy-start.64 = (f32[3,640]{1,0:T(4,128)}, f32[3,640]{1,0:T(4,128)S(1)}, u32[]{:S(2)}) copy-start(f32[3,640]{1,0:T(4,128)S(1)} %slice.274.taps) | copy-start | bytes 23044
  80.7 18.4 %copy-start.96 = (f32[256]{0:T(256)}, f32[256]{0:T(256)S(1)}, u32[]{:S(2)}) copy-start(f32[256]{0:T(256)S(1)} %multiply_reduce_fusion.2) | copy-start | bytes 3076
  81.9 17.1 %copy-start.88 = (f32[768]{0:T(1024)}, f32[768]{0:T(1024)S(1)}, u32[]{:S(2)}) copy-start(f32[768]{0:T(1024)S(1)} %get-tuple-element.237) | copy-start | bytes 9220
  81.9 68.6 %copy-start.66 = (f32[1,768]{1,0:T(1,128)}, f32[1,768]{1,0:T(1,128)S(1)}, u32[]{:S(2)}) copy-start(f32[1,768]{1,0:T(1,128)S(1)} %get-tuple-element.235.refs_2_) | copy-start | bytes 9220
  81.9 107.6 %copy-start.68 = (f32[1,768]{1,0:T(1,128)}, f32[1,768]{1,0:T(1,128)S(1)}, u32[]{:S(2)}) copy-start(f32[1,768]{1,0:T(1,128)S(1)} %get-tuple-element.234.refs_2_) | copy-start | bytes 9220
  177.0 35.9 %copy-start.6 = (bf16[4,256,768]{2,1,0:T(8,128)(2,1)}, bf16[4,256,768]{2,1,0:T(8,128)(2,1)S(1)}, u32[]{:S(2)}) copy-start(bf16[4,256,768]{2,1,0:T(8,128)(2,1)S(1)} %get-tuple-element.103) | copy-start | bytes 4718596
  177.0 35.9 %copy-start.16 = (bf16[768,768]{1,0:T(8,128)(2,1)}, bf16[768,768]{1,0:T(8,128)(2,1)S(1)}, u32[]{:S(2)}) copy-start(bf16[768,768]{1,0:T(8,128)(2,1)S(1)} %get-tuple-element.104.weight) | copy-start | bytes 3538948
  177.0 35.9 %copy-start.24 = (f32[256,768]{1,0:T(8,128)}, f32[256,768]{1,0:T(8,128)S(1)}, u32[]{:S(2)}) copy-start(f32[256,768]{1,0:T(8,128)S(1)} %get-tuple-element.106.refs_1_) | copy-start | bytes 2359300
  177.0 35.9 %copy-start.31 = (bf16[768,384]{1,0:T(8,128)(2,1)}, bf16[768,384]{1,0:T(8,128)(2,1)S(1)}, u32[]{:S(2)}) copy-start(bf16[768,384]{1,0:T(8,128)(2,1)S(1)} %get-tuple-element.110.refs_0_) | copy-start | bytes 1769476
  213.0 16.8 %copy-start.26 = (f32[256,768]{1,0:T(8,128)}, f32[256,768]{1,0:T(8,128)S(1)}, u32[]{:S(2)}) copy-start(f32[256,768]{1,0:T(8,128)S(1)} %get-tuple-element.107.refs_1_) | copy-start | bytes 2359300
  216.6 14.1 %copy-start.90 = (f32[768]{0:T(1024)S(1)}, f32[768]{0:T(1024)}, u32[]{:S(2)}) copy-start(f32[768]{0:T(1024)} %get-tuple-element.238) | copy-start | bytes 9220
  233.7 22.9 %copy-start.91 = (bf16[1,8,2,128]{3,1,2,0:T(8,128)(2,1)S(1)}, bf16[1,8,2,128]{3,1,2,0:T(8,128)(2,1)}, u32[]{:S(2)}) copy-start(bf16[1,8,2,128]{3,1,2,0:T(8,128)(2,1)} %copy.36) | copy-start | bytes 12292
  256.6 24.5 %copy-start.29 = (bf16[8,256,768]{2,1,0:T(8,128)(2,1)}, bf16[8,256,768]{2,1,0:T(8,128)(2,1)S(1)}, u32[]{:S(2)}) copy-start(bf16[8,256,768]{2,1,0:T(8,128)(2,1)S(1)} %get-tuple-element.112) | copy-start | bytes 9437188
  282.1 189.0 %reduce-scatter.6.cloned.1.call-start = ((), (), s32[]{:S(2)}) async-start(), calls=%async_computation.7 | async-start | bytes 2211840 | tf_op jit(solution)/shard_map/reduce_scatter | solution.py:1257
  285.8 13.6 %copy-start.21 = (bf16[768,768]{1,0:T(8,128)(2,1)S(1)}, bf16[768,768]{1,0:T(8,128)(2,1)}, u32[]{:S(2)}) copy-start(bf16[768,768]{1,0:T(8,128)(2,1)} %copy-done.20) | copy-start | bytes 3538948
  285.8 13.7 %copy-start.32 = (bf16[768,384]{1,0:T(8,128)(2,1)S(1)}, bf16[768,384]{1,0:T(8,128)(2,1)}, u32[]{:S(2)}) copy-start(bf16[768,384]{1,0:T(8,128)(2,1)} %copy-done.31) | copy-start | bytes 1769476
  285.8 13.7 %copy-start.34 = (bf16[768,384]{1,0:T(8,128)(2,1)S(1)}, bf16[768,384]{1,0:T(8,128)(2,1)}, u32[]{:S(2)}) copy-start(bf16[768,384]{1,0:T(8,128)(2,1)} %copy-done.33) | copy-start | bytes 1769476
  299.5 30.8 %copy-start.55 = (bf16[1024,256]{1,0:T(8,128)(2,1)S(1)}, bf16[1024,256]{1,0:T(8,128)(2,1)}, u32[]{:S(2)}) copy-start(bf16[1024,256]{1,0:T(8,128)(2,1)} %copy-done.54) | copy-start | bytes 1572868
  299.5 30.8 %copy-start.57 = (f32[1024,128]{1,0:T(8,128)S(1)}, f32[1024,128]{1,0:T(8,128)}, u32[]{:S(2)}) copy-start(f32[1024,128]{1,0:T(8,128)} %copy-done.56) | copy-start | bytes 1572868
  306.4 23.9 %copy-start.7 = (bf16[4,256,768]{2,1,0:T(8,128)(2,1)S(1)}, bf16[4,256,768]{2,1,0:T(8,128)(2,1)}, u32[]{:S(2)}) copy-start(bf16[4,256,768]{2,1,0:T(8,128)(2,1)} %copy-done.6) | copy-start | bytes 4718596
  306.4 23.9 %copy-start.17 = (bf16[768,768]{1,0:T(8,128)(2,1)S(1)}, bf16[768,768]{1,0:T(8,128)(2,1)}, u32[]{:S(2)}) copy-start(bf16[768,768]{1,0:T(8,128)(2,1)} %copy-done.16) | copy-start | bytes 3538948
  306.4 23.9 %copy-start.45 = (bf16[1024,640]{1,0:T(8,128)(2,1)S(1)}, bf16[1024,640]{1,0:T(8,128)(2,1)}, u32[]{:S(2)}) copy-start(bf16[1024,640]{1,0:T(8,128)(2,1)} %copy-done.44) | copy-start | bytes 3932164
  306.5 23.9 %copy-start.47 = (bf16[1024,640]{1,0:T(8,128)(2,1)S(1)}, bf16[1024,640]{1,0:T(8,128)(2,1)}, u32[]{:S(2)}) copy-start(bf16[1024,640]{1,0:T(8,128)(2,1)} %copy-done.46) | copy-start | bytes 3932164
  306.5 23.9 %copy-start.65 = (f32[3,640]{1,0:T(4,128)S(1)}, f32[3,640]{1,0:T(4,128)}, u32[]{:S(2)}) copy-start(f32[3,640]{1,0:T(4,128)} %copy-done.64) | copy-start | bytes 23044
  330.4 13.5 %copy-start.25 = (f32[256,768]{1,0:T(8,128)S(1)}, f32[256,768]{1,0:T(8,128)}, u32[]{:S(2)}) copy-start(f32[256,768]{1,0:T(8,128)} %copy-done.24) | copy-start | bytes 2359300
  343.9 23.6 %copy-start.70 = (f32[8,640]{1,0:T(8,128)}, f32[8,640]{1,0:T(8,128)S(1)}, u32[]{:S(2)}) copy-start(f32[8,640]{1,0:T(8,128)S(1)} %get-tuple-element.155.refs_7_) | copy-start | bytes 61444
  343.9 23.6 %copy-start.13 = (bf16[768,768]{1,0:T(8,128)(2,1)S(1)}, bf16[768,768]{1,0:T(8,128)(2,1)}, u32[]{:S(2)}) copy-start(bf16[768,768]{1,0:T(8,128)(2,1)} %copy-done.12) | copy-start | bytes 3538948
  344.0 23.6 %copy-start.15 = (bf16[768,768]{1,0:T(8,128)(2,1)S(1)}, bf16[768,768]{1,0:T(8,128)(2,1)}, u32[]{:S(2)}) copy-start(bf16[768,768]{1,0:T(8,128)(2,1)} %copy-done.14) | copy-start | bytes 3538948
  374.1 23.8 %copy-start.18 = (bf16[768,768]{1,0:T(8,128)(2,1)}, bf16[768,768]{1,0:T(8,128)(2,1)S(1)}, u32[]{:S(2)}) copy-start(bf16[768,768]{1,0:T(8,128)(2,1)S(1)} %get-tuple-element.130) | copy-start | bytes 3538948
  403.5 125.2 %reduce-scatter.8.cloned.1.call-start = ((), (), s32[]{:S(2)}) async-start(), calls=%async_computation.8 | async-start | bytes 2211840 | tf_op jit(solution)/shard_map/reduce_scatter | solution.py:1257
  426.0 17.3 %copy-start.72 = (f32[8,640]{1,0:T(8,128)}, f32[8,640]{1,0:T(8,128)S(1)}, u32[]{:S(2)}) copy-start(f32[8,640]{1,0:T(8,128)S(1)} %get-tuple-element.154.refs_6_) | copy-start | bytes 61444
  426.0 17.3 %copy-start.81 = (f32[768,256]{0,1:T(8,128)S(1)}, f32[768,256]{0,1:T(8,128)}, u32[]{:S(2)}) copy-start(f32[768,256]{0,1:T(8,128)} %copy-done.80) | copy-start | bytes 2359300
  426.0 17.3 %copy-start.89 = (f32[768]{0:T(1024)S(1)}, f32[768]{0:T(1024)}, u32[]{:S(2)}) copy-start(f32[768]{0:T(1024)} %copy-done.88) | copy-start | bytes 9220
  426.0 17.3 %copy-start.95 = (f32[256]{0:T(256)S(1)}, f32[256]{0:T(256)}, u32[]{:S(2)}) copy-start(f32[256]{0:T(256)} %get-tuple-element.248) | copy-start | bytes 3076
  426.0 17.7 %copy-start.97 = (f32[256]{0:T(256)S(1)}, f32[256]{0:T(256)}, u32[]{:S(2)}) copy-start(f32[256]{0:T(256)} %copy-done.96) | copy-start | bytes 3076
  446.0 23.6 %copy-start.85 = (bf16[4,96,768]{2,1,0:T(8,128)(2,1)S(1)}, bf16[4,96,768]{2,1,0:T(8,128)(2,1)}, u32[]{:S(2)}) copy-start(bf16[4,96,768]{2,1,0:T(8,128)(2,1)} %add_convert_fusion.1) | copy-start | bytes 1769476
  446.0 23.6 %copy-start.86 = (bf16[4,96,384]{2,1,0:T(8,128)(2,1)S(1)}, bf16[4,96,384]{2,1,0:T(8,128)(2,1)}, u32[]{:S(2)}) copy-start(bf16[4,96,384]{2,1,0:T(8,128)(2,1)} %add_convert_fusion.6) | copy-start | bytes 884740
  472.6 18.6 %copy-start.59 = (f32[8,32,768]{2,1,0:T(8,128)S(1)}, f32[8,32,768]{2,1,0:T(8,128)}, u32[]{:S(2)}) copy-start(f32[8,32,768]{2,1,0:T(8,128)} %copy-done.58) | copy-start | bytes 2359300
  472.6 36.8 %copy-start.63 = (s32[32,256]{1,0:T(8,128)S(1)}, s32[32,256]{1,0:T(8,128)}, u32[]{:S(2)}) copy-start(s32[32,256]{1,0:T(8,128)} %sub.41.ids) | copy-start | bytes 98308
  491.2 18.2 %copy-start.37 = (bf16[192,4096]{1,0:T(8,128)(2,1)S(1)}, bf16[192,4096]{1,0:T(8,128)(2,1)}, u32[]{:S(2)}) copy-start(bf16[192,4096]{1,0:T(8,128)(2,1)} %reduce-scatter.4.cloned.1.call-done.base) | copy-start | bytes 4718596
  509.4 20.2 %copy-start.87 = (bf16[1,96,2304]{2,1,0:T(8,128)(2,1)S(1)}, bf16[1,96,2304]{2,1,0:T(8,128)(2,1)}, u32[]{:S(2)}) copy-start(bf16[1,96,2304]{2,1,0:T(8,128)(2,1)} %reduce-scatter.6.cloned.1.call-done) | copy-start | bytes 1327108
  530.7 2.0 collective-permute-start
  (61 other events, 158.4 us)
Sparse Core Ops, SparseCore 0:
  10.6 36.1 all-gather.3
  48.9 57.5 all-gather.5
  108.6 114.0 all-gather.7
  282.2 116.3 reduce-scatter.3
  403.6 44.7 reduce-scatter.5
  471.2 38.5 reduce-scatter.7

commit v6 on v5

--- a/solution.py
+++ b/solution.py
@@ -1,4 +1,5 @@
 import functools
+import itertools
 import math
 
 import jax
@@ -486,7 +487,7 @@
     return [functools.partial(unit, at) for at in range(count)]
 
 
-def plane_exchange(own, out, send, recv, chores=Chores()):
+def plane_steps(own, out, send, recv):
     core, y, x, _ = place()
     other, beside, above = plane_peers()
     half = own.shape[0] // 2
@@ -519,28 +520,34 @@
         made.start()
         return made
 
-    chores.some(2)
+    yield
     to_x[0].wait_recv()
     diag_y = onward(at_x, 0, 5, above)
     pending.append(onward(at_x, 0, 6, other))
     to_y[1].wait_recv()
     diag_x = onward(at_y, 1, 7, beside)
     pending.append(onward(at_y, 1, 8, other))
-    chores.some(2)
+    yield
     to_x[1].wait_recv()
     pending.append(onward(at_x, 1, 9, other))
     to_y[0].wait_recv()
     pending.append(onward(at_y, 0, 10, other))
-    chores.some(2)
+    yield
     diag_y.wait_recv()
     pending.append(onward(at_both, 0, 11, other))
     diag_x.wait_recv()
     pending.append(onward(at_both, 1, 12, other))
-    chores.rest()
+    yield
     for made in to_x + to_y + [diag_x, diag_y]:
         made.wait_send()
     for made in pending:
         made.wait()
+
+
+def plane_exchange(own, out, send, recv, chores=Chores()):
+    for _ in plane_steps(own, out, send, recv):
+        chores.some(2)
+    chores.rest()
 
 
 def head_gather_kernel(own, table, grads, out, parts, buffers, sems, send, recv):
@@ -574,13 +581,21 @@
     )
 
 
-def plane_reduce_kernel(parts, out, *scratch):
-    greet(plane_peers())
-    plane_sum(parts, out, *scratch)
-
-
 def plane_sum(
-    parts, out, near, mixed, via_x, via_y, from_x, from_y, hop_x, hop_y, send, recv, chores=Chores()
+    parts,
+    out,
+    near,
+    mixed,
+    via_x,
+    via_y,
+    from_x,
+    from_y,
+    hop_x,
+    hop_y,
+    send,
+    recv,
+    chores=Chores(),
+    make=None,
 ):
     core, y, x, _ = place()
     other, beside, above = plane_peers()
@@ -592,7 +607,11 @@
 
     targets = [(1 - y, 1 - x), (y, 1 - x), (1 - y, x), (y, x)]
     handed = []
-    for index, (along_y, along_x) in enumerate(targets):
+
+    def hand(index):
+        along_y, along_x = targets[index]
+        if make is not None:
+            make(slot(1 - core, along_y, along_x))
         made = remote(
             parts.at[slot(1 - core, along_y, along_x)],
             near.at[index],
@@ -602,6 +621,15 @@
         )
         made.start()
         handed.append(made)
+        if make is not None:
+            make(slot(core, along_y, along_x))
+
+    for index in range(1 if make is not None else 4):
+        hand(index)
+
+    def hand_next(index):
+        if make is not None:
+            hand(index)
 
     def joined(index, where=slice(None)):
         along_y, along_x = targets[index]
@@ -617,9 +645,11 @@
     mixed[0] = joined(0).astype(bf16)
     diag_x = start(mixed.at[0, cut[0]], via_x, 4, beside)
     diag_y = start(mixed.at[0, cut[1]], via_y, 5, above)
+    hand_next(1)
     handed[1].wait_recv()
     mixed[1] = joined(1).astype(bf16)
     straight_x = start(mixed.at[1, cut[0]], from_x.at[cut[0]], 6, beside)
+    hand_next(2)
     handed[2].wait_recv()
     mixed[2] = joined(2).astype(bf16)
     straight_y = start(mixed.at[2, cut[1]], from_y.at[cut[1]], 7, above)
@@ -630,6 +660,7 @@
     diag_y.wait_recv()
     hop_x[...] = (mixed[1, cut[1]].astype(f32) + via_y[...].astype(f32)).astype(bf16)
     turned_x = start(hop_x, from_x.at[cut[1]], 9, beside)
+    hand_next(3)
     chores.rest()
     handed[3].wait_recv()
     straight_x.wait_recv()
@@ -642,28 +673,50 @@
         made.wait_send()
 
 
-def plane_scratch(count, width):
-    half = count // 2
-    return [
-        pltpu.VMEM((4, count, width), bf16),
-        pltpu.VMEM((3, count, width), bf16),
-        pltpu.VMEM((half, width), bf16),
-        pltpu.VMEM((half, width), bf16),
-        pltpu.VMEM((count, width), bf16),
-        pltpu.VMEM((count, width), bf16),
-        pltpu.VMEM((half, width), bf16),
-        pltpu.VMEM((half, width), bf16),
-    ] + [pltpu.SemaphoreType.DMA((10,))] * 2
-
-
-def plane_reduce(parts, collective_id):
-    _, count, width = parts.shape
+def plane_scratch(shape):
+    half = (shape[0] // 2,) + shape[1:]
+    shapes = [(4,) + shape, (3,) + shape, half, half, shape, shape, half, half]
+    return [pltpu.VMEM(one, bf16) for one in shapes] + [pltpu.SemaphoreType.DMA((10,))] * 2
+
+
+LOOK = 512
+
+
+def lookup_reduce_kernel(ids, table, out, parts, *scratch):
+    greet(plane_peers())
+    batches, depth, slots = out.shape
+    row = lax.broadcasted_iota(jnp.int32, (LOOK, slots), 0)
+
+    def make(part):
+        def step(batch, carry):
+            wanted = ids[batch * 8 + part]
+            total = jnp.zeros((depth, slots), f32)
+            for lead in range(0, table.shape[1], LOOK):
+                hit = jnp.where(row == wanted - lead, 1.0, 0.0).astype(bf16)
+                total += jnp.dot(table[:, lead : lead + LOOK], hit, preferred_element_type=f32)
+            parts[part, batch] = total.astype(bf16)
+            return carry
+
+        if batches > 4:
+            lax.fori_loop(0, batches, step, 0)
+        else:
+            for batch in range(batches):
+                step(batch, 0)
+
+    plane_sum(parts, out, *scratch, make=make)
+
+
+def lookup_reduce(table, ids):
+    batches, parts, _, slots = ids.shape
+    block = (batches, table.shape[0], slots)
     return comm_call(
-        plane_reduce_kernel,
-        jax.ShapeDtypeStruct((count, width), f32),
-        plane_scratch(count, width),
-        collective_id,
-        parts,
+        lookup_reduce_kernel,
+        jax.ShapeDtypeStruct(block, f32),
+        [pltpu.VMEM((parts,) + block, bf16)] + plane_scratch(block),
+        3,
+        ids.reshape(batches * parts, 1, slots),
+        table,
+        room=14,
     )
 
 
@@ -697,7 +750,7 @@
             pltpu.VMEM((2, rows.shape[0], step), bf16),
             pltpu.SemaphoreType.DMA((2,)),
         ]
-        + plane_scratch(count, width),
+        + plane_scratch((count, width)),
         4,
         parts,
         rows,
@@ -743,26 +796,36 @@
     )
 
 
-def plane_and_batch_kernel(count, own, few, out, few_out, send, recv, few_send, few_recv):
-    greet(plane_peers() + batch_peers(count))
-    copies = batch_exchange(count, [few], [few_out], few_send, few_recv)
-    plane_exchange(own, out, send, recv)
-    for copy in copies:
-        copy.wait()
-
-
-def plane_and_batch_gather(block, few, collective_id):
-    count = lax.axis_size("batch")
+def tail_gather_kernel(count, leads, *refs):
+    blocks, refs = refs[:count], refs[count:]
+    pieces, refs = refs[: len(leads)], refs[len(leads) :]
+    out, few_out, own, few, send, recv, few_send, few_recv = refs
+    me = lax.axis_index("batch")
+    for step, block in enumerate(blocks):
+        own[lax.rem(me + count - step, count)] = block[...]
+    few[...] = jnp.zeros(few.shape, few.dtype)
+    for lead, piece in zip(leads, pieces):
+        few[lead : lead + piece.shape[0], : piece.shape[1]] = piece[...]
+    greet(plane_peers())
+    both = [plane_steps(few, few_out, few_send, few_recv), plane_steps(own, out, send, recv)]
+    for _ in itertools.zip_longest(*both):
+        pass
+
+
+def tail_gather(blocks, pieces, rows):
+    count = len(blocks)
+    own = (count,) + blocks[0].shape
     return comm_call(
-        functools.partial(plane_and_batch_kernel, count),
+        functools.partial(tail_gather_kernel, count, [lead for lead, _ in pieces]),
         [
-            jax.ShapeDtypeStruct((8,) + block.shape, block.dtype),
-            jax.ShapeDtypeStruct((count,) + few.shape, few.dtype),
+            jax.ShapeDtypeStruct((8,) + own, blocks[0].dtype),
+            jax.ShapeDtypeStruct((8, rows, D), f32),
         ],
-        [pltpu.SemaphoreType.DMA((13,))] * 2 + [pltpu.SemaphoreType.DMA((count - 1,))] * 2,
-        collective_id,
-        block,
-        few,
+        [pltpu.VMEM(own, blocks[0].dtype), pltpu.VMEM((rows, D), f32)]
+        + [pltpu.SemaphoreType.DMA((13,))] * 4,
+        10,
+        *blocks,
+        *[piece for _, piece in pieces],
     )
 
 
@@ -1158,36 +1221,6 @@
     )
 
 
-LOOK = 512
-
-
-def lookup_kernel(ids, table, out):
-    for part in range(ids.shape[0]):
-        total = jnp.zeros((table.shape[0], ids.shape[2]), f32)
-        wanted = ids[part]
-        row = lax.broadcasted_iota(jnp.int32, (LOOK, ids.shape[2]), 0)
-        for lead in range(0, table.shape[1], LOOK):
-            hit = jnp.where(row == wanted - lead, 1.0, 0.0).astype(bf16)
-            total += jnp.dot(table[:, lead : lead + LOOK], hit, preferred_element_type=f32)
-        out[part, 0] = total.astype(bf16)
-
-
-def lookup(table, ids):
-    batches, parts, _, slots = ids.shape
-    depth, vocab_rows = table.shape
-    return pl.pallas_call(
-        lookup_kernel,
-        grid=(batches,),
-        out_shape=jax.ShapeDtypeStruct((parts, batches, depth, slots), bf16),
-        in_specs=[
-            pl.BlockSpec((parts, 1, slots), lambda at: (at, 0, 0)),
-            pl.BlockSpec((depth, vocab_rows), lambda at: (0, 0)),
-        ],
-        out_specs=pl.BlockSpec((parts, 1, depth, slots), lambda at: (0, at, 0, 0)),
-        compiler_params=pltpu.CompilerParams(vmem_limit_bytes=40 << 20),
-    )(ids.reshape(batches * parts, 1, slots), table)
-
-
 def spread_kernel(ids, grads, base, out, wanted):
     at = pl.program_id(0)
     columns = out.shape[1]
@@ -1317,11 +1350,8 @@
     vocab_rows = embed_table.shape[0]
     owner_start = (section * tensor_count + me) * vocab_rows
     local_ids = all_ids.reshape(batch_count, sequences * 4, 1, shard_rows) - owner_start
-    picked = lookup(table_own, local_ids)
-    total = plane_reduce(picked.reshape(8, D, shard_rows), 3).astype(bf16)
-    embedded, small = batch_trade(
-        total.reshape(batch_count, depth, shard_rows), [(0, small)], 16, 8
-    )
+    total = lookup_reduce(table_own, local_ids).astype(bf16)
+    embedded, small = batch_trade(total, [(0, small)], 16, 8)
     gains_all = jnp.sum(small[:, :5], 0)
     final_scale = gains_all[4]
     taps_here = [
@@ -1438,26 +1468,32 @@
     grad_norm, gain_1a = norm_back(grad_norm, first_rows, gains_all[0])
     grad_rows = grad_rows + grad_norm
 
-    embed_grad = (grad_rows * root_scale).astype(bf16).T
+    spread_own = (grad_rows * root_scale).astype(bf16).T.reshape(batch_count, depth, shard_rows)
+    blocks = []
+    for step in range(batch_count):
+        block = lax.dynamic_index_in_dim(
+            spread_own, lax.rem(at_batch + step, batch_count), 0, keepdims=False
+        )
+        if step > 0:
+            pairs = [(at, (at + step) % batch_count) for at in range(batch_count)]
+            block = lax.ppermute(block, "batch", pairs)
+        blocks.append(block)
+    gain_1a, second_done = tie(gain_1a, second_done)
+    first_done = over_batch(first_sum)
     pieces = [(0, gain_1a), (1, gain_1f), (2, gain_2a), (3, gain_2f), (4, grad_final_gain)]
-    traded, rows = batch_trade(
-        embed_grad.reshape(batch_count, depth, shard_rows),
-        pieces + [(8, taps_first), (16, taps_second)],
-        32,
-        9,
-    )
-    rows, first_sum, second_done = tie(rows, first_sum, second_done)
-    first_done = over_batch(first_sum)
+    every, rows = tail_gather(blocks, pieces + [(8, taps_first), (16, taps_second)], 32)
+
     gain_sums = jnp.sum(rows[:, :5], 0)
     holders = rows.reshape(2, 4, 32, D)[:, :, 8:24].reshape(2, 4, 2, 8, D)
     taps_sums = jnp.sum(lax.dynamic_index_in_dim(holders, me, 1, keepdims=False), 0)
     taps_sums = lax.dynamic_index_in_dim(taps_sums, section, 0, keepdims=False)[:3]
-    sums = jnp.concatenate([gain_sums, taps_sums])
-    every, sums = plane_and_batch_gather(traded.reshape(D, shard_rows), sums, 10)
-    sums, first_done = tie(sums, first_done)
-    every = every.reshape(8, batch_count, depth, shard_rows)
+    own_sums = jnp.concatenate([gain_sums, taps_sums])
+    own_sums, first_done = tie(own_sums, first_done)
+    sums = own_sums
+    for step in range(1, batch_count):
+        pairs = [(at, (at + step) % batch_count) for at in range(batch_count)]
+        sums = sums + lax.ppermute(own_sums, "batch", pairs)
     table_done = spread(every, local_ids, head_done).T
-    sums = jnp.sum(sums, 0)
     gain_part = lax.dynamic_slice_in_dim(sums[:5], whole_at * gain_width, gain_width, 1)
     gains_done = gain_part[:4].reshape(2, 2, gain_width)
     final_done = gain_part[4]

time: 549 us -> 548 us (level)
  Pallas kernels: 441 us -> 418 us
  starting transfers between devices: 0.96 us -> 14.8 us
    pallas_call x1 -> x0, Pallas kernels: 14.5 us -> none  [lookup(): pl.pallas_call(lookup_kernel, grid=(batches,), out_shape=jax.ShapeDtypeSt...]
    ppermute x0 -> x6, starting transfers between devices: none -> 14.4 us  [the longest x3 9.98 us: on_device(): block = lax.ppermute(block, 'batch', pairs)]
    pallas_call x17 -> x16, Pallas kernels: 343 us -> 335 us  [comm_call(): pl.pallas_call(kernel, out_shape=shapes, in_specs=in_specs, out_specs=out...]
    unnamed x209 -> x203, local copies, waits for them, and re-layouts: 33.2 us -> 35.9 us
  transfers between devices with their start and end apart: 7 -> 13, of which waited for: 1 -> 2; matrix products, arithmetic and copies ran while one was open for 9% -> 9% of each run, Pallas kernels for 72% -> 69%
where the time goes in v6:
time: 548 us; the launch traced here: 537 us
  Pallas kernels  418 us (76%)
  local copies, waits for them, and re-layouts  44.1 us (8%)
  other arithmetic  23.6 us (4%)
  matrix products  19.7 us (4%)
  between operations  16.2 us (3%)
  starting transfers between devices  14.8 us (3%)
    pallas_call x16, Pallas kernels, comm_call(): pl.pallas_call(kernel, out_shape=shapes, in_specs=in_specs, out_specs=out...  335 us
    pallas_call x4, Pallas kernels, attention_call(): pl.pallas_call(body, out_shape=out_shape, in_specs=[pl.BlockSpec(memory_s...  44.1 us
    unnamed x203, local copies, waits for them, and re-layouts  35.9 us
    pallas_call x4, Pallas kernels, local_call(): pl.pallas_call(body, out_shape=out_shape, in_specs=[whole] * len(operands...  19.7 us
    dot_general x1, matrix products, mm(): lax.dot_general(left, right, (((left_dim,), (right_dim,)), ((), ())), pre...  19.7 us
    pallas_call x1, Pallas kernels, spread(): pl.pallas_call(spread_kernel, grid=(vocab_rows // columns,), out_shape=ja...  19.3 us
  transfers between devices with their start and end apart: 13, of which 2 were waited for; matrix products, arithmetic and copies ran while one was open for 9% of the time, Pallas kernels for 69%

profile of v6, /device:TPU:0, one launch (start us, length us, event | category | flops | bytes accessed | tf_op | source)
XLA Modules:
  0.0 537.2 jit_solution(9039859526891110227)
XLA Ops:
  10.5 1.2 convert_bitcast_fusion.2
  13.8 1.3 convert_bitcast_fusion.refs_1_
  17.5 11.3 %shard_map.178 = (s32[4,16,128]{2,1,0:T(8,128)S(1)}, f32[4,8,768]{2,1,0:T(8,128)S(1)}) custom-call(s32[16,128]{1,0:T(8,128)S(1)} %reshape.217.refs_0_, f32[8,768]{1,0:T(8,128)S(1)} %pad_maximum_fusion.3.refs_1_), custom_call_target="tpu_custom_call" | custom-call | tf_op jit(solution)/shard_map/pallas_call | solution.py:119
  28.9 24.4 %shard_map.179 = f32[4,192,256]{2,1,0:T(8,128)S(1)} custom-call(s32[32,1,256]{2,1,0:T(1,128)S(1)} %bitcast.198, bf16[192,4096]{1,0:T(8,128)(2,1)S(1)} %copy-done.2), custom_call_target="tpu_custom_call" | custom-call | tf_op jit(solution)/shard_map/pallas_call | solution.py:119
  53.4 18.7 %shard_map.180 = (bf16[4,192,256]{2,1,0:T(8,128)(2,1)S(1)}, f32[8,16,768]{2,1,0:T(8,128)S(1)}) custom-call(bf16[4,192,256]{2,1,0:T(8,128)(2,1)S(1)} %convert_element_type.156.refs_0_, f32[8,768]{1,0:T(8,128)S(1)} %reduce_sum.98.refs_1_), custom_call_target="tpu_custom_call" | custom-call | tf_op jit(solution)/shard_map/pallas_call | solution.py:119
  74.1 1.3 copy-done.8
  75.4 14.6 %shard_map.181 = (bf16[4,256,768]{2,1,0:T(8,128)(2,1)S(1)}, bf16[768,768]{1,0:T(8,128)(2,1)S(1)}) custom-call(bf16[256,768]{1,0:T(8,128)(2,1)S(1)} %get-tuple-element.210.refs_0_, bf16[768,768]{1,0:T(8,128)(2,1)S(1)} %copy-done.8), custom_call_target="tpu_custom_call" | custom-call | tf_op jit(solution)/shard_map/pallas_call | solution.py:119
  90.0 8.6 %shard_map.182 = (bf16[1024,768]{1,0:T(8,128)(2,1)S(1)}, bf16[1024,640]{1,0:T(8,128)(2,1)S(1)}, bf16[1024,640]{1,0:T(8,128)(2,1)S(1)}, bf16[1024,256]{1,0:T(8,128)(2,1)S(1)}, f32[1024,128]{1,0:T(8,128)S(1)}) custom-call(s32[1]{0:T(128)} %dynamic_slice.37.length, bf16[1024,768]{1,0:T(8,128)(2,1)S(1)} %bitcast.174, ...), custom_call_target="tpu_custom_call" | custom-call | tf_op jit(solution)/shard_map/pallas_call | solution.py:978
  98.6 1.1 copy-done.4
  100.8 1.1 copy-done.34
  106.1 1.7 copy-done
  107.7 1.4 copy-done.35
  109.1 29.0 %shard_map.183 = (bf16[4,256,768]{2,1,0:T(8,128)(2,1)S(1)}, f32[256,768]{1,0:T(8,128)S(1)}, bf16[768,768]{1,0:T(8,128)(2,1)S(1)}, bf16[768,768]{1,0:T(8,128)(2,1)S(1)}) custom-call(bf16[4,256,768]{2,1,0:T(8,128)(2,1)S(1)} %bitcast.189, f32[256,768]{1,0:T(8,128)S(1)} %get-tuple-element.209.refs_1_, f32[1,768]{1,0:T(1,128)S(1)} %get-tuple-element.234.refs_2_, ...), custom_call_target="tpu_custom_call" | custom-call | tf_op jit(solution)/shard_map/pallas_call | solution.py:119
  138.2 2.7 shard_map.184
  141.3 25.7 %shard_map.185 = (bf16[4,256,768]{2,1,0:T(8,128)(2,1)S(1)}, f32[256,768]{1,0:T(8,128)S(1)}, bf16[768,768]{1,0:T(8,128)(2,1)S(1)}, bf16[768,384]{1,0:T(8,128)(2,1)S(1)}) custom-call(bf16[4,256,768]{2,1,0:T(8,128)(2,1)S(1)} %bitcast.173, f32[256,768]{1,0:T(8,128)S(1)} %get-tuple-element.99.refs_1_, f32[1,768]{1,0:T(1,128)S(1)} %get-tuple-element.233.refs_2_, ...), custom_call_target="tpu_custom_call" | custom-call | tf_op jit(solution)/shard_map/pallas_call | solution.py:119
  167.1 8.7 %shard_map.186 = (bf16[1024,768]{1,0:T(8,128)(2,1)S(1)}, bf16[1024,640]{1,0:T(8,128)(2,1)S(1)}, bf16[1024,640]{1,0:T(8,128)(2,1)S(1)}, bf16[1024,256]{1,0:T(8,128)(2,1)S(1)}, f32[1024,128]{1,0:T(8,128)S(1)}) custom-call(s32[1]{0:T(128)} %dynamic_slice.37.length, bf16[1024,768]{1,0:T(8,128)(2,1)S(1)} %bitcast.176, ...), custom_call_target="tpu_custom_call" | custom-call | tf_op jit(solution)/shard_map/pallas_call | solution.py:978
  179.5 24.8 %shard_map.187 = (bf16[4,256,768]{2,1,0:T(8,128)(2,1)S(1)}, f32[256,768]{1,0:T(8,128)S(1)}, bf16[768,768]{1,0:T(8,128)(2,1)S(1)}, bf16[768,384]{1,0:T(8,128)(2,1)S(1)}) custom-call(bf16[4,256,768]{2,1,0:T(8,128)(2,1)S(1)} %bitcast.190, f32[256,768]{1,0:T(8,128)S(1)} %get-tuple-element.103.refs_1_, f32[1,768]{1,0:T(1,128)S(1)} %get-tuple-element.232.refs_2_, ...), custom_call_target="tpu_custom_call" | custom-call | tf_op jit(solution)/shard_map/pallas_call | solution.py:119
  204.3 3.6 shard_map.188
  208.0 12.9 %shard_map.189 = f32[256,768]{1,0:T(8,128)S(1)} custom-call(bf16[4,256,768]{2,1,0:T(8,128)(2,1)S(1)} %bitcast.167), custom_call_target="tpu_custom_call" | custom-call | tf_op jit(solution)/shard_map/pallas_call | solution.py:119
  222.6 2.8 copy-done.3
  225.4 23.6 %shard_map.190 = (bf16[8,256,768]{2,1,0:T(8,128)(2,1)S(1)}, bf16[8,256,768]{2,1,0:T(8,128)(2,1)S(1)}) custom-call(bf16[256,768]{1,0:T(8,128)(2,1)S(1)} %fusion.3.refs_0_, bf16[768,4096]{1,0:T(8,128)(2,1)S(1)} %copy-done.3, bf16[2048,4096]{1,0:T(8,128)(2,1)} %bitcast.199), custom_call_target="tpu_custom_call" | custom-call | tf_op jit(solution)/shard_map/pallas_call | solution.py:119
  249.4 22.5 %shard_map.191 = (f32[256,768]{1,0:T(8,128)S(1)}, bf16[768,4096]{1,0:T(8,128)(2,1)}) custom-call(bf16[8,256,768]{2,1,0:T(8,128)(2,1)S(1)} %get-tuple-element.110.refs_0_, bf16[2048,768]{1,0:T(8,128)(2,1)S(1)} %bitcast.182, bf16[2048,128]{1,0:T(8,128)(2,1)S(1)} %broadcast_in_dim.61.refs_2_, bf16[2048,4096]{1,0:T(8,128)(2,1)} %bitcast.200), custom_call_target="tpu_custom_call" | custom-call | tf_op jit(solution)/shard_map/pallas_call | solution.py:119
  273.8 2.2 fusion.7
  276.6 1.5 fusion.18
  278.2 13.4 %shard_map.192 = bf16[4,256,768]{2,1,0:T(8,128)(2,1)S(1)} custom-call(bf16[256,768]{1,0:T(8,128)(2,1)S(1)} %get-tuple-element.193.refs_0_), custom_call_target="tpu_custom_call" | custom-call | tf_op jit(solution)/shard_map/pallas_call | solution.py:119
  291.6 6.8 %shard_map.193 = (bf16[1024,768]{1,0:T(8,128)(2,1)S(1)}, bf16[768,768]{1,0:T(8,128)(2,1)S(1)}, bf16[768,768]{1,0:T(8,128)(2,1)S(1)}) custom-call(bf16[1024,768]{1,0:T(8,128)(2,1)S(1)} %bitcast.172, bf16[1024,768]{1,0:T(8,128)(2,1)S(1)} %bitcast.171, bf16[768,768]{1,0:T(8,128)(2,1)S(1)} %copy-done.21, bf16[768,384]{1,0:T(8,128)(2,1)S(1)} %copy-done.31, ...), custom_call_target="tpu_custom_call" | custom-call | tf_op jit(solution)/shard_map/pallas_call | solution.py:1185
  298.5 23.2 %shard_map.194 = (bf16[4,256,768]{2,1,0:T(8,128)(2,1)S(1)}, f32[256,768]{1,0:T(8,128)S(1)}, f32[1,768]{1,0:T(1,128)S(1)}, bf16[4,96,768]{2,1,0:T(8,128)(2,1)S(1)...) custom-call(bf16[4,256,768]{2,1,0:T(8,128)(2,1)S(1)} %bitcast.185, ...), custom_call_target="tpu_custom_call" | custom-call | tf_op jit(solution)/shard_map/pallas_call | solution.py:119
  322.4 13.5 %shard_map.195 = (bf16[1024,768]{1,0:T(8,128)(2,1)S(1)}, bf16[768,768]{1,0:T(8,128)(2,1)S(1)}, f32[8,640]{1,0:T(8,128)S(1)}) custom-call(s32[1]{0:T(128)} %dynamic_slice.37.length, bf16[1024,768]{1,0:T(8,128)(2,1)S(1)} %bitcast.192, bf16[1024,768]{1,0:T(8,128)(2,1)S(1)} %bitcast.177, bf16[768,768]{1,0:T(8,128)(2,1)S(1)} %copy-done.19, ...), custom_call_target="tpu_custom_call" | custom-call | tf_op jit(solution)/shard_map/pallas_call | solution.py:978
  336.0 23.5 %shard_map.196 = (bf16[4,256,768]{2,1,0:T(8,128)(2,1)S(1)}, f32[256,768]{1,0:T(8,128)S(1)}, f32[1,768]{1,0:T(1,128)S(1)}, bf16[4,96,384]{2,1,0:T(8,128)(2,1)S(1)...) custom-call(bf16[4,256,768]{2,1,0:T(8,128)(2,1)S(1)} %bitcast.184, ...), custom_call_target="tpu_custom_call" | custom-call | tf_op jit(solution)/shard_map/pallas_call | solution.py:119
  359.5 6.5 %shard_map.197 = (bf16[1024,768]{1,0:T(8,128)(2,1)S(1)}, bf16[768,768]{1,0:T(8,128)(2,1)S(1)}, bf16[768,768]{1,0:T(8,128)(2,1)S(1)}) custom-call(bf16[1024,768]{1,0:T(8,128)(2,1)S(1)} %bitcast.186, bf16[1024,768]{1,0:T(8,128)(2,1)S(1)} %bitcast.169, bf16[768,768]{1,0:T(8,128)(2,1)S(1)} %copy-done.15, bf16[768,768]{1,0:T(8,128)(2,1)S(1)} %copy-done.17), custom_call_target="tpu_custom_call" | custom-call | tf_op jit(solution)/shard_map/pallas_call | solution.py:1185
  366.0 23.7 %shard_map.198 = (bf16[4,256,768]{2,1,0:T(8,128)(2,1)S(1)}, f32[256,768]{1,0:T(8,128)S(1)}, f32[1,768]{1,0:T(1,128)S(1)}, bf16[4,96,768]{2,1,0:T(8,128)(2,1)S(1)...) custom-call(bf16[4,256,768]{2,1,0:T(8,128)(2,1)S(1)} %bitcast.188, ...), custom_call_target="tpu_custom_call" | custom-call | tf_op jit(solution)/shard_map/pallas_call | solution.py:119
  389.8 1.1 copy-done.37
  394.5 1.4 pad_maximum_fusion
  396.2 1.5 sub.41.ids
  398.8 1.4 add_convert_fusion.1
  400.3 1.4 copy-done.38
  401.7 1.3 copy-done.40
  403.0 1.3 copy-done.42
  406.4 13.3 %shard_map.199 = (bf16[1024,768]{1,0:T(8,128)(2,1)S(1)}, bf16[768,768]{1,0:T(8,128)(2,1)S(1)}, f32[8,640]{1,0:T(8,128)S(1)}) custom-call(s32[1]{0:T(128)} %dynamic_slice.37.length, bf16[1024,768]{1,0:T(8,128)(2,1)S(1)} %bitcast.191, bf16[1024,768]{1,0:T(8,128)(2,1)S(1)} %bitcast.175, bf16[768,768]{1,0:T(8,128)(2,1)S(1)} %copy-done.11, ...), custom_call_target="tpu_custom_call" | custom-call | tf_op jit(solution)/shard_map/pallas_call | solution.py:978
  419.7 16.6 %shard_map.200 = (f32[256,768]{1,0:T(8,128)S(1)}, bf16[4,96,384]{2,1,0:T(8,128)(2,1)S(1)}, bf16[4,96,384]{2,1,0:T(8,128)(2,1)S(1)}, bf16[4,96,768]{2,1,0:T(8,128)(2,1)S(1)}, bf16[4,96,768]{2,1,0:T(8,128)(2,1)S(1)}) custom-call(bf16[4,256,768]{2,1,0:T(8,128)(2,1)S(1)} %bitcast.187, bf16[4,2,96,768]{3,2,1,0:T(8,128)(2,1)S(1)} %bitcast.179, ...), custom_call_target="tpu_custom_call" | custom-call | tf_op jit(solution)/shard_map/pallas_call | solution.py:119
  436.9 1.4 pad_maximum_fusion.1
  438.9 9.3 %collective-permute-start.2 = (bf16[192,256]{1,0:T(8,128)(2,1)S(1)}, bf16[192,256]{1,0:T(8,128)(2,1)S(1)}, u32[]{:S(2)}, u32[]{:S(2)}) collective-permute-start(bf16[192,256]{1,0:T(8,128)(2,1)S(1)} %get-tuple-element.211), channel_id=1, source_target_pairs={{0,12},{4,0},{8,4},{12,8},{1,13},{5,1},{9,5},{13,9},{2,14},{6,2},{... | collective-permute-start | bytes 294920 | tf_op jit(solution)/shard_map/ppermute | solution.py:1479
  448.9 19.7 %convolution_convert_fusion = bf16[2048,4096]{1,0:T(8,128)(2,1)} fusion(bf16[2048,768]{1,0:T(8,128)(2,1)} %bitcast.183, bf16[768,4096]{1,0:T(8,128)(2,1)} %all-gather.8.cloned.1.call-done.refs_1_), kind=kOutput, calls=%fused_computation | convolution fusion | flops 12893290496 | bytes 26214400 | tf_op jit(solution)/shard_map/dot_general | solution.py:22
  470.2 26.9 %shard_map.201 = (bf16[8,4,192,256]{3,2,1,0:T(8,128)(2,1)S(1)}, f32[8,32,768]{2,1,0:T(8,128)S(1)}) custom-call(bf16[192,256]{1,0:T(8,128)(2,1)S(1)} %get-tuple-element.214.refs_0_, bf16[192,256]{1,0:T(8,128)(2,1)S(1)} %copy-done.62, bf16[192,256]{1,0:T(8,128)(2,1)S(1)} %collective-permute-done.1.refs_2_, ...), custom_call_target="tpu_custom_call" | custom-call | tf_op jit(solution)/shard_map/pallas_call | solution.py:119
  497.2 3.3 collective-permute-start.5
  501.6 2.1 broadcast_select_fusion.1
  503.8 19.3 %shard_map.202 = f32[192,4096]{1,0:T(8,128)} custom-call(s32[32,256]{1,0:T(8,128)S(1)} %copy-done.60, bf16[8,4,192,256]{3,2,1,0:T(8,128)(2,1)S(1)} %get-tuple-element.155.grads, bf16[192,4096]{1,0:T(8,128)(2,1)S(1)} %copy-done.36), custom_call_target="tpu_custom_call" | custom-call | tf_op jit(solution)/shard_map/pallas_call | solution.py:1266
  525.4 1.6 fusion
  (304 shorter events, 40.7 us)
Async XLA Ops:
  7.2 66.9 %all-gather.4.cloned.1.call-start = ((), (), s32[]{:S(2)}) async-start(), calls=%async_computation.3 | async-start | bytes 1474560 | tf_op jit(solution)/shard_map/all_gather | solution.py:1332
  10.4 95.6 %all-gather.6.cloned.1.call-start = ((), (), s32[]{:S(2)}) async-start(), calls=%async_computation.4 | async-start | bytes 2949120 | tf_op jit(solution)/shard_map/all_gather | solution.py:1333
  13.8 208.9 %all-gather.8.cloned.1.call-start = ((), (), s32[]{:S(2)}) async-start(), calls=%async_computation.5 | async-start | bytes 7864320 | tf_op jit(solution)/shard_map/all_gather | solution.py:1334
  15.2 380.7 %reduce-scatter.4.cloned.1.call-start = ((), (), s32[]{:S(2)}) async-start(), calls=%async_computation.6 | async-start | bytes 7864320 | tf_op jit(solution)/shard_map/reduce_scatter | solution.py:1418
  28.9 24.4 %copy-start.57 = (s32[4,16,128]{2,1,0:T(8,128)}, s32[4,16,128]{2,1,0:T(8,128)S(1)}, u32[]{:S(2)}) copy-start(s32[4,16,128]{2,1,0:T(8,128)S(1)} %broadcast_subtract_fusion) | copy-start | bytes 98308
  72.1 94.9 %copy-start.63 = (f32[3,640]{1,0:T(4,128)}, f32[3,640]{1,0:T(4,128)S(1)}, u32[]{:S(2)}) copy-start(f32[3,640]{1,0:T(4,128)S(1)} %slice.274.taps) | copy-start | bytes 23044
  72.7 17.3 %copy-start.93 = (f32[256]{0:T(256)}, f32[256]{0:T(256)S(1)}, u32[]{:S(2)}) copy-start(f32[256]{0:T(256)S(1)} %multiply_reduce_fusion.2) | copy-start | bytes 3076
  73.9 67.1 %copy-start.65 = (f32[1,768]{1,0:T(1,128)}, f32[1,768]{1,0:T(1,128)S(1)}, u32[]{:S(2)}) copy-start(f32[1,768]{1,0:T(1,128)S(1)} %get-tuple-element.233.refs_2_) | copy-start | bytes 9220
  73.9 105.6 %copy-start.67 = (f32[1,768]{1,0:T(1,128)}, f32[1,768]{1,0:T(1,128)S(1)}, u32[]{:S(2)}) copy-start(f32[1,768]{1,0:T(1,128)S(1)} %get-tuple-element.232.refs_2_) | copy-start | bytes 9220
  167.0 37.3 %copy-start.6 = (bf16[4,256,768]{2,1,0:T(8,128)(2,1)}, bf16[4,256,768]{2,1,0:T(8,128)(2,1)S(1)}, u32[]{:S(2)}) copy-start(bf16[4,256,768]{2,1,0:T(8,128)(2,1)S(1)} %get-tuple-element.100) | copy-start | bytes 4718596
  167.0 37.3 %copy-start.18 = (bf16[768,768]{1,0:T(8,128)(2,1)}, bf16[768,768]{1,0:T(8,128)(2,1)S(1)}, u32[]{:S(2)}) copy-start(bf16[768,768]{1,0:T(8,128)(2,1)S(1)} %get-tuple-element.101.weight) | copy-start | bytes 3538948
  167.0 37.3 %copy-start.24 = (f32[256,768]{1,0:T(8,128)}, f32[256,768]{1,0:T(8,128)S(1)}, u32[]{:S(2)}) copy-start(f32[256,768]{1,0:T(8,128)S(1)} %get-tuple-element.103.refs_1_) | copy-start | bytes 2359300
  167.0 37.3 %copy-start.30 = (bf16[768,384]{1,0:T(8,128)(2,1)}, bf16[768,384]{1,0:T(8,128)(2,1)S(1)}, u32[]{:S(2)}) copy-start(bf16[768,384]{1,0:T(8,128)(2,1)S(1)} %get-tuple-element.107.refs_0_) | copy-start | bytes 1769476
  204.3 16.6 %copy-start.26 = (f32[256,768]{1,0:T(8,128)}, f32[256,768]{1,0:T(8,128)S(1)}, u32[]{:S(2)}) copy-start(f32[256,768]{1,0:T(8,128)S(1)} %get-tuple-element.104.refs_1_) | copy-start | bytes 2359300
  225.4 23.6 %copy-start.88 = (bf16[1,8,2,128]{3,1,2,0:T(8,128)(2,1)S(1)}, bf16[1,8,2,128]{3,1,2,0:T(8,128)(2,1)}, u32[]{:S(2)}) copy-start(bf16[1,8,2,128]{3,1,2,0:T(8,128)(2,1)} %copy.39) | copy-start | bytes 12292
  249.0 22.9 %copy-start.29 = (bf16[8,256,768]{2,1,0:T(8,128)(2,1)}, bf16[8,256,768]{2,1,0:T(8,128)(2,1)S(1)}, u32[]{:S(2)}) copy-start(bf16[8,256,768]{2,1,0:T(8,128)(2,1)S(1)} %get-tuple-element.109) | copy-start | bytes 9437188
  272.8 195.8 %reduce-scatter.6.cloned.1.call-start = ((), (), s32[]{:S(2)}) async-start(), calls=%async_computation.7 | async-start | bytes 2211840 | tf_op jit(solution)/shard_map/reduce_scatter | solution.py:1290
  291.6 30.8 %copy-start.54 = (bf16[1024,256]{1,0:T(8,128)(2,1)S(1)}, bf16[1024,256]{1,0:T(8,128)(2,1)}, u32[]{:S(2)}) copy-start(bf16[1024,256]{1,0:T(8,128)(2,1)} %copy-done.53) | copy-start | bytes 1572868
  291.6 30.8 %copy-start.56 = (f32[1024,128]{1,0:T(8,128)S(1)}, f32[1024,128]{1,0:T(8,128)}, u32[]{:S(2)}) copy-start(f32[1024,128]{1,0:T(8,128)} %copy-done.55) | copy-start | bytes 1572868
  298.5 23.9 %copy-start.7 = (bf16[4,256,768]{2,1,0:T(8,128)(2,1)S(1)}, bf16[4,256,768]{2,1,0:T(8,128)(2,1)}, u32[]{:S(2)}) copy-start(bf16[4,256,768]{2,1,0:T(8,128)(2,1)} %copy-done.6) | copy-start | bytes 4718596
  298.5 23.9 %copy-start.19 = (bf16[768,768]{1,0:T(8,128)(2,1)S(1)}, bf16[768,768]{1,0:T(8,128)(2,1)}, u32[]{:S(2)}) copy-start(bf16[768,768]{1,0:T(8,128)(2,1)} %copy-done.18) | copy-start | bytes 3538948
  298.5 23.9 %copy-start.44 = (bf16[1024,640]{1,0:T(8,128)(2,1)S(1)}, bf16[1024,640]{1,0:T(8,128)(2,1)}, u32[]{:S(2)}) copy-start(bf16[1024,640]{1,0:T(8,128)(2,1)} %copy-done.43) | copy-start | bytes 3932164
  298.5 23.9 %copy-start.46 = (bf16[1024,640]{1,0:T(8,128)(2,1)S(1)}, bf16[1024,640]{1,0:T(8,128)(2,1)}, u32[]{:S(2)}) copy-start(bf16[1024,640]{1,0:T(8,128)(2,1)} %copy-done.45) | copy-start | bytes 3932164
  298.5 23.9 %copy-start.64 = (f32[3,640]{1,0:T(4,128)S(1)}, f32[3,640]{1,0:T(4,128)}, u32[]{:S(2)}) copy-start(f32[3,640]{1,0:T(4,128)} %copy-done.63) | copy-start | bytes 23044
  335.9 23.5 %copy-start.69 = (f32[8,640]{1,0:T(8,128)}, f32[8,640]{1,0:T(8,128)S(1)}, u32[]{:S(2)}) copy-start(f32[8,640]{1,0:T(8,128)S(1)} %get-tuple-element.154.refs_10_) | copy-start | bytes 61444
  336.0 23.5 %copy-start.15 = (bf16[768,768]{1,0:T(8,128)(2,1)S(1)}, bf16[768,768]{1,0:T(8,128)(2,1)}, u32[]{:S(2)}) copy-start(bf16[768,768]{1,0:T(8,128)(2,1)} %copy-done.14) | copy-start | bytes 3538948
  336.0 23.5 %copy-start.17 = (bf16[768,768]{1,0:T(8,128)(2,1)S(1)}, bf16[768,768]{1,0:T(8,128)(2,1)}, u32[]{:S(2)}) copy-start(bf16[768,768]{1,0:T(8,128)(2,1)} %copy-done.16) | copy-start | bytes 3538948
  366.0 23.8 %copy-start.12 = (bf16[768,768]{1,0:T(8,128)(2,1)}, bf16[768,768]{1,0:T(8,128)(2,1)S(1)}, u32[]{:S(2)}) copy-start(bf16[768,768]{1,0:T(8,128)(2,1)S(1)} %get-tuple-element.127) | copy-start | bytes 3538948
  395.9 101.3 %reduce-scatter.8.cloned.1.call-start = ((), (), s32[]{:S(2)}) async-start(), calls=%async_computation.8 | async-start | bytes 2211840 | tf_op jit(solution)/shard_map/reduce_scatter | solution.py:1290
  419.7 16.7 %copy-start.71 = (f32[8,640]{1,0:T(8,128)}, f32[8,640]{1,0:T(8,128)S(1)}, u32[]{:S(2)}) copy-start(f32[8,640]{1,0:T(8,128)S(1)} %get-tuple-element.153.refs_9_) | copy-start | bytes 61444
  419.7 16.6 %copy-start.80 = (f32[768,256]{0,1:T(8,128)S(1)}, f32[768,256]{0,1:T(8,128)}, u32[]{:S(2)}) copy-start(f32[768,256]{0,1:T(8,128)} %copy-done.79) | copy-start | bytes 2359300
  419.7 16.6 %copy-start.85 = (f32[768]{0:T(1024)S(1)}, f32[768]{0:T(1024)}, u32[]{:S(2)}) copy-start(f32[768]{0:T(1024)} %copy-done.84) | copy-start | bytes 9220
  419.7 16.6 %copy-start.92 = (f32[256]{0:T(256)S(1)}, f32[256]{0:T(256)}, u32[]{:S(2)}) copy-start(f32[256]{0:T(256)} %get-tuple-element.246) | copy-start | bytes 3076
  419.7 17.0 %copy-start.94 = (f32[256]{0:T(256)S(1)}, f32[256]{0:T(256)}, u32[]{:S(2)}) copy-start(f32[256]{0:T(256)} %copy-done.93) | copy-start | bytes 3076
  438.9 29.8 %collective-permute-start.2 = (bf16[192,256]{1,0:T(8,128)(2,1)S(1)}, bf16[192,256]{1,0:T(8,128)(2,1)S(1)}, u32[]{:S(2)}, u32[]{:S(2)}) collective-permute-start(bf16[192,256]{1,0:T(8,128)(2,1)S(1)} %get-tuple-element.211), channel_id=1, source_target_pairs={{0,12},{4,0},{8,4},{12,8},{1,13},{5,1},{9,5},{13,9},{2,14},{6,2},{... | collective-permute-start | bytes 294920 | tf_op jit(solution)/shard_map/ppermute | solution.py:1479
  448.2 20.5 %collective-permute-start.1 = (bf16[192,256]{1,0:T(8,128)(2,1)S(1)}, bf16[192,256]{1,0:T(8,128)(2,1)S(1)}, u32[]{:S(2)}, u32[]{:S(2)}) collective-permute-start(bf16[192,256]{1,0:T(8,128)(2,1)S(1)} %get-tuple-element.212), channel_id=1, source_target_pairs={{0,8},{4,12},{8,0},{12,4},{1,9},{5,13},{9,1},{13,5},{2,10},{6,14},... | collective-permute-start | bytes 294920 | tf_op jit(solution)/shard_map/ppermute | solution.py:1479
  448.2 20.4 %copy-start.87 = (f32[768]{0:T(1024)S(1)}, f32[768]{0:T(1024)}, u32[]{:S(2)}) copy-start(f32[768]{0:T(1024)} %get-tuple-element.189) | copy-start | bytes 9220
  448.2 21.1 %copy-start.70 = (f32[8,640]{1,0:T(8,128)S(1)}, f32[8,640]{1,0:T(8,128)}, u32[]{:S(2)}) copy-start(f32[8,640]{1,0:T(8,128)} %copy-done.69) | copy-start | bytes 61444
  448.2 21.1 %copy-start.72 = (f32[8,640]{1,0:T(8,128)S(1)}, f32[8,640]{1,0:T(8,128)}, u32[]{:S(2)}) copy-start(f32[8,640]{1,0:T(8,128)} %copy-done.71) | copy-start | bytes 61444
  448.2 21.1 %copy-start.74 = (f32[1,768]{1,0:T(1,128)S(1)}, f32[1,768]{1,0:T(1,128)}, u32[]{:S(2)}) copy-start(f32[1,768]{1,0:T(1,128)} %copy-done.73) | copy-start | bytes 9220
  448.2 21.1 %copy-start.76 = (f32[1,768]{1,0:T(1,128)S(1)}, f32[1,768]{1,0:T(1,128)}, u32[]{:S(2)}) copy-start(f32[1,768]{1,0:T(1,128)} %copy-done.75) | copy-start | bytes 9220
  448.2 21.1 %copy-start.78 = (f32[1,768]{1,0:T(1,128)S(1)}, f32[1,768]{1,0:T(1,128)}, u32[]{:S(2)}) copy-start(f32[1,768]{1,0:T(1,128)} %copy-done.77) | copy-start | bytes 9220
  448.2 20.4 %collective-permute-start = (bf16[192,256]{1,0:T(8,128)(2,1)S(1)}, bf16[192,256]{1,0:T(8,128)(2,1)S(1)}, u32[]{:S(2)}, u32[]{:S(2)}) collective-permute-start(bf16[192,256]{1,0:T(8,128)(2,1)S(1)} %get-tuple-element.213), channel_id=1, source_target_pairs={{0,4},{4,8},{8,12},{12,0},{1,5},{5,9},{9,13},{13,1},{2,6},{6,10},{... | collective-permute-start | bytes 294920 | tf_op jit(solution)/shard_map/ppermute | solution.py:1479
  468.6 35.2 %copy-start.60 = (s32[32,256]{1,0:T(8,128)S(1)}, s32[32,256]{1,0:T(8,128)}, u32[]{:S(2)}) copy-start(s32[32,256]{1,0:T(8,128)} %sub.41.ids) | copy-start | bytes 98308
  497.2 25.9 %collective-permute-start.5 = (f32[8,768]{1,0:T(8,128)S(1)}, f32[8,768]{1,0:T(8,128)S(1)}, u32[]{:S(2)}, u32[]{:S(2)}) collective-permute-start(f32[8,768]{1,0:T(8,128)S(1)} %pad_maximum_fusion.4), channel_id=1, source_target_pairs={{0,12},{4,0},{8,4},{12,8},{1,13},{5,1},{9,5},{13,9},{2,14},{6,2},{... | collective-permute-start | bytes 73736 | tf_op jit(solution)/shard_map/ppermute | solution.py:1495
  500.5 22.6 %collective-permute-start.4 = (f32[8,768]{1,0:T(8,128)S(1)}, f32[8,768]{1,0:T(8,128)S(1)}, u32[]{:S(2)}, u32[]{:S(2)}) collective-permute-start(f32[8,768]{1,0:T(8,128)S(1)} %pad_maximum_fusion.4), channel_id=1, source_target_pairs={{0,8},{4,12},{8,0},{12,4},{1,9},{5,13},{9,1},{13,5},{2,10},{6,14},... | collective-permute-start | bytes 73736 | tf_op jit(solution)/shard_map/ppermute | solution.py:1495
  501.5 21.6 %collective-permute-start.3 = (f32[8,768]{1,0:T(8,128)S(1)}, f32[8,768]{1,0:T(8,128)S(1)}, u32[]{:S(2)}, u32[]{:S(2)}) collective-permute-start(f32[8,768]{1,0:T(8,128)S(1)} %pad_maximum_fusion.4), channel_id=1, source_target_pairs={{0,4},{4,8},{8,12},{12,0},{1,5},{5,9},{9,13},{13,1},{2,6},{6,10},{... | collective-permute-start | bytes 73736 | tf_op jit(solution)/shard_map/ppermute | solution.py:1495
  503.8 21.6 %collective-permute-start.6 = (bf16[96,2304]{1,0:T(8,128)(2,1)}, bf16[96,2304]{1,0:T(8,128)(2,1)}, u32[]{:S(2)}, u32[]{:S(2)}) collective-permute-start(bf16[96,2304]{1,0:T(8,128)(2,1)} %get-tuple-element.208), channel_id=1, source_target_pairs={{0,16},{16,0},{1,17},{17,1},{2,18},{18,2},{3,19},{19,3},{4,20},{20... | collective-permute-start | bytes 1327112 | tf_op jit(solution)/shard_map/ppermute | solution.py:1506
  (64 other events, 243.2 us)
Sparse Core Ops, SparseCore 0:
  10.6 36.1 all-gather.3
  48.9 57.1 all-gather.5
  108.2 114.3 all-gather.7
  273.0 117.6 reduce-scatter.3
  396.0 44.3 reduce-scatter.5
  442.8 46.2 reduce-scatter.7
